TPU v7x, 32 devices: a whole 2x2x4 slice. The times are simulated.
32 devices in a mesh: seq: 32 (over z, y, x, core).
Axes of the slice: x: 2, y: 2, z: 4, core: 2. Of those that a mesh axis runs over, the one named last changes fastest.
Arguments:
- inputs: bfloat16 [2, 8192, 1536], P(None, 'seq'), may hold values from -8 to 8
- ln_gain: float32 [1536], replicated, may hold values from 0.25 to 1.75
- w_in: bfloat16 [1536, 3072], replicated, may hold values from -0.15625 to 0.15625
- kernel: float32 [32, 1536], replicated, may hold values from -1 to 1
- bn_gain: float32 [1536], replicated, may hold values from 0.25 to 1.75
- bn_bias: float32 [1536], replicated, may hold values from -0.6 to 0.6
- w_out: bfloat16 [1536, 1536], replicated, may hold values from -0.15625 to 0.15625
- cotangent: bfloat16 [2, 8192, 1536], P(None, 'seq'), may hold values from -6 to 6
Outputs:
- outputs: bfloat16 [2, 8192, 1536], P(None, 'seq')
- d_inputs: bfloat16 [2, 8192, 1536], P(None, 'seq')
- d_w_out: float32 [1536, 1536], P('seq')
- d_kernel: float32 [32, 1536], replicated
- d_bn_gain: float32 [1536], replicated
- d_bn_bias: float32 [1536], replicated
All inputs are finite; a program needn't handle non-finite values.
Results may differ from a plain program's by a relative error of at most 0.0075.
Values may be sent and summed in bfloat16 or wider, within the bound.
No kernel may reach another device: no remote copies, remote signals or barrier semaphores. Data moves between devices by JAX's collectives and lax.ppermute only.
A program may use at most 128 MiB of HBM per device.

v0:
```python
import jax
import jax.numpy as jnp
from jax import lax
from jax.sharding import PartitionSpec as P

D = 1536
K = 32
FRAMES_DEV = 256
UTT = 2


EPSILON = 1e-05


def with_halo(block, sides, width):
    for axis, dim in sides:
        count = lax.axis_size(axis)
        forward = [(i, i + 1) for i in range(count - 1)]
        backward = [(target, source) for source, target in forward]
        low = lax.ppermute(
            lax.slice_in_dim(block, block.shape[dim] - width, None, axis=dim), axis, forward
        )
        high = lax.ppermute(lax.slice_in_dim(block, 0, width, axis=dim), axis, backward)
        block = jnp.concatenate([low, block, high], axis=dim)
    return block


def on_device(inputs, ln_gain, w_in, kernel, bn_gain, bn_bias, w_out, cotangent):
    devices_seq = lax.axis_size("seq")
    frame_total = UTT * FRAMES_DEV * devices_seq
    rows_here = UTT * FRAMES_DEV
    x_float = inputs.astype(jnp.float32)
    ln_mean = jnp.mean(x_float, axis=-1, keepdims=True)
    centred = x_float - ln_mean
    ln_rstd = lax.rsqrt(jnp.mean(centred * centred, axis=-1, keepdims=True) + EPSILON)
    ln_hat = centred * ln_rstd
    normed = (ln_hat * ln_gain).astype(jnp.bfloat16).reshape(rows_here, D)
    proj = jnp.dot(normed, w_in, preferred_element_type=jnp.float32)
    value_half = proj[:, :D]
    gate_sig = jax.nn.sigmoid(proj[:, D:])
    gated = (value_half * gate_sig).astype(jnp.bfloat16).reshape(UTT, FRAMES_DEV, D)
    padded = with_halo(gated, (("seq", 1),), 16)
    conv_out = jnp.zeros((UTT, FRAMES_DEV, D), jnp.float32)
    for tap_index in range(K):
        conv_out = conv_out + kernel[tap_index] * padded[
            :, tap_index + 1 : tap_index + 1 + FRAMES_DEV
        ].astype(jnp.float32)
    first_sum, square_sum = lax.psum(
        (jnp.sum(conv_out, axis=(0, 1)), jnp.sum(conv_out * conv_out, axis=(0, 1))), "seq"
    )
    bn_mean = first_sum / frame_total
    bn_var = square_sum / frame_total - bn_mean * bn_mean
    deviate = conv_out - bn_mean
    bn_rstd = lax.rsqrt(bn_var + EPSILON)
    normed_bn = deviate * bn_rstd
    bn_out = normed_bn * bn_gain + bn_bias
    act_sig = jax.nn.sigmoid(bn_out)
    act = (bn_out * act_sig).astype(jnp.bfloat16).reshape(rows_here, D)
    branch = lax.dot_general(
        act, w_out, (((1,), (1,)), ((), ())), preferred_element_type=jnp.float32
    )
    outputs = (
        (x_float.reshape(rows_here, D) + branch).astype(jnp.bfloat16).reshape(UTT, FRAMES_DEV, D)
    )
    cot_rows = cotangent.reshape(rows_here, D)
    d_w_out = lax.psum_scatter(
        lax.dot_general(
            cot_rows, act, (((0,), (0,)), ((), ())), preferred_element_type=jnp.float32
        ),
        "seq",
        scatter_dimension=0,
        tiled=True,
    )
    d_act = jnp.dot(cot_rows, w_out, preferred_element_type=jnp.float32)
    d_bn = d_act.reshape(UTT, FRAMES_DEV, D) * (act_sig + bn_out * act_sig * (1.0 - act_sig))
    scaled_grad = d_bn * bn_gain
    local_bias = jnp.sum(d_bn, axis=(0, 1))
    local_gain = jnp.sum(d_bn * normed_bn, axis=(0, 1))
    d_bn_bias, d_bn_gain = lax.psum((local_bias, local_gain), "seq")
    mean_grad = bn_gain * d_bn_bias / frame_total
    mean_cross = bn_gain * d_bn_gain / frame_total
    d_conv = bn_rstd * (scaled_grad - mean_grad - normed_bn * mean_cross)
    kernel_rows = []
    for tap_index in range(K):
        window = padded[:, tap_index + 1 : tap_index + 1 + FRAMES_DEV].astype(jnp.float32)
        kernel_rows.append(jnp.sum(window * d_conv, axis=(0, 1)))
    d_kernel = lax.psum(jnp.stack(kernel_rows), "seq")
    grad_padded = with_halo(d_conv.astype(jnp.bfloat16), (("seq", 1),), 16).astype(d_conv.dtype)
    d_gated = jnp.zeros((UTT, FRAMES_DEV, D), jnp.float32)
    for tap_index in range(K):
        d_gated = (
            d_gated
            + kernel[tap_index] * grad_padded[:, 31 - tap_index : 31 - tap_index + FRAMES_DEV]
        )
    d_gated = d_gated.reshape(rows_here, D)
    d_value = d_gated * gate_sig
    d_gate = d_gated * value_half * gate_sig * (1.0 - gate_sig)
    d_proj = jnp.concatenate([d_value, d_gate], axis=-1).astype(jnp.bfloat16)
    d_normed = lax.dot_general(
        d_proj, w_in, (((1,), (1,)), ((), ())), preferred_element_type=jnp.float32
    )
    d_hat = d_normed.reshape(UTT, FRAMES_DEV, D) * ln_gain
    d_layer = ln_rstd * (
        d_hat
        - jnp.mean(d_hat, axis=-1, keepdims=True)
        - ln_hat * jnp.mean(d_hat * ln_hat, axis=-1, keepdims=True)
    )
    d_inputs = (cotangent.astype(jnp.float32) + d_layer).astype(jnp.bfloat16)
    return (outputs, d_inputs, d_w_out, d_kernel, d_bn_gain, d_bn_bias)


def solution(mesh):
    return jax.shard_map(
        on_device,
        mesh=mesh,
        in_specs=(P(None, "seq", None), P(), P(), P(), P(), P(), P(), P(None, "seq", None)),
        out_specs=(P(None, "seq", None), P(None, "seq", None), P("seq", None), P(), P(), P()),
        check_vma=False,
    )
```

profile of v0, /device:TPU:0, one launch (start us, length us, event | category | flops | bytes accessed | tf_op | source)
XLA Modules:
  0.0 447.8 jit_solution(8399221036135349046)
XLA Ops:
  7.2 0.0 copy-start.1
  7.2 0.0 copy-start.18
  7.2 0.0 all-reduce.4.cloned.1.call-start
  7.2 1.8 convert_reduce_fusion
  9.1 2.0 multiply_reduce_fusion.4
  11.0 0.5 multiply_convert_fusion.1
  11.6 0.0 copy-done.22
  11.6 7.6 %fusion.148 = f32[512,3072]{1,0:T(8,128)S(1)} fusion(bf16[512,1536]{1,0:T(8,128)(2,1)S(1)} %bitcast.52, bf16[1536,3072]{1,0:T(8,128)(2,1)} %param.10), kind=kOutput, calls=%fused_computation.332 | convolution fusion | flops 4831838208 | bytes 17301504 | tf_op jit(solution)/shard_map/dot_general | solution.py:38
  19.2 0.0 copy-start.5
  19.2 0.8 multiply_convert_fusion
  20.0 1.7 copy-done
  21.8 2.4 collective-permute-start
  24.2 1.3 collective-permute-start.1
  25.5 0.3 slice_reduce_fusion.31
  25.8 0.2 slice_reduce_fusion.30
  26.1 3.4 collective-permute-done.1
  29.5 16.3 %fusion.144 = (f32[1536]{0:T(1024)}, f32[1536]{0:T(1024)}, f32[2,256,1536]{2,1,0:T(8,128)}) fusion(bf16[2,16,1536]{2,1,0:T(8,128)(2,1)S(1)} %collective-permute-done.1, bf16[2,256,1536]{2,1,0:T(8,128)(2,1)S(1)} %bitcast.41, f32[1536]{0:T(1024)S(1)} %get-tuple-element.84, f32[1536]{0:T(1024)S(1)} %get-tuple-element.85, f32[1536]{0:T(1024)S(1)} %get-tuple-element.55, ...), kind=kLoop, calls=%fused_computation.329 | loop fusion | flops 150205440 | bytes 5124096 | tf_op jit(solution)/shard_map/reduce_sum | solution.py:49
  45.8 43.9 %all-reduce.1 = (f32[1536]{0:T(1024)}, f32[1536]{0:T(1024)}) all-reduce(f32[1536]{0:T(1024)} %get-tuple-element.53, f32[1536]{0:T(1024)} %get-tuple-element.52), channel_id=1, replica_groups=mesh['seq'=32] {'seq'}, use_global_device_ids=true, to_apply=%region_5.0 | all-reduce | flops 3072 | bytes 24576 | tf_op jit(solution)/shard_map/psum | solution.py:48
  89.7 0.7 broadcast_multiply_fusion
  90.5 10.3 %fusion.143 = (f32[1536]{0:T(1024)}, f32[1536]{0:T(1024)}, bf16[2,256,1536]{2,1,0:T(8,128)(2,1)}, f32[2,256,1536]{2,1,0:T(8,128)}) fusion(f32[1536]{0:T(1024)S(1)} %get-tuple-element.103, f32[2,256,1536]{2,1,0:T(8,128)} %get-tuple-element.91, f32[1536]{0:T(1024)S(1)} %get-tuple-element.102, f32[1536]{0:T(1024)} %param.13, f32[1536]{0:T(1024)} %param.12, ...), kind=kOutput, calls=%fused_computation.328 | convolution fusion | flops 2428498944 | bytes 14192640 | tf_op jit(solution)/shard_map/dot_general | solution.py:74
  100.8 41.3 %all-reduce = (f32[1536]{0:T(1024)}, f32[1536]{0:T(1024)}) all-reduce(f32[1536]{0:T(1024)} %get-tuple-element.51, f32[1536]{0:T(1024)} %get-tuple-element.50), channel_id=1, replica_groups=mesh['seq'=32] {'seq'}, use_global_device_ids=true, to_apply=%region_9.0 | all-reduce | flops 3072 | bytes 24576 | tf_op jit(solution)/shard_map/psum | solution.py:79
  142.1 0.7 multiply_multiply_fusion.1
  142.8 8.6 %fusion.67 = (f32[1536]{0:T(1024)S(1)}, f32[1536]{0:T(1024)S(1)}, f32[1536]{0:T(1024)S(1)}, f32[1536]{0:T(1024)S(1)}, f32[1536]{0:T(1024)S(1)}, /*index=5*/f32[1...) fusion(bf16[2,16,1536]{2,1,0:T(8,128)(2,1)S(1)} %collective-permute-done.1, ...), kind=kLoop, calls=%fused_computation.160 | loop fusion | flops 47958528 | bytes 11194368 | tf_op jit(solution)/shard_map/reduce_sum | solution.py:86
  151.4 0.6 stack.130
  152.0 0.6 stack.129
  152.6 0.6 stack.128
  153.2 0.6 stack.127
  153.8 0.6 stack.126
  154.4 0.6 stack.125
  155.0 0.6 stack.124
  155.6 0.6 stack.123
  156.2 0.6 stack.122
  156.8 5.5 %fusion.52 = (f32[1536]{0:T(1024)S(1)}, f32[1536]{0:T(1024)S(1)}, f32[1536]{0:T(1024)S(1)}, f32[1536]{0:T(1024)S(1)}, f32[1536]{0:T(1024)S(1)}, /*index=5*/f32[1...) fusion(f32[2,256,1536]{2,1,0:T(8,128)S(1)} %get-tuple-element.90, ...), kind=kLoop, calls=%fused_computation.145 | loop fusion | flops 40095744 | bytes 12730368 | tf_op jit(solution)/shard_map/reduce_sum | solution.py:86
  162.3 4.1 fusion.44
  166.5 0.0 copy-start.33
  166.5 0.0 copy-start.34
  166.5 2.8 fusion.35
  169.7 2.8 stack.131
  172.5 0.0 all-reduce.4.cloned.1.call-update
  172.5 0.0 reduce-scatter.4.cloned.1.call-start
  172.5 8.2 %convolution_bitcast_fusion = f32[1536,1536]{0,1:T(8,128)} fusion(bf16[2,256,1536]{2,1,0:T(8,128)(2,1)} %get-tuple-element.94, bf16[2,256,1536]{2,1,0:T(8,128)(2,1)} %param.15), kind=kOutput, calls=%fused_computation.29 | convolution fusion | flops 2415919104 | bytes 12582912 | tf_op jit(solution)/shard_map/dot_general | solution.py:67
  180.7 9.7 %copy.19 = f32[1536,1536]{1,0:T(8,128)} copy(f32[1536,1536]{0,1:T(8,128)} %convolution_bitcast_fusion) | data formatting | bytes 18874368
  190.4 0.0 reduce-scatter.4.cloned.1.call-update
  190.4 1.4 copy-done.3
  191.8 1.5 collective-permute-start.2
  193.3 1.5 collective-permute-start.3
  194.9 6.6 %fusion.110 = bf16[512,1536]{1,0:T(8,128)(2,1)} fusion(bf16[512,1536]{1,0:T(8,128)(2,1)} %bitcast.53, bf16[1536,1536]{1,0:T(8,128)(2,1)} %param.14, bf16[512,1536]{1,0:T(8,128)(2,1)S(1)} %bitcast.50), kind=kOutput, calls=%fused_computation.250 | convolution fusion | flops 2418278400 | bytes 9437184 | tf_op jit(solution)/shard_map/dot_general | solution.py:59
  201.5 0.5 maximum_convert_fusion
  202.0 0.2 copy-done.7
  202.2 0.0 copy-done.9
  202.2 0.0 copy-done.11
  202.2 0.0 copy-done.13
  202.2 0.0 copy-done.15
  202.2 0.0 copy-done.17
  202.3 12.4 %fusion.68 = f32[2,256,1536]{2,1,0:T(8,128)S(1)} fusion(f32[2,288,1536]{2,1,0:T(8,128)S(1)} %maximum_convert_fusion, f32[1536]{0:T(1024)S(1)} %copy-done.15, f32[1536]{0:T(1024)S(1)} %copy-done.17, f32[1536]{0:T(1024)S(1)} %get-tuple-element.55, f32[1536]{0:T(1024)S(1)} %get-tuple-element.56, f32[1536]{0:T(1024)S(1)} %get-tuple-element.57, ...), kind=kLoop, calls=%fused_computation.162 | loop fusion | flops 49545216 | bytes 104005632 | tf_op jit(solution)/shard_map/add | solution.py:92
  214.7 0.0 copy-start.19
  214.7 1.6 fusion.106
  216.3 8.9 %multiply_reduce_fusion.1 = (f32[512]{0:T(512)S(1)}, f32[512,1536]{1,0:T(8,128)}) fusion(f32[1536]{0:T(1024)S(1)} %copy-done.19, bf16[1536,3072]{1,0:T(8,128)(2,1)} %param.10, bf16[512,1536]{1,0:T(8,128)(2,1)S(1)} %get-tuple-element.93, bf16[512,1536]{1,0:T(8,128)(2,1)S(1)} %get-tuple-element.92), kind=kOutput, calls=%fused_computation.240 | convolution fusion | flops 4839702016 | bytes 15736832 | tf_op jit(solution)/shard_map/dot_general | solution.py:99
  225.3 2.8 multiply_reduce_fusion
  228.1 0.5 copy-done.2
  228.5 2.4 add_convert_fusion
  231.0 65.4 %all-reduce.4.cloned.1.call-done = f32[32,1536]{1,0:T(8,128)} async-done(((f32[32,1536]{1,0:T(8,128)}), f32[32,1536]{1,0:T(8,128)}) %all-reduce.4.cloned.1.call-update) | async-done | bytes 196624 | tf_op jit(solution)/shard_map/psum | solution.py:87
  296.3 143.1 %reduce-scatter.4.cloned.1.call-done = f32[48,1536]{1,0:T(8,128)} async-done(((f32[1536,1536]{1,0:T(8,128)}), f32[48,1536]{1,0:T(8,128)}) %reduce-scatter.4.cloned.1.call-update) | async-done | bytes 294928
  439.4 1.6 copy.22
  (97 shorter events, 0.4 us)
Async XLA Ops:
  7.2 3.9 copy-start.1
  7.2 3.9 copy-start.18
  7.2 289.1 %all-reduce.4.cloned.1.call-start = ((), (), s32[]{:S(2)}) async-start(), calls=%async_computation.1 | async-start | bytes 393216 | tf_op jit(solution)/shard_map/psum | solution.py:87
  9.0 2.6 copy-start.20
  11.0 0.6 copy-start.22
  19.2 2.6 copy-start
  19.2 6.3 %copy-start.5 = (f32[32,1536]{1,0:T(8,128)S(1)}, f32[32,1536]{1,0:T(8,128)}, u32[]{:S(2)}) copy-start(f32[32,1536]{1,0:T(8,128)} %param.11) | copy-start | bytes 589828
  21.8 4.3 collective-permute-start
  24.2 5.3 %collective-permute-start.1 = (bf16[2,16,1536]{2,1,0:T(8,128)(2,1)S(1)}, bf16[2,16,1536]{2,1,0:T(8,128)(2,1)S(1)}, u32[]{:S(2)}, u32[]{:S(2)}) collective-permute-start(bf16[2,16,1536]{2,1,0:T(8,128)(2,1)S(1)} %get-tuple-element.99), channel_id=1, source_target_pairs={{1,0},{2,1},{3,2},{4,3},{5,4},{6,5},{7,6},{8,7},{9,8},{10,9},{11,1... | collective-permute-start | bytes 294920 | tf_op jit(solution)/shard_map/ppermute | solution.py:23
  26.0 3.5 copy-start.6
  26.0 19.8 %copy-start.8 = (f32[1536]{0:T(1024)}, f32[1536]{0:T(1024)S(1)}, u32[]{:S(2)}) copy-start(f32[1536]{0:T(1024)S(1)} %get-tuple-element.81) | copy-start | bytes 18436
  26.0 19.8 %copy-start.10 = (f32[1536]{0:T(1024)}, f32[1536]{0:T(1024)S(1)}, u32[]{:S(2)}) copy-start(f32[1536]{0:T(1024)S(1)} %get-tuple-element.82) | copy-start | bytes 18436
  26.1 19.8 %copy-start.12 = (f32[1536]{0:T(1024)}, f32[1536]{0:T(1024)S(1)}, u32[]{:S(2)}) copy-start(f32[1536]{0:T(1024)S(1)} %get-tuple-element.83) | copy-start | bytes 18436
  26.1 19.7 %copy-start.14 = (f32[1536]{0:T(1024)}, f32[1536]{0:T(1024)S(1)}, u32[]{:S(2)}) copy-start(f32[1536]{0:T(1024)S(1)} %get-tuple-element.84) | copy-start | bytes 18436
  26.1 19.7 %copy-start.16 = (f32[1536]{0:T(1024)}, f32[1536]{0:T(1024)S(1)}, u32[]{:S(2)}) copy-start(f32[1536]{0:T(1024)S(1)} %get-tuple-element.85) | copy-start | bytes 18436
  90.5 10.3 %copy-start.24 = (f32[1536]{0:T(1024)}, f32[1536]{0:T(1024)S(1)}, u32[]{:S(2)}) copy-start(f32[1536]{0:T(1024)S(1)} %get-tuple-element.102) | copy-start | bytes 18436
  90.5 10.3 %copy-start.25 = (f32[1536]{0:T(1024)}, f32[1536]{0:T(1024)S(1)}, u32[]{:S(2)}) copy-start(f32[1536]{0:T(1024)S(1)} %get-tuple-element.103) | copy-start | bytes 18436
  142.8 14.0 %slice-start = ((s8[6291456]{0:T(1024)(128)(4,1)}), s8[4194304]{0:T(1024)(128)(4,1)S(1)}, s32[]{:S(2)}) async-start(s8[6291456]{0:T(1024)(128)(4,1)} %bitcast.46), calls=%async_computation.3 | async-start | bytes 8388608
  142.8 14.0 %slice-start.1 = ((s8[6291456]{0:T(1024)(128)(4,1)}), s8[2097152]{0:T(1024)(128)(4,1)S(1)}, s32[]{:S(2)}) async-start(s8[6291456]{0:T(1024)(128)(4,1)} %bitcast.46), calls=%async_computation.4 | async-start | bytes 4194304
  166.4 3.2 copy-start.26
  166.4 3.2 copy-start.27
  166.4 3.2 copy-start.28
  166.4 3.2 copy-start.29
  166.4 3.2 copy-start.30
  166.4 3.2 copy-start.31
  166.5 3.2 copy-start.32
  166.5 3.2 copy-start.33
  166.5 3.2 copy-start.34
  172.5 266.9 %reduce-scatter.4.cloned.1.call-start = ((), (), s32[]{:S(2)}) async-start(), calls=%async_computation.2 | async-start | bytes 9732096
  190.4 1.4 copy-start.3
  191.8 9.7 %collective-permute-start.2 = (bf16[2,16,1536]{2,1,0:T(8,128)(2,1)S(1)}, bf16[2,16,1536]{2,1,0:T(8,128)(2,1)S(1)}, u32[]{:S(2)}, u32[]{:S(2)}) collective-permute-start(bf16[2,16,1536]{2,1,0:T(8,128)(2,1)S(1)} %get-tuple-element.96), channel_id=1, source_target_pairs={{0,1},{1,2},{2,3},{3,4},{4,5},{5,6},{6,7},{7,8},{8,9},{9,10},{10,1... | collective-permute-start | bytes 294920 | tf_op jit(solution)/shard_map/ppermute | solution.py:20
  193.3 8.2 %collective-permute-start.3 = (bf16[2,16,1536]{2,1,0:T(8,128)(2,1)S(1)}, bf16[2,16,1536]{2,1,0:T(8,128)(2,1)S(1)}, u32[]{:S(2)}, u32[]{:S(2)}) collective-permute-start(bf16[2,16,1536]{2,1,0:T(8,128)(2,1)S(1)} %get-tuple-element.97), channel_id=1, source_target_pairs={{1,0},{2,1},{3,2},{4,3},{5,4},{6,5},{7,6},{8,7},{9,8},{10,9},{11,1... | collective-permute-start | bytes 294920 | tf_op jit(solution)/shard_map/ppermute | solution.py:23
  201.5 0.7 copy-start.7
  201.5 0.7 copy-start.9
  201.5 0.7 copy-start.11
  201.5 0.7 copy-start.13
  201.5 0.8 copy-start.15
  201.5 0.8 copy-start.17
  201.5 13.1 %slice-start.2 = ((s8[6291456]{0:T(1024)(128)(4,1)}), s8[4194304]{0:T(1024)(128)(4,1)S(1)}, s32[]{:S(2)}) async-start(s8[6291456]{0:T(1024)(128)(4,1)} %bitcast.48), calls=%async_computation.5 | async-start | bytes 8388608
  202.3 12.4 %slice-start.3 = ((s8[6291456]{0:T(1024)(128)(4,1)}), s8[2097152]{0:T(1024)(128)(4,1)S(1)}, s32[]{:S(2)}) async-start(s8[6291456]{0:T(1024)(128)(4,1)} %bitcast.48), calls=%async_computation.6 | async-start | bytes 4194304
  214.7 1.6 copy-start.19
  216.3 9.0 %copy-start.21 = (f32[2,256]{1,0:T(2,128)S(1)}, f32[2,256]{1,0:T(2,128)}, u32[]{:S(2)}) copy-start(f32[2,256]{1,0:T(2,128)} %copy-done.20) | copy-start | bytes 6148
  216.3 9.0 %copy-start.23 = (f32[2,256]{1,0:T(2,128)S(1)}, f32[2,256]{1,0:T(2,128)}, u32[]{:S(2)}) copy-start(f32[2,256]{1,0:T(2,128)} %copy-done.22) | copy-start | bytes 6148
  225.2 2.8 copy-start.4
  225.2 3.3 copy-start.2
Sparse Core Ops, SparseCore 0:
  172.6 123.6 all-reduce.3
  302.8 136.5 reduce-scatter.3
where the time goes:
time: 449 us; the launch traced here: 448 us
  waiting for transfers between devices  212 us (47%)
  blocking collectives  85.2 us (19%)
  other arithmetic  63.5 us (14%)
  matrix products  41.6 us (9%)
  local copies, waits for them, and re-layouts  24.1 us (5%)
  between operations  14.8 us (3%)
  starting transfers between devices  6.78 us (2%)
    unnamed x3, waiting for transfers between devices  143 us
    psum x1, waiting for transfers between devices, on_device(): d_kernel = lax.psum(jnp.stack(kernel_rows), 'seq')  65.4 us
    psum x1, blocking collectives, on_device(): lax.psum((jnp.sum(conv_out, axis=(0, 1)), jnp.sum(conv_out * conv_out, ax...  43.9 us
    psum x1, blocking collectives, on_device(): d_bn_bias, d_bn_gain = lax.psum((local_bias, local_gain), 'seq')  41.3 us
    reduce_sum x4, other arithmetic, on_device(): kernel_rows.append(jnp.sum(window * d_conv, axis=(0, 1)))  21 us
    reduce_sum x1, other arithmetic, on_device(): jnp.sum(conv_out, axis=(0, 1))  16.3 us
    unnamed x80, local copies, waits for them, and re-layouts  15.3 us
    add x1, other arithmetic, on_device(): d_gated + kernel[tap_index] * grad_padded[:, 31 - tap_index:31 - tap_inde...  12.4 us
  transfers between devices with their start and end apart: 6, of which 3 were waited for; matrix products, arithmetic and copies ran while one was open for 12% of the time, Pallas kernels for 0%

commit v1 on v0

v1 whole, which is shorter than its diff:
```python
import functools

import jax
import jax.numpy as jnp
from jax import lax
from jax.experimental import pallas as pl
from jax.experimental.pallas import tpu as pltpu
from jax.sharding import PartitionSpec as P

EPSILON = 1e-05
BF = jnp.bfloat16
F32 = jnp.float32
LANES = 128
PAD = 16
MIB = 1 << 20


def params(mib):
    return pltpu.CompilerParams(
        vmem_limit_bytes=mib * MIB, dimension_semantics=("arbitrary",)
    )


def resident(shape):
    return pl.BlockSpec(shape, lambda j: (0,) * len(shape))


def columns(shape, width):
    return pl.BlockSpec(shape[:-1] + (width,), lambda j: (0,) * (len(shape) - 1) + (j,))


def front_body(x_ref, gain_ref, wv_ref, wg_ref, gated_ref, p_ref, q_ref, normed_ref):
    rows, d = x_ref.shape

    @pl.when(pl.program_id(0) == 0)
    def _():
        def step(i, _):
            r = pl.multiple_of(i * 16, 16)
            x = x_ref[pl.ds(r, 16), :].astype(F32)
            mu = jnp.sum(x, axis=-1, keepdims=True) * (1.0 / d)
            c = x - mu
            var = jnp.sum(c * c, axis=-1, keepdims=True) * (1.0 / d)
            hat = c * lax.rsqrt(var + EPSILON)
            normed_ref[pl.ds(r, 16), :] = (hat * gain_ref[...]).astype(BF)
            return 0

        lax.fori_loop(0, rows // 16, step, 0, unroll=4)

    value = jnp.dot(normed_ref[...], wv_ref[...], preferred_element_type=F32)
    gate = jnp.dot(normed_ref[...], wg_ref[...], preferred_element_type=F32)
    sig = jax.nn.sigmoid(gate)
    gated = value * sig
    gated_ref[...] = gated.astype(BF)
    p_ref[...] = sig.astype(BF)
    q_ref[...] = (gated * (1.0 - sig)).astype(BF)


def front(x, gain, w_in):
    rows, d = x.shape
    cw = 256
    steps = d // cw
    out = jax.ShapeDtypeStruct((rows, d), BF)
    return pl.pallas_call(
        front_body,
        grid=(steps,),
        in_specs=[
            resident((rows, d)),
            resident((1, d)),
            pl.BlockSpec((d, cw), lambda j: (0, j)),
            pl.BlockSpec((d, cw), lambda j: (0, j + steps)),
        ],
        out_specs=[columns((rows, d), cw)] * 3,
        out_shape=[out] * 3,
        scratch_shapes=[pltpu.VMEM((rows, d), BF)],
        compiler_params=params(32),
        cost_estimate=pl.CostEstimate(
            flops=4 * rows * d * d, bytes_accessed=4 * d * d + 8 * rows * d, transcendentals=rows * d
        ),
        name="front",
    )(x, gain, w_in, w_in)


def conv_body(g_ref, lo_ref, hi_ref, k_ref, conv_ref, sums_ref, pad_ref):
    utt, frames, cw = g_ref.shape
    taps = k_ref.shape[0]
    block = 64
    for l in range(cw // LANES):
        lanes = slice(l * LANES, (l + 1) * LANES)
        for u in range(utt):
            pad_ref[u, 0:PAD, :] = lo_ref[u, :, lanes].astype(F32)
            pad_ref[u, PAD : PAD + frames, :] = g_ref[u, :, lanes].astype(F32)
            pad_ref[u, PAD + frames : PAD + frames + PAD, :] = hi_ref[u, :, lanes].astype(F32)
            pad_ref[u, 2 * PAD + frames :, :] = jnp.zeros((8, LANES), F32)
        per = frames // block

        def step(i, carry):
            first, square = carry
            u = i // per
            base = pl.multiple_of((i % per) * block, block)
            acc = jnp.zeros((block, LANES), F32)
            for r in range(8):
                w = pad_ref[u, pl.ds(base + r + 1, block + taps - 8), :]
                for q in range(taps // 8):
                    acc = acc + k_ref[8 * q + r, lanes][None, :] * w[8 * q : 8 * q + block]
            conv_ref[u, pl.ds(base, block), lanes] = acc
            part = acc.reshape(block // 8, 8, LANES)
            return first + jnp.sum(part, axis=0), square + jnp.sum(part * part, axis=0)

        zero = jnp.zeros((8, LANES), F32)
        first, square = lax.fori_loop(0, utt * per, step, (zero, zero))
        sums_ref[0:1, lanes] = jnp.sum(first, axis=0, keepdims=True)
        sums_ref[1:2, lanes] = jnp.sum(square, axis=0, keepdims=True)


def conv(gated, lo, hi, kernel):
    utt, frames, d = gated.shape
    cw = 256
    return pl.pallas_call(
        conv_body,
        grid=(d // cw,),
        in_specs=[
            columns(gated.shape, cw),
            columns(lo.shape, cw),
            columns(hi.shape, cw),
            columns(kernel.shape, cw),
        ],
        out_specs=[columns(gated.shape, cw), columns((2, d), cw)],
        out_shape=[
            jax.ShapeDtypeStruct(gated.shape, F32),
            jax.ShapeDtypeStruct((2, d), F32),
        ],
        scratch_shapes=[pltpu.VMEM((utt, frames + 2 * PAD + 8, LANES), F32)],
        compiler_params=params(32),
        cost_estimate=pl.CostEstimate(
            flops=64 * gated.size, bytes_accessed=6 * gated.size, transcendentals=0
        ),
        name="conv",
    )(gated, lo, hi, kernel)


def middle_body(
    n, total, me_ref, conv_ref, sums_ref, gain_ref, bias_ref, cot_ref, w_ref,
    act_ref, dbn_ref, dsums_ref, dw_ref, cot_t, dw_s,
):
    rows, d = cot_ref.shape
    me = me_ref[0]

    @pl.when(pl.program_id(0) == 0)
    def _():
        cot_t[...] = cot_ref[...].T

    mean = sums_ref[0:1, :] * (1.0 / total)
    var = sums_ref[1:2, :] * (1.0 / total) - mean * mean
    rstd = lax.rsqrt(var + EPSILON)
    xhat = (conv_ref[...] - mean) * rstd
    out = xhat * gain_ref[...] + bias_ref[...]
    sig = jax.nn.sigmoid(out)
    act = out * sig
    act_bf = act.astype(BF)
    act_ref[...] = act_bf
    dw = jnp.dot(cot_t[...], act_bf, preferred_element_type=F32)
    if dw_s is None:
        dw_ref[...] = dw
    else:
        dw_s[...] = dw.astype(BF).reshape(dw_s.shape)
        for j in range(n):
            dw_ref[j] = dw_s[lax.bitwise_xor(me, j)]
    d_act = jnp.dot(cot_ref[...], w_ref[...], preferred_element_type=F32)
    dbn = d_act * (sig + act * (1.0 - sig))
    dbn_ref[...] = dbn
    dsums_ref[0:1, :] = jnp.sum(dbn, axis=0, keepdims=True)
    dsums_ref[1:2, :] = jnp.sum(dbn * xhat, axis=0, keepdims=True)


def middle(n, total, me, conv_out, sums, gain, bias, cot, w_out, by_owner):
    rows, d = cot.shape
    cw = 256
    if by_owner:
        dw_shape, dw_type = (n, d // n, d), BF
        scratch = [pltpu.VMEM((d, rows), BF), pltpu.VMEM((n, d // n, cw), BF)]
        body = functools.partial(middle_body, n, total)
    else:
        dw_shape, dw_type = (d, d), F32
        scratch = [pltpu.VMEM((d, rows), BF)]
        body = lambda *refs: middle_body(n, total, *refs, None)
    return pl.pallas_call(
        body,
        grid=(d // cw,),
        in_specs=[
            pl.BlockSpec(memory_space=pltpu.SMEM),
            columns((rows, d), cw),
            columns((2, d), cw),
            columns((1, d), cw),
            columns((1, d), cw),
            resident((rows, d)),
            columns((d, d), cw),
        ],
        out_specs=[
            columns((rows, d), cw),
            columns((rows, d), cw),
            columns((2, d), cw),
            columns(dw_shape, cw),
        ],
        out_shape=[
            jax.ShapeDtypeStruct((rows, d), BF),
            jax.ShapeDtypeStruct((rows, d), F32),
            jax.ShapeDtypeStruct((2, d), F32),
            jax.ShapeDtypeStruct(dw_shape, dw_type),
        ],
        scratch_shapes=scratch,
        compiler_params=params(40),
        cost_estimate=pl.CostEstimate(
            flops=4 * rows * d * d, bytes_accessed=4 * d * d + 12 * rows * d, transcendentals=rows * d
        ),
        name="middle",
    )(me, conv_out, sums, gain, bias, cot, w_out)


def branch_body(x_ref, act_ref, w_ref, out_ref):
    branch = lax.dot_general(
        act_ref[...], w_ref[...], (((1,), (1,)), ((), ())), preferred_element_type=F32
    )
    out_ref[...] = (x_ref[...].astype(F32) + branch).astype(BF)


def branch(x, act, w_out):
    rows, d = x.shape
    cw = 256
    return pl.pallas_call(
        branch_body,
        grid=(d // cw,),
        in_specs=[
            columns((rows, d), cw),
            resident((rows, d)),
            pl.BlockSpec((cw, d), lambda j: (j, 0)),
        ],
        out_specs=columns((rows, d), cw),
        out_shape=jax.ShapeDtypeStruct((rows, d), BF),
        compiler_params=params(24),
        cost_estimate=pl.CostEstimate(
            flops=2 * rows * d * d, bytes_accessed=2 * d * d + 6 * rows * d, transcendentals=0
        ),
        name="branch",
    )(x, act, w_out)


def back_conv_body(
    total, edge_ref, dbn_ref, conv_ref, dlo_ref, dhi_ref, clo_ref, chi_ref, sums_ref, dsums_ref,
    gain_ref, k_ref, g_ref, p_ref, q_ref, dk_ref, dv_ref, dg_ref, pad_ref, kacc_ref,
):
    utt, frames, cw = g_ref.shape
    taps = k_ref.shape[0]
    block = 64
    per = frames // block
    mean = sums_ref[0:1, :] * (1.0 / total)
    var = sums_ref[1:2, :] * (1.0 / total) - mean * mean
    rstd = lax.rsqrt(var + EPSILON)
    gain = gain_ref[...]
    a = rstd * gain
    b = a * rstd * (dsums_ref[1:2, :] * (1.0 / total))
    mean_grad = a * (dsums_ref[0:1, :] * (1.0 / total))
    keep_lo = edge_ref[0]
    keep_hi = edge_ref[1]
    for l in range(cw // LANES):
        lanes = slice(l * LANES, (l + 1) * LANES)
        al, bl, ml, meanl = a[:, lanes], b[:, lanes], mean_grad[:, lanes], mean[:, lanes]

        def d_conv(dbn, conv):
            return dbn.astype(F32) * al - ml - (conv.astype(F32) - meanl) * bl

        for u in range(utt):
            pad_ref[u, 0:PAD, :] = d_conv(dlo_ref[u, :, lanes], clo_ref[u, :, lanes]) * keep_lo
            pad_ref[u, PAD : PAD + frames, :] = d_conv(dbn_ref[u, :, lanes], conv_ref[u, :, lanes])
            pad_ref[u, PAD + frames : PAD + frames + PAD, :] = (
                d_conv(dhi_ref[u, :, lanes], chi_ref[u, :, lanes]) * keep_hi
            )
        kacc_ref[...] = jnp.zeros(kacc_ref.shape, F32)

        def step(i, _):
            u = i // per
            base = pl.multiple_of((i % per) * block, block)
            g = g_ref[u, pl.ds(base, block), lanes].astype(F32)
            acc = jnp.zeros((block, LANES), F32)
            for r in range(8):
                w = pad_ref[u, pl.ds(base + r, block + taps - 8), :]
                for q in range(taps // 8):
                    tap = taps - 1 - (8 * q + r)
                    part = w[8 * q : 8 * q + block]
                    acc = acc + k_ref[tap, lanes][None, :] * part
                    prod = (g * part).reshape(block // 8, 8, LANES)
                    kacc_ref[tap] += jnp.sum(prod, axis=0)
            dv_ref[u, pl.ds(base, block), lanes] = (
                acc * p_ref[u, pl.ds(base, block), lanes].astype(F32)
            ).astype(BF)
            dg_ref[u, pl.ds(base, block), lanes] = (
                acc * q_ref[u, pl.ds(base, block), lanes].astype(F32)
            ).astype(BF)
            return 0

        lax.fori_loop(0, utt * per, step, 0)
        dk_ref[:, lanes] = jnp.sum(kacc_ref[...], axis=1)


def back_conv(total, edge, dbn, conv_out, halos, sums, dsums, gain, kernel, gated, p, q):
    utt, frames, d = gated.shape
    cw = 256
    taps = kernel.shape[0]
    full = columns(gated.shape, cw)
    halo = columns((utt, PAD, d), cw)
    return pl.pallas_call(
        functools.partial(back_conv_body, total),
        grid=(d // cw,),
        in_specs=[pl.BlockSpec(memory_space=pltpu.SMEM), full, full, halo, halo, halo, halo]
        + [columns((2, d), cw), columns((2, d), cw), columns((1, d), cw), columns(kernel.shape, cw)]
        + [full, full, full],
        out_specs=[columns(kernel.shape, cw), full, full],
        out_shape=[
            jax.ShapeDtypeStruct(kernel.shape, F32),
            jax.ShapeDtypeStruct(gated.shape, BF),
            jax.ShapeDtypeStruct(gated.shape, BF),
        ],
        scratch_shapes=[
            pltpu.VMEM((utt, frames + 2 * PAD, LANES), F32),
            pltpu.VMEM((taps, 8, LANES), F32),
        ],
        compiler_params=params(32),
        cost_estimate=pl.CostEstimate(
            flops=128 * gated.size, bytes_accessed=18 * gated.size, transcendentals=0
        ),
        name="back_conv",
    )(edge, dbn, conv_out, *halos, sums, dsums, gain, kernel, gated, p, q)


def back_norm_body(x_ref, cot_ref, gain_ref, dv_ref, dg_ref, wv_ref, wg_ref, out_ref, acc_ref):
    rows, d = x_ref.shape
    j = pl.program_id(0)
    dims = (((1,), (1,)), ((), ()))
    part = lax.dot_general(dv_ref[...], wv_ref[...], dims, preferred_element_type=F32)
    part += lax.dot_general(dg_ref[...], wg_ref[...], dims, preferred_element_type=F32)

    @pl.when(j == 0)
    def _():
        acc_ref[...] = part

    @pl.when(j > 0)
    def _():
        acc_ref[...] += part

    @pl.when(j == pl.num_programs(0) - 1)
    def _():
        def step(i, _):
            r = pl.multiple_of(i * 16, 16)
            x = x_ref[pl.ds(r, 16), :].astype(F32)
            mu = jnp.sum(x, axis=-1, keepdims=True) * (1.0 / d)
            c = x - mu
            var = jnp.sum(c * c, axis=-1, keepdims=True) * (1.0 / d)
            rstd = lax.rsqrt(var + EPSILON)
            hat = c * rstd
            dh = acc_ref[pl.ds(r, 16), :] * gain_ref[...]
            m1 = jnp.sum(dh, axis=-1, keepdims=True) * (1.0 / d)
            m2 = jnp.sum(dh * hat, axis=-1, keepdims=True) * (1.0 / d)
            layer = rstd * (dh - m1 - hat * m2)
            out_ref[pl.ds(r, 16), :] = (cot_ref[pl.ds(r, 16), :].astype(F32) + layer).astype(BF)
            return 0

        lax.fori_loop(0, rows // 16, step, 0, unroll=2)


def back_norm(x, cot, gain, dv, dg, w_in):
    rows, d = x.shape
    cw = 256
    steps = d // cw
    return pl.pallas_call(
        back_norm_body,
        grid=(steps,),
        in_specs=[
            resident((rows, d)),
            resident((rows, d)),
            resident((1, d)),
            columns((rows, d), cw),
            columns((rows, d), cw),
            pl.BlockSpec((d, cw), lambda j: (0, j)),
            pl.BlockSpec((d, cw), lambda j: (0, j + steps)),
        ],
        out_specs=resident((rows, d)),
        out_shape=jax.ShapeDtypeStruct((rows, d), BF),
        scratch_shapes=[pltpu.VMEM((rows, d), F32)],
        compiler_params=params(40),
        cost_estimate=pl.CostEstimate(
            flops=4 * rows * d * d, bytes_accessed=4 * d * d + 10 * rows * d, transcendentals=0
        ),
        name="back_norm",
    )(x, cot, gain, dv, dg, w_in, w_in)


def swap(block, axis, bit):
    count = lax.axis_size(axis)
    return lax.ppermute(block, axis, [(i, i ^ bit) for i in range(count)])


def is_power(count):
    return count & (count - 1) == 0


def all_sum(block, axis, wire=None):
    count = lax.axis_size(axis)
    if not is_power(count):
        return lax.psum(block, axis)
    bit = 1
    while bit < count:
        if wire is not None:
            block = block.astype(wire)
        other = swap(block, axis, bit)
        block = block.astype(F32) + other.astype(F32)
        bit *= 2
    return block


def neighbours(block, axis, width):
    count = lax.axis_size(axis)
    up = [(i, i + 1) for i in range(count - 1)]
    down = [(i + 1, i) for i in range(count - 1)]
    low = lax.ppermute(block[:, -width:], axis, up)
    high = lax.ppermute(block[:, :width], axis, down)
    return low, high


def scatter_sum(parts, axis):
    count = parts.shape[0]
    wide = parts.shape[2] // 2
    bits = [1 << s for s in range(count.bit_length() - 1)]
    if len(bits) >= 3:
        orders = [bits, [bits[0], bits[2], bits[1]] + bits[3:]]
    else:
        orders = [bits, bits]
    held = [parts[:, :, :wide], parts[:, :, wide:]]
    labels = [list(range(count)), list(range(count))]
    for step in range(len(bits)):
        for h in range(2):
            bit = orders[h][step]
            keep = [i for i, j in enumerate(labels[h]) if not j & bit]
            send = [i for i, j in enumerate(labels[h]) if j & bit]
            block = held[h]
            size = len(labels[h])
            stride = 1
            while not labels[h][stride] & bit:
                stride *= 2
            shaped = block.reshape((size // (2 * stride), 2, stride) + block.shape[1:])
            mine = shaped[:, 0].reshape((size // 2,) + block.shape[1:])
            theirs = shaped[:, 1].reshape((size // 2,) + block.shape[1:])
            got = swap(theirs, axis, bit)
            total = mine.astype(F32) + got.astype(F32)
            held[h] = total if step == len(bits) - 1 else total.astype(BF)
            labels[h] = [labels[h][i] for i in keep]
    return jnp.concatenate([held[0][0], held[1][0]], axis=-1)


def on_device(inputs, ln_gain, w_in, kernel, bn_gain, bn_bias, w_out, cotangent):
    axis = "seq"
    n = lax.axis_size(axis)
    me = lax.axis_index(axis)
    utt, frames, d = inputs.shape
    rows = utt * frames
    total = rows * n
    x = inputs.reshape(rows, d)
    cot = cotangent.reshape(rows, d)
    ln_row, gain_row, bias_row = ln_gain[None], bn_gain[None], bn_bias[None]
    by_owner = is_power(n) and d % n == 0 and (d // n) % 16 == 0

    gated, p, q = front(x, ln_row, w_in)
    gated = gated.reshape(inputs.shape)
    lo, hi = neighbours(gated, axis, PAD)
    conv_out, sums = conv(gated, lo, hi, kernel)
    clo, chi = neighbours(conv_out.astype(BF), axis, PAD)
    sums = all_sum(sums, axis)

    act, dbn, dsums, dw = middle(
        n, total, me.reshape(1).astype(jnp.int32), conv_out.reshape(rows, d), sums, gain_row,
        bias_row, cot, w_out, by_owner,
    )
    dbn = dbn.reshape(inputs.shape)
    dlo, dhi = neighbours(dbn.astype(BF), axis, PAD)
    dsums = all_sum(dsums, axis)
    if by_owner:
        d_w_out = scatter_sum(dw, axis)
    else:
        d_w_out = lax.psum_scatter(dw, axis, scatter_dimension=0, tiled=True)
    outputs = branch(x, act, w_out)

    edge = jnp.stack([me > 0, me < n - 1]).astype(F32)
    d_kernel, dv, dg = back_conv(
        total, edge, dbn, conv_out, (dlo, dhi, clo, chi), sums, dsums, gain_row, kernel, gated,
        p.reshape(inputs.shape), q.reshape(inputs.shape),
    )
    d_kernel = all_sum(d_kernel, axis, BF)
    d_inputs = back_norm(x, cot, ln_row, dv.reshape(rows, d), dg.reshape(rows, d), w_in)
    return (
        outputs.reshape(inputs.shape), d_inputs.reshape(inputs.shape), d_w_out, d_kernel,
        dsums[1], dsums[0],
    )


def solution(mesh):
    return jax.shard_map(
        on_device,
        mesh=mesh,
        in_specs=(P(None, "seq", None), P(), P(), P(), P(), P(), P(), P(None, "seq", None)),
        out_specs=(P(None, "seq", None), P(None, "seq", None), P("seq", None), P(), P(), P()),
        check_vma=False,
    )
```

time: 449 us -> 180 us (0.40)
  waiting for transfers between devices: 212 us -> 44.7 us
  blocking collectives: 85.2 us -> 0 us
  Pallas kernels: 0 us -> 67.9 us
  other arithmetic: 63.5 us -> 3.27 us
  starting transfers between devices: 6.78 us -> 50.8 us
  matrix products: 41.6 us -> 0 us
  between operations: 14.8 us -> 1.18 us
  local copies, waits for them, and re-layouts: 24.1 us -> 12 us
    unnamed x3 -> x0, waiting for transfers between devices: 143 us -> none
    psum x2 -> x0, blocking collectives: 85.2 us -> none  [the longest x1 43.9 us: on_device(): lax.psum((jnp.sum(conv_out, axis=(0, 1)), jnp.sum(conv_out * conv_out, ax...]
    pallas_call x0 -> x6, Pallas kernels: none -> 67.9 us  [the longest x1 17.8 us: back_conv(): pl.pallas_call(functools.partial(back_conv_body, total), grid=(d // cw,),...]
    psum x1 -> x0, waiting for transfers between devices: 65.4 us -> none  [on_device(): d_kernel = lax.psum(jnp.stack(kernel_rows), 'seq')]
    ppermute x4 -> x31, starting transfers between devices: 6.7 us -> 50.8 us  [the longest x25 38.7 us: swap(): return lax.ppermute(block, axis, [(i, i ^ bit) for i in range(count)])]
    reduce_sum x8 -> x0, other arithmetic: 43.8 us -> none  [the longest x4 21 us: on_device(): kernel_rows.append(jnp.sum(window * d_conv, axis=(0, 1)))]
    dot_general x5 -> x0, matrix products: 41.6 us -> none  [the longest x1 10.3 us: on_device(): d_act = jnp.dot(cot_rows, w_out, preferred_element_type=jnp.float32)]
    ppermute x4 -> x31, waiting for transfers between devices: 3.39 us -> 44.7 us  [the longest x25 40.7 us: swap(): return lax.ppermute(block, axis, [(i, i ^ bit) for i in range(count)])]
  transfers between devices with their start and end apart: 6 -> 31, of which waited for: 3 -> 20; matrix products, arithmetic and copies ran while one was open for 12% -> 3% of each run, Pallas kernels for 0% -> 21%
where the time goes in v1:
time: 180 us
  Pallas kernels  67.9 us (38%)
  starting transfers between devices  50.8 us (28%)
  waiting for transfers between devices  44.7 us (25%)
  local copies, waits for them, and re-layouts  12 us (7%)
  other arithmetic  3.27 us (2%)
    ppermute x25, waiting for transfers between devices, swap(): return lax.ppermute(block, axis, [(i, i ^ bit) for i in range(count)])  40.7 us
    ppermute x25, starting transfers between devices, swap(): return lax.ppermute(block, axis, [(i, i ^ bit) for i in range(count)])  38.7 us
    pallas_call x1, Pallas kernels, back_conv(): pl.pallas_call(functools.partial(back_conv_body, total), grid=(d // cw,),...  17.8 us
    pallas_call x1, Pallas kernels, back_norm(): pl.pallas_call(back_norm_body, grid=(steps,), in_specs=[resident((rows, d...  15.8 us
    pallas_call x1, Pallas kernels, conv(): pl.pallas_call(conv_body, grid=(d // cw,), in_specs=[columns(gated.shape,...  10.7 us
    pallas_call x1, Pallas kernels, front(): pl.pallas_call(front_body, grid=(steps,), in_specs=[resident((rows, d)),...  9.57 us
    pallas_call x1, Pallas kernels, middle(): pl.pallas_call(body, grid=(d // cw,), in_specs=[pl.BlockSpec(memory_space...  9.28 us
    unnamed x36, local copies, waits for them, and re-layouts  8.84 us
  transfers between devices with their start and end apart: 31, of which 20 were waited for; matrix products, arithmetic and copies ran while one was open for 3% of the time, Pallas kernels for 21%

profile of v1, /device:TPU:0, one launch (start us, length us, event | category | flops | bytes accessed | tf_op | source)
XLA Modules:
  0.0 179.9 jit_solution(3705875566019160973)
XLA Ops:
  0.6 0.7 broadcast_in_dim.9.gain_ref
  1.3 3.7 %copy-done = bf16[1536,3072]{1,0:T(8,128)(2,1)S(1)} copy-done((bf16[1536,3072]{1,0:T(8,128)(2,1)S(1)}, bf16[1536,3072]{1,0:T(8,128)(2,1)}, u32[]{:S(2)}) %copy-start) | copy-done | bytes 9437208
  5.0 1.4 copy-done.1
  6.4 9.6 %front.1 = (bf16[512,1536]{1,0:T(8,128)(2,1)S(1)}, bf16[512,1536]{1,0:T(8,128)(2,1)S(1)}, bf16[512,1536]{1,0:T(8,128)(2,1)S(1)}) custom-call(bf16[512,1536]{1,0:T(8,128)(2,1)S(1)} %bitcast.126, f32[1,1536]{1,0:T(1,128)S(1)} %broadcast_in_dim.9.gain_ref, bf16[1536,3072]{1,0:T(8,128)(2,1)S(1)} %copy-done, bf16[1536,3072]{1,0:T(8,128)(2,1)S(1)} %copy-done), custom_call_target="tpu_custom_call" | custom-call | flops 4831838208 | bytes 15728640 | tf_op jit(solution)/shard_map/front/pallas_call | solution.py:63
  16.0 1.2 copy-done.9
  17.2 2.5 %collective-permute-start = (bf16[2,16,1536]{2,1,0:T(8,128)(2,1)S(1)}, bf16[2,16,1536]{2,1,0:T(8,128)(2,1)S(1)}, u32[]{:S(2)}, u32[]{:S(2)}) collective-permute-start(bf16[2,16,1536]{2,1,0:T(8,128)(2,1)S(1)} %get-tuple-element.39), channel_id=1, source_target_pairs={{0,1},{1,2},{2,3},{3,4},{4,5},{5,6},{6,7},{7,8},{8,9},{9,10},{10,1... | collective-permute-start | bytes 294920 | tf_op jit(solution)/shard_map/ppermute | solution.py:423
  19.7 1.3 collective-permute-start.1
  21.0 4.0 %collective-permute-done.1.hi_ref = bf16[2,16,1536]{2,1,0:T(8,128)(2,1)S(1)} collective-permute-done((bf16[2,16,1536]{2,1,0:T(8,128)(2,1)S(1)}, bf16[2,16,1536]{2,1,0:T(8,128)(2,1)S(1)}, u32[]{:S(2)}, u32[]{:S(2)}) %collective-permute-start.1) | collective-permute-done | bytes 98336 | tf_op jit(solution)/shard_map/ppermute | solution.py:424
  25.0 10.7 %conv.1 = (f32[2,256,1536]{2,1,0:T(8,128)S(1)}, f32[2,1536]{1,0:T(2,128)S(1)}) custom-call(bf16[2,256,1536]{2,1,0:T(8,128)(2,1)S(1)} %bitcast.133, bf16[2,16,1536]{2,1,0:T(8,128)(2,1)S(1)} %collective-permute-done.lo_ref, bf16[2,16,1536]{2,1,0:T(8,128)(2,1)S(1)} %collective-permute-done.1.hi_ref, f32[32,1536]{1,0:T(8,128)S(1)} %copy-done.11), custom_call_target="tpu_custom_call" | custom-call | flops 50331648 | bytes 4718592 | tf_op jit(solution)/shard_map/conv/pallas_call | solution.py:118
  35.8 1.1 copy-done.3
  36.9 3.2 %collective-permute-start.2 = (f32[2,1536]{1,0:T(2,128)S(1)}, f32[2,1536]{1,0:T(2,128)S(1)}, u32[]{:S(2)}, u32[]{:S(2)}) collective-permute-start(f32[2,1536]{1,0:T(2,128)S(1)} %get-tuple-element.20), channel_id=1, source_target_pairs={{0,1},{1,0},{2,3},{3,2},{4,5},{5,4},{6,7},{7,6},{8,9},{9,8},{10,11... | collective-permute-start | bytes 36872 | tf_op jit(solution)/shard_map/ppermute | solution.py:398
  40.1 0.8 collective-permute-done.2
  41.0 2.4 %collective-permute-start.3 = (f32[2,1536]{1,0:T(2,128)S(1)}, f32[2,1536]{1,0:T(2,128)S(1)}, u32[]{:S(2)}, u32[]{:S(2)}) collective-permute-start(f32[2,1536]{1,0:T(2,128)S(1)} %add.75), channel_id=1, source_target_pairs={{0,2},{1,3},{2,0},{3,1},{4,6},{5,7},{6,4},{7,5},{8,10},{9,11},{10,... | collective-permute-start | bytes 36872 | tf_op jit(solution)/shard_map/ppermute | solution.py:398
  43.4 1.7 collective-permute-done.3
  45.1 2.5 %collective-permute-start.4 = (f32[2,1536]{1,0:T(2,128)S(1)}, f32[2,1536]{1,0:T(2,128)S(1)}, u32[]{:S(2)}, u32[]{:S(2)}) collective-permute-start(f32[2,1536]{1,0:T(2,128)S(1)} %add.76), channel_id=1, source_target_pairs={{0,4},{1,5},{2,6},{3,7},{4,0},{5,1},{6,2},{7,3},{8,12},{9,13},{10,... | collective-permute-start | bytes 36872 | tf_op jit(solution)/shard_map/ppermute | solution.py:398
  47.6 1.7 collective-permute-done.4
  49.3 1.6 collective-permute-start.5
  50.9 2.1 %collective-permute-done.5 = f32[2,1536]{1,0:T(2,128)S(1)} collective-permute-done((f32[2,1536]{1,0:T(2,128)S(1)}, f32[2,1536]{1,0:T(2,128)S(1)}, u32[]{:S(2)}, u32[]{:S(2)}) %collective-permute-start.5) | collective-permute-done | bytes 12320 | tf_op jit(solution)/shard_map/ppermute | solution.py:398
  53.0 2.7 %collective-permute-start.6 = (f32[2,1536]{1,0:T(2,128)S(1)}, f32[2,1536]{1,0:T(2,128)S(1)}, u32[]{:S(2)}, u32[]{:S(2)}) collective-permute-start(f32[2,1536]{1,0:T(2,128)S(1)} %add.78), channel_id=1, source_target_pairs={{0,16},{1,17},{2,18},{3,19},{4,20},{5,21},{6,22},{7,23},{8,24},{9,... | collective-permute-start | bytes 36872 | tf_op jit(solution)/shard_map/ppermute | solution.py:398
  55.7 2.0 %collective-permute-done.6 = f32[2,1536]{1,0:T(2,128)S(1)} collective-permute-done((f32[2,1536]{1,0:T(2,128)S(1)}, f32[2,1536]{1,0:T(2,128)S(1)}, u32[]{:S(2)}, u32[]{:S(2)}) %collective-permute-start.6) | collective-permute-done | bytes 12320 | tf_op jit(solution)/shard_map/ppermute | solution.py:398
  57.7 1.4 copy-done.5
  59.1 9.3 %middle.1 = (bf16[512,1536]{1,0:T(8,128)(2,1)S(1)}, f32[512,1536]{1,0:T(8,128)S(1)}, f32[2,1536]{1,0:T(2,128)S(1)}, bf16[32,48,1536]{2,1,0:T(8,128)(2,1)S(1)}) custom-call(s32[1]{0:T(128)} %bitcast.1.me_ref, f32[512,1536]{1,0:T(8,128)S(1)} %bitcast.129, f32[2,1536]{1,0:T(2,128)S(1)} %add.79.sums_ref, f32[1,1536]{1,0:T(1,128)S(1)} %broadcast_in_dim.10.gain_ref, ...), custom_call_target="tpu_custom_call" | custom-call | flops 4831838208 | bytes 18874368 | tf_op jit(solution)/shard_map/middle/pallas_call | solution.py:186
  68.8 0.9 collective-permute-done.11
  69.7 2.1 %collective-permute-start.12 = (f32[2,1536]{1,0:T(2,128)S(1)}, f32[2,1536]{1,0:T(2,128)S(1)}, u32[]{:S(2)}, u32[]{:S(2)}) collective-permute-start(f32[2,1536]{1,0:T(2,128)S(1)} %add.80), channel_id=1, source_target_pairs={{0,2},{1,3},{2,0},{3,1},{4,6},{5,7},{6,4},{7,5},{8,10},{9,11},{10,... | collective-permute-start | bytes 36872 | tf_op jit(solution)/shard_map/ppermute | solution.py:398
  71.8 1.3 collective-permute-start.10
  73.1 3.0 %collective-permute-start.9 = (bf16[2,16,1536]{2,1,0:T(8,128)(2,1)S(1)}, bf16[2,16,1536]{2,1,0:T(8,128)(2,1)S(1)}, u32[]{:S(2)}, u32[]{:S(2)}) collective-permute-start(bf16[2,16,1536]{2,1,0:T(8,128)(2,1)S(1)} %get-tuple-element.35), channel_id=1, source_target_pairs={{0,1},{1,2},{2,3},{3,4},{4,5},{5,6},{6,7},{7,8},{8,9},{9,10},{10,1... | collective-permute-start | bytes 294920 | tf_op jit(solution)/shard_map/ppermute | solution.py:423
  76.3 2.1 %collective-permute-start.13 = (f32[2,1536]{1,0:T(2,128)S(1)}, f32[2,1536]{1,0:T(2,128)S(1)}, u32[]{:S(2)}, u32[]{:S(2)}) collective-permute-start(f32[2,1536]{1,0:T(2,128)S(1)} %add.81), channel_id=1, source_target_pairs={{0,4},{1,5},{2,6},{3,7},{4,0},{5,1},{6,2},{7,3},{8,12},{9,13},{10,... | collective-permute-start | bytes 36872 | tf_op jit(solution)/shard_map/ppermute | solution.py:398
  78.4 2.7 %collective-permute-start.7 = (bf16[2,16,1536]{2,1,0:T(8,128)(2,1)S(1)}, bf16[2,16,1536]{2,1,0:T(8,128)(2,1)S(1)}, u32[]{:S(2)}, u32[]{:S(2)}) collective-permute-start(bf16[2,16,1536]{2,1,0:T(8,128)(2,1)S(1)} %get-tuple-element.37), channel_id=1, source_target_pairs={{0,1},{1,2},{2,3},{3,4},{4,5},{5,6},{6,7},{7,8},{8,9},{9,10},{10,1... | collective-permute-start | bytes 294920 | tf_op jit(solution)/shard_map/ppermute | solution.py:423
  81.2 1.3 collective-permute-start.8
  82.5 5.0 %collective-permute-start.14 = (f32[2,1536]{1,0:T(2,128)S(1)}, f32[2,1536]{1,0:T(2,128)S(1)}, u32[]{:S(2)}, u32[]{:S(2)}) collective-permute-start(f32[2,1536]{1,0:T(2,128)S(1)} %add.82), channel_id=1, source_target_pairs={{0,8},{1,9},{2,10},{3,11},{4,12},{5,13},{6,14},{7,15},{8,0},{9,1},... | collective-permute-start | bytes 36872 | tf_op jit(solution)/shard_map/ppermute | solution.py:398
  87.5 0.3 fusion.13
  87.9 2.4 %collective-permute-done.14 = f32[2,1536]{1,0:T(2,128)S(1)} collective-permute-done((f32[2,1536]{1,0:T(2,128)S(1)}, f32[2,1536]{1,0:T(2,128)S(1)}, u32[]{:S(2)}, u32[]{:S(2)}) %collective-permute-start.14) | collective-permute-done | bytes 12320 | tf_op jit(solution)/shard_map/ppermute | solution.py:398
  90.2 2.0 %collective-permute-start.15 = (f32[2,1536]{1,0:T(2,128)S(1)}, f32[2,1536]{1,0:T(2,128)S(1)}, u32[]{:S(2)}, u32[]{:S(2)}) collective-permute-start(f32[2,1536]{1,0:T(2,128)S(1)} %add.83), channel_id=1, source_target_pairs={{0,16},{1,17},{2,18},{3,19},{4,20},{5,21},{6,22},{7,23},{8,24},{9,... | collective-permute-start | bytes 36872 | tf_op jit(solution)/shard_map/ppermute | solution.py:398
  92.3 1.1 slice_bitcast_fusion.2
  93.4 1.5 collective-permute-done.15
  95.0 17.8 %back_conv.1 = (f32[32,1536]{1,0:T(8,128)S(1)}, bf16[2,256,1536]{2,1,0:T(8,128)(2,1)S(1)}, bf16[2,256,1536]{2,1,0:T(8,128)(2,1)S(1)}) custom-call(f32[2]{0:T(128)S(1)} %add_convert_fusion.4.edge_ref, f32[2,256,1536]{2,1,0:T(8,128)S(1)} %bitcast.131, f32[2,256,1536]{2,1,0:T(8,128)S(1)} %get-tuple-element.19.conv_ref, ...), custom_call_target="tpu_custom_call" | custom-call | flops 100663296 | bytes 14155776 | tf_op jit(solution)/shard_map/back_conv/pallas_call | solution.py:310
  112.9 0.6 collective-permute-start.26
  113.6 0.8 collective-permute-done.26
  114.5 4.7 %branch.1 = bf16[512,1536]{1,0:T(8,128)(2,1)} custom-call(bf16[512,1536]{1,0:T(8,128)(2,1)S(1)} %bitcast.127, bf16[512,1536]{1,0:T(8,128)(2,1)S(1)} %get-tuple-element.21.act_ref, bf16[1536,1536]{1,0:T(8,128)(2,1)S(1)} %bitcast.136), custom_call_target="tpu_custom_call" | custom-call | flops 2415919104 | bytes 9437184 | tf_op jit(solution)/shard_map/branch/pallas_call | solution.py:229
  119.2 0.3 collective-permute-done.27
  119.6 0.6 slice_reduce_fusion
  120.3 4.1 %collective-permute-done.28 = bf16[32,1536]{1,0:T(8,128)(2,1)S(1)} collective-permute-done((bf16[32,1536]{1,0:T(8,128)(2,1)S(1)}, bf16[32,1536]{1,0:T(8,128)(2,1)S(1)}, u32[]{:S(2)}, u32[]{:S(2)}) %collective-permute-start.28) | collective-permute-done | bytes 98336 | tf_op jit(solution)/shard_map/ppermute | solution.py:398
  124.4 1.0 collective-permute-start.29
  125.4 15.8 %back_norm.1 = bf16[512,1536]{1,0:T(8,128)(2,1)} custom-call(bf16[512,1536]{1,0:T(8,128)(2,1)S(1)} %bitcast.128, bf16[512,1536]{1,0:T(8,128)(2,1)S(1)} %bitcast.138, f32[1,1536]{1,0:T(1,128)S(1)} %broadcast_in_dim.9.gain_ref, bf16[512,1536]{1,0:T(8,128)(2,1)S(1)} %bitcast.139, bf16[512,1536]{1,0:T(8,128)(2,1)S(1)} %bitcast.140, bf16[1536,3072]{1,0:T(8,128)(2,1)} %wg_ref.3, ...), custom_call_target="tpu_custom_call" | custom-call | flops 4831838208 | bytes 17301504 | tf_op jit(solution)/shard_map/back_norm/pallas_call | solution.py:373
  141.3 1.3 collective-permute-start.30
  142.6 0.3 fusion
  143.0 1.2 collective-permute-start.22
  144.2 0.3 fusion.1
  144.5 1.7 collective-permute-start.17
  146.3 1.7 collective-permute-done.30
  148.0 0.7 convert_add_fusion.8
  148.7 8.4 %collective-permute-done.22 = bf16[8,48,768]{2,1,0:T(8,128)(2,1)S(1)} collective-permute-done((bf16[8,48,768]{2,1,0:T(8,128)(2,1)S(1)}, bf16[8,48,768]{2,1,0:T(8,128)(2,1)S(1)}, u32[]{:S(2)}, u32[]{:S(2)}) %collective-permute-start.22) | collective-permute-done | bytes 589856 | tf_op jit(solution)/shard_map/ppermute | solution.py:398
  157.3 1.8 collective-permute-start.23
  159.2 1.0 collective-permute-start.18
  160.3 4.2 %collective-permute-done.23 = bf16[4,48,768]{2,1,0:T(8,128)(2,1)S(1)} collective-permute-done((bf16[4,48,768]{2,1,0:T(8,128)(2,1)S(1)}, bf16[4,48,768]{2,1,0:T(8,128)(2,1)S(1)}, u32[]{:S(2)}, u32[]{:S(2)}) %collective-permute-start.23) | collective-permute-done | bytes 294944 | tf_op jit(solution)/shard_map/ppermute | solution.py:398
  164.6 1.4 collective-permute-start.24
  166.1 1.8 collective-permute-start.19
  167.9 1.9 %collective-permute-done.24 = bf16[2,48,768]{2,1,0:T(8,128)(2,1)S(1)} collective-permute-done((bf16[2,48,768]{2,1,0:T(8,128)(2,1)S(1)}, bf16[2,48,768]{2,1,0:T(8,128)(2,1)S(1)}, u32[]{:S(2)}, u32[]{:S(2)}) %collective-permute-start.24) | collective-permute-done | bytes 147488 | tf_op jit(solution)/shard_map/ppermute | solution.py:398
  169.8 1.7 collective-permute-start.25
  171.6 1.3 collective-permute-done.19
  173.0 1.2 collective-permute-start.20
  174.2 0.9 collective-permute-done.25
  175.2 3.9 %collective-permute-done.20 = bf16[1,48,768]{2,1,0:T(8,128)(2,1)S(1)} collective-permute-done((bf16[1,48,768]{2,1,0:T(8,128)(2,1)S(1)}, bf16[1,48,768]{2,1,0:T(8,128)(2,1)S(1)}, u32[]{:S(2)}, u32[]{:S(2)}) %collective-permute-start.20) | collective-permute-done | bytes 73760 | tf_op jit(solution)/shard_map/ppermute | solution.py:398
  179.1 0.7 pad_maximum_fusion
  (89 shorter events, 2.1 us)
Async XLA Ops:
  1.3 3.7 %copy-start = (bf16[1536,3072]{1,0:T(8,128)(2,1)S(1)}, bf16[1536,3072]{1,0:T(8,128)(2,1)}, u32[]{:S(2)}) copy-start(bf16[1536,3072]{1,0:T(8,128)(2,1)} %wg_ref.3) | copy-start | bytes 28311556
  5.0 1.4 copy-start.1
  6.4 18.6 %copy-start.11 = (f32[32,1536]{1,0:T(8,128)S(1)}, f32[32,1536]{1,0:T(8,128)}, u32[]{:S(2)}) copy-start(f32[32,1536]{1,0:T(8,128)} %k_ref.3) | copy-start | bytes 589828
  16.0 1.2 copy-start.9
  17.2 18.6 %copy-start.7 = (bf16[512,1536]{1,0:T(8,128)(2,1)}, bf16[512,1536]{1,0:T(8,128)(2,1)S(1)}, u32[]{:S(2)}) copy-start(bf16[512,1536]{1,0:T(8,128)(2,1)S(1)} %get-tuple-element.24) | copy-start | bytes 4718596
  17.2 38.5 %copy-start.14 = (f32[1536]{0:T(1024)S(1)}, f32[1536]{0:T(1024)}, u32[]{:S(2)}) copy-start(f32[1536]{0:T(1024)} %param.12) | copy-start | bytes 18436
  17.2 38.5 %copy-start.15 = (f32[1536]{0:T(1024)S(1)}, f32[1536]{0:T(1024)}, u32[]{:S(2)}) copy-start(f32[1536]{0:T(1024)} %param.13) | copy-start | bytes 18436
  17.2 3.8 %collective-permute-start = (bf16[2,16,1536]{2,1,0:T(8,128)(2,1)S(1)}, bf16[2,16,1536]{2,1,0:T(8,128)(2,1)S(1)}, u32[]{:S(2)}, u32[]{:S(2)}) collective-permute-start(bf16[2,16,1536]{2,1,0:T(8,128)(2,1)S(1)} %get-tuple-element.39), channel_id=1, source_target_pairs={{0,1},{1,2},{2,3},{3,4},{4,5},{5,6},{6,7},{7,8},{8,9},{9,10},{10,1... | collective-permute-start | bytes 294920 | tf_op jit(solution)/shard_map/ppermute | solution.py:423
  19.7 5.3 %collective-permute-start.1 = (bf16[2,16,1536]{2,1,0:T(8,128)(2,1)S(1)}, bf16[2,16,1536]{2,1,0:T(8,128)(2,1)S(1)}, u32[]{:S(2)}, u32[]{:S(2)}) collective-permute-start(bf16[2,16,1536]{2,1,0:T(8,128)(2,1)S(1)} %get-tuple-element.38), channel_id=1, source_target_pairs={{1,0},{2,1},{3,2},{4,3},{5,4},{6,5},{7,6},{8,7},{9,8},{10,9},{11,1... | collective-permute-start | bytes 294920 | tf_op jit(solution)/shard_map/ppermute | solution.py:424
  35.7 1.1 copy-start.3
  36.9 4.1 %collective-permute-start.2 = (f32[2,1536]{1,0:T(2,128)S(1)}, f32[2,1536]{1,0:T(2,128)S(1)}, u32[]{:S(2)}, u32[]{:S(2)}) collective-permute-start(f32[2,1536]{1,0:T(2,128)S(1)} %get-tuple-element.20), channel_id=1, source_target_pairs={{0,1},{1,0},{2,3},{3,2},{4,5},{5,4},{6,7},{7,6},{8,9},{9,8},{10,11... | collective-permute-start | bytes 36872 | tf_op jit(solution)/shard_map/ppermute | solution.py:398
  41.0 4.1 %collective-permute-start.3 = (f32[2,1536]{1,0:T(2,128)S(1)}, f32[2,1536]{1,0:T(2,128)S(1)}, u32[]{:S(2)}, u32[]{:S(2)}) collective-permute-start(f32[2,1536]{1,0:T(2,128)S(1)} %add.75), channel_id=1, source_target_pairs={{0,2},{1,3},{2,0},{3,1},{4,6},{5,7},{6,4},{7,5},{8,10},{9,11},{10,... | collective-permute-start | bytes 36872 | tf_op jit(solution)/shard_map/ppermute | solution.py:398
  45.1 4.2 %collective-permute-start.4 = (f32[2,1536]{1,0:T(2,128)S(1)}, f32[2,1536]{1,0:T(2,128)S(1)}, u32[]{:S(2)}, u32[]{:S(2)}) collective-permute-start(f32[2,1536]{1,0:T(2,128)S(1)} %add.76), channel_id=1, source_target_pairs={{0,4},{1,5},{2,6},{3,7},{4,0},{5,1},{6,2},{7,3},{8,12},{9,13},{10,... | collective-permute-start | bytes 36872 | tf_op jit(solution)/shard_map/ppermute | solution.py:398
  49.3 3.8 %collective-permute-start.5 = (f32[2,1536]{1,0:T(2,128)S(1)}, f32[2,1536]{1,0:T(2,128)S(1)}, u32[]{:S(2)}, u32[]{:S(2)}) collective-permute-start(f32[2,1536]{1,0:T(2,128)S(1)} %add.77), channel_id=1, source_target_pairs={{0,8},{1,9},{2,10},{3,11},{4,12},{5,13},{6,14},{7,15},{8,0},{9,1},... | collective-permute-start | bytes 36872 | tf_op jit(solution)/shard_map/ppermute | solution.py:398
  53.0 4.7 %collective-permute-start.6 = (f32[2,1536]{1,0:T(2,128)S(1)}, f32[2,1536]{1,0:T(2,128)S(1)}, u32[]{:S(2)}, u32[]{:S(2)}) collective-permute-start(f32[2,1536]{1,0:T(2,128)S(1)} %add.78), channel_id=1, source_target_pairs={{0,16},{1,17},{2,18},{3,19},{4,20},{5,21},{6,22},{7,23},{8,24},{9,... | collective-permute-start | bytes 36872 | tf_op jit(solution)/shard_map/ppermute | solution.py:398
  57.7 1.4 copy-start.5
  68.4 1.2 collective-permute-start.11
  69.7 6.6 %collective-permute-start.12 = (f32[2,1536]{1,0:T(2,128)S(1)}, f32[2,1536]{1,0:T(2,128)S(1)}, u32[]{:S(2)}, u32[]{:S(2)}) collective-permute-start(f32[2,1536]{1,0:T(2,128)S(1)} %add.80), channel_id=1, source_target_pairs={{0,2},{1,3},{2,0},{3,1},{4,6},{5,7},{6,4},{7,5},{8,10},{9,11},{10,... | collective-permute-start | bytes 36872 | tf_op jit(solution)/shard_map/ppermute | solution.py:398
  71.8 23.1 %collective-permute-start.10 = (bf16[2,16,1536]{2,1,0:T(8,128)(2,1)S(1)}, bf16[2,16,1536]{2,1,0:T(8,128)(2,1)S(1)}, u32[]{:S(2)}, u32[]{:S(2)}) collective-permute-start(bf16[2,16,1536]{2,1,0:T(8,128)(2,1)S(1)} %get-tuple-element.34), channel_id=1, source_target_pairs={{1,0},{2,1},{3,2},{4,3},{5,4},{6,5},{7,6},{8,7},{9,8},{10,9},{11,1... | collective-permute-start | bytes 294920 | tf_op jit(solution)/shard_map/ppermute | solution.py:424
  73.1 21.8 %collective-permute-start.9 = (bf16[2,16,1536]{2,1,0:T(8,128)(2,1)S(1)}, bf16[2,16,1536]{2,1,0:T(8,128)(2,1)S(1)}, u32[]{:S(2)}, u32[]{:S(2)}) collective-permute-start(bf16[2,16,1536]{2,1,0:T(8,128)(2,1)S(1)} %get-tuple-element.35), channel_id=1, source_target_pairs={{0,1},{1,2},{2,3},{3,4},{4,5},{5,6},{6,7},{7,8},{8,9},{9,10},{10,1... | collective-permute-start | bytes 294920 | tf_op jit(solution)/shard_map/ppermute | solution.py:423
  76.3 6.2 %collective-permute-start.13 = (f32[2,1536]{1,0:T(2,128)S(1)}, f32[2,1536]{1,0:T(2,128)S(1)}, u32[]{:S(2)}, u32[]{:S(2)}) collective-permute-start(f32[2,1536]{1,0:T(2,128)S(1)} %add.81), channel_id=1, source_target_pairs={{0,4},{1,5},{2,6},{3,7},{4,0},{5,1},{6,2},{7,3},{8,12},{9,13},{10,... | collective-permute-start | bytes 36872 | tf_op jit(solution)/shard_map/ppermute | solution.py:398
  78.4 16.5 %collective-permute-start.7 = (bf16[2,16,1536]{2,1,0:T(8,128)(2,1)S(1)}, bf16[2,16,1536]{2,1,0:T(8,128)(2,1)S(1)}, u32[]{:S(2)}, u32[]{:S(2)}) collective-permute-start(bf16[2,16,1536]{2,1,0:T(8,128)(2,1)S(1)} %get-tuple-element.37), channel_id=1, source_target_pairs={{0,1},{1,2},{2,3},{3,4},{4,5},{5,6},{6,7},{7,8},{8,9},{9,10},{10,1... | collective-permute-start | bytes 294920 | tf_op jit(solution)/shard_map/ppermute | solution.py:423
  81.2 13.8 %collective-permute-start.8 = (bf16[2,16,1536]{2,1,0:T(8,128)(2,1)S(1)}, bf16[2,16,1536]{2,1,0:T(8,128)(2,1)S(1)}, u32[]{:S(2)}, u32[]{:S(2)}) collective-permute-start(bf16[2,16,1536]{2,1,0:T(8,128)(2,1)S(1)} %get-tuple-element.36), channel_id=1, source_target_pairs={{1,0},{2,1},{3,2},{4,3},{5,4},{6,5},{7,6},{8,7},{9,8},{10,9},{11,1... | collective-permute-start | bytes 294920 | tf_op jit(solution)/shard_map/ppermute | solution.py:424
  82.5 7.7 %collective-permute-start.14 = (f32[2,1536]{1,0:T(2,128)S(1)}, f32[2,1536]{1,0:T(2,128)S(1)}, u32[]{:S(2)}, u32[]{:S(2)}) collective-permute-start(f32[2,1536]{1,0:T(2,128)S(1)} %add.82), channel_id=1, source_target_pairs={{0,8},{1,9},{2,10},{3,11},{4,12},{5,13},{6,14},{7,15},{8,0},{9,1},... | collective-permute-start | bytes 36872 | tf_op jit(solution)/shard_map/ppermute | solution.py:398
  87.5 7.5 %copy-start.8 = (bf16[512,1536]{1,0:T(8,128)(2,1)S(1)}, bf16[512,1536]{1,0:T(8,128)(2,1)}, u32[]{:S(2)}) copy-start(bf16[512,1536]{1,0:T(8,128)(2,1)} %copy-done.7) | copy-start | bytes 4718596
  87.5 7.5 %copy-start.10 = (bf16[512,1536]{1,0:T(8,128)(2,1)S(1)}, bf16[512,1536]{1,0:T(8,128)(2,1)}, u32[]{:S(2)}) copy-start(bf16[512,1536]{1,0:T(8,128)(2,1)} %copy-done.9) | copy-start | bytes 4718596
  87.8 25.6 %copy-start.12 = (bf16[32,48,768]{2,1,0:T(8,128)(2,1)}, bf16[32,48,768]{2,1,0:T(8,128)(2,1)S(1)}, u32[]{:S(2)}) copy-start(bf16[32,48,768]{2,1,0:T(8,128)(2,1)S(1)} %get-tuple-element.33) | copy-start | bytes 7077892
  87.8 7.1 %copy-start.4 = (bf16[512,1536]{1,0:T(8,128)(2,1)S(1)}, bf16[512,1536]{1,0:T(8,128)(2,1)}, u32[]{:S(2)}) copy-start(bf16[512,1536]{1,0:T(8,128)(2,1)} %copy-done.3) | copy-start | bytes 4718596
  90.2 4.7 %collective-permute-start.15 = (f32[2,1536]{1,0:T(2,128)S(1)}, f32[2,1536]{1,0:T(2,128)S(1)}, u32[]{:S(2)}, u32[]{:S(2)}) collective-permute-start(f32[2,1536]{1,0:T(2,128)S(1)} %add.83), channel_id=1, source_target_pairs={{0,16},{1,17},{2,18},{3,19},{4,20},{5,21},{6,22},{7,23},{8,24},{9,... | collective-permute-start | bytes 36872 | tf_op jit(solution)/shard_map/ppermute | solution.py:398
  94.9 49.3 %collective-permute-start.16 = (bf16[16,48,768]{2,1,0:T(8,128)(2,1)}, bf16[16,48,768]{2,1,0:T(8,128)(2,1)S(1)}, u32[]{:S(2)}, u32[]{:S(2)}) collective-permute-start(bf16[16,48,768]{2,1,0:T(8,128)(2,1)} %slice_bitcast_fusion.2), channel_id=1, source_target_pairs={{0,1},{1,0},{2,3},{3,2},{4,5},{5,4},{6,7},{7,6},{8,9},{9,8},{10,11... | collective-permute-start | bytes 3538952 | tf_op jit(solution)/shard_map/ppermute | solution.py:398
  95.0 19.5 %slice-start = ((s8[4718592]{0:T(1024)(128)(4,1)}), s8[4194304]{0:T(1024)(128)(4,1)S(1)}, s32[]{:S(2)}) async-start(s8[4718592]{0:T(1024)(128)(4,1)} %bitcast.135), calls=%async_computation | async-start | bytes 8388608
  95.0 19.5 %slice-start.1 = ((s8[4718592]{0:T(1024)(128)(4,1)}), s8[524288]{0:T(1024)(128)(4,1)S(1)}, s32[]{:S(2)}) async-start(s8[4718592]{0:T(1024)(128)(4,1)} %bitcast.135), calls=%async_computation.1 | async-start | bytes 1048576
  112.8 1.7 copy-start.2
  112.9 1.5 collective-permute-start.26
  113.5 29.0 %collective-permute-start.21 = (bf16[16,48,768]{2,1,0:T(8,128)(2,1)S(1)}, bf16[16,48,768]{2,1,0:T(8,128)(2,1)S(1)}, u32[]{:S(2)}, u32[]{:S(2)}) collective-permute-start(bf16[16,48,768]{2,1,0:T(8,128)(2,1)S(1)} %slice_bitcast_fusion), channel_id=1, source_target_pairs={{0,1},{1,0},{2,3},{3,2},{4,5},{5,4},{6,7},{7,6},{8,9},{9,8},{10,11... | collective-permute-start | bytes 3538952 | tf_op jit(solution)/shard_map/ppermute | solution.py:398
  114.4 5.1 %collective-permute-start.27 = (bf16[32,1536]{1,0:T(8,128)(2,1)S(1)}, bf16[32,1536]{1,0:T(8,128)(2,1)S(1)}, u32[]{:S(2)}, u32[]{:S(2)}) collective-permute-start(bf16[32,1536]{1,0:T(8,128)(2,1)S(1)} %add_convert_fusion.3), channel_id=1, source_target_pairs={{0,2},{1,3},{2,0},{3,1},{4,6},{5,7},{6,4},{7,5},{8,10},{9,11},{10,... | collective-permute-start | bytes 294920 | tf_op jit(solution)/shard_map/ppermute | solution.py:398
  114.5 10.9 %copy-start.6 = (bf16[2,256,1536]{2,1,0:T(8,128)(2,1)S(1)}, bf16[2,256,1536]{2,1,0:T(8,128)(2,1)}, u32[]{:S(2)}) copy-start(bf16[2,256,1536]{2,1,0:T(8,128)(2,1)} %param.15) | copy-start | bytes 4718596
  119.6 4.8 %collective-permute-start.28 = (bf16[32,1536]{1,0:T(8,128)(2,1)S(1)}, bf16[32,1536]{1,0:T(8,128)(2,1)S(1)}, u32[]{:S(2)}, u32[]{:S(2)}) collective-permute-start(bf16[32,1536]{1,0:T(8,128)(2,1)S(1)} %add_convert_fusion.2), channel_id=1, source_target_pairs={{0,4},{1,5},{2,6},{3,7},{4,0},{5,1},{6,2},{7,3},{8,12},{9,13},{10,... | collective-permute-start | bytes 294920 | tf_op jit(solution)/shard_map/ppermute | solution.py:398
  124.4 16.9 %collective-permute-start.29 = (bf16[32,1536]{1,0:T(8,128)(2,1)S(1)}, bf16[32,1536]{1,0:T(8,128)(2,1)S(1)}, u32[]{:S(2)}, u32[]{:S(2)}) collective-permute-start(bf16[32,1536]{1,0:T(8,128)(2,1)S(1)} %add_convert_fusion.1), channel_id=1, source_target_pairs={{0,8},{1,9},{2,10},{3,11},{4,12},{5,13},{6,14},{7,15},{8,0},{9,1},... | collective-permute-start | bytes 294920 | tf_op jit(solution)/shard_map/ppermute | solution.py:398
  125.4 17.1 %copy-start.13 = (bf16[32,48,768]{2,1,0:T(8,128)(2,1)S(1)}, bf16[32,48,768]{2,1,0:T(8,128)(2,1)}, u32[]{:S(2)}) copy-start(bf16[32,48,768]{2,1,0:T(8,128)(2,1)} %copy-done.12) | copy-start | bytes 7077892
  141.3 6.7 %collective-permute-start.30 = (bf16[32,1536]{1,0:T(8,128)(2,1)S(1)}, bf16[32,1536]{1,0:T(8,128)(2,1)S(1)}, u32[]{:S(2)}, u32[]{:S(2)}) collective-permute-start(bf16[32,1536]{1,0:T(8,128)(2,1)S(1)} %add_convert_fusion), channel_id=1, source_target_pairs={{0,16},{1,17},{2,18},{3,19},{4,20},{5,21},{6,22},{7,23},{8,24},{9,... | collective-permute-start | bytes 294920 | tf_op jit(solution)/shard_map/ppermute | solution.py:398
  143.0 14.1 %collective-permute-start.22 = (bf16[8,48,768]{2,1,0:T(8,128)(2,1)S(1)}, bf16[8,48,768]{2,1,0:T(8,128)(2,1)S(1)}, u32[]{:S(2)}, u32[]{:S(2)}) collective-permute-start(bf16[8,48,768]{2,1,0:T(8,128)(2,1)S(1)} %bitcast.160), channel_id=1, source_target_pairs={{0,4},{1,5},{2,6},{3,7},{4,0},{5,1},{6,2},{7,3},{8,12},{9,13},{10,... | collective-permute-start | bytes 1769480 | tf_op jit(solution)/shard_map/ppermute | solution.py:398
  144.5 14.6 %collective-permute-start.17 = (bf16[8,48,768]{2,1,0:T(8,128)(2,1)S(1)}, bf16[8,48,768]{2,1,0:T(8,128)(2,1)S(1)}, u32[]{:S(2)}, u32[]{:S(2)}) collective-permute-start(bf16[8,48,768]{2,1,0:T(8,128)(2,1)S(1)} %slice_bitcast_fusion.4), channel_id=1, source_target_pairs={{0,2},{1,3},{2,0},{3,1},{4,6},{5,7},{6,4},{7,5},{8,10},{9,11},{10,... | collective-permute-start | bytes 1769480 | tf_op jit(solution)/shard_map/ppermute | solution.py:398
  157.3 7.2 %collective-permute-start.23 = (bf16[4,48,768]{2,1,0:T(8,128)(2,1)S(1)}, bf16[4,48,768]{2,1,0:T(8,128)(2,1)S(1)}, u32[]{:S(2)}, u32[]{:S(2)}) collective-permute-start(bf16[4,48,768]{2,1,0:T(8,128)(2,1)S(1)} %slice_bitcast_fusion.6), channel_id=1, source_target_pairs={{0,2},{1,3},{2,0},{3,1},{4,6},{5,7},{6,4},{7,5},{8,10},{9,11},{10,... | collective-permute-start | bytes 884744 | tf_op jit(solution)/shard_map/ppermute | solution.py:398
  159.2 6.8 %collective-permute-start.18 = (bf16[4,48,768]{2,1,0:T(8,128)(2,1)S(1)}, bf16[4,48,768]{2,1,0:T(8,128)(2,1)S(1)}, u32[]{:S(2)}, u32[]{:S(2)}) collective-permute-start(bf16[4,48,768]{2,1,0:T(8,128)(2,1)S(1)} %slice_bitcast_fusion.8), channel_id=1, source_target_pairs={{0,4},{1,5},{2,6},{3,7},{4,0},{5,1},{6,2},{7,3},{8,12},{9,13},{10,... | collective-permute-start | bytes 884744 | tf_op jit(solution)/shard_map/ppermute | solution.py:398
  164.6 5.2 %collective-permute-start.24 = (bf16[2,48,768]{2,1,0:T(8,128)(2,1)S(1)}, bf16[2,48,768]{2,1,0:T(8,128)(2,1)S(1)}, u32[]{:S(2)}, u32[]{:S(2)}) collective-permute-start(bf16[2,48,768]{2,1,0:T(8,128)(2,1)S(1)} %slice_bitcast_fusion.10), channel_id=1, source_target_pairs={{0,8},{1,9},{2,10},{3,11},{4,12},{5,13},{6,14},{7,15},{8,0},{9,1},... | collective-permute-start | bytes 442376 | tf_op jit(solution)/shard_map/ppermute | solution.py:398
  166.1 6.8 %collective-permute-start.19 = (bf16[2,48,768]{2,1,0:T(8,128)(2,1)S(1)}, bf16[2,48,768]{2,1,0:T(8,128)(2,1)S(1)}, u32[]{:S(2)}, u32[]{:S(2)}) collective-permute-start(bf16[2,48,768]{2,1,0:T(8,128)(2,1)S(1)} %slice_bitcast_fusion.12), channel_id=1, source_target_pairs={{0,8},{1,9},{2,10},{3,11},{4,12},{5,13},{6,14},{7,15},{8,0},{9,1},... | collective-permute-start | bytes 442376 | tf_op jit(solution)/shard_map/ppermute | solution.py:398
  169.8 5.3 %collective-permute-start.25 = (bf16[1,48,768]{2,1,0:T(8,128)(2,1)S(1)}, bf16[1,48,768]{2,1,0:T(8,128)(2,1)S(1)}, u32[]{:S(2)}, u32[]{:S(2)}) collective-permute-start(bf16[1,48,768]{2,1,0:T(8,128)(2,1)S(1)} %slice_bitcast_fusion.14), channel_id=1, source_target_pairs={{0,16},{1,17},{2,18},{3,19},{4,20},{5,21},{6,22},{7,23},{8,24},{9,... | collective-permute-start | bytes 221192 | tf_op jit(solution)/shard_map/ppermute | solution.py:398
  173.0 6.1 %collective-permute-start.20 = (bf16[1,48,768]{2,1,0:T(8,128)(2,1)S(1)}, bf16[1,48,768]{2,1,0:T(8,128)(2,1)S(1)}, u32[]{:S(2)}, u32[]{:S(2)}) collective-permute-start(bf16[1,48,768]{2,1,0:T(8,128)(2,1)S(1)} %slice_bitcast_fusion.16), channel_id=1, source_target_pairs={{0,16},{1,17},{2,18},{3,19},{4,20},{5,21},{6,22},{7,23},{8,24},{9,... | collective-permute-start | bytes 221192 | tf_op jit(solution)/shard_map/ppermute | solution.py:398

commit v2 on v0

v2 whole, which is shorter than its diff:
```python
import functools

import jax
import jax.numpy as jnp
from jax import lax
from jax.experimental import pallas as pl
from jax.experimental.pallas import tpu as pltpu
from jax.sharding import PartitionSpec as P

EPSILON = 1e-05
BF = jnp.bfloat16
F32 = jnp.float32
LANES = 128
PAD = 16
MIB = 1 << 20
VMEM_MIB = 8


def params(mib):
    return pltpu.CompilerParams(vmem_limit_bytes=mib * MIB)


WHOLE = pl.BlockSpec(memory_space=pltpu.VMEM)
SCALARS = pl.BlockSpec(memory_space=pltpu.SMEM)
ANYWHERE = pl.BlockSpec(memory_space=pl.ANY)
CW = 256


def cost(micros):
    return pl.CostEstimate(flops=0, bytes_accessed=int(micros * 3.0e6), transcendentals=0)


def shape(dims, dtype):
    return jax.ShapeDtypeStruct(dims, dtype)


def near(dims, dtype):
    return pltpu.VMEM(dims, dtype)


def turn_body(place_ref, cot_ref, *rest):
    mine_ref, other_ref, held_ref = rest[-3:]
    blocks = mine_ref.shape[0]
    per = mine_ref.shape[1]
    held_ref[...] = cot_ref[...].T
    core = place_ref[0]
    half = place_ref[1]

    def step(j, _):
        row = pl.multiple_of(lax.bitwise_xor(half, j) * (2 * per), 2 * per)
        mine_ref[j] = held_ref[pl.ds(pl.multiple_of(row + core * per, per), per), :]
        other_ref[j] = held_ref[pl.ds(pl.multiple_of(row + (1 - core) * per, per), per), :]
        return 0

    lax.fori_loop(0, blocks, step, 0, unroll=2)


def turn(n, place, cot, after):
    rows, d = cot.shape
    out = shape((n // 2, d // n, rows), BF)
    return pl.pallas_call(
        turn_body,
        in_specs=[SCALARS, WHOLE] + [ANYWHERE] * len(after),
        out_specs=[WHOLE] * 2,
        out_shape=[out] * 2,
        scratch_shapes=[pltpu.VMEM((d, rows), BF)],
        compiler_params=params(VMEM_MIB),
        cost_estimate=cost(2),
        name="turn",
    )(place, cot, *after)


def edges_out(odd, first, last, a_ref, b_ref):
    @pl.when(odd == 0)
    def _():
        a_ref[...] = last
        b_ref[...] = first

    @pl.when(odd != 0)
    def _():
        a_ref[...] = first
        b_ref[...] = last


def front_body(
    utt, place_ref, x_hbm, vec_ref, w_hbm,
    gated_ref, p_ref, q_ref, hat_ref, rstd_ref, a_ref, b_ref, normed_ref, x_ref, w_ref, x_sem, w_sem,
):
    rows, d = x_ref.shape
    frames = rows // utt
    pieces = x_sem.shape[0]
    span = rows // pieces
    steps = d // CW

    def x_copy(i):
        at = pl.ds(i * span, span)
        return pltpu.make_async_copy(x_hbm.at[at], x_ref.at[at], x_sem.at[i])

    def w_copy(j, half):
        at = pl.ds(half * d + j * CW, CW)
        return pltpu.make_async_copy(w_hbm.at[:, at], w_ref.at[:, at], w_sem.at[j, half])

    for i in range(pieces):
        x_copy(i).start()
    for j in range(steps):
        for half in range(2):
            w_copy(j, half).start()

    for i in range(pieces):
        x_copy(i).wait()

        for k in range(i * span, (i + 1) * span, 16):
            at = slice(k, k + 16)
            x = x_ref[at, :].astype(F32)
            mu = jnp.sum(x, axis=-1, keepdims=True) * (1.0 / d)
            c = x - mu
            var = jnp.sum(c * c, axis=-1, keepdims=True) * (1.0 / d)
            rstd = lax.rsqrt(var + EPSILON)
            hat = c * rstd
            rstd_ref[at, :] = rstd
            hat_ref[at, :] = hat.astype(BF)
            normed_ref[at, :] = (hat * vec_ref[0:1, :]).astype(BF)

    odd = place_ref[0] != 0
    for j in range(steps):
        cols = slice(j * CW, (j + 1) * CW)
        for half in range(2):
            w_copy(j, half).wait()
        value = jnp.dot(normed_ref[...], w_ref[:, cols], preferred_element_type=F32)
        gate = jnp.dot(
            normed_ref[...], w_ref[:, d + j * CW : d + (j + 1) * CW], preferred_element_type=F32
        )
        sig = jax.nn.sigmoid(gate)
        gated = value * sig
        held = gated.astype(BF)
        gated_ref[:, cols] = held
        p_ref[:, cols] = sig.astype(BF)
        q_ref[:, cols] = (gated * (1.0 - sig)).astype(BF)
        shaped = held.reshape(utt, frames, CW)
        first, last = shaped[:, :PAD], shaped[:, frames - PAD :]
        a_ref[:, :, cols] = jnp.where(odd, first, last)
        b_ref[:, :, cols] = jnp.where(odd, last, first)


def front(utt, place, x, vec, w_in):
    rows, d = x.shape
    out = near((rows, d), BF)
    edge = shape((utt, PAD, d), BF)
    return pl.pallas_call(
        functools.partial(front_body, utt),
        in_specs=[SCALARS, ANYWHERE, WHOLE, ANYWHERE],
        out_specs=[WHOLE] * 7,
        out_shape=[out] * 4 + [near((rows, 1), F32)] + [edge] * 2,
        scratch_shapes=[
            pltpu.VMEM((rows, d), BF),
            pltpu.VMEM((rows, d), BF),
            pltpu.VMEM((d, 2 * d), BF),
            pltpu.SemaphoreType.DMA((4,)),
            pltpu.SemaphoreType.DMA((d // CW, 2)),
        ],
        compiler_params=params(52),
        cost_estimate=cost(10),
        name="front",
    )(place, x, vec, w_in)


def lane_groups(first, last, work):
    def step(i, _):
        for slot in range(2):
            group = 2 * i + slot
            work(group, pl.ds(pl.multiple_of(group * LANES, LANES), LANES), slot)
        return 0

    lax.fori_loop(first // (2 * LANES), last // (2 * LANES), step, 0)


def conv_body(utt, place_ref, g_ref, a_ref, b_ref, k_ref, conv_ref, sums_ref, pad_ref):
    d = g_ref.shape[1]
    frames = g_ref.shape[0] // utt
    taps = k_ref.shape[0]
    block = 64
    odd = place_ref[0] != 0

    def work(_, lanes, slot):
        first = square = jnp.zeros((8, LANES), F32)
        for u in range(utt):
            a = a_ref[u, :, lanes].astype(F32)
            b = b_ref[u, :, lanes].astype(F32)
            pad_ref[slot, u, 0:PAD, :] = jnp.where(odd, a, b)
            rows = slice(u * frames, (u + 1) * frames)
            pad_ref[slot, u, PAD : PAD + frames, :] = g_ref[rows, lanes].astype(F32)
            pad_ref[slot, u, PAD + frames : PAD + frames + PAD, :] = jnp.where(odd, b, a)
            for base in range(0, frames, block):
                acc = jnp.zeros((block, LANES), F32)
                for r in range(8):
                    w = pad_ref[slot, u, base + r + 1 : base + r + 1 + block + taps - 8, :]
                    for q in range(taps // 8):
                        tap = 8 * q + r
                        acc = acc + k_ref[tap : tap + 1, lanes] * w[8 * q : 8 * q + block]
                conv_ref[u * frames + base : u * frames + base + block, lanes] = acc
                part = acc.reshape(block // 8, 8, LANES)
                first = first + jnp.sum(part, axis=0)
                square = square + jnp.sum(part * part, axis=0)
        sums_ref[0:1, lanes] = jnp.sum(first, axis=0, keepdims=True)
        sums_ref[1:2, lanes] = jnp.sum(square, axis=0, keepdims=True)

    lane_groups(0, d, work)


def conv(utt, place, gated, a, b, kernel):
    rows, d = gated.shape
    frames = rows // utt
    return pl.pallas_call(
        functools.partial(conv_body, utt),
        in_specs=[SCALARS] + [WHOLE] * 4,
        out_specs=[WHOLE] * 2,
        out_shape=[near(gated.shape, F32), shape((2, d), F32)],
        scratch_shapes=[pltpu.VMEM((2, utt, frames + 2 * PAD + 8, LANES), F32)],
        compiler_params=params(VMEM_MIB),
        cost_estimate=cost(7),
        name="conv",
    )(place, gated, a, b, kernel)


def middle_body(
    utt, total, place_ref, conv_ref, sums_ref, vec_ref, cot_ref, w_ref,
    *rest,
):
    act_ref, dbn_ref, dsums_ref, a_ref, b_ref = rest[-5:]
    rows, d = conv_ref.shape
    frames = rows // utt
    odd = place_ref[0] != 0
    for j in range(d // CW):
        cols = slice(j * CW, (j + 1) * CW)
        mean = sums_ref[0:1, cols] * (1.0 / total)
        var = sums_ref[1:2, cols] * (1.0 / total) - mean * mean
        rstd = lax.rsqrt(var + EPSILON)
        conv = conv_ref[:, cols]
        xhat = (conv - mean) * rstd
        out = xhat * vec_ref[1:2, cols] + vec_ref[2:3, cols]
        sig = jax.nn.sigmoid(out)
        act = out * sig
        act_ref[:, cols] = act.astype(BF)
        d_act = jnp.dot(cot_ref[...], w_ref[:, cols], preferred_element_type=F32)
        dbn = d_act * (sig + act * (1.0 - sig))
        dbn_ref[:, cols] = dbn
        dsums_ref[0:1, cols] = jnp.sum(dbn, axis=0, keepdims=True)
        dsums_ref[1:2, cols] = jnp.sum(dbn * xhat, axis=0, keepdims=True)
        for u in range(utt):
            low = slice(u * frames, u * frames + PAD)
            high = slice((u + 1) * frames - PAD, (u + 1) * frames)
            for at, piece in ((slice(0, PAD), dbn), (slice(PAD, 2 * PAD), conv)):
                first, last = piece[low].astype(BF), piece[high].astype(BF)
                a_ref[u, at, cols] = jnp.where(odd, first, last)
                b_ref[u, at, cols] = jnp.where(odd, last, first)


def middle(utt, total, place, conv_out, sums, vec, cot, w_out, after):
    rows, d = cot.shape
    edge = shape((utt, 2 * PAD, d), BF)
    return pl.pallas_call(
        functools.partial(middle_body, utt, total),
        in_specs=[SCALARS] + [WHOLE] * 5 + [ANYWHERE] * len(after),
        out_specs=[WHOLE] * 5,
        out_shape=[shape((rows, d), BF), near((rows, d), F32), shape((2, d), F32), edge, edge],
        compiler_params=params(VMEM_MIB),
        cost_estimate=cost(4),
        name="middle",
    )(place, conv_out, sums, vec, cot, w_out, *after)


def grad_body(bits, ca_ref, cb_ref, acta_ref, actb_ref, *rest):
    out_refs = rest[-4:]
    blocks, per, rows = ca_ref.shape
    half = out_refs[0].shape[-1]
    ca = ca_ref[...].reshape(blocks * per, rows)
    cb = cb_ref[...].reshape(blocks * per, rows)
    for side, bit in enumerate(bits):
        send_ref, keep_ref = out_refs[2 * side], out_refs[2 * side + 1]
        for c in range(half // CW):
            cols = slice(c * CW, (c + 1) * CW)
            src = slice(side * half + c * CW, side * half + (c + 1) * CW)
            dw = jnp.dot(ca, acta_ref[:, src], preferred_element_type=F32)
            dw += jnp.dot(cb, actb_ref[:, src], preferred_element_type=F32)
            sent = kept = 0
            for j in range(blocks):
                block = dw[j * per : (j + 1) * per]
                if j & bit:
                    send_ref[sent, :, cols] = block.astype(BF)
                    sent += 1
                else:
                    keep_ref[kept, :, cols] = block
                    kept += 1


def grad(bits, cot_a, cot_b, act_a, act_b, after):
    blocks, per, _ = cot_a.shape
    d = act_a.shape[1]
    half = (blocks // 2, per, d // 2)
    return pl.pallas_call(
        functools.partial(grad_body, bits),
        in_specs=[WHOLE] * 4 + [ANYWHERE] * len(after),
        out_specs=[WHOLE] * 4,
        out_shape=[shape(half, BF), shape(half, F32)] * 2,
        compiler_params=params(VMEM_MIB),
        cost_estimate=cost(3.5),
        name="grad",
    )(cot_a, cot_b, act_a, act_b, *after)


def branch_body(x_ref, act_ref, w_ref, *rest):
    out_ref = rest[-1]
    for j in range(out_ref.shape[-1] // CW):
        cols = slice(j * CW, (j + 1) * CW)
        part = lax.dot_general(
            act_ref[...], w_ref[cols, :], (((1,), (1,)), ((), ())), preferred_element_type=F32
        )
        out_ref[:, cols] = (x_ref[:, cols].astype(F32) + part).astype(BF)


def branch(x, act, w_out, after):
    rows, d = x.shape
    return pl.pallas_call(
        branch_body,
        in_specs=[WHOLE] * 3 + [ANYWHERE] * len(after),
        out_specs=WHOLE,
        out_shape=shape((rows, d), BF),
        compiler_params=params(VMEM_MIB),
        cost_estimate=cost(4),
        name="branch",
    )(x, act, w_out, *after)


def grad_taps_body(
    utt, total, place_ref, dbn_ref, conv_ref, a_ref, b_ref, sums_ref, dsums_ref, vec_ref, g_ref,
    dk_ref, dc_ref, acc_ref,
):
    d = g_ref.shape[1]
    frames = g_ref.shape[0] // utt
    taps = dk_ref.shape[0]
    block = 64
    odd = place_ref[0] != 0
    keep_lo = place_ref[2].astype(F32)
    keep_hi = place_ref[3].astype(F32)

    def work(group, lanes, slot):
        mean = sums_ref[0:1, lanes] * (1.0 / total)
        var = sums_ref[1:2, lanes] * (1.0 / total) - mean * mean
        rstd = lax.rsqrt(var + EPSILON)
        scale = rstd * vec_ref[1:2, lanes]
        cross = scale * rstd * (dsums_ref[1:2, lanes] * (1.0 / total))
        mean_grad = scale * (dsums_ref[0:1, lanes] * (1.0 / total))

        def d_conv(dbn, conv):
            return dbn.astype(F32) * scale - mean_grad - (conv.astype(F32) - mean) * cross

        for u in range(utt):
            a = d_conv(a_ref[u, :PAD, lanes], a_ref[u, PAD:, lanes])
            b = d_conv(b_ref[u, :PAD, lanes], b_ref[u, PAD:, lanes])
            rows = slice(u * frames, (u + 1) * frames)
            dc_ref[group, u, 0:PAD, :] = jnp.where(odd, a, b) * keep_lo
            dc_ref[group, u, PAD : PAD + frames, :] = d_conv(dbn_ref[rows, lanes], conv_ref[rows, lanes])
            dc_ref[group, u, PAD + frames : PAD + frames + PAD, :] = jnp.where(odd, b, a) * keep_hi
            for base in range(0, frames, block):
                g = g_ref[u * frames + base : u * frames + base + block, lanes].astype(F32)
                for r in range(8):
                    w = dc_ref[group, u, base + r : base + r + block + taps - 8, :]
                    for q in range(taps // 8):
                        tap = taps - 1 - (8 * q + r)
                        prod = g * w[8 * q : 8 * q + block]
                        prod = jnp.sum(prod.reshape(block // 8, 8, LANES), axis=0)
                        if u or base:
                            prod = acc_ref[slot, tap] + prod
                        acc_ref[slot, tap] = prod
        dk_ref[:, lanes] = jnp.sum(acc_ref[slot], axis=1).astype(BF)

    lane_groups(0, d, work)


def grad_taps(utt, total, taps, place, dbn, conv_out, halos, sums, dsums, vec, gated):
    rows, d = gated.shape
    return pl.pallas_call(
        functools.partial(grad_taps_body, utt, total),
        in_specs=[SCALARS] + [WHOLE] * 8,
        out_specs=[WHOLE] * 2,
        out_shape=[
            shape((taps, d), BF),
            near((d // LANES, utt, rows // utt + 2 * PAD, LANES), F32),
        ],
        scratch_shapes=[pltpu.VMEM((2, taps, 8, LANES), F32)],
        compiler_params=params(VMEM_MIB),
        cost_estimate=cost(9),
        name="grad_taps",
    )(place, dbn, conv_out, *halos, sums, dsums, vec, gated)


def grad_proj_body(utt, start, dc_ref, k_ref, p_ref, q_ref, *rest):
    dv_ref, dg_ref = rest[-2:]
    rows, width = dv_ref.shape
    frames = rows // utt
    taps = k_ref.shape[0]
    block = 64

    def work(group, out, slot):
        lanes = pl.ds(pl.multiple_of(out.start + start, LANES), LANES)
        for u in range(utt):
            for base in range(0, frames, block):
                at = slice(u * frames + base, u * frames + base + block)
                acc = jnp.zeros((block, LANES), F32)
                for r in range(8):
                    w = dc_ref[group + start // LANES, u, base + r : base + r + block + taps - 8, :]
                    for q in range(taps // 8):
                        tap = taps - 1 - (8 * q + r)
                        acc = acc + k_ref[tap : tap + 1, lanes] * w[8 * q : 8 * q + block]
                dv_ref[at, out] = (acc * p_ref[at, lanes].astype(F32)).astype(BF)
                dg_ref[at, out] = (acc * q_ref[at, lanes].astype(F32)).astype(BF)

    lane_groups(0, width, work)


def grad_proj(utt, start, width, d_conv, kernel, p, q, after):
    rows = p.shape[0]
    out = near((rows, width), BF)
    return pl.pallas_call(
        functools.partial(grad_proj_body, utt, start),
        in_specs=[WHOLE] * 4 + [ANYWHERE] * len(after),
        out_specs=[WHOLE] * 2,
        out_shape=[out, out],
        compiler_params=params(VMEM_MIB),
        cost_estimate=cost(4),
        name="grad_proj",
    )(d_conv, kernel, p, q, *after)


def back_norm_body(hat_ref, rstd_ref, cot_ref, vec_ref, w_ref, *rest):
    pieces = rest[:4]
    out_ref, acc_ref = rest[-2:]
    rows, d = hat_ref.shape
    wide = pieces[0].shape[1]
    dims = (((1,), (1,)), ((), ()))
    for j in range(d // CW):
        cols = slice(j * CW, (j + 1) * CW)
        part = 0.0
        for k, piece in enumerate(pieces):
            part += lax.dot_general(
                piece[...], w_ref[cols, k * wide : (k + 1) * wide], dims, preferred_element_type=F32
            )
        acc_ref[:, cols] = part * vec_ref[0:1, cols]
    for i in range(0, rows, 16):
        at = slice(i, i + 16)
        hat = hat_ref[at, :].astype(F32)
        grads = acc_ref[at, :]
        m1 = jnp.sum(grads, axis=-1, keepdims=True) * (1.0 / d)
        m2 = jnp.sum(grads * hat, axis=-1, keepdims=True) * (1.0 / d)
        layer = rstd_ref[at, :] * (grads - m1 - hat * m2)
        out_ref[at, :] = (cot_ref[at, :].astype(F32) + layer).astype(BF)


def back_norm(hat, rstd, cot, vec, w_in, pieces, after):
    rows, d = hat.shape
    return pl.pallas_call(
        back_norm_body,
        in_specs=[WHOLE] * 9 + [ANYWHERE] * len(after),
        out_specs=WHOLE,
        out_shape=shape((rows, d), BF),
        scratch_shapes=[pltpu.VMEM((rows, d), F32)],
        compiler_params=params(VMEM_MIB),
        cost_estimate=cost(7),
        name="back_norm",
    )(hat, rstd, cot, vec, w_in, *pieces, *after)


def swap(block, axis, bit):
    count = lax.axis_size(axis)
    return lax.ppermute(block, axis, [(i, i ^ bit) for i in range(count)])


def is_power(count):
    return count & (count - 1) == 0


def add_body(own_ref, got_ref, *rest):
    out_ref = rest[-1]
    out_ref[...] = (own_ref[...].astype(F32) + got_ref[...].astype(F32)).astype(out_ref.dtype)


def add(own, got, dtype, after):
    return pl.pallas_call(
        add_body,
        in_specs=[WHOLE] * 2 + [ANYWHERE] * len(after),
        out_specs=WHOLE,
        out_shape=shape(own.shape, dtype),
        compiler_params=params(4),
        cost_estimate=cost(0.5),
        name="add",
    )(own, got, *after)


def all_sum(block, axis, fill=(), far_first=False):
    count = lax.axis_size(axis)
    if not is_power(count):
        for work in fill:
            work([])
        return lax.psum(block.astype(F32), axis)
    bits = [1 << i for i in range(count.bit_length() - 1)]
    if far_first:
        bits = bits[:1] + bits[3:] + bits[1:3]
    for step, bit in enumerate(bits):
        other = swap(block, axis, bit)
        after = fill[step]([block]) if step < len(fill) else []
        block = add(block, other, F32 if bit == bits[-1] else block.dtype, after)
    return block


def nothing(_):
    return []


def beside(a, b, axis):
    count = lax.axis_size(axis)
    pairs = []
    for low in range(1, count - 1, 2):
        pairs += [(low, low + 1), (low + 1, low)]
    return swap(a, axis, 1), lax.ppermute(b, axis, pairs)


def merge_body(sides, after, *refs):
    keep_out, send_out = refs[2 * sides + after :]
    blocks = refs[0].shape[0]
    wide = refs[0].shape[2]
    for side in range(sides):
        keep_ref, got_ref = refs[2 * side : 2 * side + 2]
        cols = slice(side * wide, (side + 1) * wide)
        for j in range(blocks):
            total = keep_ref[j] + got_ref[j].astype(F32)
            if j % 2:
                send_out[j // 2, :, cols] = total.astype(BF)
            else:
                keep_out[j // 2, :, cols] = total


def merge(pairs, after):
    blocks, per, wide = pairs[0][0].shape
    dims = (blocks // 2, per, wide * len(pairs))
    return pl.pallas_call(
        functools.partial(merge_body, len(pairs), len(after)),
        in_specs=[WHOLE] * (2 * len(pairs)) + [ANYWHERE] * len(after),
        out_specs=[WHOLE] * 2,
        out_shape=[shape(dims, F32), shape(dims, BF)],
        compiler_params=params(8),
        cost_estimate=cost(1),
        name="merge",
    )(*[a for pair in pairs for a in pair], *after)


def first_swaps(parts, axis, after):
    return [
        merge([(keep, swap(send, axis, device_bit))], after)
        for (keep, send), device_bit in zip(parts, (2, 4))
    ]


def last_swaps(held, axis, after):
    count = lax.axis_size(axis)
    after = list(after)
    pairs = [
        (keep, swap(send, axis, device_bit)) for (keep, send), device_bit in zip(held, (4, 2))
    ]
    bit = 8
    if bit == count:
        return jnp.concatenate([keep + got for keep, got in pairs], axis=-1)[0]
    while True:
        keep, send = merge(pairs, after.pop(0) if after else [])
        got = swap(send, axis, bit)
        bit *= 2
        if bit == count:
            return add(keep[0], got[0], F32, [])
        pairs = [(keep, got)]


def on_device(inputs, ln_gain, w_in, kernel, bn_gain, bn_bias, w_out, cotangent):
    axis = "seq"
    n = lax.axis_size(axis)
    me = lax.axis_index(axis).astype(jnp.int32)
    utt, frames, d = inputs.shape
    rows = utt * frames
    half = d // 2
    total = rows * n
    x = inputs.reshape(rows, d)
    cot = cotangent.reshape(rows, d)
    vec = jnp.concatenate([ln_gain, bn_gain, bn_bias]).reshape(3, d)
    place = jnp.stack([me % 2, me // 2, (me > 0).astype(jnp.int32), (me < n - 1).astype(jnp.int32)])
    by_owner = is_power(n) and n >= 8 and d % n == 0 and (d // n) % 16 == 0

    gated, p, q, hat, rstd, ga, gb = front(utt, place, x, vec, w_in)
    ga, gb = beside(ga, gb, axis)
    conv_out, sums = conv(utt, place, gated, ga, gb, kernel)
    made = {}

    def turning(after):
        made["a"], other = turn(n, place, cot, after)
        made["b"] = swap(other, axis, 1)
        return [made["a"]]

    if by_owner:
        sums = all_sum(sums, axis, [nothing, turning])
        waits = [made["b"]]
    else:
        sums = all_sum(sums, axis)
        waits = []

    act, dbn, dsums, da, db = middle(utt, total, place, conv_out, sums, vec, cot, w_out, waits)
    da, db = beside(da, db, axis)

    def branching(after):
        made["outputs"] = branch(x, act, w_out, after)
        return [made["outputs"]]

    def grading(after):
        made["grad"] = grad((1, 2), made["a"], made["b"], act, act_b, after)
        return [made["grad"][0]]

    if by_owner:
        act_b = swap(act, axis, 1)
        dsums = all_sum(dsums, axis, [nothing, branching, lambda _: [da, db], grading])
        send_l, keep_l, send_r, keep_r = made["grad"]
        held = first_swaps([(keep_l, send_l), (keep_r, send_r)], axis, [dsums])
    else:
        dsums = all_sum(dsums, axis, [nothing, branching])
        dw = lax.dot_general(cot, act, (((0,), (0,)), ((), ())), preferred_element_type=F32)
        d_w_out = lax.psum_scatter(dw, axis, scatter_dimension=0, tiled=True)

    d_kernel, d_conv = grad_taps(
        utt, total, kernel.shape[0], place, dbn, conv_out, (da, db), sums, dsums, vec, gated
    )
    half = d // 2

    def projecting(start):
        def work(after):
            made[start] = grad_proj(utt, start, half, d_conv, kernel, p, q, after)
            return [made[start][0]]

        return work

    def norming(after):
        left, right = made[0], made[half]
        made["d_inputs"] = back_norm(
            hat, rstd, cot, vec, w_in, (left[0], right[0], left[1], right[1]), after
        )
        return [made["d_inputs"]]

    d_kernel_sum = all_sum(
        d_kernel, axis, [nothing, projecting(0), projecting(half), norming], far_first=True
    )
    if by_owner:
        d_w_out = last_swaps(held, axis, [[d_kernel], [made[half][0]]])
    return (
        made["outputs"].reshape(inputs.shape), made["d_inputs"].reshape(inputs.shape), d_w_out,
        d_kernel_sum, dsums[1], dsums[0],
    )


def solution(mesh):
    return jax.shard_map(
        on_device,
        mesh=mesh,
        in_specs=(P(None, "seq", None), P(), P(), P(), P(), P(), P(), P(None, "seq", None)),
        out_specs=(P(None, "seq", None), P(None, "seq", None), P("seq", None), P(), P(), P()),
        check_vma=False,
    )
```

time: 449 us -> 136 us (0.30)
  waiting for transfers between devices: 212 us -> 29.2 us
  blocking collectives: 85.2 us -> 0 us
  other arithmetic: 63.5 us -> 1.33 us
  Pallas kernels: 0 us -> 57.8 us
  matrix products: 41.6 us -> 0 us
  starting transfers between devices: 6.78 us -> 42 us
  local copies, waits for them, and re-layouts: 24.1 us -> 4.12 us
  between operations: 14.8 us -> 0.89 us
    unnamed x3 -> x0, waiting for transfers between devices: 143 us -> none
    psum x2 -> x0, blocking collectives: 85.2 us -> none  [the longest x1 43.9 us: on_device(): lax.psum((jnp.sum(conv_out, axis=(0, 1)), jnp.sum(conv_out * conv_out, ax...]
    psum x1 -> x0, waiting for transfers between devices: 65.4 us -> none  [on_device(): d_kernel = lax.psum(jnp.stack(kernel_rows), 'seq')]
    pallas_call x0 -> x30, Pallas kernels: none -> 57.8 us  [the longest x1 12.5 us: front(): pl.pallas_call(functools.partial(front_body, utt), in_specs=[SCALARS, ANY...]
    reduce_sum x8 -> x0, other arithmetic: 43.8 us -> none  [the longest x4 21 us: on_device(): kernel_rows.append(jnp.sum(window * d_conv, axis=(0, 1)))]
    dot_general x5 -> x0, matrix products: 41.6 us -> none  [the longest x1 10.3 us: on_device(): d_act = jnp.dot(cot_rows, w_out, preferred_element_type=jnp.float32)]
    ppermute x4 -> x27, starting transfers between devices: 6.7 us -> 42 us  [the longest x25 40.5 us: swap(): return lax.ppermute(block, axis, [(i, i ^ bit) for i in range(count)])]
    ppermute x4 -> x27, waiting for transfers between devices: 3.39 us -> 29.2 us  [the longest x25 29.2 us: swap(): return lax.ppermute(block, axis, [(i, i ^ bit) for i in range(count)])]
  transfers between devices with their start and end apart: 6 -> 27, of which waited for: 3 -> 15; matrix products, arithmetic and copies ran while one was open for 12% -> 0% of each run, Pallas kernels for 0% -> 21%
where the time goes in v2:
time: 136 us; the launch traced here: 135 us
  Pallas kernels  57.8 us (42%)
  starting transfers between devices  42 us (31%)
  waiting for transfers between devices  29.2 us (21%)
  local copies, waits for them, and re-layouts  4.12 us (3%)
    ppermute x25, starting transfers between devices, swap(): return lax.ppermute(block, axis, [(i, i ^ bit) for i in range(count)])  40.5 us
    ppermute x25, waiting for transfers between devices, swap(): return lax.ppermute(block, axis, [(i, i ^ bit) for i in range(count)])  29.2 us
    pallas_call x1, Pallas kernels, front(): pl.pallas_call(functools.partial(front_body, utt), in_specs=[SCALARS, ANY...  12.5 us
    pallas_call x1, Pallas kernels, grad_taps(): pl.pallas_call(functools.partial(grad_taps_body, utt, total), in_specs=[S...  8.64 us
    pallas_call x1, Pallas kernels, conv(): pl.pallas_call(functools.partial(conv_body, utt), in_specs=[SCALARS] + [W...  7.88 us
    pallas_call x2, Pallas kernels, grad_proj(): pl.pallas_call(functools.partial(grad_proj_body, utt, start), in_specs=[W...  7.88 us
    pallas_call x1, Pallas kernels, back_norm(): pl.pallas_call(back_norm_body, in_specs=[WHOLE] * 9 + [ANYWHERE] * len(af...  7.28 us
    pallas_call x1, Pallas kernels, middle(): pl.pallas_call(functools.partial(middle_body, utt, total), in_specs=[SCAL...  4.12 us
  transfers between devices with their start and end apart: 27, of which 15 were waited for; matrix products, arithmetic and copies ran while one was open for 0% of the time, Pallas kernels for 21%

profile of v2, /device:TPU:0, one launch (start us, length us, event | category | flops | bytes accessed | tf_op | source)
XLA Modules:
  0.0 135.3 jit_solution(3550195047472265439)
XLA Ops:
  0.7 0.7 pad_maximum_fusion
  1.4 0.6 reshape.28.vec_ref
  2.0 0.6 pad_add_fusion.place_ref
  2.6 12.5 %front.1 = (bf16[512,1536]{1,0:T(8,128)(2,1)S(1)}, bf16[512,1536]{1,0:T(8,128)(2,1)S(1)}, bf16[512,1536]{1,0:T(8,128)(2,1)S(1)}, bf16[512,1536]{1,0:T(8,128)(2,1...) custom-call(s32[4]{0:T(128)} %pad_add_fusion.place_ref, ...), custom_call_target="tpu_custom_call" | custom-call | bytes 30000000 | tf_op jit(solution)/shard_map/front/pallas_call | solution.py:149
  15.1 0.5 collective-permute-start
  15.6 0.7 collective-permute-start.1
  16.3 0.5 collective-permute-done.a_ref
  16.8 7.9 %conv.1 = (f32[512,1536]{1,0:T(8,128)S(1)}, f32[2,1536]{1,0:T(2,128)S(1)}) custom-call(s32[4]{0:T(128)S(1)} %copy-done.6, bf16[512,1536]{1,0:T(8,128)(2,1)S(1)} %get-tuple-element.40.g_ref, bf16[2,16,1536]{2,1,0:T(8,128)(2,1)S(1)} %collective-permute-done.a_ref, bf16[2,16,1536]{2,1,0:T(8,128)(2,1)S(1)} %collective-permute-done.1.b_ref, f32[32,1536]{1,0:T(8,128)S(1)} %copy-done.4), custom_call_target="tpu_custom_call" | custom-call | bytes 21000000 | tf_op jit(solution)/shard_map/conv/pallas_call | solution.py:213
  24.7 6.2 %collective-permute-start.2 = (f32[2,1536]{1,0:T(2,128)S(1)}, f32[2,1536]{1,0:T(2,128)S(1)}, u32[]{:S(2)}, u32[]{:S(2)}) collective-permute-start(f32[2,1536]{1,0:T(2,128)S(1)} %get-tuple-element.44.own_ref), channel_id=1, source_target_pairs={{0,1},{1,0},{2,3},{3,2},{4,5},{5,4},{6,7},{7,6},{8,9},{9,8},{10,11... | collective-permute-start | bytes 36872 | tf_op jit(solution)/shard_map/ppermute | solution.py:475
  30.9 0.8 collective-permute-done.2.got_ref
  31.8 1.1 turn.1
  32.9 0.4 collective-permute-start.7
  33.3 3.3 %collective-permute-start.3 = (f32[2,1536]{1,0:T(2,128)S(1)}, f32[2,1536]{1,0:T(2,128)S(1)}, u32[]{:S(2)}, u32[]{:S(2)}) collective-permute-start(f32[2,1536]{1,0:T(2,128)S(1)} %add.30.rest_0_.own_ref), channel_id=1, source_target_pairs={{0,2},{1,3},{2,0},{3,1},{4,6},{5,7},{6,4},{7,5},{8,10},{9,11},{10,... | collective-permute-start | bytes 36872 | tf_op jit(solution)/shard_map/ppermute | solution.py:475
  36.6 1.7 %collective-permute-done.3.got_ref = f32[2,1536]{1,0:T(2,128)S(1)} collective-permute-done((f32[2,1536]{1,0:T(2,128)S(1)}, f32[2,1536]{1,0:T(2,128)S(1)}, u32[]{:S(2)}, u32[]{:S(2)}) %collective-permute-start.3) | collective-permute-done | bytes 12320 | tf_op jit(solution)/shard_map/ppermute | solution.py:475
  38.3 1.8 %collective-permute-start.4 = (f32[2,1536]{1,0:T(2,128)S(1)}, f32[2,1536]{1,0:T(2,128)S(1)}, u32[]{:S(2)}, u32[]{:S(2)}) collective-permute-start(f32[2,1536]{1,0:T(2,128)S(1)} %add.31.own_ref), channel_id=1, source_target_pairs={{0,4},{1,5},{2,6},{3,7},{4,0},{5,1},{6,2},{7,3},{8,12},{9,13},{10,... | collective-permute-start | bytes 36872 | tf_op jit(solution)/shard_map/ppermute | solution.py:475
  40.1 1.9 %collective-permute-done.4.got_ref = f32[2,1536]{1,0:T(2,128)S(1)} collective-permute-done((f32[2,1536]{1,0:T(2,128)S(1)}, f32[2,1536]{1,0:T(2,128)S(1)}, u32[]{:S(2)}, u32[]{:S(2)}) %collective-permute-start.4) | collective-permute-done | bytes 12320 | tf_op jit(solution)/shard_map/ppermute | solution.py:475
  42.0 2.3 %collective-permute-start.5 = (f32[2,1536]{1,0:T(2,128)S(1)}, f32[2,1536]{1,0:T(2,128)S(1)}, u32[]{:S(2)}, u32[]{:S(2)}) collective-permute-start(f32[2,1536]{1,0:T(2,128)S(1)} %add.32.own_ref), channel_id=1, source_target_pairs={{0,8},{1,9},{2,10},{3,11},{4,12},{5,13},{6,14},{7,15},{8,0},{9,1},... | collective-permute-start | bytes 36872 | tf_op jit(solution)/shard_map/ppermute | solution.py:475
  44.3 1.7 %collective-permute-done.5.got_ref = f32[2,1536]{1,0:T(2,128)S(1)} collective-permute-done((f32[2,1536]{1,0:T(2,128)S(1)}, f32[2,1536]{1,0:T(2,128)S(1)}, u32[]{:S(2)}, u32[]{:S(2)}) %collective-permute-start.5) | collective-permute-done | bytes 12320 | tf_op jit(solution)/shard_map/ppermute | solution.py:475
  46.0 3.0 %collective-permute-start.6 = (f32[2,1536]{1,0:T(2,128)S(1)}, f32[2,1536]{1,0:T(2,128)S(1)}, u32[]{:S(2)}, u32[]{:S(2)}) collective-permute-start(f32[2,1536]{1,0:T(2,128)S(1)} %add.33.own_ref), channel_id=1, source_target_pairs={{0,16},{1,17},{2,18},{3,19},{4,20},{5,21},{6,22},{7,23},{8,24},{9,... | collective-permute-start | bytes 36872 | tf_op jit(solution)/shard_map/ppermute | solution.py:475
  49.0 1.7 %collective-permute-done.6.got_ref = f32[2,1536]{1,0:T(2,128)S(1)} collective-permute-done((f32[2,1536]{1,0:T(2,128)S(1)}, f32[2,1536]{1,0:T(2,128)S(1)}, u32[]{:S(2)}, u32[]{:S(2)}) %collective-permute-start.6) | collective-permute-done | bytes 12320 | tf_op jit(solution)/shard_map/ppermute | solution.py:475
  50.8 4.1 %middle.1 = (bf16[512,1536]{1,0:T(8,128)(2,1)S(1)}, f32[512,1536]{1,0:T(8,128)S(1)}, f32[2,1536]{1,0:T(2,128)S(1)}, bf16[2,32,1536]{2,1,0:T(8,128)(2,1)S(1)}, bf16[2,32,1536]{2,1,0:T(8,128)(2,1)S(1)}) custom-call(s32[4]{0:T(128)S(1)} %copy-done.6, f32[512,1536]{1,0:T(8,128)S(1)} %get-tuple-element.43.conv_ref, f32[2,1536]{1,0:T(2,128)S(1)} %add.34.sums_ref, ...), custom_call_target="tpu_custom_call" | custom-call | bytes 12000000 | tf_op jit(solution)/shard_map/middle/pallas_call | solution.py:261
  54.9 0.1 collective-permute-start.14
  55.0 0.9 collective-permute-start.10
  55.8 3.0 %collective-permute-start.9 = (bf16[2,32,1536]{2,1,0:T(8,128)(2,1)S(1)}, bf16[2,32,1536]{2,1,0:T(8,128)(2,1)S(1)}, u32[]{:S(2)}, u32[]{:S(2)}) collective-permute-start(bf16[2,32,1536]{2,1,0:T(8,128)(2,1)S(1)} %get-tuple-element.52), channel_id=1, source_target_pairs={{0,1},{1,0},{2,3},{3,2},{4,5},{5,4},{6,7},{7,6},{8,9},{9,8},{10,11... | collective-permute-start | bytes 589832 | tf_op jit(solution)/shard_map/ppermute | solution.py:475
  58.8 0.1 collective-permute-start.8
  58.9 1.1 collective-permute-done.8.got_ref
  60.0 1.3 collective-permute-start.11
  61.3 3.8 %branch.1.rest_0_ = bf16[512,1536]{1,0:T(8,128)(2,1)} custom-call(bf16[512,1536]{1,0:T(8,128)(2,1)S(1)} %bitcast.18, bf16[512,1536]{1,0:T(8,128)(2,1)S(1)} %get-tuple-element.47.act_ref.acta_ref, bf16[1536,1536]{1,0:T(8,128)(2,1)S(1)} %bitcast.13, f32[2,1536]{1,0:T(2,128)S(1)} %add.35.rest_0_.own_ref), custom_call_target="tpu_custom_call" | custom-call | bytes 12000000 | tf_op jit(solution)/shard_map/branch/pallas_call | solution.py:323
  65.1 1.4 %copy-done.2 = bf16[512,1536]{1,0:T(8,128)(2,1)S(1)} copy-done((bf16[512,1536]{1,0:T(8,128)(2,1)S(1)}, bf16[512,1536]{1,0:T(8,128)(2,1)}, u32[]{:S(2)}) %copy-start.2) | copy-done | bytes 1572888
  66.5 2.0 %collective-permute-start.12 = (f32[2,1536]{1,0:T(2,128)S(1)}, f32[2,1536]{1,0:T(2,128)S(1)}, u32[]{:S(2)}, u32[]{:S(2)}) collective-permute-start(f32[2,1536]{1,0:T(2,128)S(1)} %add.36.own_ref), channel_id=1, source_target_pairs={{0,4},{1,5},{2,6},{3,7},{4,0},{5,1},{6,2},{7,3},{8,12},{9,13},{10,... | collective-permute-start | bytes 36872 | tf_op jit(solution)/shard_map/ppermute | solution.py:475
  68.5 1.7 %collective-permute-done.12.got_ref = f32[2,1536]{1,0:T(2,128)S(1)} collective-permute-done((f32[2,1536]{1,0:T(2,128)S(1)}, f32[2,1536]{1,0:T(2,128)S(1)}, u32[]{:S(2)}, u32[]{:S(2)}) %collective-permute-start.12) | collective-permute-done | bytes 12320 | tf_op jit(solution)/shard_map/ppermute | solution.py:475
  70.3 2.6 %grad.1 = (bf16[8,48,768]{2,1,0:T(8,128)(2,1)S(1)}, f32[8,48,768]{2,1,0:T(8,128)S(1)}, bf16[8,48,768]{2,1,0:T(8,128)(2,1)S(1)}, f32[8,48,768]{2,1,0:T(8,128)S(1)}) custom-call(bf16[16,48,512]{2,1,0:T(8,128)(2,1)S(1)} %get-tuple-element.45.rest_0_.ca_ref, bf16[16,48,512]{2,1,0:T(8,128)(2,1)S(1)} %collective-permute-done.7.rest_0_.cb_ref, ...), custom_call_target="tpu_custom_call" | custom-call | bytes 10500000 | tf_op jit(solution)/shard_map/grad/pallas_call | solution.py:300
  72.9 2.0 %collective-permute-start.21 = (bf16[8,48,768]{2,1,0:T(8,128)(2,1)S(1)}, bf16[8,48,768]{2,1,0:T(8,128)(2,1)S(1)}, u32[]{:S(2)}, u32[]{:S(2)}) collective-permute-start(bf16[8,48,768]{2,1,0:T(8,128)(2,1)S(1)} %get-tuple-element.67), channel_id=1, source_target_pairs={{0,4},{1,5},{2,6},{3,7},{4,0},{5,1},{6,2},{7,3},{8,12},{9,13},{10,... | collective-permute-start | bytes 1769480 | tf_op jit(solution)/shard_map/ppermute | solution.py:475
  74.9 0.7 collective-permute-start.19
  75.6 1.6 %collective-permute-start.13 = (f32[2,1536]{1,0:T(2,128)S(1)}, f32[2,1536]{1,0:T(2,128)S(1)}, u32[]{:S(2)}, u32[]{:S(2)}) collective-permute-start(f32[2,1536]{1,0:T(2,128)S(1)} %add.37.rest_0_.own_ref), channel_id=1, source_target_pairs={{0,8},{1,9},{2,10},{3,11},{4,12},{5,13},{6,14},{7,15},{8,0},{9,1},... | collective-permute-start | bytes 36872 | tf_op jit(solution)/shard_map/ppermute | solution.py:475
  77.1 2.1 %collective-permute-done.13.got_ref = f32[2,1536]{1,0:T(2,128)S(1)} collective-permute-done((f32[2,1536]{1,0:T(2,128)S(1)}, f32[2,1536]{1,0:T(2,128)S(1)}, u32[]{:S(2)}, u32[]{:S(2)}) %collective-permute-start.13) | collective-permute-done | bytes 12320 | tf_op jit(solution)/shard_map/ppermute | solution.py:475
  79.3 2.6 %collective-permute-start.15 = (f32[2,1536]{1,0:T(2,128)S(1)}, f32[2,1536]{1,0:T(2,128)S(1)}, u32[]{:S(2)}, u32[]{:S(2)}) collective-permute-start(f32[2,1536]{1,0:T(2,128)S(1)} %add.38.own_ref), channel_id=1, source_target_pairs={{0,16},{1,17},{2,18},{3,19},{4,20},{5,21},{6,22},{7,23},{8,24},{9,... | collective-permute-start | bytes 36872 | tf_op jit(solution)/shard_map/ppermute | solution.py:475
  81.9 2.0 %collective-permute-done.15.got_ref = f32[2,1536]{1,0:T(2,128)S(1)} collective-permute-done((f32[2,1536]{1,0:T(2,128)S(1)}, f32[2,1536]{1,0:T(2,128)S(1)}, u32[]{:S(2)}, u32[]{:S(2)}) %collective-permute-start.15) | collective-permute-done | bytes 12320 | tf_op jit(solution)/shard_map/ppermute | solution.py:475
  83.9 3.4 %collective-permute-done.21.refs_1_ = bf16[8,48,768]{2,1,0:T(8,128)(2,1)S(1)} collective-permute-done((bf16[8,48,768]{2,1,0:T(8,128)(2,1)S(1)}, bf16[8,48,768]{2,1,0:T(8,128)(2,1)S(1)}, u32[]{:S(2)}, u32[]{:S(2)}) %collective-permute-start.21) | collective-permute-done | bytes 589856 | tf_op jit(solution)/shard_map/ppermute | solution.py:475
  87.2 0.1 merge.5
  87.3 0.7 collective-permute-start.22
  88.0 1.1 collective-permute-done.19.refs_1_
  89.2 0.1 merge.4
  89.3 0.7 collective-permute-start.20
  89.9 8.6 %grad_taps.1 = (bf16[32,1536]{1,0:T(8,128)(2,1)S(1)}, f32[12,2,288,128]{3,2,1,0:T(8,128)S(1)}) custom-call(s32[4]{0:T(128)S(1)} %copy-done.6, f32[512,1536]{1,0:T(8,128)S(1)} %get-tuple-element.51.dbn_ref, f32[512,1536]{1,0:T(8,128)S(1)} %get-tuple-element.43.conv_ref, bf16[2,32,1536]{2,1,0:T(8,128)(2,1)S(1)} %collective-permute-done.9.rest_0_.a_ref, ...), custom_call_target="tpu_custom_call" | custom-call | bytes 27000000 | tf_op jit(solution)/shard_map/grad_taps/pallas_call | solution.py:382
  98.6 0.1 collective-permute-start.16
  98.7 0.1 merge.6
  98.8 1.6 %collective-permute-start.23 = (bf16[2,48,1536]{2,1,0:T(8,128)(2,1)S(1)}, bf16[2,48,1536]{2,1,0:T(8,128)(2,1)S(1)}, u32[]{:S(2)}, u32[]{:S(2)}) collective-permute-start(bf16[2,48,1536]{2,1,0:T(8,128)(2,1)S(1)} %get-tuple-element.71), channel_id=1, source_target_pairs={{0,8},{1,9},{2,10},{3,11},{4,12},{5,13},{6,14},{7,15},{8,0},{9,1},... | collective-permute-start | bytes 884744 | tf_op jit(solution)/shard_map/ppermute | solution.py:475
  100.5 1.1 collective-permute-start.17
  101.6 3.9 %grad_proj.2 = (bf16[512,768]{1,0:T(8,128)(2,1)S(1)}, bf16[512,768]{1,0:T(8,128)(2,1)S(1)}) custom-call(f32[12,2,288,128]{3,2,1,0:T(8,128)S(1)} %get-tuple-element.55.dc_ref, f32[32,1536]{1,0:T(8,128)S(1)} %copy-done.4, bf16[512,1536]{1,0:T(8,128)(2,1)S(1)} %get-tuple-element.56.p_ref, bf16[512,1536]{1,0:T(8,128)(2,1)S(1)} %get-tuple-element.57.q_ref, ...), custom_call_target="tpu_custom_call" | custom-call | bytes 12000000 | tf_op jit(solution)/shard_map/grad_proj/pallas_call | solution.py:424
  105.5 4.8 %collective-permute-done.17.got_ref = bf16[32,1536]{1,0:T(8,128)(2,1)S(1)} collective-permute-done((bf16[32,1536]{1,0:T(8,128)(2,1)S(1)}, bf16[32,1536]{1,0:T(8,128)(2,1)S(1)}, u32[]{:S(2)}, u32[]{:S(2)}) %collective-permute-start.17) | collective-permute-done | bytes 98336 | tf_op jit(solution)/shard_map/ppermute | solution.py:475
  110.4 2.7 %collective-permute-start.18 = (bf16[32,1536]{1,0:T(8,128)(2,1)S(1)}, bf16[32,1536]{1,0:T(8,128)(2,1)S(1)}, u32[]{:S(2)}, u32[]{:S(2)}) collective-permute-start(bf16[32,1536]{1,0:T(8,128)(2,1)S(1)} %add.41.rest_0_.own_ref), channel_id=1, source_target_pairs={{0,16},{1,17},{2,18},{3,19},{4,20},{5,21},{6,22},{7,23},{8,24},{9,... | collective-permute-start | bytes 294920 | tf_op jit(solution)/shard_map/ppermute | solution.py:475
  113.1 4.0 %grad_proj.3 = (bf16[512,768]{1,0:T(8,128)(2,1)S(1)}, bf16[512,768]{1,0:T(8,128)(2,1)S(1)}) custom-call(f32[12,2,288,128]{3,2,1,0:T(8,128)S(1)} %get-tuple-element.55.dc_ref, f32[32,1536]{1,0:T(8,128)S(1)} %copy-done.4, bf16[512,1536]{1,0:T(8,128)(2,1)S(1)} %get-tuple-element.56.p_ref, bf16[512,1536]{1,0:T(8,128)(2,1)S(1)} %get-tuple-element.57.q_ref, ...), custom_call_target="tpu_custom_call" | custom-call | bytes 12000000 | tf_op jit(solution)/shard_map/grad_proj/pallas_call | solution.py:424
  117.0 0.8 collective-permute-done.18.got_ref
  117.9 1.8 %collective-permute-start.25 = (bf16[32,1536]{1,0:T(8,128)(2,1)S(1)}, bf16[32,1536]{1,0:T(8,128)(2,1)S(1)}, u32[]{:S(2)}, u32[]{:S(2)}) collective-permute-start(bf16[32,1536]{1,0:T(8,128)(2,1)S(1)} %add.42.rest_4_.own_ref), channel_id=1, source_target_pairs={{0,2},{1,3},{2,0},{3,1},{4,6},{5,7},{6,4},{7,5},{8,10},{9,11},{10,... | collective-permute-start | bytes 294920 | tf_op jit(solution)/shard_map/ppermute | solution.py:475
  119.7 0.1 merge.7
  119.8 0.7 collective-permute-start.24
  120.5 7.3 %back_norm.1.rest_0_ = bf16[512,1536]{1,0:T(8,128)(2,1)} custom-call(bf16[512,1536]{1,0:T(8,128)(2,1)S(1)} %get-tuple-element.49.hat_ref, f32[512,1]{1,0:T(8,128)S(1)} %get-tuple-element.50.rstd_ref, bf16[512,1536]{1,0:T(8,128)(2,1)S(1)} %bitcast.16, f32[3,1536]{1,0:T(4,128)S(1)} %copy-done.5, bf16[1536,3072]{1,0:T(8,128)(2,1)S(1)} %bitcast.11, ...), custom_call_target="tpu_custom_call" | custom-call | bytes 21000000 | tf_op jit(solution)/shard_map/back_norm/pallas_call | solution.py:461
  127.8 1.4 %copy-done.3 = bf16[512,1536]{1,0:T(8,128)(2,1)S(1)} copy-done((bf16[512,1536]{1,0:T(8,128)(2,1)S(1)}, bf16[512,1536]{1,0:T(8,128)(2,1)}, u32[]{:S(2)}) %copy-start.3) | copy-done | bytes 1572888
  129.2 0.2 collective-permute-start.26
  129.4 0.6 slice_reduce_fusion
  130.1 3.8 %collective-permute-done.26.got_ref = bf16[32,1536]{1,0:T(8,128)(2,1)S(1)} collective-permute-done((bf16[32,1536]{1,0:T(8,128)(2,1)S(1)}, bf16[32,1536]{1,0:T(8,128)(2,1)S(1)}, u32[]{:S(2)}, u32[]{:S(2)}) %collective-permute-start.26) | collective-permute-done | bytes 98336 | tf_op jit(solution)/shard_map/ppermute | solution.py:475
  133.9 0.7 add.45
  134.6 0.8 add.43
  (50 shorter events, 0.2 us)
Async XLA Ops:
  2.6 48.1 %slice-start.3 = ((s8[4718592]{0:T(1024)(128)(4,1)}), s8[4194304]{0:T(1024)(128)(4,1)S(1)}, s32[]{:S(2)}) async-start(s8[4718592]{0:T(1024)(128)(4,1)} %bitcast.12), calls=%async_computation.3 | async-start | bytes 8388608
  2.6 14.2 %copy-start.4 = (f32[32,1536]{1,0:T(8,128)S(1)}, f32[32,1536]{1,0:T(8,128)}, u32[]{:S(2)}) copy-start(f32[32,1536]{1,0:T(8,128)} %k_ref.5) | copy-start | bytes 589828
  2.6 14.2 %copy-start.6 = (s32[4]{0:T(128)S(1)}, s32[4]{0:T(128)}, u32[]{:S(2)}) copy-start(s32[4]{0:T(128)} %pad_add_fusion.place_ref) | copy-start | bytes 52
  2.6 48.1 %slice-start.4 = ((s8[4718592]{0:T(1024)(128)(4,1)}), s8[524288]{0:T(1024)(128)(4,1)S(1)}, s32[]{:S(2)}) async-start(s8[4718592]{0:T(1024)(128)(4,1)} %bitcast.12), calls=%async_computation.4 | async-start | bytes 1048576
  15.1 16.7 %copy-start = (bf16[2,256,1536]{2,1,0:T(8,128)(2,1)S(1)}, bf16[2,256,1536]{2,1,0:T(8,128)(2,1)}, u32[]{:S(2)}) copy-start(bf16[2,256,1536]{2,1,0:T(8,128)(2,1)} %param.15) | copy-start | bytes 4718596
  15.1 1.7 %collective-permute-start = (bf16[2,16,1536]{2,1,0:T(8,128)(2,1)}, bf16[2,16,1536]{2,1,0:T(8,128)(2,1)S(1)}, u32[]{:S(2)}, u32[]{:S(2)}) collective-permute-start(bf16[2,16,1536]{2,1,0:T(8,128)(2,1)} %get-tuple-element.41), channel_id=1, source_target_pairs={{0,1},{1,0},{2,3},{3,2},{4,5},{5,4},{6,7},{7,6},{8,9},{9,8},{10,11... | collective-permute-start | bytes 294920 | tf_op jit(solution)/shard_map/ppermute | solution.py:475
  15.6 1.2 collective-permute-start.1
  24.7 26.0 %copy-start.5 = (f32[3,1536]{1,0:T(4,128)S(1)}, f32[3,1536]{1,0:T(4,128)}, u32[]{:S(2)}) copy-start(f32[3,1536]{1,0:T(4,128)} %reshape.28.vec_ref) | copy-start | bytes 55300
  24.7 7.1 %collective-permute-start.2 = (f32[2,1536]{1,0:T(2,128)S(1)}, f32[2,1536]{1,0:T(2,128)S(1)}, u32[]{:S(2)}, u32[]{:S(2)}) collective-permute-start(f32[2,1536]{1,0:T(2,128)S(1)} %get-tuple-element.44.own_ref), channel_id=1, source_target_pairs={{0,1},{1,0},{2,3},{3,2},{4,5},{5,4},{6,7},{7,6},{8,9},{9,8},{10,11... | collective-permute-start | bytes 36872 | tf_op jit(solution)/shard_map/ppermute | solution.py:475
  32.9 17.8 %collective-permute-start.7 = (bf16[16,48,512]{2,1,0:T(8,128)(2,1)S(1)}, bf16[16,48,512]{2,1,0:T(8,128)(2,1)S(1)}, u32[]{:S(2)}, u32[]{:S(2)}) collective-permute-start(bf16[16,48,512]{2,1,0:T(8,128)(2,1)S(1)} %get-tuple-element.46), channel_id=1, source_target_pairs={{0,1},{1,0},{2,3},{3,2},{4,5},{5,4},{6,7},{7,6},{8,9},{9,8},{10,11... | collective-permute-start | bytes 2359304 | tf_op jit(solution)/shard_map/ppermute | solution.py:475
  33.3 5.0 %collective-permute-start.3 = (f32[2,1536]{1,0:T(2,128)S(1)}, f32[2,1536]{1,0:T(2,128)S(1)}, u32[]{:S(2)}, u32[]{:S(2)}) collective-permute-start(f32[2,1536]{1,0:T(2,128)S(1)} %add.30.rest_0_.own_ref), channel_id=1, source_target_pairs={{0,2},{1,3},{2,0},{3,1},{4,6},{5,7},{6,4},{7,5},{8,10},{9,11},{10,... | collective-permute-start | bytes 36872 | tf_op jit(solution)/shard_map/ppermute | solution.py:475
  38.3 3.7 %collective-permute-start.4 = (f32[2,1536]{1,0:T(2,128)S(1)}, f32[2,1536]{1,0:T(2,128)S(1)}, u32[]{:S(2)}, u32[]{:S(2)}) collective-permute-start(f32[2,1536]{1,0:T(2,128)S(1)} %add.31.own_ref), channel_id=1, source_target_pairs={{0,4},{1,5},{2,6},{3,7},{4,0},{5,1},{6,2},{7,3},{8,12},{9,13},{10,... | collective-permute-start | bytes 36872 | tf_op jit(solution)/shard_map/ppermute | solution.py:475
  42.0 4.0 %collective-permute-start.5 = (f32[2,1536]{1,0:T(2,128)S(1)}, f32[2,1536]{1,0:T(2,128)S(1)}, u32[]{:S(2)}, u32[]{:S(2)}) collective-permute-start(f32[2,1536]{1,0:T(2,128)S(1)} %add.32.own_ref), channel_id=1, source_target_pairs={{0,8},{1,9},{2,10},{3,11},{4,12},{5,13},{6,14},{7,15},{8,0},{9,1},... | collective-permute-start | bytes 36872 | tf_op jit(solution)/shard_map/ppermute | solution.py:475
  46.0 4.7 %collective-permute-start.6 = (f32[2,1536]{1,0:T(2,128)S(1)}, f32[2,1536]{1,0:T(2,128)S(1)}, u32[]{:S(2)}, u32[]{:S(2)}) collective-permute-start(f32[2,1536]{1,0:T(2,128)S(1)} %add.33.own_ref), channel_id=1, source_target_pairs={{0,16},{1,17},{2,18},{3,19},{4,20},{5,21},{6,22},{7,23},{8,24},{9,... | collective-permute-start | bytes 36872 | tf_op jit(solution)/shard_map/ppermute | solution.py:475
  50.8 10.5 %copy-start.1 = (bf16[2,256,1536]{2,1,0:T(8,128)(2,1)S(1)}, bf16[2,256,1536]{2,1,0:T(8,128)(2,1)}, u32[]{:S(2)}) copy-start(bf16[2,256,1536]{2,1,0:T(8,128)(2,1)} %param.8) | copy-start | bytes 4718596
  54.9 15.4 %collective-permute-start.14 = (bf16[512,1536]{1,0:T(8,128)(2,1)S(1)}, bf16[512,1536]{1,0:T(8,128)(2,1)S(1)}, u32[]{:S(2)}, u32[]{:S(2)}) collective-permute-start(bf16[512,1536]{1,0:T(8,128)(2,1)S(1)} %get-tuple-element.47.act_ref.acta_ref), channel_id=1, source_target_pairs={{0,1},{1,0},{2,3},{3,2},{4,5},{5,4},{6,7},{7,6},{8,9},{9,8},{10,11... | collective-permute-start | bytes 4718600 | tf_op jit(solution)/shard_map/ppermute | solution.py:475
  55.0 15.3 %collective-permute-start.10 = (bf16[2,32,1536]{2,1,0:T(8,128)(2,1)S(1)}, bf16[2,32,1536]{2,1,0:T(8,128)(2,1)S(1)}, u32[]{:S(2)}, u32[]{:S(2)}) collective-permute-start(bf16[2,32,1536]{2,1,0:T(8,128)(2,1)S(1)} %get-tuple-element.53), channel_id=1, source_target_pairs={{1,2},{2,1},{3,4},{4,3},{5,6},{6,5},{7,8},{8,7},{9,10},{10,9},{11,... | collective-permute-start | bytes 589832 | tf_op jit(solution)/shard_map/ppermute | solution.py:524
  55.8 14.4 %collective-permute-start.9 = (bf16[2,32,1536]{2,1,0:T(8,128)(2,1)S(1)}, bf16[2,32,1536]{2,1,0:T(8,128)(2,1)S(1)}, u32[]{:S(2)}, u32[]{:S(2)}) collective-permute-start(bf16[2,32,1536]{2,1,0:T(8,128)(2,1)S(1)} %get-tuple-element.52), channel_id=1, source_target_pairs={{0,1},{1,0},{2,3},{3,2},{4,5},{5,4},{6,7},{7,6},{8,9},{9,8},{10,11... | collective-permute-start | bytes 589832 | tf_op jit(solution)/shard_map/ppermute | solution.py:475
  58.8 1.2 collective-permute-start.8
  60.0 5.1 %collective-permute-start.11 = (f32[2,1536]{1,0:T(2,128)S(1)}, f32[2,1536]{1,0:T(2,128)S(1)}, u32[]{:S(2)}, u32[]{:S(2)}) collective-permute-start(f32[2,1536]{1,0:T(2,128)S(1)} %add.35.rest_0_.own_ref), channel_id=1, source_target_pairs={{0,2},{1,3},{2,0},{3,1},{4,6},{5,7},{6,4},{7,5},{8,10},{9,11},{10,... | collective-permute-start | bytes 36872 | tf_op jit(solution)/shard_map/ppermute | solution.py:475
  65.1 1.4 %copy-start.2 = (bf16[512,1536]{1,0:T(8,128)(2,1)S(1)}, bf16[512,1536]{1,0:T(8,128)(2,1)}, u32[]{:S(2)}) copy-start(bf16[512,1536]{1,0:T(8,128)(2,1)} %branch.1.rest_0_) | copy-start | bytes 4718596
  66.5 3.7 %collective-permute-start.12 = (f32[2,1536]{1,0:T(2,128)S(1)}, f32[2,1536]{1,0:T(2,128)S(1)}, u32[]{:S(2)}, u32[]{:S(2)}) collective-permute-start(f32[2,1536]{1,0:T(2,128)S(1)} %add.36.own_ref), channel_id=1, source_target_pairs={{0,4},{1,5},{2,6},{3,7},{4,0},{5,1},{6,2},{7,3},{8,12},{9,13},{10,... | collective-permute-start | bytes 36872 | tf_op jit(solution)/shard_map/ppermute | solution.py:475
  72.9 14.4 %collective-permute-start.21 = (bf16[8,48,768]{2,1,0:T(8,128)(2,1)S(1)}, bf16[8,48,768]{2,1,0:T(8,128)(2,1)S(1)}, u32[]{:S(2)}, u32[]{:S(2)}) collective-permute-start(bf16[8,48,768]{2,1,0:T(8,128)(2,1)S(1)} %get-tuple-element.67), channel_id=1, source_target_pairs={{0,4},{1,5},{2,6},{3,7},{4,0},{5,1},{6,2},{7,3},{8,12},{9,13},{10,... | collective-permute-start | bytes 1769480 | tf_op jit(solution)/shard_map/ppermute | solution.py:475
  74.9 14.3 %collective-permute-start.19 = (bf16[8,48,768]{2,1,0:T(8,128)(2,1)S(1)}, bf16[8,48,768]{2,1,0:T(8,128)(2,1)S(1)}, u32[]{:S(2)}, u32[]{:S(2)}) collective-permute-start(bf16[8,48,768]{2,1,0:T(8,128)(2,1)S(1)} %get-tuple-element.54.rest_0_), channel_id=1, source_target_pairs={{0,2},{1,3},{2,0},{3,1},{4,6},{5,7},{6,4},{7,5},{8,10},{9,11},{10,... | collective-permute-start | bytes 1769480 | tf_op jit(solution)/shard_map/ppermute | solution.py:475
  75.6 3.7 %collective-permute-start.13 = (f32[2,1536]{1,0:T(2,128)S(1)}, f32[2,1536]{1,0:T(2,128)S(1)}, u32[]{:S(2)}, u32[]{:S(2)}) collective-permute-start(f32[2,1536]{1,0:T(2,128)S(1)} %add.37.rest_0_.own_ref), channel_id=1, source_target_pairs={{0,8},{1,9},{2,10},{3,11},{4,12},{5,13},{6,14},{7,15},{8,0},{9,1},... | collective-permute-start | bytes 36872 | tf_op jit(solution)/shard_map/ppermute | solution.py:475
  79.3 4.6 %collective-permute-start.15 = (f32[2,1536]{1,0:T(2,128)S(1)}, f32[2,1536]{1,0:T(2,128)S(1)}, u32[]{:S(2)}, u32[]{:S(2)}) collective-permute-start(f32[2,1536]{1,0:T(2,128)S(1)} %add.38.own_ref), channel_id=1, source_target_pairs={{0,16},{1,17},{2,18},{3,19},{4,20},{5,21},{6,22},{7,23},{8,24},{9,... | collective-permute-start | bytes 36872 | tf_op jit(solution)/shard_map/ppermute | solution.py:475
  87.3 11.3 %collective-permute-start.22 = (bf16[4,48,768]{2,1,0:T(8,128)(2,1)S(1)}, bf16[4,48,768]{2,1,0:T(8,128)(2,1)S(1)}, u32[]{:S(2)}, u32[]{:S(2)}) collective-permute-start(bf16[4,48,768]{2,1,0:T(8,128)(2,1)S(1)} %get-tuple-element.69), channel_id=1, source_target_pairs={{0,2},{1,3},{2,0},{3,1},{4,6},{5,7},{6,4},{7,5},{8,10},{9,11},{10,... | collective-permute-start | bytes 884744 | tf_op jit(solution)/shard_map/ppermute | solution.py:475
  89.3 9.4 %collective-permute-start.20 = (bf16[4,48,768]{2,1,0:T(8,128)(2,1)S(1)}, bf16[4,48,768]{2,1,0:T(8,128)(2,1)S(1)}, u32[]{:S(2)}, u32[]{:S(2)}) collective-permute-start(bf16[4,48,768]{2,1,0:T(8,128)(2,1)S(1)} %get-tuple-element.65), channel_id=1, source_target_pairs={{0,4},{1,5},{2,6},{3,7},{4,0},{5,1},{6,2},{7,3},{8,12},{9,13},{10,... | collective-permute-start | bytes 884744 | tf_op jit(solution)/shard_map/ppermute | solution.py:475
  98.6 1.9 %collective-permute-start.16 = (bf16[32,1536]{1,0:T(8,128)(2,1)S(1)}, bf16[32,1536]{1,0:T(8,128)(2,1)S(1)}, u32[]{:S(2)}, u32[]{:S(2)}) collective-permute-start(bf16[32,1536]{1,0:T(8,128)(2,1)S(1)} %get-tuple-element.58.own_ref.refs_4_), channel_id=1, source_target_pairs={{0,1},{1,0},{2,3},{3,2},{4,5},{5,4},{6,7},{7,6},{8,9},{9,8},{10,11... | collective-permute-start | bytes 294920 | tf_op jit(solution)/shard_map/ppermute | solution.py:475
  98.8 20.9 %collective-permute-start.23 = (bf16[2,48,1536]{2,1,0:T(8,128)(2,1)S(1)}, bf16[2,48,1536]{2,1,0:T(8,128)(2,1)S(1)}, u32[]{:S(2)}, u32[]{:S(2)}) collective-permute-start(bf16[2,48,1536]{2,1,0:T(8,128)(2,1)S(1)} %get-tuple-element.71), channel_id=1, source_target_pairs={{0,8},{1,9},{2,10},{3,11},{4,12},{5,13},{6,14},{7,15},{8,0},{9,1},... | collective-permute-start | bytes 884744 | tf_op jit(solution)/shard_map/ppermute | solution.py:475
  100.5 9.9 %collective-permute-start.17 = (bf16[32,1536]{1,0:T(8,128)(2,1)S(1)}, bf16[32,1536]{1,0:T(8,128)(2,1)S(1)}, u32[]{:S(2)}, u32[]{:S(2)}) collective-permute-start(bf16[32,1536]{1,0:T(8,128)(2,1)S(1)} %add.40.rest_0_.own_ref), channel_id=1, source_target_pairs={{0,8},{1,9},{2,10},{3,11},{4,12},{5,13},{6,14},{7,15},{8,0},{9,1},... | collective-permute-start | bytes 294920 | tf_op jit(solution)/shard_map/ppermute | solution.py:475
  101.6 18.9 %slice-start = ((s8[9437184]{0:T(1024)(128)(4,1)}), s8[4194304]{0:T(1024)(128)(4,1)S(1)}, s32[]{:S(2)}) async-start(s8[9437184]{0:T(1024)(128)(4,1)} %bitcast.10), calls=%async_computation | async-start | bytes 8388608
  101.6 18.9 %slice-start.1 = ((s8[9437184]{0:T(1024)(128)(4,1)}), s8[4194304]{0:T(1024)(128)(4,1)S(1)}, s32[]{:S(2)}) async-start(s8[9437184]{0:T(1024)(128)(4,1)} %bitcast.10), calls=%async_computation.1 | async-start | bytes 8388608
  110.4 10.1 %slice-start.2 = ((s8[9437184]{0:T(1024)(128)(4,1)}), s8[1048576]{0:T(1024)(128)(4,1)S(1)}, s32[]{:S(2)}) async-start(s8[9437184]{0:T(1024)(128)(4,1)} %bitcast.10), calls=%async_computation.2 | async-start | bytes 2097152
  110.4 7.5 %collective-permute-start.18 = (bf16[32,1536]{1,0:T(8,128)(2,1)S(1)}, bf16[32,1536]{1,0:T(8,128)(2,1)S(1)}, u32[]{:S(2)}, u32[]{:S(2)}) collective-permute-start(bf16[32,1536]{1,0:T(8,128)(2,1)S(1)} %add.41.rest_0_.own_ref), channel_id=1, source_target_pairs={{0,16},{1,17},{2,18},{3,19},{4,20},{5,21},{6,22},{7,23},{8,24},{9,... | collective-permute-start | bytes 294920 | tf_op jit(solution)/shard_map/ppermute | solution.py:475
  117.9 9.9 %collective-permute-start.25 = (bf16[32,1536]{1,0:T(8,128)(2,1)S(1)}, bf16[32,1536]{1,0:T(8,128)(2,1)S(1)}, u32[]{:S(2)}, u32[]{:S(2)}) collective-permute-start(bf16[32,1536]{1,0:T(8,128)(2,1)S(1)} %add.42.rest_4_.own_ref), channel_id=1, source_target_pairs={{0,2},{1,3},{2,0},{3,1},{4,6},{5,7},{6,4},{7,5},{8,10},{9,11},{10,... | collective-permute-start | bytes 294920 | tf_op jit(solution)/shard_map/ppermute | solution.py:475
  119.8 14.8 %collective-permute-start.24 = (bf16[1,48,1536]{2,1,0:T(8,128)(2,1)S(1)}, bf16[1,48,1536]{2,1,0:T(8,128)(2,1)S(1)}, u32[]{:S(2)}, u32[]{:S(2)}) collective-permute-start(bf16[1,48,1536]{2,1,0:T(8,128)(2,1)S(1)} %get-tuple-element.73), channel_id=1, source_target_pairs={{0,16},{1,17},{2,18},{3,19},{4,20},{5,21},{6,22},{7,23},{8,24},{9,... | collective-permute-start | bytes 442376 | tf_op jit(solution)/shard_map/ppermute | solution.py:475
  127.8 1.4 %copy-start.3 = (bf16[512,1536]{1,0:T(8,128)(2,1)S(1)}, bf16[512,1536]{1,0:T(8,128)(2,1)}, u32[]{:S(2)}) copy-start(bf16[512,1536]{1,0:T(8,128)(2,1)} %back_norm.1.rest_0_) | copy-start | bytes 4718596
  129.2 4.7 %collective-permute-start.26 = (bf16[32,1536]{1,0:T(8,128)(2,1)S(1)}, bf16[32,1536]{1,0:T(8,128)(2,1)S(1)}, u32[]{:S(2)}, u32[]{:S(2)}) collective-permute-start(bf16[32,1536]{1,0:T(8,128)(2,1)S(1)} %add.44.own_ref), channel_id=1, source_target_pairs={{0,4},{1,5},{2,6},{3,7},{4,0},{5,1},{6,2},{7,3},{8,12},{9,13},{10,... | collective-permute-start | bytes 294920 | tf_op jit(solution)/shard_map/ppermute | solution.py:475

commit v3 on v2

--- a/solution.py
+++ b/solution.py
@@ -13,6 +13,7 @@
 LANES = 128
 PAD = 16
 MIB = 1 << 20
+AXIS = "seq"
 VMEM_MIB = 8
 
 
@@ -21,7 +22,6 @@
 
 
 WHOLE = pl.BlockSpec(memory_space=pltpu.VMEM)
-SCALARS = pl.BlockSpec(memory_space=pltpu.SMEM)
 ANYWHERE = pl.BlockSpec(memory_space=pl.ANY)
 CW = 256
 
@@ -34,17 +34,22 @@
     return jax.ShapeDtypeStruct(dims, dtype)
 
 
+def place():
+    me = lax.axis_index(AXIS)
+    last = lax.axis_size(AXIS) - 1
+    return me % 2, me // 2, (me > 0).astype(F32), (me < last).astype(F32)
+
+
 def near(dims, dtype):
     return pltpu.VMEM(dims, dtype)
 
 
-def turn_body(place_ref, cot_ref, *rest):
+def turn_body(cot_ref, *rest):
     mine_ref, other_ref, held_ref = rest[-3:]
     blocks = mine_ref.shape[0]
     per = mine_ref.shape[1]
     held_ref[...] = cot_ref[...].T
-    core = place_ref[0]
-    half = place_ref[1]
+    core, half, _, _ = place()
 
     def step(j, _):
         row = pl.multiple_of(lax.bitwise_xor(half, j) * (2 * per), 2 * per)
@@ -55,19 +60,19 @@
     lax.fori_loop(0, blocks, step, 0, unroll=2)
 
 
-def turn(n, place, cot, after):
+def turn(n, cot, after):
     rows, d = cot.shape
     out = shape((n // 2, d // n, rows), BF)
     return pl.pallas_call(
         turn_body,
-        in_specs=[SCALARS, WHOLE] + [ANYWHERE] * len(after),
+        in_specs=[WHOLE] + [ANYWHERE] * len(after),
         out_specs=[WHOLE] * 2,
         out_shape=[out] * 2,
         scratch_shapes=[pltpu.VMEM((d, rows), BF)],
         compiler_params=params(VMEM_MIB),
         cost_estimate=cost(2),
         name="turn",
-    )(place, cot, *after)
+    )(cot, *after)
 
 
 def edges_out(odd, first, last, a_ref, b_ref):
@@ -83,8 +88,8 @@
 
 
 def front_body(
-    utt, place_ref, x_hbm, vec_ref, w_hbm,
-    gated_ref, p_ref, q_ref, hat_ref, rstd_ref, a_ref, b_ref, normed_ref, x_ref, w_ref, x_sem, w_sem,
+    utt, x_hbm, ln_ref, gain_ref, bias_ref, w_hbm,
+    gated_ref, p_ref, q_ref, hat_ref, rstd_ref, vec_ref, a_ref, b_ref, normed_ref, x_ref, w_ref, x_sem, w_sem,
 ):
     rows, d = x_ref.shape
     frames = rows // utt
@@ -102,12 +107,17 @@
 
     for i in range(pieces):
         x_copy(i).start()
-    for j in range(steps):
-        for half in range(2):
-            w_copy(j, half).start()
+    for half in range(2):
+        w_copy(0, half).start()
+    vec_ref[0:1, :] = ln_ref[...].reshape(1, d)
+    vec_ref[1:2, :] = gain_ref[...].reshape(1, d)
+    vec_ref[2:3, :] = bias_ref[...].reshape(1, d)
 
     for i in range(pieces):
         x_copy(i).wait()
+        for j in range(1 + i, steps if i == pieces - 1 else 2 + i):
+            for half in range(2):
+                w_copy(j, half).start()
 
         for k in range(i * span, (i + 1) * span, 16):
             at = slice(k, k + 16)
@@ -121,7 +131,7 @@
             hat_ref[at, :] = hat.astype(BF)
             normed_ref[at, :] = (hat * vec_ref[0:1, :]).astype(BF)
 
-    odd = place_ref[0] != 0
+    odd = place()[0] != 0
     for j in range(steps):
         cols = slice(j * CW, (j + 1) * CW)
         for half in range(2):
@@ -142,15 +152,15 @@
         b_ref[:, :, cols] = jnp.where(odd, last, first)
 
 
-def front(utt, place, x, vec, w_in):
+def front(utt, x, ln_gain, bn_gain, bn_bias, w_in):
     rows, d = x.shape
     out = near((rows, d), BF)
     edge = shape((utt, PAD, d), BF)
     return pl.pallas_call(
         functools.partial(front_body, utt),
-        in_specs=[SCALARS, ANYWHERE, WHOLE, ANYWHERE],
-        out_specs=[WHOLE] * 7,
-        out_shape=[out] * 4 + [near((rows, 1), F32)] + [edge] * 2,
+        in_specs=[ANYWHERE] + [WHOLE] * 3 + [ANYWHERE],
+        out_specs=[WHOLE] * 8,
+        out_shape=[out] * 4 + [near((rows, 1), F32), near((3, d), F32)] + [edge] * 2,
         scratch_shapes=[
             pltpu.VMEM((rows, d), BF),
             pltpu.VMEM((rows, d), BF),
@@ -161,7 +171,7 @@
         compiler_params=params(52),
         cost_estimate=cost(10),
         name="front",
-    )(place, x, vec, w_in)
+    )(x, ln_gain, bn_gain, bn_bias, w_in)
 
 
 def lane_groups(first, last, work):
@@ -174,62 +184,119 @@
     lax.fori_loop(first // (2 * LANES), last // (2 * LANES), step, 0)
 
 
-def conv_body(utt, place_ref, g_ref, a_ref, b_ref, k_ref, conv_ref, sums_ref, pad_ref):
+PHASES = 4
+PIECES = 9
+
+
+def thirds(x0, x1, x2):
+    return [x1, x0 - x1, x2 - x1]
+
+
+def sequences(x):
+    tops = [
+        (x[1], x[3], x[5]),
+        (x[0] - x[1], x[2] - x[3], x[4] - x[5]),
+        (x[2] - x[1], x[4] - x[3], x[6] - x[5]),
+    ]
+    return [piece for top in tops for piece in thirds(*top)]
+
+
+def combined(h):
+    tops = [(h[0] + h[1], h[2] + h[3]), (h[0], h[2]), (h[1], h[3])]
+    return [piece for a, b in tops for piece in (a + b, a, b)]
+
+
+def assembled(products):
+    halves = []
+    for top in range(3):
+        m, p, q = (next(products) for _ in range(3))
+        halves.append((m + p, m + q))
+        if top:
+            for j in range(2):
+                yield 2 * j + top - 1, halves[0][j] + halves[top][j]
+
+
+def phase(first, size):
+    return pl.ds(first, size, PHASES)
+
+
+def fill_sequences(pad_ref, shift, seq_ref, size):
+    x = [pad_ref[phase(j + shift, size), :] for j in range(2 * PHASES - 1)]
+    for i, piece in enumerate(sequences(x)):
+        seq_ref[i] = piece
+
+
+def filtered(seq_ref, taps_ref, order, count):
+    for i in range(PIECES):
+        acc = jnp.zeros((count, LANES), F32)
+        for a in range(taps_ref.shape[1]):
+            row = order(a)
+            acc = acc + taps_ref[i, row : row + 1, :] * seq_ref[i, a : a + count, :]
+        yield acc
+
+
+def conv_body(utt, g_ref, a_ref, b_ref, k_ref, conv_ref, sums_ref, pad_ref, seq_ref, taps_ref):
     d = g_ref.shape[1]
     frames = g_ref.shape[0] // utt
-    taps = k_ref.shape[0]
-    block = 64
-    odd = place_ref[0] != 0
+    count = frames // PHASES
+    per = k_ref.shape[0] // PHASES
+    odd = place()[0] != 0
 
     def work(_, lanes, slot):
         first = square = jnp.zeros((8, LANES), F32)
+        pad_ref[slot, 0, 0 : per * PHASES, :] = k_ref[:, lanes]
+        k = [pad_ref[slot, 0, phase(i, per), :] for i in range(PHASES)]
+        for i, piece in enumerate(combined(k)):
+            taps_ref[slot, i] = piece
         for u in range(utt):
             a = a_ref[u, :, lanes].astype(F32)
             b = b_ref[u, :, lanes].astype(F32)
+            rows = slice(u * frames, (u + 1) * frames)
             pad_ref[slot, u, 0:PAD, :] = jnp.where(odd, a, b)
-            rows = slice(u * frames, (u + 1) * frames)
             pad_ref[slot, u, PAD : PAD + frames, :] = g_ref[rows, lanes].astype(F32)
             pad_ref[slot, u, PAD + frames : PAD + frames + PAD, :] = jnp.where(odd, b, a)
-            for base in range(0, frames, block):
-                acc = jnp.zeros((block, LANES), F32)
-                for r in range(8):
-                    w = pad_ref[slot, u, base + r + 1 : base + r + 1 + block + taps - 8, :]
-                    for q in range(taps // 8):
-                        tap = 8 * q + r
-                        acc = acc + k_ref[tap : tap + 1, lanes] * w[8 * q : 8 * q + block]
-                conv_ref[u * frames + base : u * frames + base + block, lanes] = acc
-                part = acc.reshape(block // 8, 8, LANES)
+            fill_sequences(pad_ref.at[slot, u], 1, seq_ref.at[slot, u], count + per)
+            products = filtered(seq_ref.at[slot, u], taps_ref.at[slot], lambda a: a, count)
+            for i, y in assembled(products):
+                pad_ref[slot, u, phase(i, count), :] = y
+                part = y.reshape(count // 8, 8, LANES)
                 first = first + jnp.sum(part, axis=0)
                 square = square + jnp.sum(part * part, axis=0)
+            conv_ref[rows, lanes] = pad_ref[slot, u, 0:frames, :]
         sums_ref[0:1, lanes] = jnp.sum(first, axis=0, keepdims=True)
         sums_ref[1:2, lanes] = jnp.sum(square, axis=0, keepdims=True)
 
     lane_groups(0, d, work)
 
 
-def conv(utt, place, gated, a, b, kernel):
+def conv(utt, gated, a, b, kernel):
     rows, d = gated.shape
     frames = rows // utt
+    per = kernel.shape[0] // PHASES
     return pl.pallas_call(
         functools.partial(conv_body, utt),
-        in_specs=[SCALARS] + [WHOLE] * 4,
+        in_specs=[WHOLE] * 4,
         out_specs=[WHOLE] * 2,
         out_shape=[near(gated.shape, F32), shape((2, d), F32)],
-        scratch_shapes=[pltpu.VMEM((2, utt, frames + 2 * PAD + 8, LANES), F32)],
+        scratch_shapes=[
+            pltpu.VMEM((2, utt, frames + 2 * PAD + 8, LANES), F32),
+            pltpu.VMEM((2, utt, PIECES, frames // PHASES + per, LANES), F32),
+            pltpu.VMEM((2, PIECES, per, LANES), F32),
+        ],
         compiler_params=params(VMEM_MIB),
         cost_estimate=cost(7),
         name="conv",
-    )(place, gated, a, b, kernel)
+    )(gated, a, b, kernel)
 
 
 def middle_body(
-    utt, total, place_ref, conv_ref, sums_ref, vec_ref, cot_ref, w_ref,
+    utt, total, conv_ref, sums_ref, vec_ref, cot_ref, w_ref,
     *rest,
 ):
     act_ref, dbn_ref, dsums_ref, a_ref, b_ref = rest[-5:]
     rows, d = conv_ref.shape
     frames = rows // utt
-    odd = place_ref[0] != 0
+    odd = place()[0] != 0
     for j in range(d // CW):
         cols = slice(j * CW, (j + 1) * CW)
         mean = sums_ref[0:1, cols] * (1.0 / total)
@@ -255,18 +322,18 @@
                 b_ref[u, at, cols] = jnp.where(odd, last, first)
 
 
-def middle(utt, total, place, conv_out, sums, vec, cot, w_out, after):
+def middle(utt, total, conv_out, sums, vec, cot, w_out, after):
     rows, d = cot.shape
     edge = shape((utt, 2 * PAD, d), BF)
     return pl.pallas_call(
         functools.partial(middle_body, utt, total),
-        in_specs=[SCALARS] + [WHOLE] * 5 + [ANYWHERE] * len(after),
+        in_specs=[WHOLE] * 5 + [ANYWHERE] * len(after),
         out_specs=[WHOLE] * 5,
         out_shape=[shape((rows, d), BF), near((rows, d), F32), shape((2, d), F32), edge, edge],
         compiler_params=params(VMEM_MIB),
         cost_estimate=cost(4),
         name="middle",
-    )(place, conv_out, sums, vec, cot, w_out, *after)
+    )(conv_out, sums, vec, cot, w_out, *after)
 
 
 def grad_body(bits, ca_ref, cb_ref, acta_ref, actb_ref, *rest):
@@ -309,13 +376,18 @@
 
 
 def branch_body(x_ref, act_ref, w_ref, *rest):
-    out_ref = rest[-1]
+    out_hbm, out_ref, sem = rest[-3:]
+    copies = []
     for j in range(out_ref.shape[-1] // CW):
         cols = slice(j * CW, (j + 1) * CW)
         part = lax.dot_general(
             act_ref[...], w_ref[cols, :], (((1,), (1,)), ((), ())), preferred_element_type=F32
         )
         out_ref[:, cols] = (x_ref[:, cols].astype(F32) + part).astype(BF)
+        copies.append(pltpu.make_async_copy(out_ref.at[:, cols], out_hbm.at[:, cols], sem.at[j]))
+        copies[-1].start()
+    for copy in copies:
+        copy.wait()
 
 
 def branch(x, act, w_out, after):
@@ -323,8 +395,9 @@
     return pl.pallas_call(
         branch_body,
         in_specs=[WHOLE] * 3 + [ANYWHERE] * len(after),
-        out_specs=WHOLE,
-        out_shape=shape((rows, d), BF),
+        out_specs=pl.BlockSpec(memory_space=pltpu.HBM),
+        out_shape=pltpu.HBM((rows, d), BF),
+        scratch_shapes=[pltpu.VMEM((rows, d), BF), pltpu.SemaphoreType.DMA((d // CW,))],
         compiler_params=params(VMEM_MIB),
         cost_estimate=cost(4),
         name="branch",
@@ -332,16 +405,16 @@
 
 
 def grad_taps_body(
-    utt, total, place_ref, dbn_ref, conv_ref, a_ref, b_ref, sums_ref, dsums_ref, vec_ref, g_ref,
-    dk_ref, dc_ref, acc_ref,
+    utt, total, dbn_ref, conv_ref, a_ref, b_ref, sums_ref, dsums_ref, vec_ref, g_ref,
+    dk_ref, seq_ref, pad_ref, held_ref, acc_ref,
 ):
     d = g_ref.shape[1]
     frames = g_ref.shape[0] // utt
+    count = frames // PHASES
     taps = dk_ref.shape[0]
-    block = 64
-    odd = place_ref[0] != 0
-    keep_lo = place_ref[2].astype(F32)
-    keep_hi = place_ref[3].astype(F32)
+    per = taps // PHASES
+    odd, _, keep_lo, keep_hi = place()
+    odd = odd != 0
 
     def work(group, lanes, slot):
         mean = sums_ref[0:1, lanes] * (1.0 / total)
@@ -358,67 +431,84 @@
             a = d_conv(a_ref[u, :PAD, lanes], a_ref[u, PAD:, lanes])
             b = d_conv(b_ref[u, :PAD, lanes], b_ref[u, PAD:, lanes])
             rows = slice(u * frames, (u + 1) * frames)
-            dc_ref[group, u, 0:PAD, :] = jnp.where(odd, a, b) * keep_lo
-            dc_ref[group, u, PAD : PAD + frames, :] = d_conv(dbn_ref[rows, lanes], conv_ref[rows, lanes])
-            dc_ref[group, u, PAD + frames : PAD + frames + PAD, :] = jnp.where(odd, b, a) * keep_hi
-            for base in range(0, frames, block):
-                g = g_ref[u * frames + base : u * frames + base + block, lanes].astype(F32)
-                for r in range(8):
-                    w = dc_ref[group, u, base + r : base + r + block + taps - 8, :]
-                    for q in range(taps // 8):
-                        tap = taps - 1 - (8 * q + r)
-                        prod = g * w[8 * q : 8 * q + block]
-                        prod = jnp.sum(prod.reshape(block // 8, 8, LANES), axis=0)
-                        if u or base:
-                            prod = acc_ref[slot, tap] + prod
-                        acc_ref[slot, tap] = prod
+            pad_ref[slot, u, 0:PAD, :] = jnp.where(odd, a, b) * keep_lo
+            pad_ref[slot, u, PAD : PAD + frames, :] = d_conv(dbn_ref[rows, lanes], conv_ref[rows, lanes])
+            pad_ref[slot, u, PAD + frames : PAD + frames + PAD, :] = jnp.where(odd, b, a) * keep_hi
+            fill_sequences(pad_ref.at[slot, u], 0, seq_ref.at[group, u], count + per)
+            pad_ref[slot, u, 0:frames, :] = g_ref[rows, lanes].astype(F32)
+            g = [pad_ref[slot, u, phase(i, count), :] for i in range(PHASES)]
+            for i, piece in enumerate(combined(g)):
+                held_ref[slot, u, i] = piece
+
+        def products():
+            for i in range(PIECES):
+                sums = [jnp.zeros((8, LANES), F32)] * per
+                for u in range(utt):
+                    for base in range(0, count, 32):
+                        g = held_ref[slot, u, i, base : base + 32, :]
+                        for a in range(per):
+                            prod = g * seq_ref[group, u, i, base + a : base + a + 32, :]
+                            sums[a] = sums[a] + jnp.sum(prod.reshape(4, 8, LANES), axis=0)
+                yield jnp.stack(sums)
+
+        for i, y in assembled(products()):
+            for a in range(per):
+                acc_ref[slot, taps - 1 - (PHASES * a + i)] = y[a]
         dk_ref[:, lanes] = jnp.sum(acc_ref[slot], axis=1).astype(BF)
 
     lane_groups(0, d, work)
 
 
-def grad_taps(utt, total, taps, place, dbn, conv_out, halos, sums, dsums, vec, gated):
+def grad_taps(utt, total, taps, dbn, conv_out, halos, sums, dsums, vec, gated):
     rows, d = gated.shape
+    frames = rows // utt
+    long = frames // PHASES + taps // PHASES
     return pl.pallas_call(
         functools.partial(grad_taps_body, utt, total),
-        in_specs=[SCALARS] + [WHOLE] * 8,
+        in_specs=[WHOLE] * 8,
         out_specs=[WHOLE] * 2,
         out_shape=[
             shape((taps, d), BF),
-            near((d // LANES, utt, rows // utt + 2 * PAD, LANES), F32),
+            near((d // LANES, utt, PIECES, long, LANES), F32),
         ],
-        scratch_shapes=[pltpu.VMEM((2, taps, 8, LANES), F32)],
+        scratch_shapes=[
+            pltpu.VMEM((2, utt, frames + 2 * PAD + 8, LANES), F32),
+            pltpu.VMEM((2, utt, PIECES, frames // PHASES, LANES), F32),
+            pltpu.VMEM((2, taps, 8, LANES), F32),
+        ],
         compiler_params=params(VMEM_MIB),
         cost_estimate=cost(9),
         name="grad_taps",
-    )(place, dbn, conv_out, *halos, sums, dsums, vec, gated)
-
-
-def grad_proj_body(utt, start, dc_ref, k_ref, p_ref, q_ref, *rest):
-    dv_ref, dg_ref = rest[-2:]
+    )(dbn, conv_out, *halos, sums, dsums, vec, gated)
+
+
+def grad_proj_body(utt, start, seq_ref, k_ref, p_ref, q_ref, *rest):
+    dv_ref, dg_ref, out_ref, taps_ref = rest[-4:]
     rows, width = dv_ref.shape
     frames = rows // utt
-    taps = k_ref.shape[0]
-    block = 64
+    count = frames // PHASES
+    per = k_ref.shape[0] // PHASES
 
     def work(group, out, slot):
         lanes = pl.ds(pl.multiple_of(out.start + start, LANES), LANES)
+        out_ref[slot, 0 : per * PHASES, :] = k_ref[:, lanes]
+        k = [out_ref[slot, phase(PHASES - 1 - i, per), :] for i in range(PHASES)]
+        for i, piece in enumerate(combined(k)):
+            taps_ref[slot, i] = piece
         for u in range(utt):
-            for base in range(0, frames, block):
-                at = slice(u * frames + base, u * frames + base + block)
-                acc = jnp.zeros((block, LANES), F32)
-                for r in range(8):
-                    w = dc_ref[group + start // LANES, u, base + r : base + r + block + taps - 8, :]
-                    for q in range(taps // 8):
-                        tap = taps - 1 - (8 * q + r)
-                        acc = acc + k_ref[tap : tap + 1, lanes] * w[8 * q : 8 * q + block]
-                dv_ref[at, out] = (acc * p_ref[at, lanes].astype(F32)).astype(BF)
-                dg_ref[at, out] = (acc * q_ref[at, lanes].astype(F32)).astype(BF)
+            products = filtered(
+                seq_ref.at[group + start // LANES, u], taps_ref.at[slot], lambda a: per - 1 - a, count
+            )
+            for i, y in assembled(products):
+                out_ref[slot, phase(u * frames + i, count), :] = y
+        acc = out_ref[slot]
+        dv_ref[:, out] = (acc * p_ref[:, lanes].astype(F32)).astype(BF)
+        dg_ref[:, out] = (acc * q_ref[:, lanes].astype(F32)).astype(BF)
 
     lane_groups(0, width, work)
 
 
-def grad_proj(utt, start, width, d_conv, kernel, p, q, after):
+def grad_proj(utt, start, width, seqs, kernel, p, q, after):
     rows = p.shape[0]
     out = near((rows, width), BF)
     return pl.pallas_call(
@@ -426,16 +516,20 @@
         in_specs=[WHOLE] * 4 + [ANYWHERE] * len(after),
         out_specs=[WHOLE] * 2,
         out_shape=[out, out],
+        scratch_shapes=[
+            pltpu.VMEM((2, rows, LANES), F32),
+            pltpu.VMEM((2, PIECES, kernel.shape[0] // PHASES, LANES), F32),
+        ],
         compiler_params=params(VMEM_MIB),
         cost_estimate=cost(4),
         name="grad_proj",
-    )(d_conv, kernel, p, q, *after)
-
-
-def back_norm_body(hat_ref, rstd_ref, cot_ref, vec_ref, w_ref, *rest):
+    )(seqs, kernel, p, q, *after)
+
+
+def back_proj_body(vec_ref, w_ref, *rest):
     pieces = rest[:4]
-    out_ref, acc_ref = rest[-2:]
-    rows, d = hat_ref.shape
+    out_ref = rest[-1]
+    rows, d = out_ref.shape
     wide = pieces[0].shape[1]
     dims = (((1,), (1,)), ((), ()))
     for j in range(d // CW):
@@ -445,7 +539,28 @@
             part += lax.dot_general(
                 piece[...], w_ref[cols, k * wide : (k + 1) * wide], dims, preferred_element_type=F32
             )
-        acc_ref[:, cols] = part * vec_ref[0:1, cols]
+        out_ref[:, cols] = part * vec_ref[0:1, cols]
+
+
+def back_proj(vec, w_in, pieces, after):
+    rows = pieces[0].shape[0]
+    d = w_in.shape[0]
+    return pl.pallas_call(
+        back_proj_body,
+        in_specs=[WHOLE] * 6 + [ANYWHERE] * len(after),
+        out_specs=WHOLE,
+        out_shape=near((rows, d), F32),
+        compiler_params=params(VMEM_MIB),
+        cost_estimate=cost(5),
+        name="back_proj",
+    )(vec, w_in, *pieces, *after)
+
+
+def back_norm_body(hat_ref, rstd_ref, cot_ref, acc_ref, *rest):
+    out_hbm, out_ref, sem = rest[-3:]
+    copies = []
+    rows, d = hat_ref.shape
+    span = rows // sem.shape[0]
     for i in range(0, rows, 16):
         at = slice(i, i + 16)
         hat = hat_ref[at, :].astype(F32)
@@ -454,20 +569,28 @@
         m2 = jnp.sum(grads * hat, axis=-1, keepdims=True) * (1.0 / d)
         layer = rstd_ref[at, :] * (grads - m1 - hat * m2)
         out_ref[at, :] = (cot_ref[at, :].astype(F32) + layer).astype(BF)
-
-
-def back_norm(hat, rstd, cot, vec, w_in, pieces, after):
+        if (i + 16) % span == 0:
+            piece = pl.ds(i + 16 - span, span)
+            copies.append(
+                pltpu.make_async_copy(out_ref.at[piece], out_hbm.at[piece], sem.at[i // span])
+            )
+            copies[-1].start()
+    for copy in copies:
+        copy.wait()
+
+
+def back_norm(hat, rstd, cot, grads, after):
     rows, d = hat.shape
     return pl.pallas_call(
         back_norm_body,
-        in_specs=[WHOLE] * 9 + [ANYWHERE] * len(after),
-        out_specs=WHOLE,
-        out_shape=shape((rows, d), BF),
-        scratch_shapes=[pltpu.VMEM((rows, d), F32)],
-        compiler_params=params(VMEM_MIB),
-        cost_estimate=cost(7),
+        in_specs=[WHOLE] * 4 + [ANYWHERE] * len(after),
+        out_specs=pl.BlockSpec(memory_space=pltpu.HBM),
+        out_shape=pltpu.HBM((rows, d), BF),
+        scratch_shapes=[pltpu.VMEM((rows, d), BF), pltpu.SemaphoreType.DMA((8,))],
+        compiler_params=params(VMEM_MIB),
+        cost_estimate=cost(3),
         name="back_norm",
-    )(hat, rstd, cot, vec, w_in, *pieces, *after)
+    )(hat, rstd, cot, grads, *after)
 
 
 def swap(block, axis, bit):
@@ -579,7 +702,7 @@
 
 
 def on_device(inputs, ln_gain, w_in, kernel, bn_gain, bn_bias, w_out, cotangent):
-    axis = "seq"
+    axis = AXIS
     n = lax.axis_size(axis)
     me = lax.axis_index(axis).astype(jnp.int32)
     utt, frames, d = inputs.shape
@@ -588,17 +711,15 @@
     total = rows * n
     x = inputs.reshape(rows, d)
     cot = cotangent.reshape(rows, d)
-    vec = jnp.concatenate([ln_gain, bn_gain, bn_bias]).reshape(3, d)
-    place = jnp.stack([me % 2, me // 2, (me > 0).astype(jnp.int32), (me < n - 1).astype(jnp.int32)])
     by_owner = is_power(n) and n >= 8 and d % n == 0 and (d // n) % 16 == 0
 
-    gated, p, q, hat, rstd, ga, gb = front(utt, place, x, vec, w_in)
+    gated, p, q, hat, rstd, vec, ga, gb = front(utt, x, ln_gain, bn_gain, bn_bias, w_in)
     ga, gb = beside(ga, gb, axis)
-    conv_out, sums = conv(utt, place, gated, ga, gb, kernel)
+    conv_out, sums = conv(utt, gated, ga, gb, kernel)
     made = {}
 
     def turning(after):
-        made["a"], other = turn(n, place, cot, after)
+        made["a"], other = turn(n, cot, after)
         made["b"] = swap(other, axis, 1)
         return [made["a"]]
 
@@ -609,7 +730,7 @@
         sums = all_sum(sums, axis)
         waits = []
 
-    act, dbn, dsums, da, db = middle(utt, total, place, conv_out, sums, vec, cot, w_out, waits)
+    act, dbn, dsums, da, db = middle(utt, total, conv_out, sums, vec, cot, w_out, waits)
     da, db = beside(da, db, axis)
 
     def branching(after):
@@ -631,7 +752,7 @@
         d_w_out = lax.psum_scatter(dw, axis, scatter_dimension=0, tiled=True)
 
     d_kernel, d_conv = grad_taps(
-        utt, total, kernel.shape[0], place, dbn, conv_out, (da, db), sums, dsums, vec, gated
+        utt, total, kernel.shape[0], dbn, conv_out, (da, db), sums, dsums, vec, gated
     )
     half = d // 2
 
@@ -642,18 +763,24 @@
 
         return work
 
+    def back_projecting(after):
+        left, right = made[0], made[half]
+        made["far"] = after
+        made["grads"] = back_proj(vec, w_in, (left[0], right[0], left[1], right[1]), after)
+        return [made["grads"]]
+
     def norming(after):
-        left, right = made[0], made[half]
-        made["d_inputs"] = back_norm(
-            hat, rstd, cot, vec, w_in, (left[0], right[0], left[1], right[1]), after
-        )
+        made["d_inputs"] = back_norm(hat, rstd, cot, made["grads"], after)
         return [made["d_inputs"]]
 
     d_kernel_sum = all_sum(
-        d_kernel, axis, [nothing, projecting(0), projecting(half), norming], far_first=True
+        d_kernel,
+        axis,
+        [nothing, projecting(0), projecting(half), back_projecting, norming],
+        far_first=True,
     )
     if by_owner:
-        d_w_out = last_swaps(held, axis, [[d_kernel], [made[half][0]]])
+        d_w_out = last_swaps(held, axis, [made["far"], [made["grads"]]])
     return (
         made["outputs"].reshape(inputs.shape), made["d_inputs"].reshape(inputs.shape), d_w_out,
         d_kernel_sum, dsums[1], dsums[0],

time: 136 us -> 116 us (0.85)
  waiting for transfers between devices: 29.2 us -> 17.5 us
  Pallas kernels: 57.8 us -> 47.8 us
  starting transfers between devices: 42 us -> 45.8 us
    ppermute x25, waiting for transfers between devices: 29.2 us -> 17.5 us  [swap(): return lax.ppermute(block, axis, [(i, i ^ bit) for i in range(count)])]
    pallas_call x6 -> x7, Pallas kernels: 41.5 us -> 34.2 us  [the longest x1 10.4 us: front(): pl.pallas_call(functools.partial(front_body, utt), in_specs=[ANYWHERE] +...]
    ppermute x25, starting transfers between devices: 40.5 us -> 44.2 us  [swap(): return lax.ppermute(block, axis, [(i, i ^ bit) for i in range(count)])]
    pallas_call x2, Pallas kernels: 7.88 us -> 5.48 us  [grad_proj(): pl.pallas_call(functools.partial(grad_proj_body, utt, start), in_specs=[W...]
  transfers between devices with their start and end apart: 27 -> 27, of which waited for: 15 -> 13; matrix products, arithmetic and copies ran while one was open for 0% -> 1% of each run, Pallas kernels for 21% -> 21%
where the time goes in v3:
time: 116 us
  Pallas kernels  47.8 us (41%)
  starting transfers between devices  45.8 us (39%)
  waiting for transfers between devices  17.5 us (15%)
  local copies, waits for them, and re-layouts  3.49 us (3%)
    ppermute x25, starting transfers between devices, swap(): return lax.ppermute(block, axis, [(i, i ^ bit) for i in range(count)])  44.2 us
    ppermute x25, waiting for transfers between devices, swap(): return lax.ppermute(block, axis, [(i, i ^ bit) for i in range(count)])  17.5 us
    pallas_call x1, Pallas kernels, front(): pl.pallas_call(functools.partial(front_body, utt), in_specs=[ANYWHERE] +...  10.4 us
    pallas_call x1, Pallas kernels, grad_taps(): pl.pallas_call(functools.partial(grad_taps_body, utt, total), in_specs=[W...  6.93 us
    pallas_call x2, Pallas kernels, grad_proj(): pl.pallas_call(functools.partial(grad_proj_body, utt, start), in_specs=[W...  5.48 us
    pallas_call x1, Pallas kernels, conv(): pl.pallas_call(functools.partial(conv_body, utt), in_specs=[WHOLE] * 4, o...  5.41 us
    pallas_call x1, Pallas kernels, back_proj(): pl.pallas_call(back_proj_body, in_specs=[WHOLE] * 6 + [ANYWHERE] * len(af...  5.08 us
    pallas_call x1, Pallas kernels, branch(): pl.pallas_call(branch_body, in_specs=[WHOLE] * 3 + [ANYWHERE] * len(after...  3.56 us
  transfers between devices with their start and end apart: 27, of which 13 were waited for; matrix products, arithmetic and copies ran while one was open for 1% of the time, Pallas kernels for 21%

profile of v3, /device:TPU:0, one launch (start us, length us, event | category | flops | bytes accessed | tf_op | source)
XLA Modules:
  0.0 115.7 jit_solution(17508971089060611374)
XLA Ops:
  0.7 10.4 %front.1 = (bf16[512,1536]{1,0:T(8,128)(2,1)S(1)}, bf16[512,1536]{1,0:T(8,128)(2,1)S(1)}, bf16[512,1536]{1,0:T(8,128)(2,1)S(1)}, bf16[512,1536]{1,0:T(8,128)(2,1...) custom-call(bf16[512,1536]{1,0:T(8,128)(2,1)} %bitcast.13, ...), custom_call_target="tpu_custom_call" | custom-call | bytes 30000000 | tf_op jit(solution)/shard_map/front/pallas_call | solution.py:159
  11.1 0.5 collective-permute-start
  11.6 0.8 collective-permute-start.1
  12.4 0.4 collective-permute-done.a_ref
  12.7 5.4 %conv.1 = (f32[512,1536]{1,0:T(8,128)S(1)}, f32[2,1536]{1,0:T(2,128)S(1)}) custom-call(bf16[512,1536]{1,0:T(8,128)(2,1)S(1)} %get-tuple-element.41.g_ref, bf16[2,16,1536]{2,1,0:T(8,128)(2,1)S(1)} %collective-permute-done.a_ref, bf16[2,16,1536]{2,1,0:T(8,128)(2,1)S(1)} %collective-permute-done.1.b_ref, f32[32,1536]{1,0:T(8,128)S(1)} %copy-done.4), custom_call_target="tpu_custom_call" | custom-call | bytes 21000000 | tf_op jit(solution)/shard_map/conv/pallas_call | solution.py:276
  18.2 6.4 %collective-permute-start.2 = (f32[2,1536]{1,0:T(2,128)S(1)}, f32[2,1536]{1,0:T(2,128)S(1)}, u32[]{:S(2)}, u32[]{:S(2)}) collective-permute-start(f32[2,1536]{1,0:T(2,128)S(1)} %get-tuple-element.45.own_ref), channel_id=1, source_target_pairs={{0,1},{1,0},{2,3},{3,2},{4,5},{5,4},{6,7},{7,6},{8,9},{9,8},{10,11... | collective-permute-start | bytes 36872 | tf_op jit(solution)/shard_map/ppermute | solution.py:598
  24.5 0.8 collective-permute-done.2.got_ref
  25.4 0.6 turn.1
  26.0 0.4 collective-permute-start.7
  26.4 3.3 %collective-permute-start.3 = (f32[2,1536]{1,0:T(2,128)S(1)}, f32[2,1536]{1,0:T(2,128)S(1)}, u32[]{:S(2)}, u32[]{:S(2)}) collective-permute-start(f32[2,1536]{1,0:T(2,128)S(1)} %add.18.rest_0_.own_ref), channel_id=1, source_target_pairs={{0,2},{1,3},{2,0},{3,1},{4,6},{5,7},{6,4},{7,5},{8,10},{9,11},{10,... | collective-permute-start | bytes 36872 | tf_op jit(solution)/shard_map/ppermute | solution.py:598
  29.7 1.7 %collective-permute-done.3.got_ref = f32[2,1536]{1,0:T(2,128)S(1)} collective-permute-done((f32[2,1536]{1,0:T(2,128)S(1)}, f32[2,1536]{1,0:T(2,128)S(1)}, u32[]{:S(2)}, u32[]{:S(2)}) %collective-permute-start.3) | collective-permute-done | bytes 12320 | tf_op jit(solution)/shard_map/ppermute | solution.py:598
  31.3 1.8 %collective-permute-start.4 = (f32[2,1536]{1,0:T(2,128)S(1)}, f32[2,1536]{1,0:T(2,128)S(1)}, u32[]{:S(2)}, u32[]{:S(2)}) collective-permute-start(f32[2,1536]{1,0:T(2,128)S(1)} %add.19.own_ref), channel_id=1, source_target_pairs={{0,4},{1,5},{2,6},{3,7},{4,0},{5,1},{6,2},{7,3},{8,12},{9,13},{10,... | collective-permute-start | bytes 36872 | tf_op jit(solution)/shard_map/ppermute | solution.py:598
  33.2 1.9 %collective-permute-done.4.got_ref = f32[2,1536]{1,0:T(2,128)S(1)} collective-permute-done((f32[2,1536]{1,0:T(2,128)S(1)}, f32[2,1536]{1,0:T(2,128)S(1)}, u32[]{:S(2)}, u32[]{:S(2)}) %collective-permute-start.4) | collective-permute-done | bytes 12320 | tf_op jit(solution)/shard_map/ppermute | solution.py:598
  35.0 2.3 %collective-permute-start.5 = (f32[2,1536]{1,0:T(2,128)S(1)}, f32[2,1536]{1,0:T(2,128)S(1)}, u32[]{:S(2)}, u32[]{:S(2)}) collective-permute-start(f32[2,1536]{1,0:T(2,128)S(1)} %add.20.own_ref), channel_id=1, source_target_pairs={{0,8},{1,9},{2,10},{3,11},{4,12},{5,13},{6,14},{7,15},{8,0},{9,1},... | collective-permute-start | bytes 36872 | tf_op jit(solution)/shard_map/ppermute | solution.py:598
  37.4 1.7 %collective-permute-done.5.got_ref = f32[2,1536]{1,0:T(2,128)S(1)} collective-permute-done((f32[2,1536]{1,0:T(2,128)S(1)}, f32[2,1536]{1,0:T(2,128)S(1)}, u32[]{:S(2)}, u32[]{:S(2)}) %collective-permute-start.5) | collective-permute-done | bytes 12320 | tf_op jit(solution)/shard_map/ppermute | solution.py:598
  39.1 3.0 %collective-permute-start.6 = (f32[2,1536]{1,0:T(2,128)S(1)}, f32[2,1536]{1,0:T(2,128)S(1)}, u32[]{:S(2)}, u32[]{:S(2)}) collective-permute-start(f32[2,1536]{1,0:T(2,128)S(1)} %add.21.own_ref), channel_id=1, source_target_pairs={{0,16},{1,17},{2,18},{3,19},{4,20},{5,21},{6,22},{7,23},{8,24},{9,... | collective-permute-start | bytes 36872 | tf_op jit(solution)/shard_map/ppermute | solution.py:598
  42.1 1.7 %collective-permute-done.6.got_ref = f32[2,1536]{1,0:T(2,128)S(1)} collective-permute-done((f32[2,1536]{1,0:T(2,128)S(1)}, f32[2,1536]{1,0:T(2,128)S(1)}, u32[]{:S(2)}, u32[]{:S(2)}) %collective-permute-start.6) | collective-permute-done | bytes 12320 | tf_op jit(solution)/shard_map/ppermute | solution.py:598
  43.8 0.0 copy-start.1
  43.8 3.5 %middle.1 = (bf16[512,1536]{1,0:T(8,128)(2,1)S(1)}, f32[512,1536]{1,0:T(8,128)S(1)}, f32[2,1536]{1,0:T(2,128)S(1)}, bf16[2,32,1536]{2,1,0:T(8,128)(2,1)S(1)}, bf16[2,32,1536]{2,1,0:T(8,128)(2,1)S(1)}) custom-call(f32[512,1536]{1,0:T(8,128)S(1)} %get-tuple-element.44.conv_ref, f32[2,1536]{1,0:T(2,128)S(1)} %add.22.sums_ref, ...), custom_call_target="tpu_custom_call" | custom-call | bytes 12000000 | tf_op jit(solution)/shard_map/middle/pallas_call | solution.py:328
  47.3 0.1 collective-permute-start.14
  47.4 0.5 collective-permute-start.9
  47.9 0.8 collective-permute-start.10
  48.7 3.0 %collective-permute-start.8 = (f32[2,1536]{1,0:T(2,128)S(1)}, f32[2,1536]{1,0:T(2,128)S(1)}, u32[]{:S(2)}, u32[]{:S(2)}) collective-permute-start(f32[2,1536]{1,0:T(2,128)S(1)} %get-tuple-element.50.own_ref), channel_id=1, source_target_pairs={{0,1},{1,0},{2,3},{3,2},{4,5},{5,4},{6,7},{7,6},{8,9},{9,8},{10,11... | collective-permute-start | bytes 36872 | tf_op jit(solution)/shard_map/ppermute | solution.py:598
  51.8 0.8 collective-permute-done.8.got_ref
  52.6 1.3 %collective-permute-start.11 = (f32[2,1536]{1,0:T(2,128)S(1)}, f32[2,1536]{1,0:T(2,128)S(1)}, u32[]{:S(2)}, u32[]{:S(2)}) collective-permute-start(f32[2,1536]{1,0:T(2,128)S(1)} %add.23.rest_0_.own_ref), channel_id=1, source_target_pairs={{0,2},{1,3},{2,0},{3,1},{4,6},{5,7},{6,4},{7,5},{8,10},{9,11},{10,... | collective-permute-start | bytes 36872 | tf_op jit(solution)/shard_map/ppermute | solution.py:598
  53.9 3.6 %branch.1.rest_0_ = bf16[512,1536]{1,0:T(8,128)(2,1)} custom-call(bf16[512,1536]{1,0:T(8,128)(2,1)S(1)} %bitcast.14, bf16[512,1536]{1,0:T(8,128)(2,1)S(1)} %get-tuple-element.49.act_ref.acta_ref, bf16[1536,1536]{1,0:T(8,128)(2,1)S(1)} %bitcast.9, f32[2,1536]{1,0:T(2,128)S(1)} %add.23.rest_0_.own_ref), custom_call_target="tpu_custom_call" | custom-call | bytes 12000000 | tf_op jit(solution)/shard_map/branch/pallas_call | solution.py:395
  57.5 0.0 copy-start.2
  57.5 1.4 %copy-done.2 = bf16[512,1536]{1,0:T(8,128)(2,1)S(1)} copy-done((bf16[512,1536]{1,0:T(8,128)(2,1)S(1)}, bf16[512,1536]{1,0:T(8,128)(2,1)}, u32[]{:S(2)}) %copy-start.2) | copy-done | bytes 1572888
  58.9 2.0 %collective-permute-start.12 = (f32[2,1536]{1,0:T(2,128)S(1)}, f32[2,1536]{1,0:T(2,128)S(1)}, u32[]{:S(2)}, u32[]{:S(2)}) collective-permute-start(f32[2,1536]{1,0:T(2,128)S(1)} %add.24.own_ref), channel_id=1, source_target_pairs={{0,4},{1,5},{2,6},{3,7},{4,0},{5,1},{6,2},{7,3},{8,12},{9,13},{10,... | collective-permute-start | bytes 36872 | tf_op jit(solution)/shard_map/ppermute | solution.py:598
  60.8 1.7 %collective-permute-done.12.got_ref = f32[2,1536]{1,0:T(2,128)S(1)} collective-permute-done((f32[2,1536]{1,0:T(2,128)S(1)}, f32[2,1536]{1,0:T(2,128)S(1)}, u32[]{:S(2)}, u32[]{:S(2)}) %collective-permute-start.12) | collective-permute-done | bytes 12320 | tf_op jit(solution)/shard_map/ppermute | solution.py:598
  62.6 2.6 %grad.1 = (bf16[8,48,768]{2,1,0:T(8,128)(2,1)S(1)}, f32[8,48,768]{2,1,0:T(8,128)S(1)}, bf16[8,48,768]{2,1,0:T(8,128)(2,1)S(1)}, f32[8,48,768]{2,1,0:T(8,128)S(1)}) custom-call(bf16[16,48,512]{2,1,0:T(8,128)(2,1)S(1)} %get-tuple-element.46.rest_0_.ca_ref, bf16[16,48,512]{2,1,0:T(8,128)(2,1)S(1)} %collective-permute-done.7.rest_0_.cb_ref, ...), custom_call_target="tpu_custom_call" | custom-call | bytes 10500000 | tf_op jit(solution)/shard_map/grad/pallas_call | solution.py:367
  65.2 2.0 %collective-permute-start.22 = (bf16[8,48,768]{2,1,0:T(8,128)(2,1)S(1)}, bf16[8,48,768]{2,1,0:T(8,128)(2,1)S(1)}, u32[]{:S(2)}, u32[]{:S(2)}) collective-permute-start(bf16[8,48,768]{2,1,0:T(8,128)(2,1)S(1)} %get-tuple-element.69), channel_id=1, source_target_pairs={{0,4},{1,5},{2,6},{3,7},{4,0},{5,1},{6,2},{7,3},{8,12},{9,13},{10,... | collective-permute-start | bytes 1769480 | tf_op jit(solution)/shard_map/ppermute | solution.py:598
  67.2 1.0 collective-permute-start.20
  68.2 1.6 %collective-permute-start.13 = (f32[2,1536]{1,0:T(2,128)S(1)}, f32[2,1536]{1,0:T(2,128)S(1)}, u32[]{:S(2)}, u32[]{:S(2)}) collective-permute-start(f32[2,1536]{1,0:T(2,128)S(1)} %add.25.rest_0_.own_ref), channel_id=1, source_target_pairs={{0,8},{1,9},{2,10},{3,11},{4,12},{5,13},{6,14},{7,15},{8,0},{9,1},... | collective-permute-start | bytes 36872 | tf_op jit(solution)/shard_map/ppermute | solution.py:598
  69.8 2.1 %collective-permute-done.13.got_ref = f32[2,1536]{1,0:T(2,128)S(1)} collective-permute-done((f32[2,1536]{1,0:T(2,128)S(1)}, f32[2,1536]{1,0:T(2,128)S(1)}, u32[]{:S(2)}, u32[]{:S(2)}) %collective-permute-start.13) | collective-permute-done | bytes 12320 | tf_op jit(solution)/shard_map/ppermute | solution.py:598
  71.9 2.6 %collective-permute-start.15 = (f32[2,1536]{1,0:T(2,128)S(1)}, f32[2,1536]{1,0:T(2,128)S(1)}, u32[]{:S(2)}, u32[]{:S(2)}) collective-permute-start(f32[2,1536]{1,0:T(2,128)S(1)} %add.26.own_ref), channel_id=1, source_target_pairs={{0,16},{1,17},{2,18},{3,19},{4,20},{5,21},{6,22},{7,23},{8,24},{9,... | collective-permute-start | bytes 36872 | tf_op jit(solution)/shard_map/ppermute | solution.py:598
  74.5 2.0 %collective-permute-done.15.got_ref = f32[2,1536]{1,0:T(2,128)S(1)} collective-permute-done((f32[2,1536]{1,0:T(2,128)S(1)}, f32[2,1536]{1,0:T(2,128)S(1)}, u32[]{:S(2)}, u32[]{:S(2)}) %collective-permute-start.15) | collective-permute-done | bytes 12320 | tf_op jit(solution)/shard_map/ppermute | solution.py:598
  76.5 6.9 %grad_taps.1 = (bf16[32,1536]{1,0:T(8,128)(2,1)S(1)}, f32[12,2,9,72,128]{4,3,2,1,0:T(8,128)S(1)}) custom-call(f32[512,1536]{1,0:T(8,128)S(1)} %get-tuple-element.53.dbn_ref, f32[512,1536]{1,0:T(8,128)S(1)} %get-tuple-element.44.conv_ref, bf16[2,32,1536]{2,1,0:T(8,128)(2,1)S(1)} %collective-permute-done.9.rest_0_.a_ref, ...), custom_call_target="tpu_custom_call" | custom-call | bytes 27000000 | tf_op jit(solution)/shard_map/grad_taps/pallas_call | solution.py:466
  83.5 0.1 collective-permute-start.16
  83.6 0.1 merge.5
  83.7 1.1 collective-permute-start.23
  84.8 0.1 merge.4
  84.9 0.1 collective-permute-start.21
  85.1 1.7 %collective-permute-start.17 = (bf16[32,1536]{1,0:T(8,128)(2,1)S(1)}, bf16[32,1536]{1,0:T(8,128)(2,1)S(1)}, u32[]{:S(2)}, u32[]{:S(2)}) collective-permute-start(bf16[32,1536]{1,0:T(8,128)(2,1)S(1)} %add.28.rest_0_.own_ref), channel_id=1, source_target_pairs={{0,8},{1,9},{2,10},{3,11},{4,12},{5,13},{6,14},{7,15},{8,0},{9,1},... | collective-permute-start | bytes 294920 | tf_op jit(solution)/shard_map/ppermute | solution.py:598
  86.8 2.7 %grad_proj.2 = (bf16[512,768]{1,0:T(8,128)(2,1)S(1)}, bf16[512,768]{1,0:T(8,128)(2,1)S(1)}) custom-call(f32[12,2,9,72,128]{4,3,2,1,0:T(8,128)S(1)} %get-tuple-element.57.seq_ref, f32[32,1536]{1,0:T(8,128)S(1)} %copy-done.4, bf16[512,1536]{1,0:T(8,128)(2,1)S(1)} %get-tuple-element.58.p_ref, bf16[512,1536]{1,0:T(8,128)(2,1)S(1)} %get-tuple-element.59.q_ref, ...), custom_call_target="tpu_custom_call" | custom-call | bytes 12000000 | tf_op jit(solution)/shard_map/grad_proj/pallas_call | solution.py:514
  89.5 0.5 collective-permute-done.17.got_ref
  90.0 0.0 slice-start.2
  90.0 2.7 %collective-permute-start.18 = (bf16[32,1536]{1,0:T(8,128)(2,1)S(1)}, bf16[32,1536]{1,0:T(8,128)(2,1)S(1)}, u32[]{:S(2)}, u32[]{:S(2)}) collective-permute-start(bf16[32,1536]{1,0:T(8,128)(2,1)S(1)} %add.29.rest_0_.own_ref), channel_id=1, source_target_pairs={{0,16},{1,17},{2,18},{3,19},{4,20},{5,21},{6,22},{7,23},{8,24},{9,... | collective-permute-start | bytes 294920 | tf_op jit(solution)/shard_map/ppermute | solution.py:598
  92.7 2.7 %grad_proj.3 = (bf16[512,768]{1,0:T(8,128)(2,1)S(1)}, bf16[512,768]{1,0:T(8,128)(2,1)S(1)}) custom-call(f32[12,2,9,72,128]{4,3,2,1,0:T(8,128)S(1)} %get-tuple-element.57.seq_ref, f32[32,1536]{1,0:T(8,128)S(1)} %copy-done.4, bf16[512,1536]{1,0:T(8,128)(2,1)S(1)} %get-tuple-element.58.p_ref, bf16[512,1536]{1,0:T(8,128)(2,1)S(1)} %get-tuple-element.59.q_ref, ...), custom_call_target="tpu_custom_call" | custom-call | bytes 12000000 | tf_op jit(solution)/shard_map/grad_proj/pallas_call | solution.py:514
  95.4 1.7 %collective-permute-done.18.got_ref = bf16[32,1536]{1,0:T(8,128)(2,1)S(1)} collective-permute-done((bf16[32,1536]{1,0:T(8,128)(2,1)S(1)}, bf16[32,1536]{1,0:T(8,128)(2,1)S(1)}, u32[]{:S(2)}, u32[]{:S(2)}) %collective-permute-start.18) | collective-permute-done | bytes 98336 | tf_op jit(solution)/shard_map/ppermute | solution.py:598
  97.2 0.1 merge.6
  97.3 0.5 collective-permute-start.24
  97.8 1.7 %collective-permute-start.19 = (bf16[32,1536]{1,0:T(8,128)(2,1)S(1)}, bf16[32,1536]{1,0:T(8,128)(2,1)S(1)}, u32[]{:S(2)}, u32[]{:S(2)}) collective-permute-start(bf16[32,1536]{1,0:T(8,128)(2,1)S(1)} %add.30.rest_4_.own_ref.refs_4_), channel_id=1, source_target_pairs={{0,2},{1,3},{2,0},{3,1},{4,6},{5,7},{6,4},{7,5},{8,10},{9,11},{10,... | collective-permute-start | bytes 294920 | tf_op jit(solution)/shard_map/ppermute | solution.py:598
  99.5 5.1 %back_proj.1.rest_0_.acc_ref.refs_2_ = f32[512,1536]{1,0:T(8,128)S(1)} custom-call(f32[3,1536]{1,0:T(4,128)S(1)} %get-tuple-element.47.vec_ref, bf16[1536,3072]{1,0:T(8,128)(2,1)S(1)} %bitcast.7, bf16[512,768]{1,0:T(8,128)(2,1)S(1)} %get-tuple-element.61.rest_0_, bf16[512,768]{1,0:T(8,128)(2,1)S(1)} %get-tuple-element.62.rest_0_.rest_1_, ...), custom_call_target="tpu_custom_call" | custom-call | bytes 15000000 | tf_op jit(solution)/shard_map/back_proj/pallas_call | solution.py:548
  104.6 0.1 merge.7
  104.6 0.0 copy-start.6
  104.7 3.4 %collective-permute-start.25 = (bf16[1,48,1536]{2,1,0:T(8,128)(2,1)S(1)}, bf16[1,48,1536]{2,1,0:T(8,128)(2,1)S(1)}, u32[]{:S(2)}, u32[]{:S(2)}) collective-permute-start(bf16[1,48,1536]{2,1,0:T(8,128)(2,1)S(1)} %get-tuple-element.75), channel_id=1, source_target_pairs={{0,16},{1,17},{2,18},{3,19},{4,20},{5,21},{6,22},{7,23},{8,24},{9,... | collective-permute-start | bytes 442376 | tf_op jit(solution)/shard_map/ppermute | solution.py:598
  108.1 1.1 collective-permute-start.26
  109.3 0.6 slice_reduce_fusion
  109.9 2.4 %back_norm.1.rest_0_ = bf16[512,1536]{1,0:T(8,128)(2,1)} custom-call(bf16[512,1536]{1,0:T(8,128)(2,1)S(1)} %copy-done.6, f32[512,1]{1,0:T(8,128)S(1)} %get-tuple-element.52.rstd_ref, bf16[512,1536]{1,0:T(8,128)(2,1)S(1)} %bitcast.12, f32[512,1536]{1,0:T(8,128)S(1)} %back_proj.1.rest_0_.acc_ref.refs_2_, bf16[32,1536]{1,0:T(8,128)(2,1)S(1)} %add.31.rest_0_.own_ref), custom_call_target="tpu_custom_call" | custom-call | bytes 9000000 | tf_op jit(solution)/shard_map/back_norm/pallas_call | solution.py:584
  112.3 0.6 collective-permute-done.26.got_ref
  112.8 1.4 %copy-done.3 = bf16[512,1536]{1,0:T(8,128)(2,1)S(1)} copy-done((bf16[512,1536]{1,0:T(8,128)(2,1)S(1)}, bf16[512,1536]{1,0:T(8,128)(2,1)}, u32[]{:S(2)}) %copy-start.3) | copy-done | bytes 1572888
  114.2 0.7 add.33
  114.9 0.7 add.32
  (48 shorter events, 0.2 us)
Async XLA Ops:
  0.6 43.1 %slice-start.3 = ((s8[4718592]{0:T(1024)(128)(4,1)}), s8[4194304]{0:T(1024)(128)(4,1)S(1)}, s32[]{:S(2)}) async-start(s8[4718592]{0:T(1024)(128)(4,1)} %bitcast.8), calls=%async_computation.3 | async-start | bytes 8388608
  0.6 12.1 %copy-start.4 = (f32[32,1536]{1,0:T(8,128)S(1)}, f32[32,1536]{1,0:T(8,128)}, u32[]{:S(2)}) copy-start(f32[32,1536]{1,0:T(8,128)} %k_ref.5) | copy-start | bytes 589828
  0.7 43.1 %slice-start.4 = ((s8[4718592]{0:T(1024)(128)(4,1)}), s8[524288]{0:T(1024)(128)(4,1)S(1)}, s32[]{:S(2)}) async-start(s8[4718592]{0:T(1024)(128)(4,1)} %bitcast.8), calls=%async_computation.4 | async-start | bytes 1048576
  11.0 14.9 %copy-start.5 = (bf16[512,1536]{1,0:T(8,128)(2,1)}, bf16[512,1536]{1,0:T(8,128)(2,1)S(1)}, u32[]{:S(2)}) copy-start(bf16[512,1536]{1,0:T(8,128)(2,1)S(1)} %get-tuple-element.51.hat_ref) | copy-start | bytes 4718596
  11.1 14.3 %copy-start = (bf16[2,256,1536]{2,1,0:T(8,128)(2,1)S(1)}, bf16[2,256,1536]{2,1,0:T(8,128)(2,1)}, u32[]{:S(2)}) copy-start(bf16[2,256,1536]{2,1,0:T(8,128)(2,1)} %param.15) | copy-start | bytes 4718596
  11.1 1.7 %collective-permute-start = (bf16[2,16,1536]{2,1,0:T(8,128)(2,1)}, bf16[2,16,1536]{2,1,0:T(8,128)(2,1)S(1)}, u32[]{:S(2)}, u32[]{:S(2)}) collective-permute-start(bf16[2,16,1536]{2,1,0:T(8,128)(2,1)} %get-tuple-element.42), channel_id=1, source_target_pairs={{0,1},{1,0},{2,3},{3,2},{4,5},{5,4},{6,7},{7,6},{8,9},{9,8},{10,11... | collective-permute-start | bytes 294920 | tf_op jit(solution)/shard_map/ppermute | solution.py:598
  11.6 1.2 %collective-permute-start.1 = (bf16[2,16,1536]{2,1,0:T(8,128)(2,1)}, bf16[2,16,1536]{2,1,0:T(8,128)(2,1)S(1)}, u32[]{:S(2)}, u32[]{:S(2)}) collective-permute-start(bf16[2,16,1536]{2,1,0:T(8,128)(2,1)} %get-tuple-element.43), channel_id=1, source_target_pairs={{1,2},{2,1},{3,4},{4,3},{5,6},{6,5},{7,8},{8,7},{9,10},{10,9},{11,... | collective-permute-start | bytes 294920 | tf_op jit(solution)/shard_map/ppermute | solution.py:647
  18.2 7.2 %collective-permute-start.2 = (f32[2,1536]{1,0:T(2,128)S(1)}, f32[2,1536]{1,0:T(2,128)S(1)}, u32[]{:S(2)}, u32[]{:S(2)}) collective-permute-start(f32[2,1536]{1,0:T(2,128)S(1)} %get-tuple-element.45.own_ref), channel_id=1, source_target_pairs={{0,1},{1,0},{2,3},{3,2},{4,5},{5,4},{6,7},{7,6},{8,9},{9,8},{10,11... | collective-permute-start | bytes 36872 | tf_op jit(solution)/shard_map/ppermute | solution.py:598
  26.0 17.8 %collective-permute-start.7 = (bf16[16,48,512]{2,1,0:T(8,128)(2,1)S(1)}, bf16[16,48,512]{2,1,0:T(8,128)(2,1)S(1)}, u32[]{:S(2)}, u32[]{:S(2)}) collective-permute-start(bf16[16,48,512]{2,1,0:T(8,128)(2,1)S(1)} %get-tuple-element.48), channel_id=1, source_target_pairs={{0,1},{1,0},{2,3},{3,2},{4,5},{5,4},{6,7},{7,6},{8,9},{9,8},{10,11... | collective-permute-start | bytes 2359304 | tf_op jit(solution)/shard_map/ppermute | solution.py:598
  26.4 5.0 %collective-permute-start.3 = (f32[2,1536]{1,0:T(2,128)S(1)}, f32[2,1536]{1,0:T(2,128)S(1)}, u32[]{:S(2)}, u32[]{:S(2)}) collective-permute-start(f32[2,1536]{1,0:T(2,128)S(1)} %add.18.rest_0_.own_ref), channel_id=1, source_target_pairs={{0,2},{1,3},{2,0},{3,1},{4,6},{5,7},{6,4},{7,5},{8,10},{9,11},{10,... | collective-permute-start | bytes 36872 | tf_op jit(solution)/shard_map/ppermute | solution.py:598
  31.3 3.7 %collective-permute-start.4 = (f32[2,1536]{1,0:T(2,128)S(1)}, f32[2,1536]{1,0:T(2,128)S(1)}, u32[]{:S(2)}, u32[]{:S(2)}) collective-permute-start(f32[2,1536]{1,0:T(2,128)S(1)} %add.19.own_ref), channel_id=1, source_target_pairs={{0,4},{1,5},{2,6},{3,7},{4,0},{5,1},{6,2},{7,3},{8,12},{9,13},{10,... | collective-permute-start | bytes 36872 | tf_op jit(solution)/shard_map/ppermute | solution.py:598
  35.0 4.0 %collective-permute-start.5 = (f32[2,1536]{1,0:T(2,128)S(1)}, f32[2,1536]{1,0:T(2,128)S(1)}, u32[]{:S(2)}, u32[]{:S(2)}) collective-permute-start(f32[2,1536]{1,0:T(2,128)S(1)} %add.20.own_ref), channel_id=1, source_target_pairs={{0,8},{1,9},{2,10},{3,11},{4,12},{5,13},{6,14},{7,15},{8,0},{9,1},... | collective-permute-start | bytes 36872 | tf_op jit(solution)/shard_map/ppermute | solution.py:598
  39.1 4.7 %collective-permute-start.6 = (f32[2,1536]{1,0:T(2,128)S(1)}, f32[2,1536]{1,0:T(2,128)S(1)}, u32[]{:S(2)}, u32[]{:S(2)}) collective-permute-start(f32[2,1536]{1,0:T(2,128)S(1)} %add.21.own_ref), channel_id=1, source_target_pairs={{0,16},{1,17},{2,18},{3,19},{4,20},{5,21},{6,22},{7,23},{8,24},{9,... | collective-permute-start | bytes 36872 | tf_op jit(solution)/shard_map/ppermute | solution.py:598
  43.8 10.1 %copy-start.1 = (bf16[2,256,1536]{2,1,0:T(8,128)(2,1)S(1)}, bf16[2,256,1536]{2,1,0:T(8,128)(2,1)}, u32[]{:S(2)}) copy-start(bf16[2,256,1536]{2,1,0:T(8,128)(2,1)} %param.8) | copy-start | bytes 4718596
  47.3 15.3 %collective-permute-start.14 = (bf16[512,1536]{1,0:T(8,128)(2,1)S(1)}, bf16[512,1536]{1,0:T(8,128)(2,1)S(1)}, u32[]{:S(2)}, u32[]{:S(2)}) collective-permute-start(bf16[512,1536]{1,0:T(8,128)(2,1)S(1)} %get-tuple-element.49.act_ref.acta_ref), channel_id=1, source_target_pairs={{0,1},{1,0},{2,3},{3,2},{4,5},{5,4},{6,7},{7,6},{8,9},{9,8},{10,11... | collective-permute-start | bytes 4718600 | tf_op jit(solution)/shard_map/ppermute | solution.py:598
  47.4 15.2 %collective-permute-start.9 = (bf16[2,32,1536]{2,1,0:T(8,128)(2,1)S(1)}, bf16[2,32,1536]{2,1,0:T(8,128)(2,1)S(1)}, u32[]{:S(2)}, u32[]{:S(2)}) collective-permute-start(bf16[2,32,1536]{2,1,0:T(8,128)(2,1)S(1)} %get-tuple-element.54), channel_id=1, source_target_pairs={{0,1},{1,0},{2,3},{3,2},{4,5},{5,4},{6,7},{7,6},{8,9},{9,8},{10,11... | collective-permute-start | bytes 589832 | tf_op jit(solution)/shard_map/ppermute | solution.py:598
  47.9 14.7 %collective-permute-start.10 = (bf16[2,32,1536]{2,1,0:T(8,128)(2,1)S(1)}, bf16[2,32,1536]{2,1,0:T(8,128)(2,1)S(1)}, u32[]{:S(2)}, u32[]{:S(2)}) collective-permute-start(bf16[2,32,1536]{2,1,0:T(8,128)(2,1)S(1)} %get-tuple-element.55), channel_id=1, source_target_pairs={{1,2},{2,1},{3,4},{4,3},{5,6},{6,5},{7,8},{8,7},{9,10},{10,9},{11,... | collective-permute-start | bytes 589832 | tf_op jit(solution)/shard_map/ppermute | solution.py:647
  48.7 3.8 %collective-permute-start.8 = (f32[2,1536]{1,0:T(2,128)S(1)}, f32[2,1536]{1,0:T(2,128)S(1)}, u32[]{:S(2)}, u32[]{:S(2)}) collective-permute-start(f32[2,1536]{1,0:T(2,128)S(1)} %get-tuple-element.50.own_ref), channel_id=1, source_target_pairs={{0,1},{1,0},{2,3},{3,2},{4,5},{5,4},{6,7},{7,6},{8,9},{9,8},{10,11... | collective-permute-start | bytes 36872 | tf_op jit(solution)/shard_map/ppermute | solution.py:598
  52.6 4.9 %collective-permute-start.11 = (f32[2,1536]{1,0:T(2,128)S(1)}, f32[2,1536]{1,0:T(2,128)S(1)}, u32[]{:S(2)}, u32[]{:S(2)}) collective-permute-start(f32[2,1536]{1,0:T(2,128)S(1)} %add.23.rest_0_.own_ref), channel_id=1, source_target_pairs={{0,2},{1,3},{2,0},{3,1},{4,6},{5,7},{6,4},{7,5},{8,10},{9,11},{10,... | collective-permute-start | bytes 36872 | tf_op jit(solution)/shard_map/ppermute | solution.py:598
  57.5 1.4 %copy-start.2 = (bf16[512,1536]{1,0:T(8,128)(2,1)S(1)}, bf16[512,1536]{1,0:T(8,128)(2,1)}, u32[]{:S(2)}) copy-start(bf16[512,1536]{1,0:T(8,128)(2,1)} %branch.1.rest_0_) | copy-start | bytes 4718596
  58.9 3.7 %collective-permute-start.12 = (f32[2,1536]{1,0:T(2,128)S(1)}, f32[2,1536]{1,0:T(2,128)S(1)}, u32[]{:S(2)}, u32[]{:S(2)}) collective-permute-start(f32[2,1536]{1,0:T(2,128)S(1)} %add.24.own_ref), channel_id=1, source_target_pairs={{0,4},{1,5},{2,6},{3,7},{4,0},{5,1},{6,2},{7,3},{8,12},{9,13},{10,... | collective-permute-start | bytes 36872 | tf_op jit(solution)/shard_map/ppermute | solution.py:598
  65.2 18.4 %collective-permute-start.22 = (bf16[8,48,768]{2,1,0:T(8,128)(2,1)S(1)}, bf16[8,48,768]{2,1,0:T(8,128)(2,1)S(1)}, u32[]{:S(2)}, u32[]{:S(2)}) collective-permute-start(bf16[8,48,768]{2,1,0:T(8,128)(2,1)S(1)} %get-tuple-element.69), channel_id=1, source_target_pairs={{0,4},{1,5},{2,6},{3,7},{4,0},{5,1},{6,2},{7,3},{8,12},{9,13},{10,... | collective-permute-start | bytes 1769480 | tf_op jit(solution)/shard_map/ppermute | solution.py:598
  67.2 17.6 %collective-permute-start.20 = (bf16[8,48,768]{2,1,0:T(8,128)(2,1)S(1)}, bf16[8,48,768]{2,1,0:T(8,128)(2,1)S(1)}, u32[]{:S(2)}, u32[]{:S(2)}) collective-permute-start(bf16[8,48,768]{2,1,0:T(8,128)(2,1)S(1)} %get-tuple-element.56.rest_0_), channel_id=1, source_target_pairs={{0,2},{1,3},{2,0},{3,1},{4,6},{5,7},{6,4},{7,5},{8,10},{9,11},{10,... | collective-permute-start | bytes 1769480 | tf_op jit(solution)/shard_map/ppermute | solution.py:598
  68.2 3.7 %collective-permute-start.13 = (f32[2,1536]{1,0:T(2,128)S(1)}, f32[2,1536]{1,0:T(2,128)S(1)}, u32[]{:S(2)}, u32[]{:S(2)}) collective-permute-start(f32[2,1536]{1,0:T(2,128)S(1)} %add.25.rest_0_.own_ref), channel_id=1, source_target_pairs={{0,8},{1,9},{2,10},{3,11},{4,12},{5,13},{6,14},{7,15},{8,0},{9,1},... | collective-permute-start | bytes 36872 | tf_op jit(solution)/shard_map/ppermute | solution.py:598
  71.9 4.6 %collective-permute-start.15 = (f32[2,1536]{1,0:T(2,128)S(1)}, f32[2,1536]{1,0:T(2,128)S(1)}, u32[]{:S(2)}, u32[]{:S(2)}) collective-permute-start(f32[2,1536]{1,0:T(2,128)S(1)} %add.26.own_ref), channel_id=1, source_target_pairs={{0,16},{1,17},{2,18},{3,19},{4,20},{5,21},{6,22},{7,23},{8,24},{9,... | collective-permute-start | bytes 36872 | tf_op jit(solution)/shard_map/ppermute | solution.py:598
  83.5 1.5 %collective-permute-start.16 = (bf16[32,1536]{1,0:T(8,128)(2,1)S(1)}, bf16[32,1536]{1,0:T(8,128)(2,1)S(1)}, u32[]{:S(2)}, u32[]{:S(2)}) collective-permute-start(bf16[32,1536]{1,0:T(8,128)(2,1)S(1)} %get-tuple-element.60.own_ref), channel_id=1, source_target_pairs={{0,1},{1,0},{2,3},{3,2},{4,5},{5,4},{6,7},{7,6},{8,9},{9,8},{10,11... | collective-permute-start | bytes 294920 | tf_op jit(solution)/shard_map/ppermute | solution.py:598
  83.7 13.5 %collective-permute-start.23 = (bf16[4,48,768]{2,1,0:T(8,128)(2,1)S(1)}, bf16[4,48,768]{2,1,0:T(8,128)(2,1)S(1)}, u32[]{:S(2)}, u32[]{:S(2)}) collective-permute-start(bf16[4,48,768]{2,1,0:T(8,128)(2,1)S(1)} %get-tuple-element.71), channel_id=1, source_target_pairs={{0,2},{1,3},{2,0},{3,1},{4,6},{5,7},{6,4},{7,5},{8,10},{9,11},{10,... | collective-permute-start | bytes 884744 | tf_op jit(solution)/shard_map/ppermute | solution.py:598
  84.9 12.3 %collective-permute-start.21 = (bf16[4,48,768]{2,1,0:T(8,128)(2,1)S(1)}, bf16[4,48,768]{2,1,0:T(8,128)(2,1)S(1)}, u32[]{:S(2)}, u32[]{:S(2)}) collective-permute-start(bf16[4,48,768]{2,1,0:T(8,128)(2,1)S(1)} %get-tuple-element.67), channel_id=1, source_target_pairs={{0,4},{1,5},{2,6},{3,7},{4,0},{5,1},{6,2},{7,3},{8,12},{9,13},{10,... | collective-permute-start | bytes 884744 | tf_op jit(solution)/shard_map/ppermute | solution.py:598
  85.1 4.9 %collective-permute-start.17 = (bf16[32,1536]{1,0:T(8,128)(2,1)S(1)}, bf16[32,1536]{1,0:T(8,128)(2,1)S(1)}, u32[]{:S(2)}, u32[]{:S(2)}) collective-permute-start(bf16[32,1536]{1,0:T(8,128)(2,1)S(1)} %add.28.rest_0_.own_ref), channel_id=1, source_target_pairs={{0,8},{1,9},{2,10},{3,11},{4,12},{5,13},{6,14},{7,15},{8,0},{9,1},... | collective-permute-start | bytes 294920 | tf_op jit(solution)/shard_map/ppermute | solution.py:598
  86.8 12.7 %slice-start = ((s8[9437184]{0:T(1024)(128)(4,1)}), s8[4194304]{0:T(1024)(128)(4,1)S(1)}, s32[]{:S(2)}) async-start(s8[9437184]{0:T(1024)(128)(4,1)} %bitcast.6), calls=%async_computation | async-start | bytes 8388608
  86.8 12.7 %slice-start.1 = ((s8[9437184]{0:T(1024)(128)(4,1)}), s8[4194304]{0:T(1024)(128)(4,1)S(1)}, s32[]{:S(2)}) async-start(s8[9437184]{0:T(1024)(128)(4,1)} %bitcast.6), calls=%async_computation.1 | async-start | bytes 8388608
  90.0 9.5 %slice-start.2 = ((s8[9437184]{0:T(1024)(128)(4,1)}), s8[1048576]{0:T(1024)(128)(4,1)S(1)}, s32[]{:S(2)}) async-start(s8[9437184]{0:T(1024)(128)(4,1)} %bitcast.6), calls=%async_computation.2 | async-start | bytes 2097152
  90.0 7.1 %collective-permute-start.18 = (bf16[32,1536]{1,0:T(8,128)(2,1)S(1)}, bf16[32,1536]{1,0:T(8,128)(2,1)S(1)}, u32[]{:S(2)}, u32[]{:S(2)}) collective-permute-start(bf16[32,1536]{1,0:T(8,128)(2,1)S(1)} %add.29.rest_0_.own_ref), channel_id=1, source_target_pairs={{0,16},{1,17},{2,18},{3,19},{4,20},{5,21},{6,22},{7,23},{8,24},{9,... | collective-permute-start | bytes 294920 | tf_op jit(solution)/shard_map/ppermute | solution.py:598
  97.3 7.3 %collective-permute-start.24 = (bf16[2,48,1536]{2,1,0:T(8,128)(2,1)S(1)}, bf16[2,48,1536]{2,1,0:T(8,128)(2,1)S(1)}, u32[]{:S(2)}, u32[]{:S(2)}) collective-permute-start(bf16[2,48,1536]{2,1,0:T(8,128)(2,1)S(1)} %get-tuple-element.73), channel_id=1, source_target_pairs={{0,8},{1,9},{2,10},{3,11},{4,12},{5,13},{6,14},{7,15},{8,0},{9,1},... | collective-permute-start | bytes 884744 | tf_op jit(solution)/shard_map/ppermute | solution.py:598
  97.8 10.3 %collective-permute-start.19 = (bf16[32,1536]{1,0:T(8,128)(2,1)S(1)}, bf16[32,1536]{1,0:T(8,128)(2,1)S(1)}, u32[]{:S(2)}, u32[]{:S(2)}) collective-permute-start(bf16[32,1536]{1,0:T(8,128)(2,1)S(1)} %add.30.rest_4_.own_ref.refs_4_), channel_id=1, source_target_pairs={{0,2},{1,3},{2,0},{3,1},{4,6},{5,7},{6,4},{7,5},{8,10},{9,11},{10,... | collective-permute-start | bytes 294920 | tf_op jit(solution)/shard_map/ppermute | solution.py:598
  104.6 5.3 %copy-start.6 = (bf16[512,1536]{1,0:T(8,128)(2,1)S(1)}, bf16[512,1536]{1,0:T(8,128)(2,1)}, u32[]{:S(2)}) copy-start(bf16[512,1536]{1,0:T(8,128)(2,1)} %copy-done.5) | copy-start | bytes 4718596
  104.7 10.3 %collective-permute-start.25 = (bf16[1,48,1536]{2,1,0:T(8,128)(2,1)S(1)}, bf16[1,48,1536]{2,1,0:T(8,128)(2,1)S(1)}, u32[]{:S(2)}, u32[]{:S(2)}) collective-permute-start(bf16[1,48,1536]{2,1,0:T(8,128)(2,1)S(1)} %get-tuple-element.75), channel_id=1, source_target_pairs={{0,16},{1,17},{2,18},{3,19},{4,20},{5,21},{6,22},{7,23},{8,24},{9,... | collective-permute-start | bytes 442376 | tf_op jit(solution)/shard_map/ppermute | solution.py:598
  108.1 4.7 %collective-permute-start.26 = (bf16[32,1536]{1,0:T(8,128)(2,1)S(1)}, bf16[32,1536]{1,0:T(8,128)(2,1)S(1)}, u32[]{:S(2)}, u32[]{:S(2)}) collective-permute-start(bf16[32,1536]{1,0:T(8,128)(2,1)S(1)} %add.31.rest_0_.own_ref), channel_id=1, source_target_pairs={{0,4},{1,5},{2,6},{3,7},{4,0},{5,1},{6,2},{7,3},{8,12},{9,13},{10,... | collective-permute-start | bytes 294920 | tf_op jit(solution)/shard_map/ppermute | solution.py:598
  112.8 1.4 %copy-start.3 = (bf16[512,1536]{1,0:T(8,128)(2,1)S(1)}, bf16[512,1536]{1,0:T(8,128)(2,1)}, u32[]{:S(2)}) copy-start(bf16[512,1536]{1,0:T(8,128)(2,1)} %back_norm.1.rest_0_) | copy-start | bytes 4718596

commit v4 on v3

--- a/solution.py
+++ b/solution.py
@@ -12,6 +12,7 @@
 F32 = jnp.float32
 LANES = 128
 PAD = 16
+HALO = 2 * PAD
 MIB = 1 << 20
 AXIS = "seq"
 VMEM_MIB = 8
@@ -23,6 +24,7 @@
 
 WHOLE = pl.BlockSpec(memory_space=pltpu.VMEM)
 ANYWHERE = pl.BlockSpec(memory_space=pl.ANY)
+FAR = pl.BlockSpec(memory_space=pltpu.HBM)
 CW = 256
 
 
@@ -38,6 +40,10 @@
     me = lax.axis_index(AXIS)
     last = lax.axis_size(AXIS) - 1
     return me % 2, me // 2, (me > 0).astype(F32), (me < last).astype(F32)
+
+
+def far(array):
+    return pltpu.with_memory_space_constraint(array, pltpu.HBM)
 
 
 def near(dims, dtype):
@@ -88,8 +94,9 @@
 
 
 def front_body(
-    utt, x_hbm, ln_ref, gain_ref, bias_ref, w_hbm,
-    gated_ref, p_ref, q_ref, hat_ref, rstd_ref, vec_ref, a_ref, b_ref, normed_ref, x_ref, w_ref, x_sem, w_sem,
+    utt, x_hbm, ln_hbm, gain_hbm, bias_hbm, w_hbm, cot_hbm,
+    gated_ref, p_ref, q_ref, hat_ref, rstd_ref, vec_ref, a_ref, b_ref, normed_ref, x_ref, w_ref, cot_ref,
+    ln_ref, gain_ref, bias_ref, x_sem, w_sem, cot_sem, row_sem,
 ):
     rows, d = x_ref.shape
     frames = rows // utt
@@ -105,13 +112,31 @@
         at = pl.ds(half * d + j * CW, CW)
         return pltpu.make_async_copy(w_hbm.at[:, at], w_ref.at[:, at], w_sem.at[j, half])
 
+    row_copies = [
+        pltpu.make_async_copy(source, target, row_sem.at[i])
+        for i, (source, target) in enumerate(
+            ((ln_hbm, ln_ref), (gain_hbm, gain_ref), (bias_hbm, bias_ref))
+        )
+    ]
+    for copy in row_copies:
+        copy.start()
     for i in range(pieces):
         x_copy(i).start()
     for half in range(2):
         w_copy(0, half).start()
-    vec_ref[0:1, :] = ln_ref[...].reshape(1, d)
-    vec_ref[1:2, :] = gain_ref[...].reshape(1, d)
-    vec_ref[2:3, :] = bias_ref[...].reshape(1, d)
+    cots = []
+    for u in range(utt):
+        for side, at in enumerate((u * frames, (u + 1) * frames - PAD)):
+            cots.append(
+                pltpu.make_async_copy(
+                    cot_hbm.at[pl.ds(at, PAD)], cot_ref.at[u, side], cot_sem.at[u, side]
+                )
+            )
+            cots[-1].start()
+    for copy in row_copies:
+        copy.wait()
+    for i, row_ref in enumerate((ln_ref, gain_ref, bias_ref)):
+        vec_ref[i : i + 1, :] = row_ref[...].reshape(1, d)
 
     for i in range(pieces):
         x_copy(i).wait()
@@ -147,31 +172,42 @@
         p_ref[:, cols] = sig.astype(BF)
         q_ref[:, cols] = (gated * (1.0 - sig)).astype(BF)
         shaped = held.reshape(utt, frames, CW)
-        first, last = shaped[:, :PAD], shaped[:, frames - PAD :]
-        a_ref[:, :, cols] = jnp.where(odd, first, last)
-        b_ref[:, :, cols] = jnp.where(odd, last, first)
-
-
-def front(utt, x, ln_gain, bn_gain, bn_bias, w_in):
+        first, last = shaped[:, :HALO], shaped[:, frames - HALO :]
+        a_ref[:, :HALO, cols] = jnp.where(odd, first, last)
+        b_ref[:, :HALO, cols] = jnp.where(odd, last, first)
+    for copy in cots:
+        copy.wait()
+    first, last = cot_ref[:, 0], cot_ref[:, 1]
+    a_ref[:, HALO:, :] = jnp.where(odd, first, last)
+    b_ref[:, HALO:, :] = jnp.where(odd, last, first)
+
+
+def front(utt, x, ln_gain, bn_gain, bn_bias, w_in, cot):
     rows, d = x.shape
     out = near((rows, d), BF)
-    edge = shape((utt, PAD, d), BF)
+    edge = shape((utt, HALO + PAD, d), BF)
     return pl.pallas_call(
         functools.partial(front_body, utt),
-        in_specs=[ANYWHERE] + [WHOLE] * 3 + [ANYWHERE],
+        in_specs=[FAR] * 6,
         out_specs=[WHOLE] * 8,
         out_shape=[out] * 4 + [near((rows, 1), F32), near((3, d), F32)] + [edge] * 2,
         scratch_shapes=[
             pltpu.VMEM((rows, d), BF),
             pltpu.VMEM((rows, d), BF),
             pltpu.VMEM((d, 2 * d), BF),
+            pltpu.VMEM((utt, 2, PAD, d), BF),
+            pltpu.VMEM((d,), F32),
+            pltpu.VMEM((d,), F32),
+            pltpu.VMEM((d,), F32),
             pltpu.SemaphoreType.DMA((4,)),
             pltpu.SemaphoreType.DMA((d // CW, 2)),
+            pltpu.SemaphoreType.DMA((utt, 2)),
+            pltpu.SemaphoreType.DMA((3,)),
         ],
-        compiler_params=params(52),
+        compiler_params=params(24),
         cost_estimate=cost(10),
         name="front",
-    )(x, ln_gain, bn_gain, bn_bias, w_in)
+    )(*[far(a) for a in (x, ln_gain, bn_gain, bn_bias, w_in, cot)])
 
 
 def lane_groups(first, last, work):
@@ -235,105 +271,209 @@
         yield acc
 
 
-def conv_body(utt, g_ref, a_ref, b_ref, k_ref, conv_ref, sums_ref, pad_ref, seq_ref, taps_ref):
+def tap_factors(k_ref, lanes, held_ref, taps_ref):
+    per = k_ref.shape[0] // PHASES
+    held_ref[0 : per * PHASES, :] = k_ref[:, lanes]
+    for i, piece in enumerate(combined([held_ref[phase(i, per), :] for i in range(PHASES)])):
+        taps_ref[i] = piece
+
+
+def conv_piece(pad_ref, seq_ref, taps_ref, count):
+    fill_sequences(pad_ref, 1, seq_ref, count + taps_ref.shape[1])
+    for i, y in assembled(filtered(seq_ref, taps_ref, lambda a: a, count)):
+        pad_ref[phase(i, count), :] = y
+
+
+def squares(values):
+    values = values.reshape(values.shape[0] // 8, 8, LANES)
+    return jnp.sum(values, axis=0), jnp.sum(values * values, axis=0)
+
+
+def conv_mid_body(utt, g_ref, k_ref, conv_ref, sums_ref, pad_ref, seq_ref, taps_ref):
     d = g_ref.shape[1]
     frames = g_ref.shape[0] // utt
-    count = frames // PHASES
-    per = k_ref.shape[0] // PHASES
-    odd = place()[0] != 0
+    mid = frames - HALO
 
     def work(_, lanes, slot):
         first = square = jnp.zeros((8, LANES), F32)
-        pad_ref[slot, 0, 0 : per * PHASES, :] = k_ref[:, lanes]
-        k = [pad_ref[slot, 0, phase(i, per), :] for i in range(PHASES)]
-        for i, piece in enumerate(combined(k)):
-            taps_ref[slot, i] = piece
+        tap_factors(k_ref, lanes, pad_ref.at[slot, 0], taps_ref.at[slot])
         for u in range(utt):
-            a = a_ref[u, :, lanes].astype(F32)
-            b = b_ref[u, :, lanes].astype(F32)
-            rows = slice(u * frames, (u + 1) * frames)
-            pad_ref[slot, u, 0:PAD, :] = jnp.where(odd, a, b)
-            pad_ref[slot, u, PAD : PAD + frames, :] = g_ref[rows, lanes].astype(F32)
-            pad_ref[slot, u, PAD + frames : PAD + frames + PAD, :] = jnp.where(odd, b, a)
-            fill_sequences(pad_ref.at[slot, u], 1, seq_ref.at[slot, u], count + per)
-            products = filtered(seq_ref.at[slot, u], taps_ref.at[slot], lambda a: a, count)
-            for i, y in assembled(products):
-                pad_ref[slot, u, phase(i, count), :] = y
-                part = y.reshape(count // 8, 8, LANES)
-                first = first + jnp.sum(part, axis=0)
-                square = square + jnp.sum(part * part, axis=0)
-            conv_ref[rows, lanes] = pad_ref[slot, u, 0:frames, :]
+            pad = pad_ref.at[slot, u]
+            pad[0:frames, :] = g_ref[u * frames : (u + 1) * frames, lanes].astype(F32)
+            conv_piece(pad, seq_ref.at[slot, u], taps_ref.at[slot], mid // PHASES)
+            y = pad[0:mid, :]
+            start = u * (frames + HALO) + HALO
+            conv_ref[start : start + mid, lanes] = y
+            one, two = squares(y)
+            first, square = first + one, square + two
         sums_ref[0:1, lanes] = jnp.sum(first, axis=0, keepdims=True)
         sums_ref[1:2, lanes] = jnp.sum(square, axis=0, keepdims=True)
 
     lane_groups(0, d, work)
 
 
-def conv(utt, gated, a, b, kernel):
+def conv_scratch(utt, pieces, frames, count, per):
+    return [
+        pltpu.VMEM((2, utt * pieces, frames + 8, LANES), F32),
+        pltpu.VMEM((2, utt * pieces, PIECES, count + per, LANES), F32),
+        pltpu.VMEM((2, PIECES, per, LANES), F32),
+    ]
+
+
+def conv_mid(utt, gated, kernel):
     rows, d = gated.shape
     frames = rows // utt
     per = kernel.shape[0] // PHASES
     return pl.pallas_call(
-        functools.partial(conv_body, utt),
-        in_specs=[WHOLE] * 4,
+        functools.partial(conv_mid_body, utt),
+        in_specs=[WHOLE] * 2,
         out_specs=[WHOLE] * 2,
-        out_shape=[near(gated.shape, F32), shape((2, d), F32)],
-        scratch_shapes=[
-            pltpu.VMEM((2, utt, frames + 2 * PAD + 8, LANES), F32),
-            pltpu.VMEM((2, utt, PIECES, frames // PHASES + per, LANES), F32),
-            pltpu.VMEM((2, PIECES, per, LANES), F32),
-        ],
-        compiler_params=params(VMEM_MIB),
-        cost_estimate=cost(7),
-        name="conv",
-    )(gated, a, b, kernel)
-
-
-def middle_body(
-    utt, total, conv_ref, sums_ref, vec_ref, cot_ref, w_ref,
-    *rest,
-):
-    act_ref, dbn_ref, dsums_ref, a_ref, b_ref = rest[-5:]
-    rows, d = conv_ref.shape
-    frames = rows // utt
+        out_shape=[near((utt * (frames + HALO), d), F32), near((2, d), F32)],
+        scratch_shapes=conv_scratch(utt, 1, frames, (frames - HALO) // PHASES, per),
+        compiler_params=params(VMEM_MIB),
+        cost_estimate=cost(5),
+        name="conv_mid",
+    )(gated, kernel)
+
+
+def conv_end_body(utt, g_ref, a_ref, b_ref, k_ref, _, some_ref, *rest):
+    conv_ref, sums_ref, pad_ref, seq_ref, taps_ref = rest[-5:]
+    d = g_ref.shape[1]
+    frames = g_ref.shape[0] // utt
     odd = place()[0] != 0
+
+    def work(_, lanes, slot):
+        first = square = jnp.zeros((8, LANES), F32)
+        tap_factors(k_ref, lanes, pad_ref.at[slot, 0], taps_ref.at[slot])
+        for u in range(utt):
+            a = a_ref[u, :HALO, lanes].astype(F32)
+            b = b_ref[u, :HALO, lanes].astype(F32)
+            start = u * (frames + HALO)
+            for side in range(2):
+                pad = pad_ref.at[slot, 2 * u + side]
+                at = u * frames + side * (frames - HALO)
+                here = g_ref[at : at + HALO, lanes].astype(F32)
+                beside = jnp.where(odd, b, a) if side else jnp.where(odd, a, b)
+                pad[side * HALO : (side + 1) * HALO, :] = beside
+                pad[(1 - side) * HALO : (2 - side) * HALO, :] = here
+                conv_piece(pad, seq_ref.at[slot, 2 * u + side], taps_ref.at[slot], HALO // PHASES)
+                out = start + side * frames
+                conv_ref[out : out + HALO, lanes] = pad[0:HALO, :]
+                own = (1 - side) * PAD
+                one, two = squares(pad[own : own + PAD, :])
+                first, square = first + one, square + two
+        sums_ref[0:1, lanes] = some_ref[0:1, lanes] + jnp.sum(first, axis=0, keepdims=True)
+        sums_ref[1:2, lanes] = some_ref[1:2, lanes] + jnp.sum(square, axis=0, keepdims=True)
+
+    lane_groups(0, d, work)
+
+
+def conv_end(utt, gated, a, b, kernel, conv_some, sums_some, after):
+    rows, d = gated.shape
+    per = kernel.shape[0] // PHASES
+    return pl.pallas_call(
+        functools.partial(conv_end_body, utt),
+        in_specs=[WHOLE] * 6 + [ANYWHERE] * len(after),
+        out_specs=[WHOLE] * 2,
+        out_shape=[near(conv_some.shape, F32), shape((2, d), F32)],
+        scratch_shapes=conv_scratch(utt, 2, 2 * HALO, HALO // PHASES, per),
+        input_output_aliases={4: 0},
+        compiler_params=params(VMEM_MIB),
+        cost_estimate=cost(2),
+        name="conv_end",
+    )(gated, a, b, kernel, conv_some, sums_some, *after)
+
+
+def act_grad_body(cot_ref, w_ref, out_ref):
+    for j in range(out_ref.shape[1] // CW):
+        cols = slice(j * CW, (j + 1) * CW)
+        out_ref[:, cols] = jnp.dot(cot_ref[...], w_ref[:, cols], preferred_element_type=F32)
+
+
+def act_grad(cot, w_out):
+    return pl.pallas_call(
+        act_grad_body,
+        in_specs=[WHOLE] * 2,
+        out_specs=WHOLE,
+        out_shape=near(cot.shape, F32),
+        compiler_params=params(VMEM_MIB),
+        cost_estimate=cost(3),
+        name="act_grad",
+    )(cot, w_out)
+
+
+def act_grad_end_body(a_ref, b_ref, w_ref, *rest):
+    out_ref = rest[-1]
+    utt = a_ref.shape[0]
+    odd = place()[0] != 0
+    pieces = []
+    for u in range(utt):
+        a, b = a_ref[u, HALO:, :], b_ref[u, HALO:, :]
+        pieces += [jnp.where(odd, a, b), jnp.where(odd, b, a)]
+    cot = jnp.concatenate(pieces, axis=0)
+    out_ref[...] = jnp.dot(cot, w_ref[...], preferred_element_type=F32)
+
+
+def act_grad_end(a, b, w_out, after):
+    utt, _, d = a.shape
+    return pl.pallas_call(
+        act_grad_end_body,
+        in_specs=[WHOLE] * 3 + [ANYWHERE] * len(after),
+        out_specs=WHOLE,
+        out_shape=near((utt * HALO, d), F32),
+        compiler_params=params(VMEM_MIB),
+        cost_estimate=cost(2),
+        name="act_grad_end",
+    )(a, b, w_out, *after)
+
+
+def middle_body(utt, total, conv_ref, sums_ref, vec_ref, own_ref, end_ref, *rest):
+    act_ref, dbn_ref, dsums_ref = rest[-3:]
+    d = conv_ref.shape[1]
+    frames = own_ref.shape[0] // utt
     for j in range(d // CW):
         cols = slice(j * CW, (j + 1) * CW)
         mean = sums_ref[0:1, cols] * (1.0 / total)
         var = sums_ref[1:2, cols] * (1.0 / total) - mean * mean
         rstd = lax.rsqrt(var + EPSILON)
-        conv = conv_ref[:, cols]
-        xhat = (conv - mean) * rstd
-        out = xhat * vec_ref[1:2, cols] + vec_ref[2:3, cols]
-        sig = jax.nn.sigmoid(out)
-        act = out * sig
-        act_ref[:, cols] = act.astype(BF)
-        d_act = jnp.dot(cot_ref[...], w_ref[:, cols], preferred_element_type=F32)
-        dbn = d_act * (sig + act * (1.0 - sig))
-        dbn_ref[:, cols] = dbn
-        dsums_ref[0:1, cols] = jnp.sum(dbn, axis=0, keepdims=True)
-        dsums_ref[1:2, cols] = jnp.sum(dbn * xhat, axis=0, keepdims=True)
+
+        def back(at, d_act):
+            xhat = (conv_ref[at, cols] - mean) * rstd
+            out = xhat * vec_ref[1:2, cols] + vec_ref[2:3, cols]
+            sig = jax.nn.sigmoid(out)
+            act = out * sig
+            dbn = d_act * (sig + act * (1.0 - sig))
+            dbn_ref[at, cols] = dbn
+            return xhat, act, dbn
+
+        bias = gain = 0.0
         for u in range(utt):
-            low = slice(u * frames, u * frames + PAD)
-            high = slice((u + 1) * frames - PAD, (u + 1) * frames)
-            for at, piece in ((slice(0, PAD), dbn), (slice(PAD, 2 * PAD), conv)):
-                first, last = piece[low].astype(BF), piece[high].astype(BF)
-                a_ref[u, at, cols] = jnp.where(odd, first, last)
-                b_ref[u, at, cols] = jnp.where(odd, last, first)
-
-
-def middle(utt, total, conv_out, sums, vec, cot, w_out, after):
-    rows, d = cot.shape
-    edge = shape((utt, 2 * PAD, d), BF)
+            start = u * (frames + HALO)
+            back(slice(start, start + PAD), end_ref[u * HALO : u * HALO + PAD, cols])
+            rows = slice(u * frames, (u + 1) * frames)
+            xhat, act, dbn = back(slice(start + PAD, start + PAD + frames), own_ref[rows, cols])
+            act_ref[rows, cols] = act.astype(BF)
+            bias += jnp.sum(dbn, axis=0, keepdims=True)
+            gain += jnp.sum(dbn * xhat, axis=0, keepdims=True)
+            back(
+                slice(start + PAD + frames, start + HALO + frames),
+                end_ref[u * HALO + PAD : (u + 1) * HALO, cols],
+            )
+        dsums_ref[0:1, cols] = bias
+        dsums_ref[1:2, cols] = gain
+
+
+def middle(utt, total, conv_out, sums, vec, own, end, after):
+    rows, d = own.shape
     return pl.pallas_call(
         functools.partial(middle_body, utt, total),
         in_specs=[WHOLE] * 5 + [ANYWHERE] * len(after),
-        out_specs=[WHOLE] * 5,
-        out_shape=[shape((rows, d), BF), near((rows, d), F32), shape((2, d), F32), edge, edge],
-        compiler_params=params(VMEM_MIB),
-        cost_estimate=cost(4),
+        out_specs=[WHOLE] * 3,
+        out_shape=[shape((rows, d), BF), near(conv_out.shape, F32), shape((2, d), F32)],
+        compiler_params=params(VMEM_MIB),
+        cost_estimate=cost(3),
         name="middle",
-    )(conv_out, sums, vec, cot, w_out, *after)
+    )(conv_out, sums, vec, own, end, *after)
 
 
 def grad_body(bits, ca_ref, cb_ref, acta_ref, actb_ref, *rest):
@@ -376,7 +516,8 @@
 
 
 def branch_body(x_ref, act_ref, w_ref, *rest):
-    out_hbm, out_ref, sem = rest[-3:]
+    out_hbm, done_ref, out_ref, sem = rest[-4:]
+    done_ref[...] = jnp.zeros(done_ref.shape, F32)
     copies = []
     for j in range(out_ref.shape[-1] // CW):
         cols = slice(j * CW, (j + 1) * CW)
@@ -395,8 +536,8 @@
     return pl.pallas_call(
         branch_body,
         in_specs=[WHOLE] * 3 + [ANYWHERE] * len(after),
-        out_specs=pl.BlockSpec(memory_space=pltpu.HBM),
-        out_shape=pltpu.HBM((rows, d), BF),
+        out_specs=[FAR, WHOLE],
+        out_shape=[pltpu.HBM((rows, d), BF), near((8, LANES), F32)],
         scratch_shapes=[pltpu.VMEM((rows, d), BF), pltpu.SemaphoreType.DMA((d // CW,))],
         compiler_params=params(VMEM_MIB),
         cost_estimate=cost(4),
@@ -405,7 +546,7 @@
 
 
 def grad_taps_body(
-    utt, total, dbn_ref, conv_ref, a_ref, b_ref, sums_ref, dsums_ref, vec_ref, g_ref,
+    utt, total, dbn_ref, conv_ref, sums_ref, dsums_ref, vec_ref, g_ref,
     dk_ref, seq_ref, pad_ref, held_ref, acc_ref,
 ):
     d = g_ref.shape[1]
@@ -413,8 +554,7 @@
     count = frames // PHASES
     taps = dk_ref.shape[0]
     per = taps // PHASES
-    odd, _, keep_lo, keep_hi = place()
-    odd = odd != 0
+    _, _, keep_lo, keep_hi = place()
 
     def work(group, lanes, slot):
         mean = sums_ref[0:1, lanes] * (1.0 / total)
@@ -424,16 +564,17 @@
         cross = scale * rstd * (dsums_ref[1:2, lanes] * (1.0 / total))
         mean_grad = scale * (dsums_ref[0:1, lanes] * (1.0 / total))
 
-        def d_conv(dbn, conv):
-            return dbn.astype(F32) * scale - mean_grad - (conv.astype(F32) - mean) * cross
+        def d_conv(at):
+            return dbn_ref[at, lanes] * scale - mean_grad - (conv_ref[at, lanes] - mean) * cross
 
         for u in range(utt):
-            a = d_conv(a_ref[u, :PAD, lanes], a_ref[u, PAD:, lanes])
-            b = d_conv(b_ref[u, :PAD, lanes], b_ref[u, PAD:, lanes])
+            start = u * (frames + HALO)
+            end = start + PAD + frames
             rows = slice(u * frames, (u + 1) * frames)
-            pad_ref[slot, u, 0:PAD, :] = jnp.where(odd, a, b) * keep_lo
-            pad_ref[slot, u, PAD : PAD + frames, :] = d_conv(dbn_ref[rows, lanes], conv_ref[rows, lanes])
-            pad_ref[slot, u, PAD + frames : PAD + frames + PAD, :] = jnp.where(odd, b, a) * keep_hi
+            pad = pad_ref.at[slot, u]
+            pad[0:PAD, :] = d_conv(slice(start, start + PAD)) * keep_lo
+            pad[PAD : PAD + frames, :] = d_conv(slice(start + PAD, end))
+            pad[PAD + frames : HALO + frames, :] = d_conv(slice(end, end + PAD)) * keep_hi
             fill_sequences(pad_ref.at[slot, u], 0, seq_ref.at[group, u], count + per)
             pad_ref[slot, u, 0:frames, :] = g_ref[rows, lanes].astype(F32)
             g = [pad_ref[slot, u, phase(i, count), :] for i in range(PHASES)]
@@ -459,13 +600,13 @@
     lane_groups(0, d, work)
 
 
-def grad_taps(utt, total, taps, dbn, conv_out, halos, sums, dsums, vec, gated):
+def grad_taps(utt, total, taps, dbn, conv_out, sums, dsums, vec, gated):
     rows, d = gated.shape
     frames = rows // utt
     long = frames // PHASES + taps // PHASES
     return pl.pallas_call(
         functools.partial(grad_taps_body, utt, total),
-        in_specs=[WHOLE] * 8,
+        in_specs=[WHOLE] * 6,
         out_specs=[WHOLE] * 2,
         out_shape=[
             shape((taps, d), BF),
@@ -479,7 +620,7 @@
         compiler_params=params(VMEM_MIB),
         cost_estimate=cost(9),
         name="grad_taps",
-    )(dbn, conv_out, *halos, sums, dsums, vec, gated)
+    )(dbn, conv_out, sums, dsums, vec, gated)
 
 
 def grad_proj_body(utt, start, seq_ref, k_ref, p_ref, q_ref, *rest):
@@ -557,7 +698,8 @@
 
 
 def back_norm_body(hat_ref, rstd_ref, cot_ref, acc_ref, *rest):
-    out_hbm, out_ref, sem = rest[-3:]
+    out_hbm, done_ref, out_ref, sem = rest[-4:]
+    done_ref[...] = jnp.zeros(done_ref.shape, F32)
     copies = []
     rows, d = hat_ref.shape
     span = rows // sem.shape[0]
@@ -584,8 +726,8 @@
     return pl.pallas_call(
         back_norm_body,
         in_specs=[WHOLE] * 4 + [ANYWHERE] * len(after),
-        out_specs=pl.BlockSpec(memory_space=pltpu.HBM),
-        out_shape=pltpu.HBM((rows, d), BF),
+        out_specs=[FAR, WHOLE],
+        out_shape=[pltpu.HBM((rows, d), BF), near((8, LANES), F32)],
         scratch_shapes=[pltpu.VMEM((rows, d), BF), pltpu.SemaphoreType.DMA((8,))],
         compiler_params=params(VMEM_MIB),
         cost_estimate=cost(3),
@@ -713,9 +855,11 @@
     cot = cotangent.reshape(rows, d)
     by_owner = is_power(n) and n >= 8 and d % n == 0 and (d // n) % 16 == 0
 
-    gated, p, q, hat, rstd, vec, ga, gb = front(utt, x, ln_gain, bn_gain, bn_bias, w_in)
+    gated, p, q, hat, rstd, vec, ga, gb = front(utt, x, ln_gain, bn_gain, bn_bias, w_in, cot)
     ga, gb = beside(ga, gb, axis)
-    conv_out, sums = conv(utt, gated, ga, gb, kernel)
+    conv_some, sums_some = conv_mid(utt, gated, kernel)
+    own = act_grad(cot, w_out)
+    conv_out, sums = conv_end(utt, gated, ga, gb, kernel, conv_some, sums_some, [own])
     made = {}
 
     def turning(after):
@@ -723,19 +867,22 @@
         made["b"] = swap(other, axis, 1)
         return [made["a"]]
 
+    def ending(after):
+        made["end"] = act_grad_end(ga, gb, w_out, after)
+        return [made["end"]]
+
     if by_owner:
-        sums = all_sum(sums, axis, [nothing, turning])
+        sums = all_sum(sums, axis, [nothing, turning, nothing, nothing, ending])
         waits = [made["b"]]
     else:
-        sums = all_sum(sums, axis)
+        sums = all_sum(sums, axis, [nothing, ending])
         waits = []
 
-    act, dbn, dsums, da, db = middle(utt, total, conv_out, sums, vec, cot, w_out, waits)
-    da, db = beside(da, db, axis)
+    act, dbn, dsums = middle(utt, total, conv_out, sums, vec, own, made["end"], waits)
 
     def branching(after):
-        made["outputs"] = branch(x, act, w_out, after)
-        return [made["outputs"]]
+        made["outputs"], done = branch(x, act, w_out, after)
+        return [done]
 
     def grading(after):
         made["grad"] = grad((1, 2), made["a"], made["b"], act, act_b, after)
@@ -743,7 +890,7 @@
 
     if by_owner:
         act_b = swap(act, axis, 1)
-        dsums = all_sum(dsums, axis, [nothing, branching, lambda _: [da, db], grading])
+        dsums = all_sum(dsums, axis, [nothing, branching, nothing, grading])
         send_l, keep_l, send_r, keep_r = made["grad"]
         held = first_swaps([(keep_l, send_l), (keep_r, send_r)], axis, [dsums])
     else:
@@ -752,7 +899,7 @@
         d_w_out = lax.psum_scatter(dw, axis, scatter_dimension=0, tiled=True)
 
     d_kernel, d_conv = grad_taps(
-        utt, total, kernel.shape[0], dbn, conv_out, (da, db), sums, dsums, vec, gated
+        utt, total, kernel.shape[0], dbn, conv_out, sums, dsums, vec, gated
     )
     half = d // 2
 
@@ -770,8 +917,8 @@
         return [made["grads"]]
 
     def norming(after):
-        made["d_inputs"] = back_norm(hat, rstd, cot, made["grads"], after)
-        return [made["d_inputs"]]
+        made["d_inputs"], done = back_norm(hat, rstd, cot, made["grads"], after)
+        return [done]
 
     d_kernel_sum = all_sum(
         d_kernel,

time: 116 us -> 109 us (0.940)
  starting transfers between devices: 45.8 us -> 36.8 us
  local copies, waits for them, and re-layouts: 3.49 us -> 0.67 us
  waiting for transfers between devices: 17.5 us -> 20.2 us
  Pallas kernels: 47.8 us -> 50.1 us
    ppermute x25 -> x24, starting transfers between devices: 44.2 us -> 36 us  [swap(): return lax.ppermute(block, axis, [(i, i ^ bit) for i in range(count)])]
    pallas_call x2 -> x5, Pallas kernels: 15.8 us -> 19.8 us  [the longest x1 9.07 us: front(): pl.pallas_call(functools.partial(front_body, utt), in_specs=[FAR] * 6, ou...]
    unnamed x24 -> x16, local copies, waits for them, and re-layouts: 2.87 us -> 0.04 us
    ppermute x25 -> x24, waiting for transfers between devices: 17.5 us -> 20.2 us  [swap(): return lax.ppermute(block, axis, [(i, i ^ bit) for i in range(count)])]
    pallas_call x1, Pallas kernels: 3.5 us -> 1.72 us  [middle(): pl.pallas_call(functools.partial(middle_body, utt, total), in_specs=[WHOL...]
  transfers between devices with their start and end apart: 27 -> 25, of which waited for: 13 -> 14; matrix products, arithmetic and copies ran while one was open for 1% -> 1% of each run, Pallas kernels for 21% -> 31%
where the time goes in v4:
time: 109 us
  Pallas kernels  50.1 us (46%)
  starting transfers between devices  36.8 us (34%)
  waiting for transfers between devices  20.2 us (19%)
    ppermute x24, starting transfers between devices, swap(): return lax.ppermute(block, axis, [(i, i ^ bit) for i in range(count)])  36 us
    ppermute x24, waiting for transfers between devices, swap(): return lax.ppermute(block, axis, [(i, i ^ bit) for i in range(count)])  20.2 us
    pallas_call x1, Pallas kernels, front(): pl.pallas_call(functools.partial(front_body, utt), in_specs=[FAR] * 6, ou...  9.07 us
    pallas_call x1, Pallas kernels, grad_taps(): pl.pallas_call(functools.partial(grad_taps_body, utt, total), in_specs=[W...  6.87 us
    pallas_call x2, Pallas kernels, grad_proj(): pl.pallas_call(functools.partial(grad_proj_body, utt, start), in_specs=[W...  5.7 us
    pallas_call x1, Pallas kernels, conv_mid(): pl.pallas_call(functools.partial(conv_mid_body, utt), in_specs=[WHOLE] *...  5.15 us
    pallas_call x1, Pallas kernels, back_proj(): pl.pallas_call(back_proj_body, in_specs=[WHOLE] * 6 + [ANYWHERE] * len(af...  5.07 us
    pallas_call x1, Pallas kernels, branch(): pl.pallas_call(branch_body, in_specs=[WHOLE] * 3 + [ANYWHERE] * len(after...  3.56 us
  transfers between devices with their start and end apart: 25, of which 14 were waited for; matrix products, arithmetic and copies ran while one was open for 1% of the time, Pallas kernels for 31%

profile of v4, /device:TPU:0, one launch (start us, length us, event | category | flops | bytes accessed | tf_op | source)
XLA Modules:
  0.0 108.7 jit_solution(6508518459175657217)
XLA Ops:
  0.6 0.0 slice-start
  0.6 0.0 slice-start.1
  0.7 9.1 %front.1 = (bf16[512,1536]{1,0:T(8,128)(2,1)S(1)}, bf16[512,1536]{1,0:T(8,128)(2,1)S(1)}, bf16[512,1536]{1,0:T(8,128)(2,1)S(1)}, bf16[512,1536]{1,0:T(8,128)(2,1...) custom-call(bf16[512,1536]{1,0:T(8,128)(2,1)} %bitcast.14, ...), custom_call_target="tpu_custom_call" | custom-call | bytes 30000000 | tf_op jit(solution)/shard_map/front/pallas_call | solution.py:189
  9.7 0.5 collective-permute-start
  10.3 0.8 collective-permute-start.1
  11.1 2.6 %act_grad.1.rest_0_.own_ref = f32[512,1536]{1,0:T(8,128)S(1)} custom-call(bf16[512,1536]{1,0:T(8,128)(2,1)S(1)} %bitcast.11, bf16[1536,1536]{1,0:T(8,128)(2,1)S(1)} %bitcast.7), custom_call_target="tpu_custom_call" | custom-call | bytes 9000000 | tf_op jit(solution)/shard_map/act_grad/pallas_call | solution.py:394
  13.7 5.2 %conv_mid.1 = (f32[576,1536]{1,0:T(8,128)S(1)}, f32[2,1536]{1,0:T(2,128)S(1)}) custom-call(bf16[512,1536]{1,0:T(8,128)(2,1)S(1)} %get-tuple-element.45.g_ref, f32[32,1536]{1,0:T(8,128)S(1)} %copy-done.2), custom_call_target="tpu_custom_call" | custom-call | bytes 15000000 | tf_op jit(solution)/shard_map/conv_mid/pallas_call | solution.py:327
  18.9 0.0 collective-permute-done.a_ref
  18.9 2.0 %conv_end.1 = (f32[576,1536]{1,0:T(8,128)S(1)}, f32[2,1536]{1,0:T(2,128)S(1)}) custom-call(bf16[512,1536]{1,0:T(8,128)(2,1)S(1)} %get-tuple-element.45.g_ref, bf16[2,48,1536]{2,1,0:T(8,128)(2,1)S(1)} %collective-permute-done.a_ref, bf16[2,48,1536]{2,1,0:T(8,128)(2,1)S(1)} %collective-permute-done.1.b_ref, ...), custom_call_target="tpu_custom_call", output_to_operand_aliasing={{0}: (4, {})} | custom-call | bytes 6000000 | tf_op jit(solution)/shard_map/conv_end/pallas_call | solution.py:374
  20.9 3.9 %collective-permute-start.2 = (f32[2,1536]{1,0:T(2,128)S(1)}, f32[2,1536]{1,0:T(2,128)S(1)}, u32[]{:S(2)}, u32[]{:S(2)}) collective-permute-start(f32[2,1536]{1,0:T(2,128)S(1)} %get-tuple-element.51.own_ref), channel_id=1, source_target_pairs={{0,1},{1,0},{2,3},{3,2},{4,5},{5,4},{6,7},{7,6},{8,9},{9,8},{10,11... | collective-permute-start | bytes 36872 | tf_op jit(solution)/shard_map/ppermute | solution.py:740
  24.8 0.8 collective-permute-done.2.got_ref
  25.7 0.6 turn.1
  26.3 0.4 collective-permute-start.7
  26.7 2.1 %collective-permute-start.3 = (f32[2,1536]{1,0:T(2,128)S(1)}, f32[2,1536]{1,0:T(2,128)S(1)}, u32[]{:S(2)}, u32[]{:S(2)}) collective-permute-start(f32[2,1536]{1,0:T(2,128)S(1)} %add.18.rest_0_.own_ref), channel_id=1, source_target_pairs={{0,2},{1,3},{2,0},{3,1},{4,6},{5,7},{6,4},{7,5},{8,10},{9,11},{10,... | collective-permute-start | bytes 36872 | tf_op jit(solution)/shard_map/ppermute | solution.py:740
  28.8 1.7 %collective-permute-done.3.got_ref = f32[2,1536]{1,0:T(2,128)S(1)} collective-permute-done((f32[2,1536]{1,0:T(2,128)S(1)}, f32[2,1536]{1,0:T(2,128)S(1)}, u32[]{:S(2)}, u32[]{:S(2)}) %collective-permute-start.3) | collective-permute-done | bytes 12320 | tf_op jit(solution)/shard_map/ppermute | solution.py:740
  30.5 1.5 %collective-permute-start.4 = (f32[2,1536]{1,0:T(2,128)S(1)}, f32[2,1536]{1,0:T(2,128)S(1)}, u32[]{:S(2)}, u32[]{:S(2)}) collective-permute-start(f32[2,1536]{1,0:T(2,128)S(1)} %add.19.own_ref), channel_id=1, source_target_pairs={{0,4},{1,5},{2,6},{3,7},{4,0},{5,1},{6,2},{7,3},{8,12},{9,13},{10,... | collective-permute-start | bytes 36872 | tf_op jit(solution)/shard_map/ppermute | solution.py:740
  32.0 2.2 %collective-permute-done.4.got_ref = f32[2,1536]{1,0:T(2,128)S(1)} collective-permute-done((f32[2,1536]{1,0:T(2,128)S(1)}, f32[2,1536]{1,0:T(2,128)S(1)}, u32[]{:S(2)}, u32[]{:S(2)}) %collective-permute-start.4) | collective-permute-done | bytes 12320 | tf_op jit(solution)/shard_map/ppermute | solution.py:740
  34.2 2.5 %collective-permute-start.5 = (f32[2,1536]{1,0:T(2,128)S(1)}, f32[2,1536]{1,0:T(2,128)S(1)}, u32[]{:S(2)}, u32[]{:S(2)}) collective-permute-start(f32[2,1536]{1,0:T(2,128)S(1)} %add.20.own_ref), channel_id=1, source_target_pairs={{0,8},{1,9},{2,10},{3,11},{4,12},{5,13},{6,14},{7,15},{8,0},{9,1},... | collective-permute-start | bytes 36872 | tf_op jit(solution)/shard_map/ppermute | solution.py:740
  36.6 1.7 %collective-permute-done.5.got_ref = f32[2,1536]{1,0:T(2,128)S(1)} collective-permute-done((f32[2,1536]{1,0:T(2,128)S(1)}, f32[2,1536]{1,0:T(2,128)S(1)}, u32[]{:S(2)}, u32[]{:S(2)}) %collective-permute-start.5) | collective-permute-done | bytes 12320 | tf_op jit(solution)/shard_map/ppermute | solution.py:740
  38.3 3.0 %collective-permute-start.6 = (f32[2,1536]{1,0:T(2,128)S(1)}, f32[2,1536]{1,0:T(2,128)S(1)}, u32[]{:S(2)}, u32[]{:S(2)}) collective-permute-start(f32[2,1536]{1,0:T(2,128)S(1)} %add.21.rest_0_.own_ref), channel_id=1, source_target_pairs={{0,16},{1,17},{2,18},{3,19},{4,20},{5,21},{6,22},{7,23},{8,24},{9,... | collective-permute-start | bytes 36872 | tf_op jit(solution)/shard_map/ppermute | solution.py:740
  41.4 0.9 act_grad_end.1.rest_0_.end_ref
  42.3 0.7 collective-permute-done.6.got_ref
  43.0 1.7 %middle.1 = (bf16[512,1536]{1,0:T(8,128)(2,1)S(1)}, f32[576,1536]{1,0:T(8,128)S(1)}, f32[2,1536]{1,0:T(2,128)S(1)}) custom-call(f32[576,1536]{1,0:T(8,128)S(1)} %get-tuple-element.50.conv_ref, f32[2,1536]{1,0:T(2,128)S(1)} %add.22.sums_ref, f32[3,1536]{1,0:T(4,128)S(1)} %get-tuple-element.53.vec_ref, f32[512,1536]{1,0:T(8,128)S(1)} %act_grad.1.rest_0_.own_ref, ...), custom_call_target="tpu_custom_call" | custom-call | bytes 9000000 | tf_op jit(solution)/shard_map/middle/pallas_call | solution.py:468
  44.8 0.1 collective-permute-start.12
  44.8 0.5 collective-permute-start.8
  45.3 2.9 %collective-permute-done.8.got_ref = f32[2,1536]{1,0:T(2,128)S(1)} collective-permute-done((f32[2,1536]{1,0:T(2,128)S(1)}, f32[2,1536]{1,0:T(2,128)S(1)}, u32[]{:S(2)}, u32[]{:S(2)}) %collective-permute-start.8) | collective-permute-done | bytes 12320 | tf_op jit(solution)/shard_map/ppermute | solution.py:740
  48.3 1.5 %collective-permute-start.9 = (f32[2,1536]{1,0:T(2,128)S(1)}, f32[2,1536]{1,0:T(2,128)S(1)}, u32[]{:S(2)}, u32[]{:S(2)}) collective-permute-start(f32[2,1536]{1,0:T(2,128)S(1)} %add.23.rest_0_.own_ref), channel_id=1, source_target_pairs={{0,2},{1,3},{2,0},{3,1},{4,6},{5,7},{6,4},{7,5},{8,10},{9,11},{10,... | collective-permute-start | bytes 36872 | tf_op jit(solution)/shard_map/ppermute | solution.py:740
  49.7 3.6 %branch.1 = (bf16[512,1536]{1,0:T(8,128)(2,1)}, f32[8,128]{1,0:T(8,128)S(1)}) custom-call(bf16[512,1536]{1,0:T(8,128)(2,1)S(1)} %bitcast.15, bf16[512,1536]{1,0:T(8,128)(2,1)S(1)} %get-tuple-element.55.act_ref.acta_ref, bf16[1536,1536]{1,0:T(8,128)(2,1)S(1)} %bitcast.7, f32[2,1536]{1,0:T(2,128)S(1)} %add.23.rest_0_.own_ref), custom_call_target="tpu_custom_call" | custom-call | bytes 12000000 | tf_op jit(solution)/shard_map/branch/pallas_call | solution.py:536
  53.3 1.0 collective-permute-start.10
  54.3 2.8 %collective-permute-done.10.got_ref = f32[2,1536]{1,0:T(2,128)S(1)} collective-permute-done((f32[2,1536]{1,0:T(2,128)S(1)}, f32[2,1536]{1,0:T(2,128)S(1)}, u32[]{:S(2)}, u32[]{:S(2)}) %collective-permute-start.10) | collective-permute-done | bytes 12320 | tf_op jit(solution)/shard_map/ppermute | solution.py:740
  57.1 2.6 %grad.1 = (bf16[8,48,768]{2,1,0:T(8,128)(2,1)S(1)}, f32[8,48,768]{2,1,0:T(8,128)S(1)}, bf16[8,48,768]{2,1,0:T(8,128)(2,1)S(1)}, f32[8,48,768]{2,1,0:T(8,128)S(1)}) custom-call(bf16[16,48,512]{2,1,0:T(8,128)(2,1)S(1)} %get-tuple-element.52.rest_0_.ca_ref, bf16[16,48,512]{2,1,0:T(8,128)(2,1)S(1)} %collective-permute-done.7.rest_0_.cb_ref, ...), custom_call_target="tpu_custom_call" | custom-call | bytes 10500000 | tf_op jit(solution)/shard_map/grad/pallas_call | solution.py:507
  59.7 1.0 collective-permute-start.20
  60.7 0.8 collective-permute-start.18
  61.5 1.9 %collective-permute-start.11 = (f32[2,1536]{1,0:T(2,128)S(1)}, f32[2,1536]{1,0:T(2,128)S(1)}, u32[]{:S(2)}, u32[]{:S(2)}) collective-permute-start(f32[2,1536]{1,0:T(2,128)S(1)} %add.25.rest_0_.own_ref), channel_id=1, source_target_pairs={{0,8},{1,9},{2,10},{3,11},{4,12},{5,13},{6,14},{7,15},{8,0},{9,1},... | collective-permute-start | bytes 36872 | tf_op jit(solution)/shard_map/ppermute | solution.py:740
  63.4 1.8 %collective-permute-done.11.got_ref = f32[2,1536]{1,0:T(2,128)S(1)} collective-permute-done((f32[2,1536]{1,0:T(2,128)S(1)}, f32[2,1536]{1,0:T(2,128)S(1)}, u32[]{:S(2)}, u32[]{:S(2)}) %collective-permute-start.11) | collective-permute-done | bytes 12320 | tf_op jit(solution)/shard_map/ppermute | solution.py:740
  65.2 2.9 %collective-permute-start.13 = (f32[2,1536]{1,0:T(2,128)S(1)}, f32[2,1536]{1,0:T(2,128)S(1)}, u32[]{:S(2)}, u32[]{:S(2)}) collective-permute-start(f32[2,1536]{1,0:T(2,128)S(1)} %add.26.own_ref), channel_id=1, source_target_pairs={{0,16},{1,17},{2,18},{3,19},{4,20},{5,21},{6,22},{7,23},{8,24},{9,... | collective-permute-start | bytes 36872 | tf_op jit(solution)/shard_map/ppermute | solution.py:740
  68.1 1.7 %collective-permute-done.13.got_ref = f32[2,1536]{1,0:T(2,128)S(1)} collective-permute-done((f32[2,1536]{1,0:T(2,128)S(1)}, f32[2,1536]{1,0:T(2,128)S(1)}, u32[]{:S(2)}, u32[]{:S(2)}) %collective-permute-start.13) | collective-permute-done | bytes 12320 | tf_op jit(solution)/shard_map/ppermute | solution.py:740
  69.8 6.9 %grad_taps.1 = (bf16[32,1536]{1,0:T(8,128)(2,1)S(1)}, f32[12,2,9,72,128]{4,3,2,1,0:T(8,128)S(1)}) custom-call(f32[576,1536]{1,0:T(8,128)S(1)} %get-tuple-element.60.dbn_ref, f32[576,1536]{1,0:T(8,128)S(1)} %get-tuple-element.50.conv_ref, f32[2,1536]{1,0:T(2,128)S(1)} %add.22.sums_ref, f32[2,1536]{1,0:T(2,128)S(1)} %add.27.dsums_ref.refs_2_, ...), custom_call_target="tpu_custom_call" | custom-call | bytes 27000000 | tf_op jit(solution)/shard_map/grad_taps/pallas_call | solution.py:607
  76.6 0.1 collective-permute-start.14
  76.7 0.1 merge.5
  76.9 1.3 %collective-permute-start.21 = (bf16[4,48,768]{2,1,0:T(8,128)(2,1)S(1)}, bf16[4,48,768]{2,1,0:T(8,128)(2,1)S(1)}, u32[]{:S(2)}, u32[]{:S(2)}) collective-permute-start(bf16[4,48,768]{2,1,0:T(8,128)(2,1)S(1)} %get-tuple-element.78), channel_id=1, source_target_pairs={{0,2},{1,3},{2,0},{3,1},{4,6},{5,7},{6,4},{7,5},{8,10},{9,11},{10,... | collective-permute-start | bytes 884744 | tf_op jit(solution)/shard_map/ppermute | solution.py:740
  78.2 0.1 merge.4
  78.3 1.2 %collective-permute-start.19 = (bf16[4,48,768]{2,1,0:T(8,128)(2,1)S(1)}, bf16[4,48,768]{2,1,0:T(8,128)(2,1)S(1)}, u32[]{:S(2)}, u32[]{:S(2)}) collective-permute-start(bf16[4,48,768]{2,1,0:T(8,128)(2,1)S(1)} %get-tuple-element.74), channel_id=1, source_target_pairs={{0,4},{1,5},{2,6},{3,7},{4,0},{5,1},{6,2},{7,3},{8,12},{9,13},{10,... | collective-permute-start | bytes 884744 | tf_op jit(solution)/shard_map/ppermute | solution.py:740
  79.5 1.6 %collective-permute-start.15 = (bf16[32,1536]{1,0:T(8,128)(2,1)S(1)}, bf16[32,1536]{1,0:T(8,128)(2,1)S(1)}, u32[]{:S(2)}, u32[]{:S(2)}) collective-permute-start(bf16[32,1536]{1,0:T(8,128)(2,1)S(1)} %add.28.rest_0_.own_ref), channel_id=1, source_target_pairs={{0,8},{1,9},{2,10},{3,11},{4,12},{5,13},{6,14},{7,15},{8,0},{9,1},... | collective-permute-start | bytes 294920 | tf_op jit(solution)/shard_map/ppermute | solution.py:740
  81.1 2.7 %grad_proj.2 = (bf16[512,768]{1,0:T(8,128)(2,1)S(1)}, bf16[512,768]{1,0:T(8,128)(2,1)S(1)}) custom-call(f32[12,2,9,72,128]{4,3,2,1,0:T(8,128)S(1)} %get-tuple-element.63.seq_ref, f32[32,1536]{1,0:T(8,128)S(1)} %copy-done.2, bf16[512,1536]{1,0:T(8,128)(2,1)S(1)} %get-tuple-element.64.p_ref, bf16[512,1536]{1,0:T(8,128)(2,1)S(1)} %get-tuple-element.65.q_ref, ...), custom_call_target="tpu_custom_call" | custom-call | bytes 12000000 | tf_op jit(solution)/shard_map/grad_proj/pallas_call | solution.py:655
  83.9 0.3 collective-permute-done.15.got_ref
  84.2 0.0 slice-start.4
  84.2 2.6 %collective-permute-start.16 = (bf16[32,1536]{1,0:T(8,128)(2,1)S(1)}, bf16[32,1536]{1,0:T(8,128)(2,1)S(1)}, u32[]{:S(2)}, u32[]{:S(2)}) collective-permute-start(bf16[32,1536]{1,0:T(8,128)(2,1)S(1)} %add.29.rest_0_.own_ref), channel_id=1, source_target_pairs={{0,16},{1,17},{2,18},{3,19},{4,20},{5,21},{6,22},{7,23},{8,24},{9,... | collective-permute-start | bytes 294920 | tf_op jit(solution)/shard_map/ppermute | solution.py:740
  86.9 3.0 %grad_proj.3 = (bf16[512,768]{1,0:T(8,128)(2,1)S(1)}, bf16[512,768]{1,0:T(8,128)(2,1)S(1)}) custom-call(f32[12,2,9,72,128]{4,3,2,1,0:T(8,128)S(1)} %get-tuple-element.63.seq_ref, f32[32,1536]{1,0:T(8,128)S(1)} %copy-done.2, bf16[512,1536]{1,0:T(8,128)(2,1)S(1)} %get-tuple-element.64.p_ref, bf16[512,1536]{1,0:T(8,128)(2,1)S(1)} %get-tuple-element.65.q_ref, ...), custom_call_target="tpu_custom_call" | custom-call | bytes 12000000 | tf_op jit(solution)/shard_map/grad_proj/pallas_call | solution.py:655
  89.8 1.5 %collective-permute-done.16.got_ref = bf16[32,1536]{1,0:T(8,128)(2,1)S(1)} collective-permute-done((bf16[32,1536]{1,0:T(8,128)(2,1)S(1)}, bf16[32,1536]{1,0:T(8,128)(2,1)S(1)}, u32[]{:S(2)}, u32[]{:S(2)}) %collective-permute-start.16) | collective-permute-done | bytes 98336 | tf_op jit(solution)/shard_map/ppermute | solution.py:740
  91.4 0.1 merge.6
  91.5 0.6 collective-permute-start.22
  92.1 0.9 collective-permute-start.17
  93.0 5.1 %back_proj.1.rest_0_.acc_ref.refs_2_ = f32[512,1536]{1,0:T(8,128)S(1)} custom-call(f32[3,1536]{1,0:T(4,128)S(1)} %get-tuple-element.53.vec_ref, bf16[1536,3072]{1,0:T(8,128)(2,1)S(1)} %bitcast.9, bf16[512,768]{1,0:T(8,128)(2,1)S(1)} %get-tuple-element.67.rest_0_, bf16[512,768]{1,0:T(8,128)(2,1)S(1)} %get-tuple-element.68.rest_0_.rest_1_, ...), custom_call_target="tpu_custom_call" | custom-call | bytes 15000000 | tf_op jit(solution)/shard_map/back_proj/pallas_call | solution.py:689
  98.1 0.6 collective-permute-done.22.refs_1_
  98.7 0.1 merge.7
  98.7 3.4 %collective-permute-start.23 = (bf16[1,48,1536]{2,1,0:T(8,128)(2,1)S(1)}, bf16[1,48,1536]{2,1,0:T(8,128)(2,1)S(1)}, u32[]{:S(2)}, u32[]{:S(2)}) collective-permute-start(bf16[1,48,1536]{2,1,0:T(8,128)(2,1)S(1)} %get-tuple-element.82), channel_id=1, source_target_pairs={{0,16},{1,17},{2,18},{3,19},{4,20},{5,21},{6,22},{7,23},{8,24},{9,... | collective-permute-start | bytes 442376 | tf_op jit(solution)/shard_map/ppermute | solution.py:740
  102.1 0.7 collective-permute-start.24
  102.8 0.6 slice_reduce_fusion
  103.5 2.3 %back_norm.1 = (bf16[512,1536]{1,0:T(8,128)(2,1)}, f32[8,128]{1,0:T(8,128)S(1)}) custom-call(bf16[512,1536]{1,0:T(8,128)(2,1)S(1)} %get-tuple-element.58.hat_ref, f32[512,1]{1,0:T(8,128)S(1)} %get-tuple-element.59.rstd_ref, bf16[512,1536]{1,0:T(8,128)(2,1)S(1)} %bitcast.13, f32[512,1536]{1,0:T(8,128)S(1)} %back_proj.1.rest_0_.acc_ref.refs_2_, ...), custom_call_target="tpu_custom_call" | custom-call | bytes 9000000 | tf_op jit(solution)/shard_map/back_norm/pallas_call | solution.py:726
  105.8 1.0 collective-permute-done.24.got_ref
  106.8 0.7 add.33
  107.5 0.5 collective-permute-done.23
  108.0 0.7 add.32
  (39 shorter events, 0.2 us)
Async XLA Ops:
  0.6 10.4 %slice-start = ((s8[4718592]{0:T(1024)(128)(4,1)}), s8[4194304]{0:T(1024)(128)(4,1)S(1)}, s32[]{:S(2)}) async-start(s8[4718592]{0:T(1024)(128)(4,1)} %bitcast.6), calls=%async_computation | async-start | bytes 8388608
  0.6 10.4 %slice-start.1 = ((s8[4718592]{0:T(1024)(128)(4,1)}), s8[524288]{0:T(1024)(128)(4,1)S(1)}, s32[]{:S(2)}) async-start(s8[4718592]{0:T(1024)(128)(4,1)} %bitcast.6), calls=%async_computation.1 | async-start | bytes 1048576
  0.7 10.4 %copy-start = (bf16[2,256,1536]{2,1,0:T(8,128)(2,1)S(1)}, bf16[2,256,1536]{2,1,0:T(8,128)(2,1)}, u32[]{:S(2)}) copy-start(bf16[2,256,1536]{2,1,0:T(8,128)(2,1)} %param.15) | copy-start | bytes 4718596
  9.7 9.1 %collective-permute-start = (bf16[2,48,1536]{2,1,0:T(8,128)(2,1)S(1)}, bf16[2,48,1536]{2,1,0:T(8,128)(2,1)S(1)}, u32[]{:S(2)}, u32[]{:S(2)}) collective-permute-start(bf16[2,48,1536]{2,1,0:T(8,128)(2,1)S(1)} %get-tuple-element.46), channel_id=1, source_target_pairs={{0,1},{1,0},{2,3},{3,2},{4,5},{5,4},{6,7},{7,6},{8,9},{9,8},{10,11... | collective-permute-start | bytes 884744 | tf_op jit(solution)/shard_map/ppermute | solution.py:740
  10.3 3.4 %copy-start.2 = (f32[32,1536]{1,0:T(8,128)S(1)}, f32[32,1536]{1,0:T(8,128)}, u32[]{:S(2)}) copy-start(f32[32,1536]{1,0:T(8,128)} %k_ref.7) | copy-start | bytes 589828
  10.3 8.6 %collective-permute-start.1 = (bf16[2,48,1536]{2,1,0:T(8,128)(2,1)S(1)}, bf16[2,48,1536]{2,1,0:T(8,128)(2,1)S(1)}, u32[]{:S(2)}, u32[]{:S(2)}) collective-permute-start(bf16[2,48,1536]{2,1,0:T(8,128)(2,1)S(1)} %get-tuple-element.47), channel_id=1, source_target_pairs={{1,2},{2,1},{3,4},{4,3},{5,6},{6,5},{7,8},{8,7},{9,10},{10,9},{11,... | collective-permute-start | bytes 884744 | tf_op jit(solution)/shard_map/ppermute | solution.py:789
  20.9 4.8 %collective-permute-start.2 = (f32[2,1536]{1,0:T(2,128)S(1)}, f32[2,1536]{1,0:T(2,128)S(1)}, u32[]{:S(2)}, u32[]{:S(2)}) collective-permute-start(f32[2,1536]{1,0:T(2,128)S(1)} %get-tuple-element.51.own_ref), channel_id=1, source_target_pairs={{0,1},{1,0},{2,3},{3,2},{4,5},{5,4},{6,7},{7,6},{8,9},{9,8},{10,11... | collective-permute-start | bytes 36872 | tf_op jit(solution)/shard_map/ppermute | solution.py:740
  26.3 16.8 %collective-permute-start.7 = (bf16[16,48,512]{2,1,0:T(8,128)(2,1)S(1)}, bf16[16,48,512]{2,1,0:T(8,128)(2,1)S(1)}, u32[]{:S(2)}, u32[]{:S(2)}) collective-permute-start(bf16[16,48,512]{2,1,0:T(8,128)(2,1)S(1)} %get-tuple-element.54), channel_id=1, source_target_pairs={{0,1},{1,0},{2,3},{3,2},{4,5},{5,4},{6,7},{7,6},{8,9},{9,8},{10,11... | collective-permute-start | bytes 2359304 | tf_op jit(solution)/shard_map/ppermute | solution.py:740
  26.7 3.8 %collective-permute-start.3 = (f32[2,1536]{1,0:T(2,128)S(1)}, f32[2,1536]{1,0:T(2,128)S(1)}, u32[]{:S(2)}, u32[]{:S(2)}) collective-permute-start(f32[2,1536]{1,0:T(2,128)S(1)} %add.18.rest_0_.own_ref), channel_id=1, source_target_pairs={{0,2},{1,3},{2,0},{3,1},{4,6},{5,7},{6,4},{7,5},{8,10},{9,11},{10,... | collective-permute-start | bytes 36872 | tf_op jit(solution)/shard_map/ppermute | solution.py:740
  30.5 3.7 %collective-permute-start.4 = (f32[2,1536]{1,0:T(2,128)S(1)}, f32[2,1536]{1,0:T(2,128)S(1)}, u32[]{:S(2)}, u32[]{:S(2)}) collective-permute-start(f32[2,1536]{1,0:T(2,128)S(1)} %add.19.own_ref), channel_id=1, source_target_pairs={{0,4},{1,5},{2,6},{3,7},{4,0},{5,1},{6,2},{7,3},{8,12},{9,13},{10,... | collective-permute-start | bytes 36872 | tf_op jit(solution)/shard_map/ppermute | solution.py:740
  34.2 4.1 %collective-permute-start.5 = (f32[2,1536]{1,0:T(2,128)S(1)}, f32[2,1536]{1,0:T(2,128)S(1)}, u32[]{:S(2)}, u32[]{:S(2)}) collective-permute-start(f32[2,1536]{1,0:T(2,128)S(1)} %add.20.own_ref), channel_id=1, source_target_pairs={{0,8},{1,9},{2,10},{3,11},{4,12},{5,13},{6,14},{7,15},{8,0},{9,1},... | collective-permute-start | bytes 36872 | tf_op jit(solution)/shard_map/ppermute | solution.py:740
  38.3 4.7 %collective-permute-start.6 = (f32[2,1536]{1,0:T(2,128)S(1)}, f32[2,1536]{1,0:T(2,128)S(1)}, u32[]{:S(2)}, u32[]{:S(2)}) collective-permute-start(f32[2,1536]{1,0:T(2,128)S(1)} %add.21.rest_0_.own_ref), channel_id=1, source_target_pairs={{0,16},{1,17},{2,18},{3,19},{4,20},{5,21},{6,22},{7,23},{8,24},{9,... | collective-permute-start | bytes 36872 | tf_op jit(solution)/shard_map/ppermute | solution.py:740
  43.0 6.7 %copy-start.1 = (bf16[2,256,1536]{2,1,0:T(8,128)(2,1)S(1)}, bf16[2,256,1536]{2,1,0:T(8,128)(2,1)}, u32[]{:S(2)}) copy-start(bf16[2,256,1536]{2,1,0:T(8,128)(2,1)} %param.8) | copy-start | bytes 4718596
  44.8 12.3 %collective-permute-start.12 = (bf16[512,1536]{1,0:T(8,128)(2,1)S(1)}, bf16[512,1536]{1,0:T(8,128)(2,1)S(1)}, u32[]{:S(2)}, u32[]{:S(2)}) collective-permute-start(bf16[512,1536]{1,0:T(8,128)(2,1)S(1)} %get-tuple-element.55.act_ref.acta_ref), channel_id=1, source_target_pairs={{0,1},{1,0},{2,3},{3,2},{4,5},{5,4},{6,7},{7,6},{8,9},{9,8},{10,11... | collective-permute-start | bytes 4718600 | tf_op jit(solution)/shard_map/ppermute | solution.py:740
  44.8 3.4 %collective-permute-start.8 = (f32[2,1536]{1,0:T(2,128)S(1)}, f32[2,1536]{1,0:T(2,128)S(1)}, u32[]{:S(2)}, u32[]{:S(2)}) collective-permute-start(f32[2,1536]{1,0:T(2,128)S(1)} %get-tuple-element.56.own_ref), channel_id=1, source_target_pairs={{0,1},{1,0},{2,3},{3,2},{4,5},{5,4},{6,7},{7,6},{8,9},{9,8},{10,11... | collective-permute-start | bytes 36872 | tf_op jit(solution)/shard_map/ppermute | solution.py:740
  48.3 5.0 %collective-permute-start.9 = (f32[2,1536]{1,0:T(2,128)S(1)}, f32[2,1536]{1,0:T(2,128)S(1)}, u32[]{:S(2)}, u32[]{:S(2)}) collective-permute-start(f32[2,1536]{1,0:T(2,128)S(1)} %add.23.rest_0_.own_ref), channel_id=1, source_target_pairs={{0,2},{1,3},{2,0},{3,1},{4,6},{5,7},{6,4},{7,5},{8,10},{9,11},{10,... | collective-permute-start | bytes 36872 | tf_op jit(solution)/shard_map/ppermute | solution.py:740
  53.3 3.8 %collective-permute-start.10 = (f32[2,1536]{1,0:T(2,128)S(1)}, f32[2,1536]{1,0:T(2,128)S(1)}, u32[]{:S(2)}, u32[]{:S(2)}) collective-permute-start(f32[2,1536]{1,0:T(2,128)S(1)} %add.24.own_ref), channel_id=1, source_target_pairs={{0,4},{1,5},{2,6},{3,7},{4,0},{5,1},{6,2},{7,3},{8,12},{9,13},{10,... | collective-permute-start | bytes 36872 | tf_op jit(solution)/shard_map/ppermute | solution.py:740
  59.7 17.0 %collective-permute-start.20 = (bf16[8,48,768]{2,1,0:T(8,128)(2,1)S(1)}, bf16[8,48,768]{2,1,0:T(8,128)(2,1)S(1)}, u32[]{:S(2)}, u32[]{:S(2)}) collective-permute-start(bf16[8,48,768]{2,1,0:T(8,128)(2,1)S(1)} %get-tuple-element.76), channel_id=1, source_target_pairs={{0,4},{1,5},{2,6},{3,7},{4,0},{5,1},{6,2},{7,3},{8,12},{9,13},{10,... | collective-permute-start | bytes 1769480 | tf_op jit(solution)/shard_map/ppermute | solution.py:740
  60.7 17.5 %collective-permute-start.18 = (bf16[8,48,768]{2,1,0:T(8,128)(2,1)S(1)}, bf16[8,48,768]{2,1,0:T(8,128)(2,1)S(1)}, u32[]{:S(2)}, u32[]{:S(2)}) collective-permute-start(bf16[8,48,768]{2,1,0:T(8,128)(2,1)S(1)} %get-tuple-element.62.rest_0_), channel_id=1, source_target_pairs={{0,2},{1,3},{2,0},{3,1},{4,6},{5,7},{6,4},{7,5},{8,10},{9,11},{10,... | collective-permute-start | bytes 1769480 | tf_op jit(solution)/shard_map/ppermute | solution.py:740
  61.5 3.7 %collective-permute-start.11 = (f32[2,1536]{1,0:T(2,128)S(1)}, f32[2,1536]{1,0:T(2,128)S(1)}, u32[]{:S(2)}, u32[]{:S(2)}) collective-permute-start(f32[2,1536]{1,0:T(2,128)S(1)} %add.25.rest_0_.own_ref), channel_id=1, source_target_pairs={{0,8},{1,9},{2,10},{3,11},{4,12},{5,13},{6,14},{7,15},{8,0},{9,1},... | collective-permute-start | bytes 36872 | tf_op jit(solution)/shard_map/ppermute | solution.py:740
  65.2 4.6 %collective-permute-start.13 = (f32[2,1536]{1,0:T(2,128)S(1)}, f32[2,1536]{1,0:T(2,128)S(1)}, u32[]{:S(2)}, u32[]{:S(2)}) collective-permute-start(f32[2,1536]{1,0:T(2,128)S(1)} %add.26.own_ref), channel_id=1, source_target_pairs={{0,16},{1,17},{2,18},{3,19},{4,20},{5,21},{6,22},{7,23},{8,24},{9,... | collective-permute-start | bytes 36872 | tf_op jit(solution)/shard_map/ppermute | solution.py:740
  76.6 2.8 %collective-permute-start.14 = (bf16[32,1536]{1,0:T(8,128)(2,1)S(1)}, bf16[32,1536]{1,0:T(8,128)(2,1)S(1)}, u32[]{:S(2)}, u32[]{:S(2)}) collective-permute-start(bf16[32,1536]{1,0:T(8,128)(2,1)S(1)} %get-tuple-element.66.own_ref), channel_id=1, source_target_pairs={{0,1},{1,0},{2,3},{3,2},{4,5},{5,4},{6,7},{7,6},{8,9},{9,8},{10,11... | collective-permute-start | bytes 294920 | tf_op jit(solution)/shard_map/ppermute | solution.py:740
  76.9 14.5 %collective-permute-start.21 = (bf16[4,48,768]{2,1,0:T(8,128)(2,1)S(1)}, bf16[4,48,768]{2,1,0:T(8,128)(2,1)S(1)}, u32[]{:S(2)}, u32[]{:S(2)}) collective-permute-start(bf16[4,48,768]{2,1,0:T(8,128)(2,1)S(1)} %get-tuple-element.78), channel_id=1, source_target_pairs={{0,2},{1,3},{2,0},{3,1},{4,6},{5,7},{6,4},{7,5},{8,10},{9,11},{10,... | collective-permute-start | bytes 884744 | tf_op jit(solution)/shard_map/ppermute | solution.py:740
  78.3 13.1 %collective-permute-start.19 = (bf16[4,48,768]{2,1,0:T(8,128)(2,1)S(1)}, bf16[4,48,768]{2,1,0:T(8,128)(2,1)S(1)}, u32[]{:S(2)}, u32[]{:S(2)}) collective-permute-start(bf16[4,48,768]{2,1,0:T(8,128)(2,1)S(1)} %get-tuple-element.74), channel_id=1, source_target_pairs={{0,4},{1,5},{2,6},{3,7},{4,0},{5,1},{6,2},{7,3},{8,12},{9,13},{10,... | collective-permute-start | bytes 884744 | tf_op jit(solution)/shard_map/ppermute | solution.py:740
  79.5 4.7 %collective-permute-start.15 = (bf16[32,1536]{1,0:T(8,128)(2,1)S(1)}, bf16[32,1536]{1,0:T(8,128)(2,1)S(1)}, u32[]{:S(2)}, u32[]{:S(2)}) collective-permute-start(bf16[32,1536]{1,0:T(8,128)(2,1)S(1)} %add.28.rest_0_.own_ref), channel_id=1, source_target_pairs={{0,8},{1,9},{2,10},{3,11},{4,12},{5,13},{6,14},{7,15},{8,0},{9,1},... | collective-permute-start | bytes 294920 | tf_op jit(solution)/shard_map/ppermute | solution.py:740
  81.1 11.9 %slice-start.2 = ((s8[9437184]{0:T(1024)(128)(4,1)}), s8[4194304]{0:T(1024)(128)(4,1)S(1)}, s32[]{:S(2)}) async-start(s8[9437184]{0:T(1024)(128)(4,1)} %bitcast.8), calls=%async_computation.2 | async-start | bytes 8388608
  81.1 11.9 %slice-start.3 = ((s8[9437184]{0:T(1024)(128)(4,1)}), s8[4194304]{0:T(1024)(128)(4,1)S(1)}, s32[]{:S(2)}) async-start(s8[9437184]{0:T(1024)(128)(4,1)} %bitcast.8), calls=%async_computation.3 | async-start | bytes 8388608
  84.2 8.8 %slice-start.4 = ((s8[9437184]{0:T(1024)(128)(4,1)}), s8[1048576]{0:T(1024)(128)(4,1)S(1)}, s32[]{:S(2)}) async-start(s8[9437184]{0:T(1024)(128)(4,1)} %bitcast.8), calls=%async_computation.4 | async-start | bytes 2097152
  84.2 7.1 %collective-permute-start.16 = (bf16[32,1536]{1,0:T(8,128)(2,1)S(1)}, bf16[32,1536]{1,0:T(8,128)(2,1)S(1)}, u32[]{:S(2)}, u32[]{:S(2)}) collective-permute-start(bf16[32,1536]{1,0:T(8,128)(2,1)S(1)} %add.29.rest_0_.own_ref), channel_id=1, source_target_pairs={{0,16},{1,17},{2,18},{3,19},{4,20},{5,21},{6,22},{7,23},{8,24},{9,... | collective-permute-start | bytes 294920 | tf_op jit(solution)/shard_map/ppermute | solution.py:740
  91.5 7.2 %collective-permute-start.22 = (bf16[2,48,1536]{2,1,0:T(8,128)(2,1)S(1)}, bf16[2,48,1536]{2,1,0:T(8,128)(2,1)S(1)}, u32[]{:S(2)}, u32[]{:S(2)}) collective-permute-start(bf16[2,48,1536]{2,1,0:T(8,128)(2,1)S(1)} %get-tuple-element.80), channel_id=1, source_target_pairs={{0,8},{1,9},{2,10},{3,11},{4,12},{5,13},{6,14},{7,15},{8,0},{9,1},... | collective-permute-start | bytes 884744 | tf_op jit(solution)/shard_map/ppermute | solution.py:740
  92.1 10.0 %collective-permute-start.17 = (bf16[32,1536]{1,0:T(8,128)(2,1)S(1)}, bf16[32,1536]{1,0:T(8,128)(2,1)S(1)}, u32[]{:S(2)}, u32[]{:S(2)}) collective-permute-start(bf16[32,1536]{1,0:T(8,128)(2,1)S(1)} %add.30.rest_4_.own_ref.refs_4_), channel_id=1, source_target_pairs={{0,2},{1,3},{2,0},{3,1},{4,6},{5,7},{6,4},{7,5},{8,10},{9,11},{10,... | collective-permute-start | bytes 294920 | tf_op jit(solution)/shard_map/ppermute | solution.py:740
  98.7 9.2 %collective-permute-start.23 = (bf16[1,48,1536]{2,1,0:T(8,128)(2,1)S(1)}, bf16[1,48,1536]{2,1,0:T(8,128)(2,1)S(1)}, u32[]{:S(2)}, u32[]{:S(2)}) collective-permute-start(bf16[1,48,1536]{2,1,0:T(8,128)(2,1)S(1)} %get-tuple-element.82), channel_id=1, source_target_pairs={{0,16},{1,17},{2,18},{3,19},{4,20},{5,21},{6,22},{7,23},{8,24},{9,... | collective-permute-start | bytes 442376 | tf_op jit(solution)/shard_map/ppermute | solution.py:740
  102.1 4.7 %collective-permute-start.24 = (bf16[32,1536]{1,0:T(8,128)(2,1)S(1)}, bf16[32,1536]{1,0:T(8,128)(2,1)S(1)}, u32[]{:S(2)}, u32[]{:S(2)}) collective-permute-start(bf16[32,1536]{1,0:T(8,128)(2,1)S(1)} %add.31.rest_0_.own_ref), channel_id=1, source_target_pairs={{0,4},{1,5},{2,6},{3,7},{4,0},{5,1},{6,2},{7,3},{8,12},{9,13},{10,... | collective-permute-start | bytes 294920 | tf_op jit(solution)/shard_map/ppermute | solution.py:740

commit v5 on v4

--- a/solution.py
+++ b/solution.py
@@ -384,22 +384,24 @@
     )(gated, a, b, kernel, conv_some, sums_some, *after)
 
 
-def act_grad_body(cot_ref, w_ref, out_ref):
+def act_grad_body(start, cot_ref, w_ref, *rest):
+    out_ref = rest[-1]
     for j in range(out_ref.shape[1] // CW):
         cols = slice(j * CW, (j + 1) * CW)
-        out_ref[:, cols] = jnp.dot(cot_ref[...], w_ref[:, cols], preferred_element_type=F32)
-
-
-def act_grad(cot, w_out):
-    return pl.pallas_call(
-        act_grad_body,
-        in_specs=[WHOLE] * 2,
+        source = slice(start + j * CW, start + (j + 1) * CW)
+        out_ref[:, cols] = jnp.dot(cot_ref[...], w_ref[:, source], preferred_element_type=F32)
+
+
+def act_grad(start, width, cot, w_out, after):
+    return pl.pallas_call(
+        functools.partial(act_grad_body, start),
+        in_specs=[WHOLE] * 2 + [ANYWHERE] * len(after),
         out_specs=WHOLE,
-        out_shape=near(cot.shape, F32),
-        compiler_params=params(VMEM_MIB),
-        cost_estimate=cost(3),
+        out_shape=near((cot.shape[0], width), F32),
+        compiler_params=params(VMEM_MIB),
+        cost_estimate=cost(1.5),
         name="act_grad",
-    )(cot, w_out)
+    )(cot, w_out, *after)
 
 
 def act_grad_end_body(a_ref, b_ref, w_ref, *rest):
@@ -427,12 +429,15 @@
     )(a, b, w_out, *after)
 
 
-def middle_body(utt, total, conv_ref, sums_ref, vec_ref, own_ref, end_ref, *rest):
+def middle_body(utt, total, conv_ref, sums_ref, vec_ref, left_ref, right_ref, end_ref, *rest):
     act_ref, dbn_ref, dsums_ref = rest[-3:]
     d = conv_ref.shape[1]
-    frames = own_ref.shape[0] // utt
+    frames = left_ref.shape[0] // utt
+    per_half = left_ref.shape[1] // CW
     for j in range(d // CW):
         cols = slice(j * CW, (j + 1) * CW)
+        own_ref = (left_ref, right_ref)[j // per_half]
+        own_cols = slice(j % per_half * CW, (j % per_half + 1) * CW)
         mean = sums_ref[0:1, cols] * (1.0 / total)
         var = sums_ref[1:2, cols] * (1.0 / total) - mean * mean
         rstd = lax.rsqrt(var + EPSILON)
@@ -451,7 +456,7 @@
             start = u * (frames + HALO)
             back(slice(start, start + PAD), end_ref[u * HALO : u * HALO + PAD, cols])
             rows = slice(u * frames, (u + 1) * frames)
-            xhat, act, dbn = back(slice(start + PAD, start + PAD + frames), own_ref[rows, cols])
+            xhat, act, dbn = back(slice(start + PAD, start + PAD + frames), own_ref[rows, own_cols])
             act_ref[rows, cols] = act.astype(BF)
             bias += jnp.sum(dbn, axis=0, keepdims=True)
             gain += jnp.sum(dbn * xhat, axis=0, keepdims=True)
@@ -463,17 +468,18 @@
         dsums_ref[1:2, cols] = gain
 
 
-def middle(utt, total, conv_out, sums, vec, own, end, after):
-    rows, d = own.shape
+def middle(utt, total, conv_out, sums, vec, left, right, end, after):
+    rows = left.shape[0]
+    d = conv_out.shape[1]
     return pl.pallas_call(
         functools.partial(middle_body, utt, total),
-        in_specs=[WHOLE] * 5 + [ANYWHERE] * len(after),
+        in_specs=[WHOLE] * 6 + [ANYWHERE] * len(after),
         out_specs=[WHOLE] * 3,
         out_shape=[shape((rows, d), BF), near(conv_out.shape, F32), shape((2, d), F32)],
         compiler_params=params(VMEM_MIB),
         cost_estimate=cost(3),
         name="middle",
-    )(conv_out, sums, vec, own, end, *after)
+    )(conv_out, sums, vec, left, right, end, *after)
 
 
 def grad_body(bits, ca_ref, cb_ref, acta_ref, actb_ref, *rest):
@@ -515,39 +521,41 @@
     )(cot_a, cot_b, act_a, act_b, *after)
 
 
-def branch_body(x_ref, act_ref, w_ref, *rest):
+def branch_body(start, x_ref, act_ref, w_ref, *rest):
     out_hbm, done_ref, out_ref, sem = rest[-4:]
     done_ref[...] = jnp.zeros(done_ref.shape, F32)
     copies = []
-    for j in range(out_ref.shape[-1] // CW):
-        cols = slice(j * CW, (j + 1) * CW)
+    for j in range(sem.shape[0]):
+        cols = slice(start + j * CW, start + (j + 1) * CW)
+        here = slice(j * CW, (j + 1) * CW)
         part = lax.dot_general(
             act_ref[...], w_ref[cols, :], (((1,), (1,)), ((), ())), preferred_element_type=F32
         )
-        out_ref[:, cols] = (x_ref[:, cols].astype(F32) + part).astype(BF)
-        copies.append(pltpu.make_async_copy(out_ref.at[:, cols], out_hbm.at[:, cols], sem.at[j]))
+        out_ref[:, here] = (x_ref[:, cols].astype(F32) + part).astype(BF)
+        copies.append(pltpu.make_async_copy(out_ref.at[:, here], out_hbm.at[:, cols], sem.at[j]))
         copies[-1].start()
     for copy in copies:
         copy.wait()
 
 
-def branch(x, act, w_out, after):
+def branch(start, width, x, act, w_out, some, after):
     rows, d = x.shape
     return pl.pallas_call(
-        branch_body,
-        in_specs=[WHOLE] * 3 + [ANYWHERE] * len(after),
+        functools.partial(branch_body, start),
+        in_specs=[WHOLE] * 3 + [FAR] * len(some) + [ANYWHERE] * len(after),
         out_specs=[FAR, WHOLE],
         out_shape=[pltpu.HBM((rows, d), BF), near((8, LANES), F32)],
-        scratch_shapes=[pltpu.VMEM((rows, d), BF), pltpu.SemaphoreType.DMA((d // CW,))],
-        compiler_params=params(VMEM_MIB),
-        cost_estimate=cost(4),
+        scratch_shapes=[pltpu.VMEM((rows, width), BF), pltpu.SemaphoreType.DMA((width // CW,))],
+        input_output_aliases={3: 0} if some else {},
+        compiler_params=params(VMEM_MIB),
+        cost_estimate=cost(2),
         name="branch",
-    )(x, act, w_out, *after)
+    )(x, act, w_out, *some, *after)
 
 
 def grad_taps_body(
     utt, total, dbn_ref, conv_ref, sums_ref, dsums_ref, vec_ref, g_ref,
-    dk_ref, seq_ref, pad_ref, held_ref, acc_ref,
+    dk_ref, seq_ref, bias_ref, gain_ref, pad_ref, held_ref, acc_ref,
 ):
     d = g_ref.shape[1]
     frames = g_ref.shape[0] // utt
@@ -555,6 +563,8 @@
     taps = dk_ref.shape[0]
     per = taps // PHASES
     _, _, keep_lo, keep_hi = place()
+    bias_ref[...] = dsums_ref[0:1, :].reshape(d)
+    gain_ref[...] = dsums_ref[1:2, :].reshape(d)
 
     def work(group, lanes, slot):
         mean = sums_ref[0:1, lanes] * (1.0 / total)
@@ -607,10 +617,12 @@
     return pl.pallas_call(
         functools.partial(grad_taps_body, utt, total),
         in_specs=[WHOLE] * 6,
-        out_specs=[WHOLE] * 2,
+        out_specs=[WHOLE] * 4,
         out_shape=[
             shape((taps, d), BF),
             near((d // LANES, utt, PIECES, long, LANES), F32),
+            shape((d,), F32),
+            shape((d,), F32),
         ],
         scratch_shapes=[
             pltpu.VMEM((2, utt, frames + 2 * PAD + 8, LANES), F32),
@@ -667,37 +679,35 @@
     )(seqs, kernel, p, q, *after)
 
 
-def back_proj_body(vec_ref, w_ref, *rest):
+def back_proj_body(start, vec_ref, w_ref, *rest):
     pieces = rest[:4]
     out_ref = rest[-1]
-    rows, d = out_ref.shape
     wide = pieces[0].shape[1]
     dims = (((1,), (1,)), ((), ()))
-    for j in range(d // CW):
-        cols = slice(j * CW, (j + 1) * CW)
+    for j in range(out_ref.shape[1] // CW):
+        cols = slice(start + j * CW, start + (j + 1) * CW)
         part = 0.0
         for k, piece in enumerate(pieces):
             part += lax.dot_general(
                 piece[...], w_ref[cols, k * wide : (k + 1) * wide], dims, preferred_element_type=F32
             )
-        out_ref[:, cols] = part * vec_ref[0:1, cols]
-
-
-def back_proj(vec, w_in, pieces, after):
+        out_ref[:, j * CW : (j + 1) * CW] = part * vec_ref[0:1, cols]
+
+
+def back_proj(start, width, vec, w_in, pieces, after):
     rows = pieces[0].shape[0]
-    d = w_in.shape[0]
-    return pl.pallas_call(
-        back_proj_body,
+    return pl.pallas_call(
+        functools.partial(back_proj_body, start),
         in_specs=[WHOLE] * 6 + [ANYWHERE] * len(after),
         out_specs=WHOLE,
-        out_shape=near((rows, d), F32),
-        compiler_params=params(VMEM_MIB),
-        cost_estimate=cost(5),
+        out_shape=near((rows, width), F32),
+        compiler_params=params(VMEM_MIB),
+        cost_estimate=cost(2.6),
         name="back_proj",
     )(vec, w_in, *pieces, *after)
 
 
-def back_norm_body(hat_ref, rstd_ref, cot_ref, acc_ref, *rest):
+def back_norm_body(hat_ref, rstd_ref, cot_ref, left_ref, right_ref, *rest):
     out_hbm, done_ref, out_ref, sem = rest[-4:]
     done_ref[...] = jnp.zeros(done_ref.shape, F32)
     copies = []
@@ -705,12 +715,14 @@
     span = rows // sem.shape[0]
     for i in range(0, rows, 16):
         at = slice(i, i + 16)
-        hat = hat_ref[at, :].astype(F32)
-        grads = acc_ref[at, :]
-        m1 = jnp.sum(grads, axis=-1, keepdims=True) * (1.0 / d)
-        m2 = jnp.sum(grads * hat, axis=-1, keepdims=True) * (1.0 / d)
-        layer = rstd_ref[at, :] * (grads - m1 - hat * m2)
-        out_ref[at, :] = (cot_ref[at, :].astype(F32) + layer).astype(BF)
+        hats = [hat_ref[at, : d // 2].astype(F32), hat_ref[at, d // 2 :].astype(F32)]
+        grads = [left_ref[at, :], right_ref[at, :]]
+        m1 = sum(jnp.sum(g, axis=-1, keepdims=True) for g in grads) * (1.0 / d)
+        m2 = sum(jnp.sum(g * h, axis=-1, keepdims=True) for g, h in zip(grads, hats)) * (1.0 / d)
+        rstd = rstd_ref[at, :]
+        for k, cols in enumerate((slice(0, d // 2), slice(d // 2, d))):
+            layer = rstd * (grads[k] - m1 - hats[k] * m2)
+            out_ref[at, cols] = (cot_ref[at, cols].astype(F32) + layer).astype(BF)
         if (i + 16) % span == 0:
             piece = pl.ds(i + 16 - span, span)
             copies.append(
@@ -721,18 +733,18 @@
         copy.wait()
 
 
-def back_norm(hat, rstd, cot, grads, after):
+def back_norm(hat, rstd, cot, left, right, after):
     rows, d = hat.shape
     return pl.pallas_call(
         back_norm_body,
-        in_specs=[WHOLE] * 4 + [ANYWHERE] * len(after),
+        in_specs=[WHOLE] * 5 + [ANYWHERE] * len(after),
         out_specs=[FAR, WHOLE],
         out_shape=[pltpu.HBM((rows, d), BF), near((8, LANES), F32)],
         scratch_shapes=[pltpu.VMEM((rows, d), BF), pltpu.SemaphoreType.DMA((8,))],
         compiler_params=params(VMEM_MIB),
         cost_estimate=cost(3),
         name="back_norm",
-    )(hat, rstd, cot, grads, *after)
+    )(hat, rstd, cot, left, right, *after)
 
 
 def swap(block, axis, bit):
@@ -761,18 +773,38 @@
     )(own, got, *after)
 
 
-def all_sum(block, axis, fill=(), far_first=False):
+def last_add_body(a_ref, b_ref, c_ref, d_ref, *rest):
+    one_ref, two_ref = rest[-2:]
+    one_ref[...] = a_ref[...].astype(F32) + b_ref[...].astype(F32)
+    two_ref[...] = c_ref[...].astype(F32) + d_ref[...].astype(F32)
+
+
+def last_add(one, two, after):
+    return pl.pallas_call(
+        last_add_body,
+        in_specs=[WHOLE] * 4 + [ANYWHERE] * len(after),
+        out_specs=[WHOLE] * 2,
+        out_shape=[shape(one[0].shape, F32), shape(two[0].shape, F32)],
+        compiler_params=params(4),
+        cost_estimate=cost(0.7),
+        name="last_add",
+    )(*one, *two, *after)
+
+
+def all_sum(block, axis, fill=(), order=None, whole=True):
     count = lax.axis_size(axis)
     if not is_power(count):
         for work in fill:
             work([])
         return lax.psum(block.astype(F32), axis)
     bits = [1 << i for i in range(count.bit_length() - 1)]
-    if far_first:
-        bits = bits[:1] + bits[3:] + bits[1:3]
+    if order is not None:
+        bits = order(bits)
     for step, bit in enumerate(bits):
         other = swap(block, axis, bit)
         after = fill[step]([block]) if step < len(fill) else []
+        if bit == bits[-1] and not whole:
+            return (block, other), after
         block = add(block, other, F32 if bit == bits[-1] else block.dtype, after)
     return block
 
@@ -833,13 +865,14 @@
     ]
     bit = 8
     if bit == count:
-        return jnp.concatenate([keep + got for keep, got in pairs], axis=-1)[0]
+        both = [jnp.concatenate(side, axis=-1)[0] for side in zip(*pairs)]
+        return both[0], both[1]
     while True:
         keep, send = merge(pairs, after.pop(0) if after else [])
         got = swap(send, axis, bit)
         bit *= 2
         if bit == count:
-            return add(keep[0], got[0], F32, [])
+            return keep[0], got[0]
         pairs = [(keep, got)]
 
 
@@ -858,79 +891,96 @@
     gated, p, q, hat, rstd, vec, ga, gb = front(utt, x, ln_gain, bn_gain, bn_bias, w_in, cot)
     ga, gb = beside(ga, gb, axis)
     conv_some, sums_some = conv_mid(utt, gated, kernel)
-    own = act_grad(cot, w_out)
-    conv_out, sums = conv_end(utt, gated, ga, gb, kernel, conv_some, sums_some, [own])
+    conv_out, sums = conv_end(utt, gated, ga, gb, kernel, conv_some, sums_some, [])
     made = {}
-
-    def turning(after):
-        made["a"], other = turn(n, cot, after)
-        made["b"] = swap(other, axis, 1)
-        return [made["a"]]
+    half = d // 2
+
+    def act_grading(start):
+        def work(after):
+            made["d_act", start] = act_grad(start, half, cot, w_out, after)
+            return [made["d_act", start]]
+
+        return work
 
     def ending(after):
-        made["end"] = act_grad_end(ga, gb, w_out, after)
-        return [made["end"]]
-
+        made["d_act_end"] = act_grad_end(ga, gb, w_out, after)
+        if not by_owner:
+            return [made["d_act_end"]]
+        made["cot"], other = turn(n, cot, after)
+        made["cot_beside"] = swap(other, axis, 1)
+        return [made["d_act_end"], made["cot"]]
+
+    sums = all_sum(sums, axis, [nothing, act_grading(0), act_grading(half), nothing, ending])
+    act, dbn, dsums = middle(
+        utt, total, conv_out, sums, vec, made["d_act", 0], made["d_act", half], made["d_act_end"], []
+    )
+
+    def branching(start):
+        def work(after):
+            some = [made["outputs"]] if start else []
+            made["outputs"], done = branch(start, half, x, act, w_out, some, after)
+            return [done]
+
+        return work
+
+    def grading(after):
+        if not by_owner:
+            return []
+        act_b = swap(act, axis, 1)
+        made["grad"] = grad((1, 2), made["cot"], made["cot_beside"], act, act_b, after)
+        return [made["grad"][0]]
+
+    dsums = all_sum(
+        dsums, axis, [branching(0), branching(half), grading], lambda bits: bits[1:] + bits[:1]
+    )
     if by_owner:
-        sums = all_sum(sums, axis, [nothing, turning, nothing, nothing, ending])
-        waits = [made["b"]]
-    else:
-        sums = all_sum(sums, axis, [nothing, ending])
-        waits = []
-
-    act, dbn, dsums = middle(utt, total, conv_out, sums, vec, own, made["end"], waits)
-
-    def branching(after):
-        made["outputs"], done = branch(x, act, w_out, after)
-        return [done]
-
-    def grading(after):
-        made["grad"] = grad((1, 2), made["a"], made["b"], act, act_b, after)
-        return [made["grad"][0]]
-
-    if by_owner:
-        act_b = swap(act, axis, 1)
-        dsums = all_sum(dsums, axis, [nothing, branching, nothing, grading])
         send_l, keep_l, send_r, keep_r = made["grad"]
         held = first_swaps([(keep_l, send_l), (keep_r, send_r)], axis, [dsums])
     else:
-        dsums = all_sum(dsums, axis, [nothing, branching])
         dw = lax.dot_general(cot, act, (((0,), (0,)), ((), ())), preferred_element_type=F32)
         d_w_out = lax.psum_scatter(dw, axis, scatter_dimension=0, tiled=True)
 
-    d_kernel, d_conv = grad_taps(
+    d_kernel, d_conv, d_bn_bias, d_bn_gain = grad_taps(
         utt, total, kernel.shape[0], dbn, conv_out, sums, dsums, vec, gated
     )
-    half = d // 2
-
-    def projecting(start):
+
+    def projecting(after):
+        for start in (0, half):
+            made[start] = grad_proj(utt, start, half, d_conv, kernel, p, q, after)
+        return [made[0][0], made[half][0]]
+
+    def back_projecting(start):
         def work(after):
-            made[start] = grad_proj(utt, start, half, d_conv, kernel, p, q, after)
-            return [made[start][0]]
+            left, right = made[0], made[half]
+            pieces = (left[0], right[0], left[1], right[1])
+            made["far"] = after
+            made["grads", start] = back_proj(start, half, vec, w_in, pieces, after)
+            return [made["grads", start]]
 
         return work
 
-    def back_projecting(after):
-        left, right = made[0], made[half]
-        made["far"] = after
-        made["grads"] = back_proj(vec, w_in, (left[0], right[0], left[1], right[1]), after)
-        return [made["grads"]]
-
     def norming(after):
-        made["d_inputs"], done = back_norm(hat, rstd, cot, made["grads"], after)
+        made["d_inputs"], done = back_norm(
+            hat, rstd, cot, made["grads", 0], made["grads", half], after
+        )
         return [done]
 
-    d_kernel_sum = all_sum(
+    terms = all_sum(
         d_kernel,
         axis,
-        [nothing, projecting(0), projecting(half), back_projecting, norming],
-        far_first=True,
+        [nothing, projecting, back_projecting(0), back_projecting(half), norming],
+        lambda bits: bits[:1] + bits[:2:-1] + bits[1:3],
+        whole=not by_owner,
     )
     if by_owner:
-        d_w_out = last_swaps(held, axis, [made["far"], [made["grads"]]])
+        terms, after = terms
+        own = last_swaps(held, axis, [made["far"], [made["grads", half]]])
+        d_w_out, d_kernel_sum = last_add(own, terms, after)
+    else:
+        d_kernel_sum = terms
     return (
         made["outputs"].reshape(inputs.shape), made["d_inputs"].reshape(inputs.shape), d_w_out,
-        d_kernel_sum, dsums[1], dsums[0],
+        d_kernel_sum, d_bn_gain, d_bn_bias,
     )
 
 

time: 109 us -> 105 us (0.963)
  waiting for transfers between devices: 20.2 us -> 13.4 us
  starting transfers between devices: 36.8 us -> 40.5 us
    ppermute x24, waiting for transfers between devices: 20.2 us -> 13.4 us  [swap(): return lax.ppermute(block, axis, [(i, i ^ bit) for i in range(count)])]
    ppermute x24, starting transfers between devices: 36 us -> 39.7 us  [swap(): return lax.ppermute(block, axis, [(i, i ^ bit) for i in range(count)])]
    pallas_call x4 -> x8, Pallas kernels: 13.5 us -> 15.6 us  [the longest x2 5.28 us: back_proj(): pl.pallas_call(functools.partial(back_proj_body, start), in_specs=[WHOLE]...]
    pallas_call x16 -> x14, Pallas kernels: 1.58 us -> 0.14 us  [add(): pl.pallas_call(add_body, in_specs=[WHOLE] * 2 + [ANYWHERE] * len(after),...]
  transfers between devices with their start and end apart: 25 -> 25, of which waited for: 14 -> 13; matrix products, arithmetic and copies ran while one was open for 1% -> 0% of each run, Pallas kernels for 31% -> 33%
where the time goes in v5:
time: 105 us
  Pallas kernels  50.4 us (48%)
  starting transfers between devices  40.5 us (39%)
  waiting for transfers between devices  13.4 us (13%)
    ppermute x24, starting transfers between devices, swap(): return lax.ppermute(block, axis, [(i, i ^ bit) for i in range(count)])  39.7 us
    ppermute x24, waiting for transfers between devices, swap(): return lax.ppermute(block, axis, [(i, i ^ bit) for i in range(count)])  13.4 us
    pallas_call x1, Pallas kernels, front(): pl.pallas_call(functools.partial(front_body, utt), in_specs=[FAR] * 6, ou...  8.77 us
    pallas_call x1, Pallas kernels, grad_taps(): pl.pallas_call(functools.partial(grad_taps_body, utt, total), in_specs=[W...  7.11 us
    pallas_call x2, Pallas kernels, grad_proj(): pl.pallas_call(functools.partial(grad_proj_body, utt, start), in_specs=[W...  5.49 us
    pallas_call x2, Pallas kernels, back_proj(): pl.pallas_call(functools.partial(back_proj_body, start), in_specs=[WHOLE]...  5.28 us
    pallas_call x1, Pallas kernels, conv_mid(): pl.pallas_call(functools.partial(conv_mid_body, utt), in_specs=[WHOLE] *...  4.97 us
    pallas_call x2, Pallas kernels, branch(): pl.pallas_call(functools.partial(branch_body, start), in_specs=[WHOLE] *...  4.47 us
  transfers between devices with their start and end apart: 25, of which 13 were waited for; matrix products, arithmetic and copies ran while one was open for 0% of the time, Pallas kernels for 33%

profile of v5, /device:TPU:0, one launch (start us, length us, event | category | flops | bytes accessed | tf_op | source)
XLA Modules:
  0.0 105.3 jit_solution(11594086893549896933)
XLA Ops:
  0.6 8.8 %front.1 = (bf16[512,1536]{1,0:T(8,128)(2,1)S(1)}, bf16[512,1536]{1,0:T(8,128)(2,1)S(1)}, bf16[512,1536]{1,0:T(8,128)(2,1)S(1)}, bf16[512,1536]{1,0:T(8,128)(2,1...) custom-call(bf16[512,1536]{1,0:T(8,128)(2,1)} %bitcast.13, ...), custom_call_target="tpu_custom_call" | custom-call | bytes 30000000 | tf_op jit(solution)/shard_map/front/pallas_call | solution.py:189
  9.4 0.5 collective-permute-start
  9.9 0.8 collective-permute-start.1
  10.8 0.0 copy-start.1
  10.8 5.0 %conv_mid.1 = (f32[576,1536]{1,0:T(8,128)S(1)}, f32[2,1536]{1,0:T(2,128)S(1)}) custom-call(bf16[512,1536]{1,0:T(8,128)(2,1)S(1)} %get-tuple-element.51.g_ref, f32[32,1536]{1,0:T(8,128)S(1)} %copy-done.3), custom_call_target="tpu_custom_call" | custom-call | bytes 15000000 | tf_op jit(solution)/shard_map/conv_mid/pallas_call | solution.py:327
  15.8 0.0 collective-permute-done.a_ref
  15.8 0.0 collective-permute-done.1.b_ref
  15.8 0.0 copy-start
  15.8 2.0 %conv_end.1 = (f32[576,1536]{1,0:T(8,128)S(1)}, f32[2,1536]{1,0:T(2,128)S(1)}) custom-call(bf16[512,1536]{1,0:T(8,128)(2,1)S(1)} %get-tuple-element.51.g_ref, bf16[2,48,1536]{2,1,0:T(8,128)(2,1)S(1)} %collective-permute-done.a_ref, bf16[2,48,1536]{2,1,0:T(8,128)(2,1)S(1)} %collective-permute-done.1.b_ref, ...), custom_call_target="tpu_custom_call", output_to_operand_aliasing={{0}: (4, {})} | custom-call | bytes 6000000 | tf_op jit(solution)/shard_map/conv_end/pallas_call | solution.py:374
  17.8 5.5 %collective-permute-start.2 = (f32[2,1536]{1,0:T(2,128)S(1)}, f32[2,1536]{1,0:T(2,128)S(1)}, u32[]{:S(2)}, u32[]{:S(2)}) collective-permute-start(f32[2,1536]{1,0:T(2,128)S(1)} %get-tuple-element.57.own_ref), channel_id=1, source_target_pairs={{0,1},{1,0},{2,3},{3,2},{4,5},{5,4},{6,7},{7,6},{8,9},{9,8},{10,11... | collective-permute-start | bytes 36872 | tf_op jit(solution)/shard_map/ppermute | solution.py:752
  23.3 0.8 collective-permute-done.2.got_ref
  24.2 3.1 %collective-permute-start.3 = (f32[2,1536]{1,0:T(2,128)S(1)}, f32[2,1536]{1,0:T(2,128)S(1)}, u32[]{:S(2)}, u32[]{:S(2)}) collective-permute-start(f32[2,1536]{1,0:T(2,128)S(1)} %add.14.rest_0_.own_ref), channel_id=1, source_target_pairs={{0,2},{1,3},{2,0},{3,1},{4,6},{5,7},{6,4},{7,5},{8,10},{9,11},{10,... | collective-permute-start | bytes 36872 | tf_op jit(solution)/shard_map/ppermute | solution.py:752
  27.3 1.4 %act_grad.2.rest_0_.left_ref = f32[512,768]{1,0:T(8,128)S(1)} custom-call(bf16[512,1536]{1,0:T(8,128)(2,1)S(1)} %bitcast.9, bf16[1536,1536]{1,0:T(8,128)(2,1)S(1)} %copy-done, f32[2,1536]{1,0:T(2,128)S(1)} %add.14.rest_0_.own_ref), custom_call_target="tpu_custom_call" | custom-call | bytes 4500000 | tf_op jit(solution)/shard_map/act_grad/pallas_call | solution.py:396
  28.7 0.3 collective-permute-done.3.got_ref
  29.0 1.6 %collective-permute-start.4 = (f32[2,1536]{1,0:T(2,128)S(1)}, f32[2,1536]{1,0:T(2,128)S(1)}, u32[]{:S(2)}, u32[]{:S(2)}) collective-permute-start(f32[2,1536]{1,0:T(2,128)S(1)} %add.15.rest_0_.own_ref), channel_id=1, source_target_pairs={{0,4},{1,5},{2,6},{3,7},{4,0},{5,1},{6,2},{7,3},{8,12},{9,13},{10,... | collective-permute-start | bytes 36872 | tf_op jit(solution)/shard_map/ppermute | solution.py:752
  30.6 1.4 %act_grad.3.rest_0_.right_ref = f32[512,768]{1,0:T(8,128)S(1)} custom-call(bf16[512,1536]{1,0:T(8,128)(2,1)S(1)} %bitcast.10, bf16[1536,1536]{1,0:T(8,128)(2,1)S(1)} %copy-done, f32[2,1536]{1,0:T(2,128)S(1)} %add.15.rest_0_.own_ref), custom_call_target="tpu_custom_call" | custom-call | bytes 4500000 | tf_op jit(solution)/shard_map/act_grad/pallas_call | solution.py:396
  32.0 0.7 collective-permute-done.4.got_ref
  32.7 1.8 %collective-permute-start.5 = (f32[2,1536]{1,0:T(2,128)S(1)}, f32[2,1536]{1,0:T(2,128)S(1)}, u32[]{:S(2)}, u32[]{:S(2)}) collective-permute-start(f32[2,1536]{1,0:T(2,128)S(1)} %add.16.own_ref), channel_id=1, source_target_pairs={{0,8},{1,9},{2,10},{3,11},{4,12},{5,13},{6,14},{7,15},{8,0},{9,1},... | collective-permute-start | bytes 36872 | tf_op jit(solution)/shard_map/ppermute | solution.py:752
  34.5 1.9 %collective-permute-done.5.got_ref = f32[2,1536]{1,0:T(2,128)S(1)} collective-permute-done((f32[2,1536]{1,0:T(2,128)S(1)}, f32[2,1536]{1,0:T(2,128)S(1)}, u32[]{:S(2)}, u32[]{:S(2)}) %collective-permute-start.5) | collective-permute-done | bytes 12320 | tf_op jit(solution)/shard_map/ppermute | solution.py:752
  36.4 2.9 %collective-permute-start.6 = (f32[2,1536]{1,0:T(2,128)S(1)}, f32[2,1536]{1,0:T(2,128)S(1)}, u32[]{:S(2)}, u32[]{:S(2)}) collective-permute-start(f32[2,1536]{1,0:T(2,128)S(1)} %add.17.rest_0_.own_ref), channel_id=1, source_target_pairs={{0,16},{1,17},{2,18},{3,19},{4,20},{5,21},{6,22},{7,23},{8,24},{9,... | collective-permute-start | bytes 36872 | tf_op jit(solution)/shard_map/ppermute | solution.py:752
  39.3 0.6 turn.1
  39.9 0.9 act_grad_end.1.rest_0_.end_ref
  40.8 0.2 collective-permute-done.6.got_ref
  41.0 1.7 %middle.1 = (bf16[512,1536]{1,0:T(8,128)(2,1)S(1)}, f32[576,1536]{1,0:T(8,128)S(1)}, f32[2,1536]{1,0:T(2,128)S(1)}) custom-call(f32[576,1536]{1,0:T(8,128)S(1)} %get-tuple-element.56.conv_ref, f32[2,1536]{1,0:T(2,128)S(1)} %add.18.sums_ref, f32[3,1536]{1,0:T(4,128)S(1)} %get-tuple-element.59.vec_ref, f32[512,768]{1,0:T(8,128)S(1)} %act_grad.2.rest_0_.left_ref, ...), custom_call_target="tpu_custom_call" | custom-call | bytes 9000000 | tf_op jit(solution)/shard_map/middle/pallas_call | solution.py:474
  42.7 0.1 collective-permute-start.11
  42.8 0.5 collective-permute-start.10
  43.3 2.0 %collective-permute-start.7 = (f32[2,1536]{1,0:T(2,128)S(1)}, f32[2,1536]{1,0:T(2,128)S(1)}, u32[]{:S(2)}, u32[]{:S(2)}) collective-permute-start(f32[2,1536]{1,0:T(2,128)S(1)} %get-tuple-element.61.rest_0_.own_ref), channel_id=1, source_target_pairs={{0,2},{1,3},{2,0},{3,1},{4,6},{5,7},{6,4},{7,5},{8,10},{9,11},{10,... | collective-permute-start | bytes 36872 | tf_op jit(solution)/shard_map/ppermute | solution.py:752
  45.3 2.2 %branch.2 = (bf16[512,1536]{1,0:T(8,128)(2,1)}, f32[8,128]{1,0:T(8,128)S(1)}) custom-call(bf16[512,1536]{1,0:T(8,128)(2,1)S(1)} %bitcast.14, bf16[512,1536]{1,0:T(8,128)(2,1)S(1)} %get-tuple-element.60.act_ref.acta_ref, bf16[1536,1536]{1,0:T(8,128)(2,1)S(1)} %copy-done, f32[2,1536]{1,0:T(2,128)S(1)} %get-tuple-element.61.rest_0_.own_ref), custom_call_target="tpu_custom_call" | custom-call | bytes 6000000 | tf_op jit(solution)/shard_map/branch/pallas_call | solution.py:543
  47.6 1.3 %collective-permute-start.8 = (f32[2,1536]{1,0:T(2,128)S(1)}, f32[2,1536]{1,0:T(2,128)S(1)}, u32[]{:S(2)}, u32[]{:S(2)}) collective-permute-start(f32[2,1536]{1,0:T(2,128)S(1)} %add.19.rest_1_.own_ref), channel_id=1, source_target_pairs={{0,4},{1,5},{2,6},{3,7},{4,0},{5,1},{6,2},{7,3},{8,12},{9,13},{10,... | collective-permute-start | bytes 36872 | tf_op jit(solution)/shard_map/ppermute | solution.py:752
  48.9 2.2 %branch.3 = (bf16[512,1536]{1,0:T(8,128)(2,1)}, f32[8,128]{1,0:T(8,128)S(1)}) custom-call(bf16[512,1536]{1,0:T(8,128)(2,1)S(1)} %bitcast.15, bf16[512,1536]{1,0:T(8,128)(2,1)S(1)} %get-tuple-element.60.act_ref.acta_ref, bf16[1536,1536]{1,0:T(8,128)(2,1)S(1)} %copy-done, ...), custom_call_target="tpu_custom_call", output_to_operand_aliasing={{0}: (3, {})} | custom-call | bytes 6000000 | tf_op jit(solution)/shard_map/branch/pallas_call | solution.py:543
  51.2 0.2 collective-permute-done.8.got_ref
  51.4 2.6 %grad.1 = (bf16[8,48,768]{2,1,0:T(8,128)(2,1)S(1)}, f32[8,48,768]{2,1,0:T(8,128)S(1)}, bf16[8,48,768]{2,1,0:T(8,128)(2,1)S(1)}, f32[8,48,768]{2,1,0:T(8,128)S(1)}) custom-call(bf16[16,48,512]{2,1,0:T(8,128)(2,1)S(1)} %get-tuple-element.58.rest_1_.ca_ref, bf16[16,48,512]{2,1,0:T(8,128)(2,1)S(1)} %collective-permute-done.10.cb_ref, ...), custom_call_target="tpu_custom_call" | custom-call | bytes 10500000 | tf_op jit(solution)/shard_map/grad/pallas_call | solution.py:513
  54.0 1.3 %collective-permute-start.20 = (bf16[8,48,768]{2,1,0:T(8,128)(2,1)S(1)}, bf16[8,48,768]{2,1,0:T(8,128)(2,1)S(1)}, u32[]{:S(2)}, u32[]{:S(2)}) collective-permute-start(bf16[8,48,768]{2,1,0:T(8,128)(2,1)S(1)} %get-tuple-element.84), channel_id=1, source_target_pairs={{0,4},{1,5},{2,6},{3,7},{4,0},{5,1},{6,2},{7,3},{8,12},{9,13},{10,... | collective-permute-start | bytes 1769480 | tf_op jit(solution)/shard_map/ppermute | solution.py:752
  55.3 0.7 collective-permute-start.18
  56.0 1.8 %collective-permute-start.9 = (f32[2,1536]{1,0:T(2,128)S(1)}, f32[2,1536]{1,0:T(2,128)S(1)}, u32[]{:S(2)}, u32[]{:S(2)}) collective-permute-start(f32[2,1536]{1,0:T(2,128)S(1)} %add.20.rest_0_.own_ref), channel_id=1, source_target_pairs={{0,8},{1,9},{2,10},{3,11},{4,12},{5,13},{6,14},{7,15},{8,0},{9,1},... | collective-permute-start | bytes 36872 | tf_op jit(solution)/shard_map/ppermute | solution.py:752
  57.9 1.9 %collective-permute-done.9.got_ref = f32[2,1536]{1,0:T(2,128)S(1)} collective-permute-done((f32[2,1536]{1,0:T(2,128)S(1)}, f32[2,1536]{1,0:T(2,128)S(1)}, u32[]{:S(2)}, u32[]{:S(2)}) %collective-permute-start.9) | collective-permute-done | bytes 12320 | tf_op jit(solution)/shard_map/ppermute | solution.py:752
  59.7 2.8 %collective-permute-start.12 = (f32[2,1536]{1,0:T(2,128)S(1)}, f32[2,1536]{1,0:T(2,128)S(1)}, u32[]{:S(2)}, u32[]{:S(2)}) collective-permute-start(f32[2,1536]{1,0:T(2,128)S(1)} %add.21.own_ref), channel_id=1, source_target_pairs={{0,16},{1,17},{2,18},{3,19},{4,20},{5,21},{6,22},{7,23},{8,24},{9,... | collective-permute-start | bytes 36872 | tf_op jit(solution)/shard_map/ppermute | solution.py:752
  62.6 1.8 %collective-permute-done.12.got_ref = f32[2,1536]{1,0:T(2,128)S(1)} collective-permute-done((f32[2,1536]{1,0:T(2,128)S(1)}, f32[2,1536]{1,0:T(2,128)S(1)}, u32[]{:S(2)}, u32[]{:S(2)}) %collective-permute-start.12) | collective-permute-done | bytes 12320 | tf_op jit(solution)/shard_map/ppermute | solution.py:752
  64.3 1.2 %collective-permute-done.13.got_ref = f32[2,1536]{1,0:T(2,128)S(1)} collective-permute-done((f32[2,1536]{1,0:T(2,128)S(1)}, f32[2,1536]{1,0:T(2,128)S(1)}, u32[]{:S(2)}, u32[]{:S(2)}) %collective-permute-start.13) | collective-permute-done | bytes 12320 | tf_op jit(solution)/shard_map/ppermute | solution.py:752
  65.5 7.1 %grad_taps.1 = (bf16[32,1536]{1,0:T(8,128)(2,1)S(1)}, f32[12,2,9,72,128]{4,3,2,1,0:T(8,128)S(1)}, f32[1536]{0:T(1024)}, f32[1536]{0:T(1024)}) custom-call(f32[576,1536]{1,0:T(8,128)S(1)} %get-tuple-element.67.dbn_ref, f32[576,1536]{1,0:T(8,128)S(1)} %get-tuple-element.56.conv_ref, f32[2,1536]{1,0:T(2,128)S(1)} %add.18.sums_ref, ...), custom_call_target="tpu_custom_call" | custom-call | bytes 27000000 | tf_op jit(solution)/shard_map/grad_taps/pallas_call | solution.py:617
  72.6 0.2 collective-permute-start.14
  72.8 0.1 merge.5
  72.9 1.4 %collective-permute-start.21 = (bf16[4,48,768]{2,1,0:T(8,128)(2,1)S(1)}, bf16[4,48,768]{2,1,0:T(8,128)(2,1)S(1)}, u32[]{:S(2)}, u32[]{:S(2)}) collective-permute-start(bf16[4,48,768]{2,1,0:T(8,128)(2,1)S(1)} %get-tuple-element.86), channel_id=1, source_target_pairs={{0,2},{1,3},{2,0},{3,1},{4,6},{5,7},{6,4},{7,5},{8,10},{9,11},{10,... | collective-permute-start | bytes 884744 | tf_op jit(solution)/shard_map/ppermute | solution.py:752
  74.2 0.1 merge.4
  74.3 0.9 collective-permute-start.19
  75.2 2.8 %collective-permute-start.15 = (bf16[32,1536]{1,0:T(8,128)(2,1)S(1)}, bf16[32,1536]{1,0:T(8,128)(2,1)S(1)}, u32[]{:S(2)}, u32[]{:S(2)}) collective-permute-start(bf16[32,1536]{1,0:T(8,128)(2,1)S(1)} %add.24.rest_0_.own_ref), channel_id=1, source_target_pairs={{0,16},{1,17},{2,18},{3,19},{4,20},{5,21},{6,22},{7,23},{8,24},{9,... | collective-permute-start | bytes 294920 | tf_op jit(solution)/shard_map/ppermute | solution.py:752
  78.0 2.7 %grad_proj.3 = (bf16[512,768]{1,0:T(8,128)(2,1)S(1)}, bf16[512,768]{1,0:T(8,128)(2,1)S(1)}) custom-call(f32[12,2,9,72,128]{4,3,2,1,0:T(8,128)S(1)} %get-tuple-element.71.seq_ref, f32[32,1536]{1,0:T(8,128)S(1)} %copy-done.3, bf16[512,1536]{1,0:T(8,128)(2,1)S(1)} %get-tuple-element.72.p_ref, bf16[512,1536]{1,0:T(8,128)(2,1)S(1)} %get-tuple-element.73.q_ref, ...), custom_call_target="tpu_custom_call" | custom-call | bytes 12000000 | tf_op jit(solution)/shard_map/grad_proj/pallas_call | solution.py:667
  80.8 0.0 slice-start.2
  80.8 2.7 %grad_proj.2 = (bf16[512,768]{1,0:T(8,128)(2,1)S(1)}, bf16[512,768]{1,0:T(8,128)(2,1)S(1)}) custom-call(f32[12,2,9,72,128]{4,3,2,1,0:T(8,128)S(1)} %get-tuple-element.71.seq_ref, f32[32,1536]{1,0:T(8,128)S(1)} %copy-done.3, bf16[512,1536]{1,0:T(8,128)(2,1)S(1)} %get-tuple-element.72.p_ref, bf16[512,1536]{1,0:T(8,128)(2,1)S(1)} %get-tuple-element.73.q_ref, ...), custom_call_target="tpu_custom_call" | custom-call | bytes 12000000 | tf_op jit(solution)/shard_map/grad_proj/pallas_call | solution.py:667
  83.6 1.7 %collective-permute-start.16 = (bf16[32,1536]{1,0:T(8,128)(2,1)S(1)}, bf16[32,1536]{1,0:T(8,128)(2,1)S(1)}, u32[]{:S(2)}, u32[]{:S(2)}) collective-permute-start(bf16[32,1536]{1,0:T(8,128)(2,1)S(1)} %add.25.rest_4_.own_ref), channel_id=1, source_target_pairs={{0,8},{1,9},{2,10},{3,11},{4,12},{5,13},{6,14},{7,15},{8,0},{9,1},... | collective-permute-start | bytes 294920 | tf_op jit(solution)/shard_map/ppermute | solution.py:752
  85.3 2.6 %back_proj.2.rest_0_.left_ref = f32[512,768]{1,0:T(8,128)S(1)} custom-call(f32[3,1536]{1,0:T(4,128)S(1)} %get-tuple-element.59.vec_ref, bf16[1536,3072]{1,0:T(8,128)(2,1)S(1)} %bitcast.7, bf16[512,768]{1,0:T(8,128)(2,1)S(1)} %get-tuple-element.75.rest_0_, bf16[512,768]{1,0:T(8,128)(2,1)S(1)} %get-tuple-element.76.rest_1_, ...), custom_call_target="tpu_custom_call" | custom-call | bytes 7800000 | tf_op jit(solution)/shard_map/back_proj/pallas_call | solution.py:699
  87.9 0.4 collective-permute-done.16.got_ref
  88.3 0.1 merge.6
  88.4 1.7 %collective-permute-start.22 = (bf16[2,48,1536]{2,1,0:T(8,128)(2,1)S(1)}, bf16[2,48,1536]{2,1,0:T(8,128)(2,1)S(1)}, u32[]{:S(2)}, u32[]{:S(2)}) collective-permute-start(bf16[2,48,1536]{2,1,0:T(8,128)(2,1)S(1)} %get-tuple-element.88), channel_id=1, source_target_pairs={{0,8},{1,9},{2,10},{3,11},{4,12},{5,13},{6,14},{7,15},{8,0},{9,1},... | collective-permute-start | bytes 884744 | tf_op jit(solution)/shard_map/ppermute | solution.py:752
  90.1 1.2 %collective-permute-start.17 = (bf16[32,1536]{1,0:T(8,128)(2,1)S(1)}, bf16[32,1536]{1,0:T(8,128)(2,1)S(1)}, u32[]{:S(2)}, u32[]{:S(2)}) collective-permute-start(bf16[32,1536]{1,0:T(8,128)(2,1)S(1)} %add.26.rest_4_.own_ref.refs_4_), channel_id=1, source_target_pairs={{0,2},{1,3},{2,0},{3,1},{4,6},{5,7},{6,4},{7,5},{8,10},{9,11},{10,... | collective-permute-start | bytes 294920 | tf_op jit(solution)/shard_map/ppermute | solution.py:752
  91.3 2.6 %back_proj.3.rest_0_.right_ref.refs_2_ = f32[512,768]{1,0:T(8,128)S(1)} custom-call(f32[3,1536]{1,0:T(4,128)S(1)} %get-tuple-element.59.vec_ref, bf16[1536,3072]{1,0:T(8,128)(2,1)S(1)} %bitcast.7, bf16[512,768]{1,0:T(8,128)(2,1)S(1)} %get-tuple-element.75.rest_0_, bf16[512,768]{1,0:T(8,128)(2,1)S(1)} %get-tuple-element.76.rest_1_, ...), custom_call_target="tpu_custom_call" | custom-call | bytes 7800000 | tf_op jit(solution)/shard_map/back_proj/pallas_call | solution.py:699
  94.0 2.3 %collective-permute-done.22.refs_1_ = bf16[2,48,1536]{2,1,0:T(8,128)(2,1)S(1)} collective-permute-done((bf16[2,48,1536]{2,1,0:T(8,128)(2,1)S(1)}, bf16[2,48,1536]{2,1,0:T(8,128)(2,1)S(1)}, u32[]{:S(2)}, u32[]{:S(2)}) %collective-permute-start.22) | collective-permute-done | bytes 294944 | tf_op jit(solution)/shard_map/ppermute | solution.py:752
  96.3 0.1 merge.7
  96.4 2.4 %collective-permute-start.23 = (bf16[1,48,1536]{2,1,0:T(8,128)(2,1)S(1)}, bf16[1,48,1536]{2,1,0:T(8,128)(2,1)S(1)}, u32[]{:S(2)}, u32[]{:S(2)}) collective-permute-start(bf16[1,48,1536]{2,1,0:T(8,128)(2,1)S(1)} %get-tuple-element.90), channel_id=1, source_target_pairs={{0,16},{1,17},{2,18},{3,19},{4,20},{5,21},{6,22},{7,23},{8,24},{9,... | collective-permute-start | bytes 442376 | tf_op jit(solution)/shard_map/ppermute | solution.py:752
  98.8 1.5 %collective-permute-start.24 = (bf16[32,1536]{1,0:T(8,128)(2,1)S(1)}, bf16[32,1536]{1,0:T(8,128)(2,1)S(1)}, u32[]{:S(2)}, u32[]{:S(2)}) collective-permute-start(bf16[32,1536]{1,0:T(8,128)(2,1)S(1)} %add.27.rest_0_.c_ref), channel_id=1, source_target_pairs={{0,4},{1,5},{2,6},{3,7},{4,0},{5,1},{6,2},{7,3},{8,12},{9,13},{10,... | collective-permute-start | bytes 294920 | tf_op jit(solution)/shard_map/ppermute | solution.py:752
  100.3 2.3 %back_norm.1 = (bf16[512,1536]{1,0:T(8,128)(2,1)}, f32[8,128]{1,0:T(8,128)S(1)}) custom-call(bf16[512,1536]{1,0:T(8,128)(2,1)S(1)} %get-tuple-element.65.hat_ref, f32[512,1]{1,0:T(8,128)S(1)} %get-tuple-element.66.rstd_ref, bf16[512,1536]{1,0:T(8,128)(2,1)S(1)} %bitcast.12, f32[512,768]{1,0:T(8,128)S(1)} %back_proj.2.rest_0_.left_ref, ...), custom_call_target="tpu_custom_call" | custom-call | bytes 9000000 | tf_op jit(solution)/shard_map/back_norm/pallas_call | solution.py:738
  102.6 0.9 collective-permute-done.24.d_ref
  103.5 1.0 collective-permute-done.23
  104.4 0.8 last_add.1
  (37 shorter events, 0.2 us)
Async XLA Ops:
  0.6 10.2 %copy-start.3 = (f32[32,1536]{1,0:T(8,128)S(1)}, f32[32,1536]{1,0:T(8,128)}, u32[]{:S(2)}) copy-start(f32[32,1536]{1,0:T(8,128)} %k_ref.7) | copy-start | bytes 589828
  9.4 6.4 %collective-permute-start = (bf16[2,48,1536]{2,1,0:T(8,128)(2,1)S(1)}, bf16[2,48,1536]{2,1,0:T(8,128)(2,1)S(1)}, u32[]{:S(2)}, u32[]{:S(2)}) collective-permute-start(bf16[2,48,1536]{2,1,0:T(8,128)(2,1)S(1)} %get-tuple-element.52), channel_id=1, source_target_pairs={{0,1},{1,0},{2,3},{3,2},{4,5},{5,4},{6,7},{7,6},{8,9},{9,8},{10,11... | collective-permute-start | bytes 884744 | tf_op jit(solution)/shard_map/ppermute | solution.py:752
  9.9 5.9 %collective-permute-start.1 = (bf16[2,48,1536]{2,1,0:T(8,128)(2,1)S(1)}, bf16[2,48,1536]{2,1,0:T(8,128)(2,1)S(1)}, u32[]{:S(2)}, u32[]{:S(2)}) collective-permute-start(bf16[2,48,1536]{2,1,0:T(8,128)(2,1)S(1)} %get-tuple-element.53), channel_id=1, source_target_pairs={{1,2},{2,1},{3,4},{4,3},{5,6},{6,5},{7,8},{8,7},{9,10},{10,9},{11,... | collective-permute-start | bytes 884744 | tf_op jit(solution)/shard_map/ppermute | solution.py:821
  10.8 16.5 %copy-start.1 = (bf16[2,256,1536]{2,1,0:T(8,128)(2,1)S(1)}, bf16[2,256,1536]{2,1,0:T(8,128)(2,1)}, u32[]{:S(2)}) copy-start(bf16[2,256,1536]{2,1,0:T(8,128)(2,1)} %param.15) | copy-start | bytes 4718596
  15.8 11.5 %copy-start = (bf16[1536,1536]{1,0:T(8,128)(2,1)S(1)}, bf16[1536,1536]{1,0:T(8,128)(2,1)}, u32[]{:S(2)}) copy-start(bf16[1536,1536]{1,0:T(8,128)(2,1)} %w_ref.11) | copy-start | bytes 14155780
  17.8 6.3 %collective-permute-start.2 = (f32[2,1536]{1,0:T(2,128)S(1)}, f32[2,1536]{1,0:T(2,128)S(1)}, u32[]{:S(2)}, u32[]{:S(2)}) collective-permute-start(f32[2,1536]{1,0:T(2,128)S(1)} %get-tuple-element.57.own_ref), channel_id=1, source_target_pairs={{0,1},{1,0},{2,3},{3,2},{4,5},{5,4},{6,7},{7,6},{8,9},{9,8},{10,11... | collective-permute-start | bytes 36872 | tf_op jit(solution)/shard_map/ppermute | solution.py:752
  24.2 4.8 %collective-permute-start.3 = (f32[2,1536]{1,0:T(2,128)S(1)}, f32[2,1536]{1,0:T(2,128)S(1)}, u32[]{:S(2)}, u32[]{:S(2)}) collective-permute-start(f32[2,1536]{1,0:T(2,128)S(1)} %add.14.rest_0_.own_ref), channel_id=1, source_target_pairs={{0,2},{1,3},{2,0},{3,1},{4,6},{5,7},{6,4},{7,5},{8,10},{9,11},{10,... | collective-permute-start | bytes 36872 | tf_op jit(solution)/shard_map/ppermute | solution.py:752
  29.0 3.7 %collective-permute-start.4 = (f32[2,1536]{1,0:T(2,128)S(1)}, f32[2,1536]{1,0:T(2,128)S(1)}, u32[]{:S(2)}, u32[]{:S(2)}) collective-permute-start(f32[2,1536]{1,0:T(2,128)S(1)} %add.15.rest_0_.own_ref), channel_id=1, source_target_pairs={{0,4},{1,5},{2,6},{3,7},{4,0},{5,1},{6,2},{7,3},{8,12},{9,13},{10,... | collective-permute-start | bytes 36872 | tf_op jit(solution)/shard_map/ppermute | solution.py:752
  32.7 3.7 %collective-permute-start.5 = (f32[2,1536]{1,0:T(2,128)S(1)}, f32[2,1536]{1,0:T(2,128)S(1)}, u32[]{:S(2)}, u32[]{:S(2)}) collective-permute-start(f32[2,1536]{1,0:T(2,128)S(1)} %add.16.own_ref), channel_id=1, source_target_pairs={{0,8},{1,9},{2,10},{3,11},{4,12},{5,13},{6,14},{7,15},{8,0},{9,1},... | collective-permute-start | bytes 36872 | tf_op jit(solution)/shard_map/ppermute | solution.py:752
  36.4 4.6 %collective-permute-start.6 = (f32[2,1536]{1,0:T(2,128)S(1)}, f32[2,1536]{1,0:T(2,128)S(1)}, u32[]{:S(2)}, u32[]{:S(2)}) collective-permute-start(f32[2,1536]{1,0:T(2,128)S(1)} %add.17.rest_0_.own_ref), channel_id=1, source_target_pairs={{0,16},{1,17},{2,18},{3,19},{4,20},{5,21},{6,22},{7,23},{8,24},{9,... | collective-permute-start | bytes 36872 | tf_op jit(solution)/shard_map/ppermute | solution.py:752
  41.0 4.3 %copy-start.2 = (bf16[2,256,1536]{2,1,0:T(8,128)(2,1)S(1)}, bf16[2,256,1536]{2,1,0:T(8,128)(2,1)}, u32[]{:S(2)}) copy-start(bf16[2,256,1536]{2,1,0:T(8,128)(2,1)} %param.8) | copy-start | bytes 4718596
  42.7 8.6 %collective-permute-start.11 = (bf16[512,1536]{1,0:T(8,128)(2,1)S(1)}, bf16[512,1536]{1,0:T(8,128)(2,1)S(1)}, u32[]{:S(2)}, u32[]{:S(2)}) collective-permute-start(bf16[512,1536]{1,0:T(8,128)(2,1)S(1)} %get-tuple-element.60.act_ref.acta_ref), channel_id=1, source_target_pairs={{0,1},{1,0},{2,3},{3,2},{4,5},{5,4},{6,7},{7,6},{8,9},{9,8},{10,11... | collective-permute-start | bytes 4718600 | tf_op jit(solution)/shard_map/ppermute | solution.py:752
  42.8 8.6 %collective-permute-start.10 = (bf16[16,48,512]{2,1,0:T(8,128)(2,1)S(1)}, bf16[16,48,512]{2,1,0:T(8,128)(2,1)S(1)}, u32[]{:S(2)}, u32[]{:S(2)}) collective-permute-start(bf16[16,48,512]{2,1,0:T(8,128)(2,1)S(1)} %get-tuple-element.69), channel_id=1, source_target_pairs={{0,1},{1,0},{2,3},{3,2},{4,5},{5,4},{6,7},{7,6},{8,9},{9,8},{10,11... | collective-permute-start | bytes 2359304 | tf_op jit(solution)/shard_map/ppermute | solution.py:752
  43.3 4.3 %collective-permute-start.7 = (f32[2,1536]{1,0:T(2,128)S(1)}, f32[2,1536]{1,0:T(2,128)S(1)}, u32[]{:S(2)}, u32[]{:S(2)}) collective-permute-start(f32[2,1536]{1,0:T(2,128)S(1)} %get-tuple-element.61.rest_0_.own_ref), channel_id=1, source_target_pairs={{0,2},{1,3},{2,0},{3,1},{4,6},{5,7},{6,4},{7,5},{8,10},{9,11},{10,... | collective-permute-start | bytes 36872 | tf_op jit(solution)/shard_map/ppermute | solution.py:752
  47.6 3.8 %collective-permute-start.8 = (f32[2,1536]{1,0:T(2,128)S(1)}, f32[2,1536]{1,0:T(2,128)S(1)}, u32[]{:S(2)}, u32[]{:S(2)}) collective-permute-start(f32[2,1536]{1,0:T(2,128)S(1)} %add.19.rest_1_.own_ref), channel_id=1, source_target_pairs={{0,4},{1,5},{2,6},{3,7},{4,0},{5,1},{6,2},{7,3},{8,12},{9,13},{10,... | collective-permute-start | bytes 36872 | tf_op jit(solution)/shard_map/ppermute | solution.py:752
  54.0 18.8 %collective-permute-start.20 = (bf16[8,48,768]{2,1,0:T(8,128)(2,1)S(1)}, bf16[8,48,768]{2,1,0:T(8,128)(2,1)S(1)}, u32[]{:S(2)}, u32[]{:S(2)}) collective-permute-start(bf16[8,48,768]{2,1,0:T(8,128)(2,1)S(1)} %get-tuple-element.84), channel_id=1, source_target_pairs={{0,4},{1,5},{2,6},{3,7},{4,0},{5,1},{6,2},{7,3},{8,12},{9,13},{10,... | collective-permute-start | bytes 1769480 | tf_op jit(solution)/shard_map/ppermute | solution.py:752
  55.3 19.0 %collective-permute-start.18 = (bf16[8,48,768]{2,1,0:T(8,128)(2,1)S(1)}, bf16[8,48,768]{2,1,0:T(8,128)(2,1)S(1)}, u32[]{:S(2)}, u32[]{:S(2)}) collective-permute-start(bf16[8,48,768]{2,1,0:T(8,128)(2,1)S(1)} %get-tuple-element.70.rest_0_), channel_id=1, source_target_pairs={{0,2},{1,3},{2,0},{3,1},{4,6},{5,7},{6,4},{7,5},{8,10},{9,11},{10,... | collective-permute-start | bytes 1769480 | tf_op jit(solution)/shard_map/ppermute | solution.py:752
  56.0 3.7 %collective-permute-start.9 = (f32[2,1536]{1,0:T(2,128)S(1)}, f32[2,1536]{1,0:T(2,128)S(1)}, u32[]{:S(2)}, u32[]{:S(2)}) collective-permute-start(f32[2,1536]{1,0:T(2,128)S(1)} %add.20.rest_0_.own_ref), channel_id=1, source_target_pairs={{0,8},{1,9},{2,10},{3,11},{4,12},{5,13},{6,14},{7,15},{8,0},{9,1},... | collective-permute-start | bytes 36872 | tf_op jit(solution)/shard_map/ppermute | solution.py:752
  59.7 4.6 %collective-permute-start.12 = (f32[2,1536]{1,0:T(2,128)S(1)}, f32[2,1536]{1,0:T(2,128)S(1)}, u32[]{:S(2)}, u32[]{:S(2)}) collective-permute-start(f32[2,1536]{1,0:T(2,128)S(1)} %add.21.own_ref), channel_id=1, source_target_pairs={{0,16},{1,17},{2,18},{3,19},{4,20},{5,21},{6,22},{7,23},{8,24},{9,... | collective-permute-start | bytes 36872 | tf_op jit(solution)/shard_map/ppermute | solution.py:752
  64.3 1.2 %collective-permute-start.13 = (f32[2,1536]{1,0:T(2,128)S(1)}, f32[2,1536]{1,0:T(2,128)S(1)}, u32[]{:S(2)}, u32[]{:S(2)}) collective-permute-start(f32[2,1536]{1,0:T(2,128)S(1)} %add.22.own_ref), channel_id=1, source_target_pairs={{0,1},{1,0},{2,3},{3,2},{4,5},{5,4},{6,7},{7,6},{8,9},{9,8},{10,11... | collective-permute-start | bytes 36872 | tf_op jit(solution)/shard_map/ppermute | solution.py:752
  72.6 2.6 %collective-permute-start.14 = (bf16[32,1536]{1,0:T(8,128)(2,1)S(1)}, bf16[32,1536]{1,0:T(8,128)(2,1)S(1)}, u32[]{:S(2)}, u32[]{:S(2)}) collective-permute-start(bf16[32,1536]{1,0:T(8,128)(2,1)S(1)} %get-tuple-element.74.own_ref), channel_id=1, source_target_pairs={{0,1},{1,0},{2,3},{3,2},{4,5},{5,4},{6,7},{7,6},{8,9},{9,8},{10,11... | collective-permute-start | bytes 294920 | tf_op jit(solution)/shard_map/ppermute | solution.py:752
  72.9 15.4 %collective-permute-start.21 = (bf16[4,48,768]{2,1,0:T(8,128)(2,1)S(1)}, bf16[4,48,768]{2,1,0:T(8,128)(2,1)S(1)}, u32[]{:S(2)}, u32[]{:S(2)}) collective-permute-start(bf16[4,48,768]{2,1,0:T(8,128)(2,1)S(1)} %get-tuple-element.86), channel_id=1, source_target_pairs={{0,2},{1,3},{2,0},{3,1},{4,6},{5,7},{6,4},{7,5},{8,10},{9,11},{10,... | collective-permute-start | bytes 884744 | tf_op jit(solution)/shard_map/ppermute | solution.py:752
  74.3 14.0 %collective-permute-start.19 = (bf16[4,48,768]{2,1,0:T(8,128)(2,1)S(1)}, bf16[4,48,768]{2,1,0:T(8,128)(2,1)S(1)}, u32[]{:S(2)}, u32[]{:S(2)}) collective-permute-start(bf16[4,48,768]{2,1,0:T(8,128)(2,1)S(1)} %get-tuple-element.82), channel_id=1, source_target_pairs={{0,4},{1,5},{2,6},{3,7},{4,0},{5,1},{6,2},{7,3},{8,12},{9,13},{10,... | collective-permute-start | bytes 884744 | tf_op jit(solution)/shard_map/ppermute | solution.py:752
  75.2 8.3 %collective-permute-start.15 = (bf16[32,1536]{1,0:T(8,128)(2,1)S(1)}, bf16[32,1536]{1,0:T(8,128)(2,1)S(1)}, u32[]{:S(2)}, u32[]{:S(2)}) collective-permute-start(bf16[32,1536]{1,0:T(8,128)(2,1)S(1)} %add.24.rest_0_.own_ref), channel_id=1, source_target_pairs={{0,16},{1,17},{2,18},{3,19},{4,20},{5,21},{6,22},{7,23},{8,24},{9,... | collective-permute-start | bytes 294920 | tf_op jit(solution)/shard_map/ppermute | solution.py:752
  78.0 7.2 %slice-start = ((s8[9437184]{0:T(1024)(128)(4,1)}), s8[4194304]{0:T(1024)(128)(4,1)S(1)}, s32[]{:S(2)}) async-start(s8[9437184]{0:T(1024)(128)(4,1)} %bitcast.6), calls=%async_computation | async-start | bytes 8388608
  78.0 7.2 %slice-start.1 = ((s8[9437184]{0:T(1024)(128)(4,1)}), s8[4194304]{0:T(1024)(128)(4,1)S(1)}, s32[]{:S(2)}) async-start(s8[9437184]{0:T(1024)(128)(4,1)} %bitcast.6), calls=%async_computation.1 | async-start | bytes 8388608
  80.8 4.5 %slice-start.2 = ((s8[9437184]{0:T(1024)(128)(4,1)}), s8[1048576]{0:T(1024)(128)(4,1)S(1)}, s32[]{:S(2)}) async-start(s8[9437184]{0:T(1024)(128)(4,1)} %bitcast.6), calls=%async_computation.2 | async-start | bytes 2097152
  83.6 4.7 %collective-permute-start.16 = (bf16[32,1536]{1,0:T(8,128)(2,1)S(1)}, bf16[32,1536]{1,0:T(8,128)(2,1)S(1)}, u32[]{:S(2)}, u32[]{:S(2)}) collective-permute-start(bf16[32,1536]{1,0:T(8,128)(2,1)S(1)} %add.25.rest_4_.own_ref), channel_id=1, source_target_pairs={{0,8},{1,9},{2,10},{3,11},{4,12},{5,13},{6,14},{7,15},{8,0},{9,1},... | collective-permute-start | bytes 294920 | tf_op jit(solution)/shard_map/ppermute | solution.py:752
  88.4 7.9 %collective-permute-start.22 = (bf16[2,48,1536]{2,1,0:T(8,128)(2,1)S(1)}, bf16[2,48,1536]{2,1,0:T(8,128)(2,1)S(1)}, u32[]{:S(2)}, u32[]{:S(2)}) collective-permute-start(bf16[2,48,1536]{2,1,0:T(8,128)(2,1)S(1)} %get-tuple-element.88), channel_id=1, source_target_pairs={{0,8},{1,9},{2,10},{3,11},{4,12},{5,13},{6,14},{7,15},{8,0},{9,1},... | collective-permute-start | bytes 884744 | tf_op jit(solution)/shard_map/ppermute | solution.py:752
  90.1 8.7 %collective-permute-start.17 = (bf16[32,1536]{1,0:T(8,128)(2,1)S(1)}, bf16[32,1536]{1,0:T(8,128)(2,1)S(1)}, u32[]{:S(2)}, u32[]{:S(2)}) collective-permute-start(bf16[32,1536]{1,0:T(8,128)(2,1)S(1)} %add.26.rest_4_.own_ref.refs_4_), channel_id=1, source_target_pairs={{0,2},{1,3},{2,0},{3,1},{4,6},{5,7},{6,4},{7,5},{8,10},{9,11},{10,... | collective-permute-start | bytes 294920 | tf_op jit(solution)/shard_map/ppermute | solution.py:752
  96.4 8.1 %collective-permute-start.23 = (bf16[1,48,1536]{2,1,0:T(8,128)(2,1)S(1)}, bf16[1,48,1536]{2,1,0:T(8,128)(2,1)S(1)}, u32[]{:S(2)}, u32[]{:S(2)}) collective-permute-start(bf16[1,48,1536]{2,1,0:T(8,128)(2,1)S(1)} %get-tuple-element.90), channel_id=1, source_target_pairs={{0,16},{1,17},{2,18},{3,19},{4,20},{5,21},{6,22},{7,23},{8,24},{9,... | collective-permute-start | bytes 442376 | tf_op jit(solution)/shard_map/ppermute | solution.py:752
  98.8 4.7 %collective-permute-start.24 = (bf16[32,1536]{1,0:T(8,128)(2,1)S(1)}, bf16[32,1536]{1,0:T(8,128)(2,1)S(1)}, u32[]{:S(2)}, u32[]{:S(2)}) collective-permute-start(bf16[32,1536]{1,0:T(8,128)(2,1)S(1)} %add.27.rest_0_.c_ref), channel_id=1, source_target_pairs={{0,4},{1,5},{2,6},{3,7},{4,0},{5,1},{6,2},{7,3},{8,12},{9,13},{10,... | collective-permute-start | bytes 294920 | tf_op jit(solution)/shard_map/ppermute | solution.py:752

commit v6 on v5

--- a/solution.py
+++ b/solution.py
@@ -140,7 +140,7 @@
 
     for i in range(pieces):
         x_copy(i).wait()
-        for j in range(1 + i, steps if i == pieces - 1 else 2 + i):
+        for j in range(1 + 3 * i, min(steps, 4 + 3 * i)):
             for half in range(2):
                 w_copy(j, half).start()
 
@@ -199,7 +199,7 @@
             pltpu.VMEM((d,), F32),
             pltpu.VMEM((d,), F32),
             pltpu.VMEM((d,), F32),
-            pltpu.SemaphoreType.DMA((4,)),
+            pltpu.SemaphoreType.DMA((2,)),
             pltpu.SemaphoreType.DMA((d // CW, 2)),
             pltpu.SemaphoreType.DMA((utt, 2)),
             pltpu.SemaphoreType.DMA((3,)),
@@ -262,12 +262,13 @@
         seq_ref[i] = piece
 
 
-def filtered(seq_ref, taps_ref, order, count):
+def filtered(seq_refs, taps_ref, order, count):
     for i in range(PIECES):
-        acc = jnp.zeros((count, LANES), F32)
+        acc = jnp.zeros((count * len(seq_refs), LANES), F32)
         for a in range(taps_ref.shape[1]):
             row = order(a)
-            acc = acc + taps_ref[i, row : row + 1, :] * seq_ref[i, a : a + count, :]
+            rows = [seq_ref[i, a : a + count, :] for seq_ref in seq_refs]
+            acc = acc + taps_ref[i, row : row + 1, :] * jnp.concatenate(rows, axis=0)
         yield acc
 
 
@@ -278,10 +279,12 @@
         taps_ref[i] = piece
 
 
-def conv_piece(pad_ref, seq_ref, taps_ref, count):
-    fill_sequences(pad_ref, 1, seq_ref, count + taps_ref.shape[1])
-    for i, y in assembled(filtered(seq_ref, taps_ref, lambda a: a, count)):
-        pad_ref[phase(i, count), :] = y
+def conv_pieces(pad_refs, seq_refs, taps_ref, count):
+    for pad_ref, seq_ref in zip(pad_refs, seq_refs):
+        fill_sequences(pad_ref, 1, seq_ref, count + taps_ref.shape[1])
+    for i, y in assembled(filtered(seq_refs, taps_ref, lambda a: a, count)):
+        for j, pad_ref in enumerate(pad_refs):
+            pad_ref[phase(i, count), :] = y[j * count : (j + 1) * count]
 
 
 def squares(values):
@@ -300,7 +303,7 @@
         for u in range(utt):
             pad = pad_ref.at[slot, u]
             pad[0:frames, :] = g_ref[u * frames : (u + 1) * frames, lanes].astype(F32)
-            conv_piece(pad, seq_ref.at[slot, u], taps_ref.at[slot], mid // PHASES)
+            conv_pieces([pad], [seq_ref.at[slot, u]], taps_ref.at[slot], mid // PHASES)
             y = pad[0:mid, :]
             start = u * (frames + HALO) + HALO
             conv_ref[start : start + mid, lanes] = y
@@ -348,7 +351,6 @@
         for u in range(utt):
             a = a_ref[u, :HALO, lanes].astype(F32)
             b = b_ref[u, :HALO, lanes].astype(F32)
-            start = u * (frames + HALO)
             for side in range(2):
                 pad = pad_ref.at[slot, 2 * u + side]
                 at = u * frames + side * (frames - HALO)
@@ -356,8 +358,16 @@
                 beside = jnp.where(odd, b, a) if side else jnp.where(odd, a, b)
                 pad[side * HALO : (side + 1) * HALO, :] = beside
                 pad[(1 - side) * HALO : (2 - side) * HALO, :] = here
-                conv_piece(pad, seq_ref.at[slot, 2 * u + side], taps_ref.at[slot], HALO // PHASES)
-                out = start + side * frames
+        conv_pieces(
+            [pad_ref.at[slot, j] for j in range(2 * utt)],
+            [seq_ref.at[slot, j] for j in range(2 * utt)],
+            taps_ref.at[slot],
+            HALO // PHASES,
+        )
+        for u in range(utt):
+            for side in range(2):
+                pad = pad_ref.at[slot, 2 * u + side]
+                out = u * (frames + HALO) + side * frames
                 conv_ref[out : out + HALO, lanes] = pad[0:HALO, :]
                 own = (1 - side) * PAD
                 one, two = squares(pad[own : own + PAD, :])
@@ -650,7 +660,10 @@
             taps_ref[slot, i] = piece
         for u in range(utt):
             products = filtered(
-                seq_ref.at[group + start // LANES, u], taps_ref.at[slot], lambda a: per - 1 - a, count
+                [seq_ref.at[group + start // LANES, u]],
+                taps_ref.at[slot],
+                lambda a: per - 1 - a,
+                count,
             )
             for i, y in assembled(products):
                 out_ref[slot, phase(u * frames + i, count), :] = y

time: 105 us -> 105 us (level)
  no operation moved by 1% of the time
where the time goes in v6:
time: 105 us
  Pallas kernels  49.9 us (48%)
  starting transfers between devices  40.3 us (38%)
  waiting for transfers between devices  13.4 us (13%)
    ppermute x24, starting transfers between devices, swap(): return lax.ppermute(block, axis, [(i, i ^ bit) for i in range(count)])  39.4 us
    ppermute x24, waiting for transfers between devices, swap(): return lax.ppermute(block, axis, [(i, i ^ bit) for i in range(count)])  13.4 us
    pallas_call x1, Pallas kernels, front(): pl.pallas_call(functools.partial(front_body, utt), in_specs=[FAR] * 6, ou...  8.49 us
    pallas_call x1, Pallas kernels, grad_taps(): pl.pallas_call(functools.partial(grad_taps_body, utt, total), in_specs=[W...  7.11 us
    pallas_call x2, Pallas kernels, grad_proj(): pl.pallas_call(functools.partial(grad_proj_body, utt, start), in_specs=[W...  5.7 us
    pallas_call x2, Pallas kernels, back_proj(): pl.pallas_call(functools.partial(back_proj_body, start), in_specs=[WHOLE]...  5.28 us
    pallas_call x1, Pallas kernels, conv_mid(): pl.pallas_call(functools.partial(conv_mid_body, utt), in_specs=[WHOLE] *...  4.97 us
    pallas_call x2, Pallas kernels, branch(): pl.pallas_call(functools.partial(branch_body, start), in_specs=[WHOLE] *...  4.46 us
  transfers between devices with their start and end apart: 25, of which 13 were waited for; matrix products, arithmetic and copies ran while one was open for 0% of the time, Pallas kernels for 33%

profile of v6, /device:TPU:0, one launch (start us, length us, event | category | flops | bytes accessed | tf_op | source)
XLA Modules:
  0.0 104.6 jit_solution(6789188596148517294)
XLA Ops:
  0.6 8.5 %front.1 = (bf16[512,1536]{1,0:T(8,128)(2,1)S(1)}, bf16[512,1536]{1,0:T(8,128)(2,1)S(1)}, bf16[512,1536]{1,0:T(8,128)(2,1)S(1)}, bf16[512,1536]{1,0:T(8,128)(2,1...) custom-call(bf16[512,1536]{1,0:T(8,128)(2,1)} %bitcast.13, ...), custom_call_target="tpu_custom_call" | custom-call | bytes 30000000 | tf_op jit(solution)/shard_map/front/pallas_call | solution.py:189
  9.1 0.5 collective-permute-start
  9.7 0.8 collective-permute-start.1
  10.5 0.0 copy-start.1
  10.5 5.0 %conv_mid.1 = (f32[576,1536]{1,0:T(8,128)S(1)}, f32[2,1536]{1,0:T(2,128)S(1)}) custom-call(bf16[512,1536]{1,0:T(8,128)(2,1)S(1)} %get-tuple-element.51.g_ref, f32[32,1536]{1,0:T(8,128)S(1)} %copy-done.3), custom_call_target="tpu_custom_call" | custom-call | bytes 15000000 | tf_op jit(solution)/shard_map/conv_mid/pallas_call | solution.py:330
  15.5 0.0 collective-permute-done.1.b_ref
  15.5 0.0 copy-start
  15.5 1.6 %conv_end.1 = (f32[576,1536]{1,0:T(8,128)S(1)}, f32[2,1536]{1,0:T(2,128)S(1)}) custom-call(bf16[512,1536]{1,0:T(8,128)(2,1)S(1)} %get-tuple-element.51.g_ref, bf16[2,48,1536]{2,1,0:T(8,128)(2,1)S(1)} %collective-permute-done.a_ref, bf16[2,48,1536]{2,1,0:T(8,128)(2,1)S(1)} %collective-permute-done.1.b_ref, ...), custom_call_target="tpu_custom_call", output_to_operand_aliasing={{0}: (4, {})} | custom-call | bytes 6000000 | tf_op jit(solution)/shard_map/conv_end/pallas_call | solution.py:384
  17.2 5.5 %collective-permute-start.2 = (f32[2,1536]{1,0:T(2,128)S(1)}, f32[2,1536]{1,0:T(2,128)S(1)}, u32[]{:S(2)}, u32[]{:S(2)}) collective-permute-start(f32[2,1536]{1,0:T(2,128)S(1)} %get-tuple-element.57.own_ref), channel_id=1, source_target_pairs={{0,1},{1,0},{2,3},{3,2},{4,5},{5,4},{6,7},{7,6},{8,9},{9,8},{10,11... | collective-permute-start | bytes 36872 | tf_op jit(solution)/shard_map/ppermute | solution.py:765
  22.7 0.8 collective-permute-done.2.got_ref
  23.5 3.1 %collective-permute-start.3 = (f32[2,1536]{1,0:T(2,128)S(1)}, f32[2,1536]{1,0:T(2,128)S(1)}, u32[]{:S(2)}, u32[]{:S(2)}) collective-permute-start(f32[2,1536]{1,0:T(2,128)S(1)} %add.14.rest_0_.own_ref), channel_id=1, source_target_pairs={{0,2},{1,3},{2,0},{3,1},{4,6},{5,7},{6,4},{7,5},{8,10},{9,11},{10,... | collective-permute-start | bytes 36872 | tf_op jit(solution)/shard_map/ppermute | solution.py:765
  26.7 1.4 %act_grad.2.rest_0_.left_ref = f32[512,768]{1,0:T(8,128)S(1)} custom-call(bf16[512,1536]{1,0:T(8,128)(2,1)S(1)} %bitcast.9, bf16[1536,1536]{1,0:T(8,128)(2,1)S(1)} %copy-done, f32[2,1536]{1,0:T(2,128)S(1)} %add.14.rest_0_.own_ref), custom_call_target="tpu_custom_call" | custom-call | bytes 4500000 | tf_op jit(solution)/shard_map/act_grad/pallas_call | solution.py:406
  28.1 0.3 collective-permute-done.3.got_ref
  28.3 1.6 %collective-permute-start.4 = (f32[2,1536]{1,0:T(2,128)S(1)}, f32[2,1536]{1,0:T(2,128)S(1)}, u32[]{:S(2)}, u32[]{:S(2)}) collective-permute-start(f32[2,1536]{1,0:T(2,128)S(1)} %add.15.rest_0_.own_ref), channel_id=1, source_target_pairs={{0,4},{1,5},{2,6},{3,7},{4,0},{5,1},{6,2},{7,3},{8,12},{9,13},{10,... | collective-permute-start | bytes 36872 | tf_op jit(solution)/shard_map/ppermute | solution.py:765
  30.0 1.4 %act_grad.3.rest_0_.right_ref = f32[512,768]{1,0:T(8,128)S(1)} custom-call(bf16[512,1536]{1,0:T(8,128)(2,1)S(1)} %bitcast.10, bf16[1536,1536]{1,0:T(8,128)(2,1)S(1)} %copy-done, f32[2,1536]{1,0:T(2,128)S(1)} %add.15.rest_0_.own_ref), custom_call_target="tpu_custom_call" | custom-call | bytes 4500000 | tf_op jit(solution)/shard_map/act_grad/pallas_call | solution.py:406
  31.3 0.7 collective-permute-done.4.got_ref
  32.0 1.8 %collective-permute-start.5 = (f32[2,1536]{1,0:T(2,128)S(1)}, f32[2,1536]{1,0:T(2,128)S(1)}, u32[]{:S(2)}, u32[]{:S(2)}) collective-permute-start(f32[2,1536]{1,0:T(2,128)S(1)} %add.16.own_ref), channel_id=1, source_target_pairs={{0,8},{1,9},{2,10},{3,11},{4,12},{5,13},{6,14},{7,15},{8,0},{9,1},... | collective-permute-start | bytes 36872 | tf_op jit(solution)/shard_map/ppermute | solution.py:765
  33.8 1.9 %collective-permute-done.5.got_ref = f32[2,1536]{1,0:T(2,128)S(1)} collective-permute-done((f32[2,1536]{1,0:T(2,128)S(1)}, f32[2,1536]{1,0:T(2,128)S(1)}, u32[]{:S(2)}, u32[]{:S(2)}) %collective-permute-start.5) | collective-permute-done | bytes 12320 | tf_op jit(solution)/shard_map/ppermute | solution.py:765
  35.7 2.9 %collective-permute-start.6 = (f32[2,1536]{1,0:T(2,128)S(1)}, f32[2,1536]{1,0:T(2,128)S(1)}, u32[]{:S(2)}, u32[]{:S(2)}) collective-permute-start(f32[2,1536]{1,0:T(2,128)S(1)} %add.17.rest_0_.own_ref), channel_id=1, source_target_pairs={{0,16},{1,17},{2,18},{3,19},{4,20},{5,21},{6,22},{7,23},{8,24},{9,... | collective-permute-start | bytes 36872 | tf_op jit(solution)/shard_map/ppermute | solution.py:765
  38.7 0.6 turn.1
  39.3 0.9 act_grad_end.1.rest_0_.end_ref
  40.2 0.2 collective-permute-done.6.got_ref
  40.3 1.7 %middle.1 = (bf16[512,1536]{1,0:T(8,128)(2,1)S(1)}, f32[576,1536]{1,0:T(8,128)S(1)}, f32[2,1536]{1,0:T(2,128)S(1)}) custom-call(f32[576,1536]{1,0:T(8,128)S(1)} %get-tuple-element.56.conv_ref, f32[2,1536]{1,0:T(2,128)S(1)} %add.18.sums_ref, f32[3,1536]{1,0:T(4,128)S(1)} %get-tuple-element.59.vec_ref, f32[512,768]{1,0:T(8,128)S(1)} %act_grad.2.rest_0_.left_ref, ...), custom_call_target="tpu_custom_call" | custom-call | bytes 9000000 | tf_op jit(solution)/shard_map/middle/pallas_call | solution.py:484
  42.1 0.1 collective-permute-start.11
  42.2 0.5 collective-permute-start.10
  42.7 2.0 %collective-permute-start.7 = (f32[2,1536]{1,0:T(2,128)S(1)}, f32[2,1536]{1,0:T(2,128)S(1)}, u32[]{:S(2)}, u32[]{:S(2)}) collective-permute-start(f32[2,1536]{1,0:T(2,128)S(1)} %get-tuple-element.61.rest_0_.own_ref), channel_id=1, source_target_pairs={{0,2},{1,3},{2,0},{3,1},{4,6},{5,7},{6,4},{7,5},{8,10},{9,11},{10,... | collective-permute-start | bytes 36872 | tf_op jit(solution)/shard_map/ppermute | solution.py:765
  44.7 2.2 %branch.2 = (bf16[512,1536]{1,0:T(8,128)(2,1)}, f32[8,128]{1,0:T(8,128)S(1)}) custom-call(bf16[512,1536]{1,0:T(8,128)(2,1)S(1)} %bitcast.14, bf16[512,1536]{1,0:T(8,128)(2,1)S(1)} %get-tuple-element.60.act_ref.acta_ref, bf16[1536,1536]{1,0:T(8,128)(2,1)S(1)} %copy-done, f32[2,1536]{1,0:T(2,128)S(1)} %get-tuple-element.61.rest_0_.own_ref), custom_call_target="tpu_custom_call" | custom-call | bytes 6000000 | tf_op jit(solution)/shard_map/branch/pallas_call | solution.py:553
  46.9 0.0 collective-permute-done.7.got_ref
  46.9 1.3 %collective-permute-start.8 = (f32[2,1536]{1,0:T(2,128)S(1)}, f32[2,1536]{1,0:T(2,128)S(1)}, u32[]{:S(2)}, u32[]{:S(2)}) collective-permute-start(f32[2,1536]{1,0:T(2,128)S(1)} %add.19.rest_1_.own_ref), channel_id=1, source_target_pairs={{0,4},{1,5},{2,6},{3,7},{4,0},{5,1},{6,2},{7,3},{8,12},{9,13},{10,... | collective-permute-start | bytes 36872 | tf_op jit(solution)/shard_map/ppermute | solution.py:765
  48.2 2.2 %branch.3 = (bf16[512,1536]{1,0:T(8,128)(2,1)}, f32[8,128]{1,0:T(8,128)S(1)}) custom-call(bf16[512,1536]{1,0:T(8,128)(2,1)S(1)} %bitcast.15, bf16[512,1536]{1,0:T(8,128)(2,1)S(1)} %get-tuple-element.60.act_ref.acta_ref, bf16[1536,1536]{1,0:T(8,128)(2,1)S(1)} %copy-done, ...), custom_call_target="tpu_custom_call", output_to_operand_aliasing={{0}: (3, {})} | custom-call | bytes 6000000 | tf_op jit(solution)/shard_map/branch/pallas_call | solution.py:553
  50.5 0.2 collective-permute-done.8.got_ref
  50.7 2.6 %grad.1 = (bf16[8,48,768]{2,1,0:T(8,128)(2,1)S(1)}, f32[8,48,768]{2,1,0:T(8,128)S(1)}, bf16[8,48,768]{2,1,0:T(8,128)(2,1)S(1)}, f32[8,48,768]{2,1,0:T(8,128)S(1)}) custom-call(bf16[16,48,512]{2,1,0:T(8,128)(2,1)S(1)} %get-tuple-element.58.rest_1_.ca_ref, bf16[16,48,512]{2,1,0:T(8,128)(2,1)S(1)} %collective-permute-done.10.cb_ref, ...), custom_call_target="tpu_custom_call" | custom-call | bytes 10500000 | tf_op jit(solution)/shard_map/grad/pallas_call | solution.py:523
  53.3 1.3 %collective-permute-start.20 = (bf16[8,48,768]{2,1,0:T(8,128)(2,1)S(1)}, bf16[8,48,768]{2,1,0:T(8,128)(2,1)S(1)}, u32[]{:S(2)}, u32[]{:S(2)}) collective-permute-start(bf16[8,48,768]{2,1,0:T(8,128)(2,1)S(1)} %get-tuple-element.84), channel_id=1, source_target_pairs={{0,4},{1,5},{2,6},{3,7},{4,0},{5,1},{6,2},{7,3},{8,12},{9,13},{10,... | collective-permute-start | bytes 1769480 | tf_op jit(solution)/shard_map/ppermute | solution.py:765
  54.6 0.7 collective-permute-start.18
  55.4 1.8 %collective-permute-start.9 = (f32[2,1536]{1,0:T(2,128)S(1)}, f32[2,1536]{1,0:T(2,128)S(1)}, u32[]{:S(2)}, u32[]{:S(2)}) collective-permute-start(f32[2,1536]{1,0:T(2,128)S(1)} %add.20.rest_0_.own_ref), channel_id=1, source_target_pairs={{0,8},{1,9},{2,10},{3,11},{4,12},{5,13},{6,14},{7,15},{8,0},{9,1},... | collective-permute-start | bytes 36872 | tf_op jit(solution)/shard_map/ppermute | solution.py:765
  57.2 1.9 %collective-permute-done.9.got_ref = f32[2,1536]{1,0:T(2,128)S(1)} collective-permute-done((f32[2,1536]{1,0:T(2,128)S(1)}, f32[2,1536]{1,0:T(2,128)S(1)}, u32[]{:S(2)}, u32[]{:S(2)}) %collective-permute-start.9) | collective-permute-done | bytes 12320 | tf_op jit(solution)/shard_map/ppermute | solution.py:765
  59.1 2.8 %collective-permute-start.12 = (f32[2,1536]{1,0:T(2,128)S(1)}, f32[2,1536]{1,0:T(2,128)S(1)}, u32[]{:S(2)}, u32[]{:S(2)}) collective-permute-start(f32[2,1536]{1,0:T(2,128)S(1)} %add.21.own_ref), channel_id=1, source_target_pairs={{0,16},{1,17},{2,18},{3,19},{4,20},{5,21},{6,22},{7,23},{8,24},{9,... | collective-permute-start | bytes 36872 | tf_op jit(solution)/shard_map/ppermute | solution.py:765
  61.9 1.8 %collective-permute-done.12.got_ref = f32[2,1536]{1,0:T(2,128)S(1)} collective-permute-done((f32[2,1536]{1,0:T(2,128)S(1)}, f32[2,1536]{1,0:T(2,128)S(1)}, u32[]{:S(2)}, u32[]{:S(2)}) %collective-permute-start.12) | collective-permute-done | bytes 12320 | tf_op jit(solution)/shard_map/ppermute | solution.py:765
  63.7 1.2 %collective-permute-done.13.got_ref = f32[2,1536]{1,0:T(2,128)S(1)} collective-permute-done((f32[2,1536]{1,0:T(2,128)S(1)}, f32[2,1536]{1,0:T(2,128)S(1)}, u32[]{:S(2)}, u32[]{:S(2)}) %collective-permute-start.13) | collective-permute-done | bytes 12320 | tf_op jit(solution)/shard_map/ppermute | solution.py:765
  64.8 7.1 %grad_taps.1 = (bf16[32,1536]{1,0:T(8,128)(2,1)S(1)}, f32[12,2,9,72,128]{4,3,2,1,0:T(8,128)S(1)}, f32[1536]{0:T(1024)}, f32[1536]{0:T(1024)}) custom-call(f32[576,1536]{1,0:T(8,128)S(1)} %get-tuple-element.67.dbn_ref, f32[576,1536]{1,0:T(8,128)S(1)} %get-tuple-element.56.conv_ref, f32[2,1536]{1,0:T(2,128)S(1)} %add.18.sums_ref, ...), custom_call_target="tpu_custom_call" | custom-call | bytes 27000000 | tf_op jit(solution)/shard_map/grad_taps/pallas_call | solution.py:627
  72.0 0.2 collective-permute-start.14
  72.1 0.1 merge.5
  72.2 1.4 %collective-permute-start.21 = (bf16[4,48,768]{2,1,0:T(8,128)(2,1)S(1)}, bf16[4,48,768]{2,1,0:T(8,128)(2,1)S(1)}, u32[]{:S(2)}, u32[]{:S(2)}) collective-permute-start(bf16[4,48,768]{2,1,0:T(8,128)(2,1)S(1)} %get-tuple-element.86), channel_id=1, source_target_pairs={{0,2},{1,3},{2,0},{3,1},{4,6},{5,7},{6,4},{7,5},{8,10},{9,11},{10,... | collective-permute-start | bytes 884744 | tf_op jit(solution)/shard_map/ppermute | solution.py:765
  73.6 0.1 merge.4
  73.7 0.8 collective-permute-start.19
  74.6 2.8 %collective-permute-start.15 = (bf16[32,1536]{1,0:T(8,128)(2,1)S(1)}, bf16[32,1536]{1,0:T(8,128)(2,1)S(1)}, u32[]{:S(2)}, u32[]{:S(2)}) collective-permute-start(bf16[32,1536]{1,0:T(8,128)(2,1)S(1)} %add.24.rest_0_.own_ref), channel_id=1, source_target_pairs={{0,16},{1,17},{2,18},{3,19},{4,20},{5,21},{6,22},{7,23},{8,24},{9,... | collective-permute-start | bytes 294920 | tf_op jit(solution)/shard_map/ppermute | solution.py:765
  77.4 2.7 %grad_proj.3 = (bf16[512,768]{1,0:T(8,128)(2,1)S(1)}, bf16[512,768]{1,0:T(8,128)(2,1)S(1)}) custom-call(f32[12,2,9,72,128]{4,3,2,1,0:T(8,128)S(1)} %get-tuple-element.71.seq_ref, f32[32,1536]{1,0:T(8,128)S(1)} %copy-done.3, bf16[512,1536]{1,0:T(8,128)(2,1)S(1)} %get-tuple-element.72.p_ref, bf16[512,1536]{1,0:T(8,128)(2,1)S(1)} %get-tuple-element.73.q_ref, ...), custom_call_target="tpu_custom_call" | custom-call | bytes 12000000 | tf_op jit(solution)/shard_map/grad_proj/pallas_call | solution.py:680
  80.1 0.0 slice-start.2
  80.1 3.0 %grad_proj.2 = (bf16[512,768]{1,0:T(8,128)(2,1)S(1)}, bf16[512,768]{1,0:T(8,128)(2,1)S(1)}) custom-call(f32[12,2,9,72,128]{4,3,2,1,0:T(8,128)S(1)} %get-tuple-element.71.seq_ref, f32[32,1536]{1,0:T(8,128)S(1)} %copy-done.3, bf16[512,1536]{1,0:T(8,128)(2,1)S(1)} %get-tuple-element.72.p_ref, bf16[512,1536]{1,0:T(8,128)(2,1)S(1)} %get-tuple-element.73.q_ref, ...), custom_call_target="tpu_custom_call" | custom-call | bytes 12000000 | tf_op jit(solution)/shard_map/grad_proj/pallas_call | solution.py:680
  83.1 1.7 %collective-permute-start.16 = (bf16[32,1536]{1,0:T(8,128)(2,1)S(1)}, bf16[32,1536]{1,0:T(8,128)(2,1)S(1)}, u32[]{:S(2)}, u32[]{:S(2)}) collective-permute-start(bf16[32,1536]{1,0:T(8,128)(2,1)S(1)} %add.25.rest_4_.own_ref), channel_id=1, source_target_pairs={{0,8},{1,9},{2,10},{3,11},{4,12},{5,13},{6,14},{7,15},{8,0},{9,1},... | collective-permute-start | bytes 294920 | tf_op jit(solution)/shard_map/ppermute | solution.py:765
  84.8 2.6 %back_proj.2.rest_0_.left_ref = f32[512,768]{1,0:T(8,128)S(1)} custom-call(f32[3,1536]{1,0:T(4,128)S(1)} %get-tuple-element.59.vec_ref, bf16[1536,3072]{1,0:T(8,128)(2,1)S(1)} %bitcast.7, bf16[512,768]{1,0:T(8,128)(2,1)S(1)} %get-tuple-element.75.rest_0_, bf16[512,768]{1,0:T(8,128)(2,1)S(1)} %get-tuple-element.76.rest_1_, ...), custom_call_target="tpu_custom_call" | custom-call | bytes 7800000 | tf_op jit(solution)/shard_map/back_proj/pallas_call | solution.py:712
  87.5 0.4 collective-permute-done.16.got_ref
  87.9 0.1 merge.6
  88.0 1.7 %collective-permute-start.22 = (bf16[2,48,1536]{2,1,0:T(8,128)(2,1)S(1)}, bf16[2,48,1536]{2,1,0:T(8,128)(2,1)S(1)}, u32[]{:S(2)}, u32[]{:S(2)}) collective-permute-start(bf16[2,48,1536]{2,1,0:T(8,128)(2,1)S(1)} %get-tuple-element.88), channel_id=1, source_target_pairs={{0,8},{1,9},{2,10},{3,11},{4,12},{5,13},{6,14},{7,15},{8,0},{9,1},... | collective-permute-start | bytes 884744 | tf_op jit(solution)/shard_map/ppermute | solution.py:765
  89.7 1.2 %collective-permute-start.17 = (bf16[32,1536]{1,0:T(8,128)(2,1)S(1)}, bf16[32,1536]{1,0:T(8,128)(2,1)S(1)}, u32[]{:S(2)}, u32[]{:S(2)}) collective-permute-start(bf16[32,1536]{1,0:T(8,128)(2,1)S(1)} %add.26.rest_4_.own_ref.refs_4_), channel_id=1, source_target_pairs={{0,2},{1,3},{2,0},{3,1},{4,6},{5,7},{6,4},{7,5},{8,10},{9,11},{10,... | collective-permute-start | bytes 294920 | tf_op jit(solution)/shard_map/ppermute | solution.py:765
  90.9 2.6 %back_proj.3.rest_0_.right_ref.refs_2_ = f32[512,768]{1,0:T(8,128)S(1)} custom-call(f32[3,1536]{1,0:T(4,128)S(1)} %get-tuple-element.59.vec_ref, bf16[1536,3072]{1,0:T(8,128)(2,1)S(1)} %bitcast.7, bf16[512,768]{1,0:T(8,128)(2,1)S(1)} %get-tuple-element.75.rest_0_, bf16[512,768]{1,0:T(8,128)(2,1)S(1)} %get-tuple-element.76.rest_1_, ...), custom_call_target="tpu_custom_call" | custom-call | bytes 7800000 | tf_op jit(solution)/shard_map/back_proj/pallas_call | solution.py:712
  93.5 2.3 %collective-permute-done.22.refs_1_ = bf16[2,48,1536]{2,1,0:T(8,128)(2,1)S(1)} collective-permute-done((bf16[2,48,1536]{2,1,0:T(8,128)(2,1)S(1)}, bf16[2,48,1536]{2,1,0:T(8,128)(2,1)S(1)}, u32[]{:S(2)}, u32[]{:S(2)}) %collective-permute-start.22) | collective-permute-done | bytes 294944 | tf_op jit(solution)/shard_map/ppermute | solution.py:765
  95.9 0.1 merge.7
  95.9 2.2 %collective-permute-start.23 = (bf16[1,48,1536]{2,1,0:T(8,128)(2,1)S(1)}, bf16[1,48,1536]{2,1,0:T(8,128)(2,1)S(1)}, u32[]{:S(2)}, u32[]{:S(2)}) collective-permute-start(bf16[1,48,1536]{2,1,0:T(8,128)(2,1)S(1)} %get-tuple-element.90), channel_id=1, source_target_pairs={{0,16},{1,17},{2,18},{3,19},{4,20},{5,21},{6,22},{7,23},{8,24},{9,... | collective-permute-start | bytes 442376 | tf_op jit(solution)/shard_map/ppermute | solution.py:765
  98.1 1.5 %collective-permute-start.24 = (bf16[32,1536]{1,0:T(8,128)(2,1)S(1)}, bf16[32,1536]{1,0:T(8,128)(2,1)S(1)}, u32[]{:S(2)}, u32[]{:S(2)}) collective-permute-start(bf16[32,1536]{1,0:T(8,128)(2,1)S(1)} %add.27.rest_0_.c_ref), channel_id=1, source_target_pairs={{0,4},{1,5},{2,6},{3,7},{4,0},{5,1},{6,2},{7,3},{8,12},{9,13},{10,... | collective-permute-start | bytes 294920 | tf_op jit(solution)/shard_map/ppermute | solution.py:765
  99.6 2.3 %back_norm.1 = (bf16[512,1536]{1,0:T(8,128)(2,1)}, f32[8,128]{1,0:T(8,128)S(1)}) custom-call(bf16[512,1536]{1,0:T(8,128)(2,1)S(1)} %get-tuple-element.65.hat_ref, f32[512,1]{1,0:T(8,128)S(1)} %get-tuple-element.66.rstd_ref, bf16[512,1536]{1,0:T(8,128)(2,1)S(1)} %bitcast.12, f32[512,768]{1,0:T(8,128)S(1)} %back_proj.2.rest_0_.left_ref, ...), custom_call_target="tpu_custom_call" | custom-call | bytes 9000000 | tf_op jit(solution)/shard_map/back_norm/pallas_call | solution.py:751
  101.9 0.9 collective-permute-done.24.d_ref
  102.8 1.0 collective-permute-done.23
  103.8 0.8 last_add.1
  (37 shorter events, 0.2 us)
Async XLA Ops:
  0.6 9.9 %copy-start.3 = (f32[32,1536]{1,0:T(8,128)S(1)}, f32[32,1536]{1,0:T(8,128)}, u32[]{:S(2)}) copy-start(f32[32,1536]{1,0:T(8,128)} %k_ref.7) | copy-start | bytes 589828
  9.1 6.4 %collective-permute-start = (bf16[2,48,1536]{2,1,0:T(8,128)(2,1)S(1)}, bf16[2,48,1536]{2,1,0:T(8,128)(2,1)S(1)}, u32[]{:S(2)}, u32[]{:S(2)}) collective-permute-start(bf16[2,48,1536]{2,1,0:T(8,128)(2,1)S(1)} %get-tuple-element.52), channel_id=1, source_target_pairs={{0,1},{1,0},{2,3},{3,2},{4,5},{5,4},{6,7},{7,6},{8,9},{9,8},{10,11... | collective-permute-start | bytes 884744 | tf_op jit(solution)/shard_map/ppermute | solution.py:765
  9.7 5.9 %collective-permute-start.1 = (bf16[2,48,1536]{2,1,0:T(8,128)(2,1)S(1)}, bf16[2,48,1536]{2,1,0:T(8,128)(2,1)S(1)}, u32[]{:S(2)}, u32[]{:S(2)}) collective-permute-start(bf16[2,48,1536]{2,1,0:T(8,128)(2,1)S(1)} %get-tuple-element.53), channel_id=1, source_target_pairs={{1,2},{2,1},{3,4},{4,3},{5,6},{6,5},{7,8},{8,7},{9,10},{10,9},{11,... | collective-permute-start | bytes 884744 | tf_op jit(solution)/shard_map/ppermute | solution.py:834
  10.5 16.1 %copy-start.1 = (bf16[2,256,1536]{2,1,0:T(8,128)(2,1)S(1)}, bf16[2,256,1536]{2,1,0:T(8,128)(2,1)}, u32[]{:S(2)}) copy-start(bf16[2,256,1536]{2,1,0:T(8,128)(2,1)} %param.15) | copy-start | bytes 4718596
  15.5 11.1 %copy-start = (bf16[1536,1536]{1,0:T(8,128)(2,1)S(1)}, bf16[1536,1536]{1,0:T(8,128)(2,1)}, u32[]{:S(2)}) copy-start(bf16[1536,1536]{1,0:T(8,128)(2,1)} %w_ref.11) | copy-start | bytes 14155780
  17.2 6.3 %collective-permute-start.2 = (f32[2,1536]{1,0:T(2,128)S(1)}, f32[2,1536]{1,0:T(2,128)S(1)}, u32[]{:S(2)}, u32[]{:S(2)}) collective-permute-start(f32[2,1536]{1,0:T(2,128)S(1)} %get-tuple-element.57.own_ref), channel_id=1, source_target_pairs={{0,1},{1,0},{2,3},{3,2},{4,5},{5,4},{6,7},{7,6},{8,9},{9,8},{10,11... | collective-permute-start | bytes 36872 | tf_op jit(solution)/shard_map/ppermute | solution.py:765
  23.5 4.8 %collective-permute-start.3 = (f32[2,1536]{1,0:T(2,128)S(1)}, f32[2,1536]{1,0:T(2,128)S(1)}, u32[]{:S(2)}, u32[]{:S(2)}) collective-permute-start(f32[2,1536]{1,0:T(2,128)S(1)} %add.14.rest_0_.own_ref), channel_id=1, source_target_pairs={{0,2},{1,3},{2,0},{3,1},{4,6},{5,7},{6,4},{7,5},{8,10},{9,11},{10,... | collective-permute-start | bytes 36872 | tf_op jit(solution)/shard_map/ppermute | solution.py:765
  28.3 3.7 %collective-permute-start.4 = (f32[2,1536]{1,0:T(2,128)S(1)}, f32[2,1536]{1,0:T(2,128)S(1)}, u32[]{:S(2)}, u32[]{:S(2)}) collective-permute-start(f32[2,1536]{1,0:T(2,128)S(1)} %add.15.rest_0_.own_ref), channel_id=1, source_target_pairs={{0,4},{1,5},{2,6},{3,7},{4,0},{5,1},{6,2},{7,3},{8,12},{9,13},{10,... | collective-permute-start | bytes 36872 | tf_op jit(solution)/shard_map/ppermute | solution.py:765
  32.0 3.7 %collective-permute-start.5 = (f32[2,1536]{1,0:T(2,128)S(1)}, f32[2,1536]{1,0:T(2,128)S(1)}, u32[]{:S(2)}, u32[]{:S(2)}) collective-permute-start(f32[2,1536]{1,0:T(2,128)S(1)} %add.16.own_ref), channel_id=1, source_target_pairs={{0,8},{1,9},{2,10},{3,11},{4,12},{5,13},{6,14},{7,15},{8,0},{9,1},... | collective-permute-start | bytes 36872 | tf_op jit(solution)/shard_map/ppermute | solution.py:765
  35.7 4.6 %collective-permute-start.6 = (f32[2,1536]{1,0:T(2,128)S(1)}, f32[2,1536]{1,0:T(2,128)S(1)}, u32[]{:S(2)}, u32[]{:S(2)}) collective-permute-start(f32[2,1536]{1,0:T(2,128)S(1)} %add.17.rest_0_.own_ref), channel_id=1, source_target_pairs={{0,16},{1,17},{2,18},{3,19},{4,20},{5,21},{6,22},{7,23},{8,24},{9,... | collective-permute-start | bytes 36872 | tf_op jit(solution)/shard_map/ppermute | solution.py:765
  40.3 4.3 %copy-start.2 = (bf16[2,256,1536]{2,1,0:T(8,128)(2,1)S(1)}, bf16[2,256,1536]{2,1,0:T(8,128)(2,1)}, u32[]{:S(2)}) copy-start(bf16[2,256,1536]{2,1,0:T(8,128)(2,1)} %param.8) | copy-start | bytes 4718596
  42.1 8.6 %collective-permute-start.11 = (bf16[512,1536]{1,0:T(8,128)(2,1)S(1)}, bf16[512,1536]{1,0:T(8,128)(2,1)S(1)}, u32[]{:S(2)}, u32[]{:S(2)}) collective-permute-start(bf16[512,1536]{1,0:T(8,128)(2,1)S(1)} %get-tuple-element.60.act_ref.acta_ref), channel_id=1, source_target_pairs={{0,1},{1,0},{2,3},{3,2},{4,5},{5,4},{6,7},{7,6},{8,9},{9,8},{10,11... | collective-permute-start | bytes 4718600 | tf_op jit(solution)/shard_map/ppermute | solution.py:765
  42.2 8.6 %collective-permute-start.10 = (bf16[16,48,512]{2,1,0:T(8,128)(2,1)S(1)}, bf16[16,48,512]{2,1,0:T(8,128)(2,1)S(1)}, u32[]{:S(2)}, u32[]{:S(2)}) collective-permute-start(bf16[16,48,512]{2,1,0:T(8,128)(2,1)S(1)} %get-tuple-element.69), channel_id=1, source_target_pairs={{0,1},{1,0},{2,3},{3,2},{4,5},{5,4},{6,7},{7,6},{8,9},{9,8},{10,11... | collective-permute-start | bytes 2359304 | tf_op jit(solution)/shard_map/ppermute | solution.py:765
  42.7 4.3 %collective-permute-start.7 = (f32[2,1536]{1,0:T(2,128)S(1)}, f32[2,1536]{1,0:T(2,128)S(1)}, u32[]{:S(2)}, u32[]{:S(2)}) collective-permute-start(f32[2,1536]{1,0:T(2,128)S(1)} %get-tuple-element.61.rest_0_.own_ref), channel_id=1, source_target_pairs={{0,2},{1,3},{2,0},{3,1},{4,6},{5,7},{6,4},{7,5},{8,10},{9,11},{10,... | collective-permute-start | bytes 36872 | tf_op jit(solution)/shard_map/ppermute | solution.py:765
  46.9 3.8 %collective-permute-start.8 = (f32[2,1536]{1,0:T(2,128)S(1)}, f32[2,1536]{1,0:T(2,128)S(1)}, u32[]{:S(2)}, u32[]{:S(2)}) collective-permute-start(f32[2,1536]{1,0:T(2,128)S(1)} %add.19.rest_1_.own_ref), channel_id=1, source_target_pairs={{0,4},{1,5},{2,6},{3,7},{4,0},{5,1},{6,2},{7,3},{8,12},{9,13},{10,... | collective-permute-start | bytes 36872 | tf_op jit(solution)/shard_map/ppermute | solution.py:765
  53.3 18.8 %collective-permute-start.20 = (bf16[8,48,768]{2,1,0:T(8,128)(2,1)S(1)}, bf16[8,48,768]{2,1,0:T(8,128)(2,1)S(1)}, u32[]{:S(2)}, u32[]{:S(2)}) collective-permute-start(bf16[8,48,768]{2,1,0:T(8,128)(2,1)S(1)} %get-tuple-element.84), channel_id=1, source_target_pairs={{0,4},{1,5},{2,6},{3,7},{4,0},{5,1},{6,2},{7,3},{8,12},{9,13},{10,... | collective-permute-start | bytes 1769480 | tf_op jit(solution)/shard_map/ppermute | solution.py:765
  54.6 19.0 %collective-permute-start.18 = (bf16[8,48,768]{2,1,0:T(8,128)(2,1)S(1)}, bf16[8,48,768]{2,1,0:T(8,128)(2,1)S(1)}, u32[]{:S(2)}, u32[]{:S(2)}) collective-permute-start(bf16[8,48,768]{2,1,0:T(8,128)(2,1)S(1)} %get-tuple-element.70.rest_0_), channel_id=1, source_target_pairs={{0,2},{1,3},{2,0},{3,1},{4,6},{5,7},{6,4},{7,5},{8,10},{9,11},{10,... | collective-permute-start | bytes 1769480 | tf_op jit(solution)/shard_map/ppermute | solution.py:765
  55.4 3.7 %collective-permute-start.9 = (f32[2,1536]{1,0:T(2,128)S(1)}, f32[2,1536]{1,0:T(2,128)S(1)}, u32[]{:S(2)}, u32[]{:S(2)}) collective-permute-start(f32[2,1536]{1,0:T(2,128)S(1)} %add.20.rest_0_.own_ref), channel_id=1, source_target_pairs={{0,8},{1,9},{2,10},{3,11},{4,12},{5,13},{6,14},{7,15},{8,0},{9,1},... | collective-permute-start | bytes 36872 | tf_op jit(solution)/shard_map/ppermute | solution.py:765
  59.1 4.6 %collective-permute-start.12 = (f32[2,1536]{1,0:T(2,128)S(1)}, f32[2,1536]{1,0:T(2,128)S(1)}, u32[]{:S(2)}, u32[]{:S(2)}) collective-permute-start(f32[2,1536]{1,0:T(2,128)S(1)} %add.21.own_ref), channel_id=1, source_target_pairs={{0,16},{1,17},{2,18},{3,19},{4,20},{5,21},{6,22},{7,23},{8,24},{9,... | collective-permute-start | bytes 36872 | tf_op jit(solution)/shard_map/ppermute | solution.py:765
  63.7 1.2 %collective-permute-start.13 = (f32[2,1536]{1,0:T(2,128)S(1)}, f32[2,1536]{1,0:T(2,128)S(1)}, u32[]{:S(2)}, u32[]{:S(2)}) collective-permute-start(f32[2,1536]{1,0:T(2,128)S(1)} %add.22.own_ref), channel_id=1, source_target_pairs={{0,1},{1,0},{2,3},{3,2},{4,5},{5,4},{6,7},{7,6},{8,9},{9,8},{10,11... | collective-permute-start | bytes 36872 | tf_op jit(solution)/shard_map/ppermute | solution.py:765
  72.0 2.6 %collective-permute-start.14 = (bf16[32,1536]{1,0:T(8,128)(2,1)S(1)}, bf16[32,1536]{1,0:T(8,128)(2,1)S(1)}, u32[]{:S(2)}, u32[]{:S(2)}) collective-permute-start(bf16[32,1536]{1,0:T(8,128)(2,1)S(1)} %get-tuple-element.74.own_ref), channel_id=1, source_target_pairs={{0,1},{1,0},{2,3},{3,2},{4,5},{5,4},{6,7},{7,6},{8,9},{9,8},{10,11... | collective-permute-start | bytes 294920 | tf_op jit(solution)/shard_map/ppermute | solution.py:765
  72.2 15.6 %collective-permute-start.21 = (bf16[4,48,768]{2,1,0:T(8,128)(2,1)S(1)}, bf16[4,48,768]{2,1,0:T(8,128)(2,1)S(1)}, u32[]{:S(2)}, u32[]{:S(2)}) collective-permute-start(bf16[4,48,768]{2,1,0:T(8,128)(2,1)S(1)} %get-tuple-element.86), channel_id=1, source_target_pairs={{0,2},{1,3},{2,0},{3,1},{4,6},{5,7},{6,4},{7,5},{8,10},{9,11},{10,... | collective-permute-start | bytes 884744 | tf_op jit(solution)/shard_map/ppermute | solution.py:765
  73.7 14.2 %collective-permute-start.19 = (bf16[4,48,768]{2,1,0:T(8,128)(2,1)S(1)}, bf16[4,48,768]{2,1,0:T(8,128)(2,1)S(1)}, u32[]{:S(2)}, u32[]{:S(2)}) collective-permute-start(bf16[4,48,768]{2,1,0:T(8,128)(2,1)S(1)} %get-tuple-element.82), channel_id=1, source_target_pairs={{0,4},{1,5},{2,6},{3,7},{4,0},{5,1},{6,2},{7,3},{8,12},{9,13},{10,... | collective-permute-start | bytes 884744 | tf_op jit(solution)/shard_map/ppermute | solution.py:765
  74.6 8.5 %collective-permute-start.15 = (bf16[32,1536]{1,0:T(8,128)(2,1)S(1)}, bf16[32,1536]{1,0:T(8,128)(2,1)S(1)}, u32[]{:S(2)}, u32[]{:S(2)}) collective-permute-start(bf16[32,1536]{1,0:T(8,128)(2,1)S(1)} %add.24.rest_0_.own_ref), channel_id=1, source_target_pairs={{0,16},{1,17},{2,18},{3,19},{4,20},{5,21},{6,22},{7,23},{8,24},{9,... | collective-permute-start | bytes 294920 | tf_op jit(solution)/shard_map/ppermute | solution.py:765
  77.4 7.4 %slice-start = ((s8[9437184]{0:T(1024)(128)(4,1)}), s8[4194304]{0:T(1024)(128)(4,1)S(1)}, s32[]{:S(2)}) async-start(s8[9437184]{0:T(1024)(128)(4,1)} %bitcast.6), calls=%async_computation | async-start | bytes 8388608
  77.4 7.4 %slice-start.1 = ((s8[9437184]{0:T(1024)(128)(4,1)}), s8[4194304]{0:T(1024)(128)(4,1)S(1)}, s32[]{:S(2)}) async-start(s8[9437184]{0:T(1024)(128)(4,1)} %bitcast.6), calls=%async_computation.1 | async-start | bytes 8388608
  80.1 4.7 %slice-start.2 = ((s8[9437184]{0:T(1024)(128)(4,1)}), s8[1048576]{0:T(1024)(128)(4,1)S(1)}, s32[]{:S(2)}) async-start(s8[9437184]{0:T(1024)(128)(4,1)} %bitcast.6), calls=%async_computation.2 | async-start | bytes 2097152
  83.1 4.7 %collective-permute-start.16 = (bf16[32,1536]{1,0:T(8,128)(2,1)S(1)}, bf16[32,1536]{1,0:T(8,128)(2,1)S(1)}, u32[]{:S(2)}, u32[]{:S(2)}) collective-permute-start(bf16[32,1536]{1,0:T(8,128)(2,1)S(1)} %add.25.rest_4_.own_ref), channel_id=1, source_target_pairs={{0,8},{1,9},{2,10},{3,11},{4,12},{5,13},{6,14},{7,15},{8,0},{9,1},... | collective-permute-start | bytes 294920 | tf_op jit(solution)/shard_map/ppermute | solution.py:765
  88.0 7.9 %collective-permute-start.22 = (bf16[2,48,1536]{2,1,0:T(8,128)(2,1)S(1)}, bf16[2,48,1536]{2,1,0:T(8,128)(2,1)S(1)}, u32[]{:S(2)}, u32[]{:S(2)}) collective-permute-start(bf16[2,48,1536]{2,1,0:T(8,128)(2,1)S(1)} %get-tuple-element.88), channel_id=1, source_target_pairs={{0,8},{1,9},{2,10},{3,11},{4,12},{5,13},{6,14},{7,15},{8,0},{9,1},... | collective-permute-start | bytes 884744 | tf_op jit(solution)/shard_map/ppermute | solution.py:765
  89.7 8.4 %collective-permute-start.17 = (bf16[32,1536]{1,0:T(8,128)(2,1)S(1)}, bf16[32,1536]{1,0:T(8,128)(2,1)S(1)}, u32[]{:S(2)}, u32[]{:S(2)}) collective-permute-start(bf16[32,1536]{1,0:T(8,128)(2,1)S(1)} %add.26.rest_4_.own_ref.refs_4_), channel_id=1, source_target_pairs={{0,2},{1,3},{2,0},{3,1},{4,6},{5,7},{6,4},{7,5},{8,10},{9,11},{10,... | collective-permute-start | bytes 294920 | tf_op jit(solution)/shard_map/ppermute | solution.py:765
  95.9 7.9 %collective-permute-start.23 = (bf16[1,48,1536]{2,1,0:T(8,128)(2,1)S(1)}, bf16[1,48,1536]{2,1,0:T(8,128)(2,1)S(1)}, u32[]{:S(2)}, u32[]{:S(2)}) collective-permute-start(bf16[1,48,1536]{2,1,0:T(8,128)(2,1)S(1)} %get-tuple-element.90), channel_id=1, source_target_pairs={{0,16},{1,17},{2,18},{3,19},{4,20},{5,21},{6,22},{7,23},{8,24},{9,... | collective-permute-start | bytes 442376 | tf_op jit(solution)/shard_map/ppermute | solution.py:765
  98.1 4.7 %collective-permute-start.24 = (bf16[32,1536]{1,0:T(8,128)(2,1)S(1)}, bf16[32,1536]{1,0:T(8,128)(2,1)S(1)}, u32[]{:S(2)}, u32[]{:S(2)}) collective-permute-start(bf16[32,1536]{1,0:T(8,128)(2,1)S(1)} %add.27.rest_0_.c_ref), channel_id=1, source_target_pairs={{0,4},{1,5},{2,6},{3,7},{4,0},{5,1},{6,2},{7,3},{8,12},{9,13},{10,... | collective-permute-start | bytes 294920 | tf_op jit(solution)/shard_map/ppermute | solution.py:765

commit v7 on v6

--- a/solution.py
+++ b/solution.py
@@ -667,7 +667,7 @@
             )
             for i, y in assembled(products):
                 out_ref[slot, phase(u * frames + i, count), :] = y
-        acc = out_ref[slot]
+        acc = out_ref[slot, 0:rows, :]
         dv_ref[:, out] = (acc * p_ref[:, lanes].astype(F32)).astype(BF)
         dg_ref[:, out] = (acc * q_ref[:, lanes].astype(F32)).astype(BF)
 
@@ -683,7 +683,7 @@
         out_specs=[WHOLE] * 2,
         out_shape=[out, out],
         scratch_shapes=[
-            pltpu.VMEM((2, rows, LANES), F32),
+            pltpu.VMEM((2, rows + 8, LANES), F32),
             pltpu.VMEM((2, PIECES, kernel.shape[0] // PHASES, LANES), F32),
         ],
         compiler_params=params(VMEM_MIB),

time: 105 us -> 105 us (level)
  no operation moved by 1% of the time
where the time goes in v7:
time: 105 us
  Pallas kernels  49.9 us (48%)
  starting transfers between devices  40.3 us (38%)
  waiting for transfers between devices  13.4 us (13%)
    ppermute x24, starting transfers between devices, swap(): return lax.ppermute(block, axis, [(i, i ^ bit) for i in range(count)])  39.5 us
    ppermute x24, waiting for transfers between devices, swap(): return lax.ppermute(block, axis, [(i, i ^ bit) for i in range(count)])  13.4 us
    pallas_call x1, Pallas kernels, front(): pl.pallas_call(functools.partial(front_body, utt), in_specs=[FAR] * 6, ou...  8.49 us
    pallas_call x1, Pallas kernels, grad_taps(): pl.pallas_call(functools.partial(grad_taps_body, utt, total), in_specs=[W...  7.11 us
    pallas_call x2, Pallas kernels, grad_proj(): pl.pallas_call(functools.partial(grad_proj_body, utt, start), in_specs=[W...  5.69 us
    pallas_call x2, Pallas kernels, back_proj(): pl.pallas_call(functools.partial(back_proj_body, start), in_specs=[WHOLE]...  5.28 us
    pallas_call x1, Pallas kernels, conv_mid(): pl.pallas_call(functools.partial(conv_mid_body, utt), in_specs=[WHOLE] *...  4.97 us
    pallas_call x2, Pallas kernels, branch(): pl.pallas_call(functools.partial(branch_body, start), in_specs=[WHOLE] *...  4.46 us
  transfers between devices with their start and end apart: 25, of which 13 were waited for; matrix products, arithmetic and copies ran while one was open for 0% of the time, Pallas kernels for 33%

profile of v7, /device:TPU:0, one launch (start us, length us, event | category | flops | bytes accessed | tf_op | source)
XLA Modules:
  0.0 104.6 jit_solution(10409650981175828586)
XLA Ops:
  0.6 8.5 %front.1 = (bf16[512,1536]{1,0:T(8,128)(2,1)S(1)}, bf16[512,1536]{1,0:T(8,128)(2,1)S(1)}, bf16[512,1536]{1,0:T(8,128)(2,1)S(1)}, bf16[512,1536]{1,0:T(8,128)(2,1...) custom-call(bf16[512,1536]{1,0:T(8,128)(2,1)} %bitcast.13, ...), custom_call_target="tpu_custom_call" | custom-call | bytes 30000000 | tf_op jit(solution)/shard_map/front/pallas_call | solution.py:189
  9.1 0.5 collective-permute-start
  9.7 0.8 collective-permute-start.1
  10.5 0.0 copy-start.1
  10.5 5.0 %conv_mid.1 = (f32[576,1536]{1,0:T(8,128)S(1)}, f32[2,1536]{1,0:T(2,128)S(1)}) custom-call(bf16[512,1536]{1,0:T(8,128)(2,1)S(1)} %get-tuple-element.51.g_ref, f32[32,1536]{1,0:T(8,128)S(1)} %copy-done.3), custom_call_target="tpu_custom_call" | custom-call | bytes 15000000 | tf_op jit(solution)/shard_map/conv_mid/pallas_call | solution.py:330
  15.5 0.0 collective-permute-done.1.b_ref
  15.5 0.0 copy-start
  15.5 1.6 %conv_end.1 = (f32[576,1536]{1,0:T(8,128)S(1)}, f32[2,1536]{1,0:T(2,128)S(1)}) custom-call(bf16[512,1536]{1,0:T(8,128)(2,1)S(1)} %get-tuple-element.51.g_ref, bf16[2,48,1536]{2,1,0:T(8,128)(2,1)S(1)} %collective-permute-done.a_ref, bf16[2,48,1536]{2,1,0:T(8,128)(2,1)S(1)} %collective-permute-done.1.b_ref, ...), custom_call_target="tpu_custom_call", output_to_operand_aliasing={{0}: (4, {})} | custom-call | bytes 6000000 | tf_op jit(solution)/shard_map/conv_end/pallas_call | solution.py:384
  17.2 5.5 %collective-permute-start.2 = (f32[2,1536]{1,0:T(2,128)S(1)}, f32[2,1536]{1,0:T(2,128)S(1)}, u32[]{:S(2)}, u32[]{:S(2)}) collective-permute-start(f32[2,1536]{1,0:T(2,128)S(1)} %get-tuple-element.57.own_ref), channel_id=1, source_target_pairs={{0,1},{1,0},{2,3},{3,2},{4,5},{5,4},{6,7},{7,6},{8,9},{9,8},{10,11... | collective-permute-start | bytes 36872 | tf_op jit(solution)/shard_map/ppermute | solution.py:765
  22.7 0.8 collective-permute-done.2.got_ref
  23.5 3.1 %collective-permute-start.3 = (f32[2,1536]{1,0:T(2,128)S(1)}, f32[2,1536]{1,0:T(2,128)S(1)}, u32[]{:S(2)}, u32[]{:S(2)}) collective-permute-start(f32[2,1536]{1,0:T(2,128)S(1)} %add.14.rest_0_.own_ref), channel_id=1, source_target_pairs={{0,2},{1,3},{2,0},{3,1},{4,6},{5,7},{6,4},{7,5},{8,10},{9,11},{10,... | collective-permute-start | bytes 36872 | tf_op jit(solution)/shard_map/ppermute | solution.py:765
  26.7 1.4 %act_grad.2.rest_0_.left_ref = f32[512,768]{1,0:T(8,128)S(1)} custom-call(bf16[512,1536]{1,0:T(8,128)(2,1)S(1)} %bitcast.9, bf16[1536,1536]{1,0:T(8,128)(2,1)S(1)} %copy-done, f32[2,1536]{1,0:T(2,128)S(1)} %add.14.rest_0_.own_ref), custom_call_target="tpu_custom_call" | custom-call | bytes 4500000 | tf_op jit(solution)/shard_map/act_grad/pallas_call | solution.py:406
  28.1 0.3 collective-permute-done.3.got_ref
  28.3 1.6 %collective-permute-start.4 = (f32[2,1536]{1,0:T(2,128)S(1)}, f32[2,1536]{1,0:T(2,128)S(1)}, u32[]{:S(2)}, u32[]{:S(2)}) collective-permute-start(f32[2,1536]{1,0:T(2,128)S(1)} %add.15.rest_0_.own_ref), channel_id=1, source_target_pairs={{0,4},{1,5},{2,6},{3,7},{4,0},{5,1},{6,2},{7,3},{8,12},{9,13},{10,... | collective-permute-start | bytes 36872 | tf_op jit(solution)/shard_map/ppermute | solution.py:765
  30.0 1.4 %act_grad.3.rest_0_.right_ref = f32[512,768]{1,0:T(8,128)S(1)} custom-call(bf16[512,1536]{1,0:T(8,128)(2,1)S(1)} %bitcast.10, bf16[1536,1536]{1,0:T(8,128)(2,1)S(1)} %copy-done, f32[2,1536]{1,0:T(2,128)S(1)} %add.15.rest_0_.own_ref), custom_call_target="tpu_custom_call" | custom-call | bytes 4500000 | tf_op jit(solution)/shard_map/act_grad/pallas_call | solution.py:406
  31.3 0.7 collective-permute-done.4.got_ref
  32.0 1.8 %collective-permute-start.5 = (f32[2,1536]{1,0:T(2,128)S(1)}, f32[2,1536]{1,0:T(2,128)S(1)}, u32[]{:S(2)}, u32[]{:S(2)}) collective-permute-start(f32[2,1536]{1,0:T(2,128)S(1)} %add.16.own_ref), channel_id=1, source_target_pairs={{0,8},{1,9},{2,10},{3,11},{4,12},{5,13},{6,14},{7,15},{8,0},{9,1},... | collective-permute-start | bytes 36872 | tf_op jit(solution)/shard_map/ppermute | solution.py:765
  33.8 1.9 %collective-permute-done.5.got_ref = f32[2,1536]{1,0:T(2,128)S(1)} collective-permute-done((f32[2,1536]{1,0:T(2,128)S(1)}, f32[2,1536]{1,0:T(2,128)S(1)}, u32[]{:S(2)}, u32[]{:S(2)}) %collective-permute-start.5) | collective-permute-done | bytes 12320 | tf_op jit(solution)/shard_map/ppermute | solution.py:765
  35.7 2.9 %collective-permute-start.6 = (f32[2,1536]{1,0:T(2,128)S(1)}, f32[2,1536]{1,0:T(2,128)S(1)}, u32[]{:S(2)}, u32[]{:S(2)}) collective-permute-start(f32[2,1536]{1,0:T(2,128)S(1)} %add.17.rest_0_.own_ref), channel_id=1, source_target_pairs={{0,16},{1,17},{2,18},{3,19},{4,20},{5,21},{6,22},{7,23},{8,24},{9,... | collective-permute-start | bytes 36872 | tf_op jit(solution)/shard_map/ppermute | solution.py:765
  38.7 0.6 turn.1
  39.3 0.9 act_grad_end.1.rest_0_.end_ref
  40.2 0.2 collective-permute-done.6.got_ref
  40.3 1.7 %middle.1 = (bf16[512,1536]{1,0:T(8,128)(2,1)S(1)}, f32[576,1536]{1,0:T(8,128)S(1)}, f32[2,1536]{1,0:T(2,128)S(1)}) custom-call(f32[576,1536]{1,0:T(8,128)S(1)} %get-tuple-element.56.conv_ref, f32[2,1536]{1,0:T(2,128)S(1)} %add.18.sums_ref, f32[3,1536]{1,0:T(4,128)S(1)} %get-tuple-element.59.vec_ref, f32[512,768]{1,0:T(8,128)S(1)} %act_grad.2.rest_0_.left_ref, ...), custom_call_target="tpu_custom_call" | custom-call | bytes 9000000 | tf_op jit(solution)/shard_map/middle/pallas_call | solution.py:484
  42.1 0.1 collective-permute-start.11
  42.2 0.5 collective-permute-start.10
  42.7 2.0 %collective-permute-start.7 = (f32[2,1536]{1,0:T(2,128)S(1)}, f32[2,1536]{1,0:T(2,128)S(1)}, u32[]{:S(2)}, u32[]{:S(2)}) collective-permute-start(f32[2,1536]{1,0:T(2,128)S(1)} %get-tuple-element.61.rest_0_.own_ref), channel_id=1, source_target_pairs={{0,2},{1,3},{2,0},{3,1},{4,6},{5,7},{6,4},{7,5},{8,10},{9,11},{10,... | collective-permute-start | bytes 36872 | tf_op jit(solution)/shard_map/ppermute | solution.py:765
  44.7 2.2 %branch.2 = (bf16[512,1536]{1,0:T(8,128)(2,1)}, f32[8,128]{1,0:T(8,128)S(1)}) custom-call(bf16[512,1536]{1,0:T(8,128)(2,1)S(1)} %bitcast.14, bf16[512,1536]{1,0:T(8,128)(2,1)S(1)} %get-tuple-element.60.act_ref.acta_ref, bf16[1536,1536]{1,0:T(8,128)(2,1)S(1)} %copy-done, f32[2,1536]{1,0:T(2,128)S(1)} %get-tuple-element.61.rest_0_.own_ref), custom_call_target="tpu_custom_call" | custom-call | bytes 6000000 | tf_op jit(solution)/shard_map/branch/pallas_call | solution.py:553
  46.9 0.0 collective-permute-done.7.got_ref
  46.9 1.3 %collective-permute-start.8 = (f32[2,1536]{1,0:T(2,128)S(1)}, f32[2,1536]{1,0:T(2,128)S(1)}, u32[]{:S(2)}, u32[]{:S(2)}) collective-permute-start(f32[2,1536]{1,0:T(2,128)S(1)} %add.19.rest_1_.own_ref), channel_id=1, source_target_pairs={{0,4},{1,5},{2,6},{3,7},{4,0},{5,1},{6,2},{7,3},{8,12},{9,13},{10,... | collective-permute-start | bytes 36872 | tf_op jit(solution)/shard_map/ppermute | solution.py:765
  48.2 2.2 %branch.3 = (bf16[512,1536]{1,0:T(8,128)(2,1)}, f32[8,128]{1,0:T(8,128)S(1)}) custom-call(bf16[512,1536]{1,0:T(8,128)(2,1)S(1)} %bitcast.15, bf16[512,1536]{1,0:T(8,128)(2,1)S(1)} %get-tuple-element.60.act_ref.acta_ref, bf16[1536,1536]{1,0:T(8,128)(2,1)S(1)} %copy-done, ...), custom_call_target="tpu_custom_call", output_to_operand_aliasing={{0}: (3, {})} | custom-call | bytes 6000000 | tf_op jit(solution)/shard_map/branch/pallas_call | solution.py:553
  50.5 0.2 collective-permute-done.8.got_ref
  50.7 2.6 %grad.1 = (bf16[8,48,768]{2,1,0:T(8,128)(2,1)S(1)}, f32[8,48,768]{2,1,0:T(8,128)S(1)}, bf16[8,48,768]{2,1,0:T(8,128)(2,1)S(1)}, f32[8,48,768]{2,1,0:T(8,128)S(1)}) custom-call(bf16[16,48,512]{2,1,0:T(8,128)(2,1)S(1)} %get-tuple-element.58.rest_1_.ca_ref, bf16[16,48,512]{2,1,0:T(8,128)(2,1)S(1)} %collective-permute-done.10.cb_ref, ...), custom_call_target="tpu_custom_call" | custom-call | bytes 10500000 | tf_op jit(solution)/shard_map/grad/pallas_call | solution.py:523
  53.3 1.3 %collective-permute-start.20 = (bf16[8,48,768]{2,1,0:T(8,128)(2,1)S(1)}, bf16[8,48,768]{2,1,0:T(8,128)(2,1)S(1)}, u32[]{:S(2)}, u32[]{:S(2)}) collective-permute-start(bf16[8,48,768]{2,1,0:T(8,128)(2,1)S(1)} %get-tuple-element.84), channel_id=1, source_target_pairs={{0,4},{1,5},{2,6},{3,7},{4,0},{5,1},{6,2},{7,3},{8,12},{9,13},{10,... | collective-permute-start | bytes 1769480 | tf_op jit(solution)/shard_map/ppermute | solution.py:765
  54.6 0.7 collective-permute-start.18
  55.4 1.8 %collective-permute-start.9 = (f32[2,1536]{1,0:T(2,128)S(1)}, f32[2,1536]{1,0:T(2,128)S(1)}, u32[]{:S(2)}, u32[]{:S(2)}) collective-permute-start(f32[2,1536]{1,0:T(2,128)S(1)} %add.20.rest_0_.own_ref), channel_id=1, source_target_pairs={{0,8},{1,9},{2,10},{3,11},{4,12},{5,13},{6,14},{7,15},{8,0},{9,1},... | collective-permute-start | bytes 36872 | tf_op jit(solution)/shard_map/ppermute | solution.py:765
  57.2 1.9 %collective-permute-done.9.got_ref = f32[2,1536]{1,0:T(2,128)S(1)} collective-permute-done((f32[2,1536]{1,0:T(2,128)S(1)}, f32[2,1536]{1,0:T(2,128)S(1)}, u32[]{:S(2)}, u32[]{:S(2)}) %collective-permute-start.9) | collective-permute-done | bytes 12320 | tf_op jit(solution)/shard_map/ppermute | solution.py:765
  59.1 2.8 %collective-permute-start.12 = (f32[2,1536]{1,0:T(2,128)S(1)}, f32[2,1536]{1,0:T(2,128)S(1)}, u32[]{:S(2)}, u32[]{:S(2)}) collective-permute-start(f32[2,1536]{1,0:T(2,128)S(1)} %add.21.own_ref), channel_id=1, source_target_pairs={{0,16},{1,17},{2,18},{3,19},{4,20},{5,21},{6,22},{7,23},{8,24},{9,... | collective-permute-start | bytes 36872 | tf_op jit(solution)/shard_map/ppermute | solution.py:765
  61.9 1.8 %collective-permute-done.12.got_ref = f32[2,1536]{1,0:T(2,128)S(1)} collective-permute-done((f32[2,1536]{1,0:T(2,128)S(1)}, f32[2,1536]{1,0:T(2,128)S(1)}, u32[]{:S(2)}, u32[]{:S(2)}) %collective-permute-start.12) | collective-permute-done | bytes 12320 | tf_op jit(solution)/shard_map/ppermute | solution.py:765
  63.7 1.2 %collective-permute-done.13.got_ref = f32[2,1536]{1,0:T(2,128)S(1)} collective-permute-done((f32[2,1536]{1,0:T(2,128)S(1)}, f32[2,1536]{1,0:T(2,128)S(1)}, u32[]{:S(2)}, u32[]{:S(2)}) %collective-permute-start.13) | collective-permute-done | bytes 12320 | tf_op jit(solution)/shard_map/ppermute | solution.py:765
  64.8 7.1 %grad_taps.1 = (bf16[32,1536]{1,0:T(8,128)(2,1)S(1)}, f32[12,2,9,72,128]{4,3,2,1,0:T(8,128)S(1)}, f32[1536]{0:T(1024)}, f32[1536]{0:T(1024)}) custom-call(f32[576,1536]{1,0:T(8,128)S(1)} %get-tuple-element.67.dbn_ref, f32[576,1536]{1,0:T(8,128)S(1)} %get-tuple-element.56.conv_ref, f32[2,1536]{1,0:T(2,128)S(1)} %add.18.sums_ref, ...), custom_call_target="tpu_custom_call" | custom-call | bytes 27000000 | tf_op jit(solution)/shard_map/grad_taps/pallas_call | solution.py:627
  72.0 0.2 collective-permute-start.14
  72.1 0.1 merge.5
  72.2 1.4 %collective-permute-start.21 = (bf16[4,48,768]{2,1,0:T(8,128)(2,1)S(1)}, bf16[4,48,768]{2,1,0:T(8,128)(2,1)S(1)}, u32[]{:S(2)}, u32[]{:S(2)}) collective-permute-start(bf16[4,48,768]{2,1,0:T(8,128)(2,1)S(1)} %get-tuple-element.86), channel_id=1, source_target_pairs={{0,2},{1,3},{2,0},{3,1},{4,6},{5,7},{6,4},{7,5},{8,10},{9,11},{10,... | collective-permute-start | bytes 884744 | tf_op jit(solution)/shard_map/ppermute | solution.py:765
  73.6 0.1 merge.4
  73.7 0.8 collective-permute-start.19
  74.6 2.8 %collective-permute-start.15 = (bf16[32,1536]{1,0:T(8,128)(2,1)S(1)}, bf16[32,1536]{1,0:T(8,128)(2,1)S(1)}, u32[]{:S(2)}, u32[]{:S(2)}) collective-permute-start(bf16[32,1536]{1,0:T(8,128)(2,1)S(1)} %add.24.rest_0_.own_ref), channel_id=1, source_target_pairs={{0,16},{1,17},{2,18},{3,19},{4,20},{5,21},{6,22},{7,23},{8,24},{9,... | collective-permute-start | bytes 294920 | tf_op jit(solution)/shard_map/ppermute | solution.py:765
  77.4 2.7 %grad_proj.3 = (bf16[512,768]{1,0:T(8,128)(2,1)S(1)}, bf16[512,768]{1,0:T(8,128)(2,1)S(1)}) custom-call(f32[12,2,9,72,128]{4,3,2,1,0:T(8,128)S(1)} %get-tuple-element.71.seq_ref, f32[32,1536]{1,0:T(8,128)S(1)} %copy-done.3, bf16[512,1536]{1,0:T(8,128)(2,1)S(1)} %get-tuple-element.72.p_ref, bf16[512,1536]{1,0:T(8,128)(2,1)S(1)} %get-tuple-element.73.q_ref, ...), custom_call_target="tpu_custom_call" | custom-call | bytes 12000000 | tf_op jit(solution)/shard_map/grad_proj/pallas_call | solution.py:680
  80.1 0.0 slice-start.2
  80.1 2.9 %grad_proj.2 = (bf16[512,768]{1,0:T(8,128)(2,1)S(1)}, bf16[512,768]{1,0:T(8,128)(2,1)S(1)}) custom-call(f32[12,2,9,72,128]{4,3,2,1,0:T(8,128)S(1)} %get-tuple-element.71.seq_ref, f32[32,1536]{1,0:T(8,128)S(1)} %copy-done.3, bf16[512,1536]{1,0:T(8,128)(2,1)S(1)} %get-tuple-element.72.p_ref, bf16[512,1536]{1,0:T(8,128)(2,1)S(1)} %get-tuple-element.73.q_ref, ...), custom_call_target="tpu_custom_call" | custom-call | bytes 12000000 | tf_op jit(solution)/shard_map/grad_proj/pallas_call | solution.py:680
  83.1 1.7 %collective-permute-start.16 = (bf16[32,1536]{1,0:T(8,128)(2,1)S(1)}, bf16[32,1536]{1,0:T(8,128)(2,1)S(1)}, u32[]{:S(2)}, u32[]{:S(2)}) collective-permute-start(bf16[32,1536]{1,0:T(8,128)(2,1)S(1)} %add.25.rest_4_.own_ref), channel_id=1, source_target_pairs={{0,8},{1,9},{2,10},{3,11},{4,12},{5,13},{6,14},{7,15},{8,0},{9,1},... | collective-permute-start | bytes 294920 | tf_op jit(solution)/shard_map/ppermute | solution.py:765
  84.8 2.6 %back_proj.2.rest_0_.left_ref = f32[512,768]{1,0:T(8,128)S(1)} custom-call(f32[3,1536]{1,0:T(4,128)S(1)} %get-tuple-element.59.vec_ref, bf16[1536,3072]{1,0:T(8,128)(2,1)S(1)} %bitcast.7, bf16[512,768]{1,0:T(8,128)(2,1)S(1)} %get-tuple-element.75.rest_0_, bf16[512,768]{1,0:T(8,128)(2,1)S(1)} %get-tuple-element.76.rest_1_, ...), custom_call_target="tpu_custom_call" | custom-call | bytes 7800000 | tf_op jit(solution)/shard_map/back_proj/pallas_call | solution.py:712
  87.5 0.4 collective-permute-done.16.got_ref
  87.9 0.1 merge.6
  88.0 1.7 %collective-permute-start.22 = (bf16[2,48,1536]{2,1,0:T(8,128)(2,1)S(1)}, bf16[2,48,1536]{2,1,0:T(8,128)(2,1)S(1)}, u32[]{:S(2)}, u32[]{:S(2)}) collective-permute-start(bf16[2,48,1536]{2,1,0:T(8,128)(2,1)S(1)} %get-tuple-element.88), channel_id=1, source_target_pairs={{0,8},{1,9},{2,10},{3,11},{4,12},{5,13},{6,14},{7,15},{8,0},{9,1},... | collective-permute-start | bytes 884744 | tf_op jit(solution)/shard_map/ppermute | solution.py:765
  89.6 1.2 %collective-permute-start.17 = (bf16[32,1536]{1,0:T(8,128)(2,1)S(1)}, bf16[32,1536]{1,0:T(8,128)(2,1)S(1)}, u32[]{:S(2)}, u32[]{:S(2)}) collective-permute-start(bf16[32,1536]{1,0:T(8,128)(2,1)S(1)} %add.26.rest_4_.own_ref.refs_4_), channel_id=1, source_target_pairs={{0,2},{1,3},{2,0},{3,1},{4,6},{5,7},{6,4},{7,5},{8,10},{9,11},{10,... | collective-permute-start | bytes 294920 | tf_op jit(solution)/shard_map/ppermute | solution.py:765
  90.9 2.6 %back_proj.3.rest_0_.right_ref.refs_2_ = f32[512,768]{1,0:T(8,128)S(1)} custom-call(f32[3,1536]{1,0:T(4,128)S(1)} %get-tuple-element.59.vec_ref, bf16[1536,3072]{1,0:T(8,128)(2,1)S(1)} %bitcast.7, bf16[512,768]{1,0:T(8,128)(2,1)S(1)} %get-tuple-element.75.rest_0_, bf16[512,768]{1,0:T(8,128)(2,1)S(1)} %get-tuple-element.76.rest_1_, ...), custom_call_target="tpu_custom_call" | custom-call | bytes 7800000 | tf_op jit(solution)/shard_map/back_proj/pallas_call | solution.py:712
  93.5 2.3 %collective-permute-done.22.refs_1_ = bf16[2,48,1536]{2,1,0:T(8,128)(2,1)S(1)} collective-permute-done((bf16[2,48,1536]{2,1,0:T(8,128)(2,1)S(1)}, bf16[2,48,1536]{2,1,0:T(8,128)(2,1)S(1)}, u32[]{:S(2)}, u32[]{:S(2)}) %collective-permute-start.22) | collective-permute-done | bytes 294944 | tf_op jit(solution)/shard_map/ppermute | solution.py:765
  95.8 0.1 merge.7
  95.9 2.2 %collective-permute-start.23 = (bf16[1,48,1536]{2,1,0:T(8,128)(2,1)S(1)}, bf16[1,48,1536]{2,1,0:T(8,128)(2,1)S(1)}, u32[]{:S(2)}, u32[]{:S(2)}) collective-permute-start(bf16[1,48,1536]{2,1,0:T(8,128)(2,1)S(1)} %get-tuple-element.90), channel_id=1, source_target_pairs={{0,16},{1,17},{2,18},{3,19},{4,20},{5,21},{6,22},{7,23},{8,24},{9,... | collective-permute-start | bytes 442376 | tf_op jit(solution)/shard_map/ppermute | solution.py:765
  98.1 1.5 %collective-permute-start.24 = (bf16[32,1536]{1,0:T(8,128)(2,1)S(1)}, bf16[32,1536]{1,0:T(8,128)(2,1)S(1)}, u32[]{:S(2)}, u32[]{:S(2)}) collective-permute-start(bf16[32,1536]{1,0:T(8,128)(2,1)S(1)} %add.27.rest_0_.c_ref), channel_id=1, source_target_pairs={{0,4},{1,5},{2,6},{3,7},{4,0},{5,1},{6,2},{7,3},{8,12},{9,13},{10,... | collective-permute-start | bytes 294920 | tf_op jit(solution)/shard_map/ppermute | solution.py:765
  99.6 2.3 %back_norm.1 = (bf16[512,1536]{1,0:T(8,128)(2,1)}, f32[8,128]{1,0:T(8,128)S(1)}) custom-call(bf16[512,1536]{1,0:T(8,128)(2,1)S(1)} %get-tuple-element.65.hat_ref, f32[512,1]{1,0:T(8,128)S(1)} %get-tuple-element.66.rstd_ref, bf16[512,1536]{1,0:T(8,128)(2,1)S(1)} %bitcast.12, f32[512,768]{1,0:T(8,128)S(1)} %back_proj.2.rest_0_.left_ref, ...), custom_call_target="tpu_custom_call" | custom-call | bytes 9000000 | tf_op jit(solution)/shard_map/back_norm/pallas_call | solution.py:751
  101.9 0.9 collective-permute-done.24.d_ref
  102.8 1.0 collective-permute-done.23
  103.8 0.8 last_add.1
  (37 shorter events, 0.2 us)
Async XLA Ops:
  0.6 9.9 %copy-start.3 = (f32[32,1536]{1,0:T(8,128)S(1)}, f32[32,1536]{1,0:T(8,128)}, u32[]{:S(2)}) copy-start(f32[32,1536]{1,0:T(8,128)} %k_ref.7) | copy-start | bytes 589828
  9.1 6.4 %collective-permute-start = (bf16[2,48,1536]{2,1,0:T(8,128)(2,1)S(1)}, bf16[2,48,1536]{2,1,0:T(8,128)(2,1)S(1)}, u32[]{:S(2)}, u32[]{:S(2)}) collective-permute-start(bf16[2,48,1536]{2,1,0:T(8,128)(2,1)S(1)} %get-tuple-element.52), channel_id=1, source_target_pairs={{0,1},{1,0},{2,3},{3,2},{4,5},{5,4},{6,7},{7,6},{8,9},{9,8},{10,11... | collective-permute-start | bytes 884744 | tf_op jit(solution)/shard_map/ppermute | solution.py:765
  9.7 5.9 %collective-permute-start.1 = (bf16[2,48,1536]{2,1,0:T(8,128)(2,1)S(1)}, bf16[2,48,1536]{2,1,0:T(8,128)(2,1)S(1)}, u32[]{:S(2)}, u32[]{:S(2)}) collective-permute-start(bf16[2,48,1536]{2,1,0:T(8,128)(2,1)S(1)} %get-tuple-element.53), channel_id=1, source_target_pairs={{1,2},{2,1},{3,4},{4,3},{5,6},{6,5},{7,8},{8,7},{9,10},{10,9},{11,... | collective-permute-start | bytes 884744 | tf_op jit(solution)/shard_map/ppermute | solution.py:834
  10.5 16.1 %copy-start.1 = (bf16[2,256,1536]{2,1,0:T(8,128)(2,1)S(1)}, bf16[2,256,1536]{2,1,0:T(8,128)(2,1)}, u32[]{:S(2)}) copy-start(bf16[2,256,1536]{2,1,0:T(8,128)(2,1)} %param.15) | copy-start | bytes 4718596
  15.5 11.1 %copy-start = (bf16[1536,1536]{1,0:T(8,128)(2,1)S(1)}, bf16[1536,1536]{1,0:T(8,128)(2,1)}, u32[]{:S(2)}) copy-start(bf16[1536,1536]{1,0:T(8,128)(2,1)} %w_ref.11) | copy-start | bytes 14155780
  17.2 6.3 %collective-permute-start.2 = (f32[2,1536]{1,0:T(2,128)S(1)}, f32[2,1536]{1,0:T(2,128)S(1)}, u32[]{:S(2)}, u32[]{:S(2)}) collective-permute-start(f32[2,1536]{1,0:T(2,128)S(1)} %get-tuple-element.57.own_ref), channel_id=1, source_target_pairs={{0,1},{1,0},{2,3},{3,2},{4,5},{5,4},{6,7},{7,6},{8,9},{9,8},{10,11... | collective-permute-start | bytes 36872 | tf_op jit(solution)/shard_map/ppermute | solution.py:765
  23.5 4.8 %collective-permute-start.3 = (f32[2,1536]{1,0:T(2,128)S(1)}, f32[2,1536]{1,0:T(2,128)S(1)}, u32[]{:S(2)}, u32[]{:S(2)}) collective-permute-start(f32[2,1536]{1,0:T(2,128)S(1)} %add.14.rest_0_.own_ref), channel_id=1, source_target_pairs={{0,2},{1,3},{2,0},{3,1},{4,6},{5,7},{6,4},{7,5},{8,10},{9,11},{10,... | collective-permute-start | bytes 36872 | tf_op jit(solution)/shard_map/ppermute | solution.py:765
  28.3 3.7 %collective-permute-start.4 = (f32[2,1536]{1,0:T(2,128)S(1)}, f32[2,1536]{1,0:T(2,128)S(1)}, u32[]{:S(2)}, u32[]{:S(2)}) collective-permute-start(f32[2,1536]{1,0:T(2,128)S(1)} %add.15.rest_0_.own_ref), channel_id=1, source_target_pairs={{0,4},{1,5},{2,6},{3,7},{4,0},{5,1},{6,2},{7,3},{8,12},{9,13},{10,... | collective-permute-start | bytes 36872 | tf_op jit(solution)/shard_map/ppermute | solution.py:765
  32.0 3.7 %collective-permute-start.5 = (f32[2,1536]{1,0:T(2,128)S(1)}, f32[2,1536]{1,0:T(2,128)S(1)}, u32[]{:S(2)}, u32[]{:S(2)}) collective-permute-start(f32[2,1536]{1,0:T(2,128)S(1)} %add.16.own_ref), channel_id=1, source_target_pairs={{0,8},{1,9},{2,10},{3,11},{4,12},{5,13},{6,14},{7,15},{8,0},{9,1},... | collective-permute-start | bytes 36872 | tf_op jit(solution)/shard_map/ppermute | solution.py:765
  35.7 4.6 %collective-permute-start.6 = (f32[2,1536]{1,0:T(2,128)S(1)}, f32[2,1536]{1,0:T(2,128)S(1)}, u32[]{:S(2)}, u32[]{:S(2)}) collective-permute-start(f32[2,1536]{1,0:T(2,128)S(1)} %add.17.rest_0_.own_ref), channel_id=1, source_target_pairs={{0,16},{1,17},{2,18},{3,19},{4,20},{5,21},{6,22},{7,23},{8,24},{9,... | collective-permute-start | bytes 36872 | tf_op jit(solution)/shard_map/ppermute | solution.py:765
  40.3 4.3 %copy-start.2 = (bf16[2,256,1536]{2,1,0:T(8,128)(2,1)S(1)}, bf16[2,256,1536]{2,1,0:T(8,128)(2,1)}, u32[]{:S(2)}) copy-start(bf16[2,256,1536]{2,1,0:T(8,128)(2,1)} %param.8) | copy-start | bytes 4718596
  42.1 8.6 %collective-permute-start.11 = (bf16[512,1536]{1,0:T(8,128)(2,1)S(1)}, bf16[512,1536]{1,0:T(8,128)(2,1)S(1)}, u32[]{:S(2)}, u32[]{:S(2)}) collective-permute-start(bf16[512,1536]{1,0:T(8,128)(2,1)S(1)} %get-tuple-element.60.act_ref.acta_ref), channel_id=1, source_target_pairs={{0,1},{1,0},{2,3},{3,2},{4,5},{5,4},{6,7},{7,6},{8,9},{9,8},{10,11... | collective-permute-start | bytes 4718600 | tf_op jit(solution)/shard_map/ppermute | solution.py:765
  42.2 8.6 %collective-permute-start.10 = (bf16[16,48,512]{2,1,0:T(8,128)(2,1)S(1)}, bf16[16,48,512]{2,1,0:T(8,128)(2,1)S(1)}, u32[]{:S(2)}, u32[]{:S(2)}) collective-permute-start(bf16[16,48,512]{2,1,0:T(8,128)(2,1)S(1)} %get-tuple-element.69), channel_id=1, source_target_pairs={{0,1},{1,0},{2,3},{3,2},{4,5},{5,4},{6,7},{7,6},{8,9},{9,8},{10,11... | collective-permute-start | bytes 2359304 | tf_op jit(solution)/shard_map/ppermute | solution.py:765
  42.7 4.3 %collective-permute-start.7 = (f32[2,1536]{1,0:T(2,128)S(1)}, f32[2,1536]{1,0:T(2,128)S(1)}, u32[]{:S(2)}, u32[]{:S(2)}) collective-permute-start(f32[2,1536]{1,0:T(2,128)S(1)} %get-tuple-element.61.rest_0_.own_ref), channel_id=1, source_target_pairs={{0,2},{1,3},{2,0},{3,1},{4,6},{5,7},{6,4},{7,5},{8,10},{9,11},{10,... | collective-permute-start | bytes 36872 | tf_op jit(solution)/shard_map/ppermute | solution.py:765
  46.9 3.8 %collective-permute-start.8 = (f32[2,1536]{1,0:T(2,128)S(1)}, f32[2,1536]{1,0:T(2,128)S(1)}, u32[]{:S(2)}, u32[]{:S(2)}) collective-permute-start(f32[2,1536]{1,0:T(2,128)S(1)} %add.19.rest_1_.own_ref), channel_id=1, source_target_pairs={{0,4},{1,5},{2,6},{3,7},{4,0},{5,1},{6,2},{7,3},{8,12},{9,13},{10,... | collective-permute-start | bytes 36872 | tf_op jit(solution)/shard_map/ppermute | solution.py:765
  53.3 18.8 %collective-permute-start.20 = (bf16[8,48,768]{2,1,0:T(8,128)(2,1)S(1)}, bf16[8,48,768]{2,1,0:T(8,128)(2,1)S(1)}, u32[]{:S(2)}, u32[]{:S(2)}) collective-permute-start(bf16[8,48,768]{2,1,0:T(8,128)(2,1)S(1)} %get-tuple-element.84), channel_id=1, source_target_pairs={{0,4},{1,5},{2,6},{3,7},{4,0},{5,1},{6,2},{7,3},{8,12},{9,13},{10,... | collective-permute-start | bytes 1769480 | tf_op jit(solution)/shard_map/ppermute | solution.py:765
  54.6 19.0 %collective-permute-start.18 = (bf16[8,48,768]{2,1,0:T(8,128)(2,1)S(1)}, bf16[8,48,768]{2,1,0:T(8,128)(2,1)S(1)}, u32[]{:S(2)}, u32[]{:S(2)}) collective-permute-start(bf16[8,48,768]{2,1,0:T(8,128)(2,1)S(1)} %get-tuple-element.70.rest_0_), channel_id=1, source_target_pairs={{0,2},{1,3},{2,0},{3,1},{4,6},{5,7},{6,4},{7,5},{8,10},{9,11},{10,... | collective-permute-start | bytes 1769480 | tf_op jit(solution)/shard_map/ppermute | solution.py:765
  55.4 3.7 %collective-permute-start.9 = (f32[2,1536]{1,0:T(2,128)S(1)}, f32[2,1536]{1,0:T(2,128)S(1)}, u32[]{:S(2)}, u32[]{:S(2)}) collective-permute-start(f32[2,1536]{1,0:T(2,128)S(1)} %add.20.rest_0_.own_ref), channel_id=1, source_target_pairs={{0,8},{1,9},{2,10},{3,11},{4,12},{5,13},{6,14},{7,15},{8,0},{9,1},... | collective-permute-start | bytes 36872 | tf_op jit(solution)/shard_map/ppermute | solution.py:765
  59.1 4.6 %collective-permute-start.12 = (f32[2,1536]{1,0:T(2,128)S(1)}, f32[2,1536]{1,0:T(2,128)S(1)}, u32[]{:S(2)}, u32[]{:S(2)}) collective-permute-start(f32[2,1536]{1,0:T(2,128)S(1)} %add.21.own_ref), channel_id=1, source_target_pairs={{0,16},{1,17},{2,18},{3,19},{4,20},{5,21},{6,22},{7,23},{8,24},{9,... | collective-permute-start | bytes 36872 | tf_op jit(solution)/shard_map/ppermute | solution.py:765
  63.7 1.2 %collective-permute-start.13 = (f32[2,1536]{1,0:T(2,128)S(1)}, f32[2,1536]{1,0:T(2,128)S(1)}, u32[]{:S(2)}, u32[]{:S(2)}) collective-permute-start(f32[2,1536]{1,0:T(2,128)S(1)} %add.22.own_ref), channel_id=1, source_target_pairs={{0,1},{1,0},{2,3},{3,2},{4,5},{5,4},{6,7},{7,6},{8,9},{9,8},{10,11... | collective-permute-start | bytes 36872 | tf_op jit(solution)/shard_map/ppermute | solution.py:765
  72.0 2.6 %collective-permute-start.14 = (bf16[32,1536]{1,0:T(8,128)(2,1)S(1)}, bf16[32,1536]{1,0:T(8,128)(2,1)S(1)}, u32[]{:S(2)}, u32[]{:S(2)}) collective-permute-start(bf16[32,1536]{1,0:T(8,128)(2,1)S(1)} %get-tuple-element.74.own_ref), channel_id=1, source_target_pairs={{0,1},{1,0},{2,3},{3,2},{4,5},{5,4},{6,7},{7,6},{8,9},{9,8},{10,11... | collective-permute-start | bytes 294920 | tf_op jit(solution)/shard_map/ppermute | solution.py:765
  72.2 15.6 %collective-permute-start.21 = (bf16[4,48,768]{2,1,0:T(8,128)(2,1)S(1)}, bf16[4,48,768]{2,1,0:T(8,128)(2,1)S(1)}, u32[]{:S(2)}, u32[]{:S(2)}) collective-permute-start(bf16[4,48,768]{2,1,0:T(8,128)(2,1)S(1)} %get-tuple-element.86), channel_id=1, source_target_pairs={{0,2},{1,3},{2,0},{3,1},{4,6},{5,7},{6,4},{7,5},{8,10},{9,11},{10,... | collective-permute-start | bytes 884744 | tf_op jit(solution)/shard_map/ppermute | solution.py:765
  73.7 14.2 %collective-permute-start.19 = (bf16[4,48,768]{2,1,0:T(8,128)(2,1)S(1)}, bf16[4,48,768]{2,1,0:T(8,128)(2,1)S(1)}, u32[]{:S(2)}, u32[]{:S(2)}) collective-permute-start(bf16[4,48,768]{2,1,0:T(8,128)(2,1)S(1)} %get-tuple-element.82), channel_id=1, source_target_pairs={{0,4},{1,5},{2,6},{3,7},{4,0},{5,1},{6,2},{7,3},{8,12},{9,13},{10,... | collective-permute-start | bytes 884744 | tf_op jit(solution)/shard_map/ppermute | solution.py:765
  74.6 8.5 %collective-permute-start.15 = (bf16[32,1536]{1,0:T(8,128)(2,1)S(1)}, bf16[32,1536]{1,0:T(8,128)(2,1)S(1)}, u32[]{:S(2)}, u32[]{:S(2)}) collective-permute-start(bf16[32,1536]{1,0:T(8,128)(2,1)S(1)} %add.24.rest_0_.own_ref), channel_id=1, source_target_pairs={{0,16},{1,17},{2,18},{3,19},{4,20},{5,21},{6,22},{7,23},{8,24},{9,... | collective-permute-start | bytes 294920 | tf_op jit(solution)/shard_map/ppermute | solution.py:765
  77.4 7.4 %slice-start = ((s8[9437184]{0:T(1024)(128)(4,1)}), s8[4194304]{0:T(1024)(128)(4,1)S(1)}, s32[]{:S(2)}) async-start(s8[9437184]{0:T(1024)(128)(4,1)} %bitcast.6), calls=%async_computation | async-start | bytes 8388608
  77.4 7.4 %slice-start.1 = ((s8[9437184]{0:T(1024)(128)(4,1)}), s8[4194304]{0:T(1024)(128)(4,1)S(1)}, s32[]{:S(2)}) async-start(s8[9437184]{0:T(1024)(128)(4,1)} %bitcast.6), calls=%async_computation.1 | async-start | bytes 8388608
  80.1 4.7 %slice-start.2 = ((s8[9437184]{0:T(1024)(128)(4,1)}), s8[1048576]{0:T(1024)(128)(4,1)S(1)}, s32[]{:S(2)}) async-start(s8[9437184]{0:T(1024)(128)(4,1)} %bitcast.6), calls=%async_computation.2 | async-start | bytes 2097152
  83.1 4.7 %collective-permute-start.16 = (bf16[32,1536]{1,0:T(8,128)(2,1)S(1)}, bf16[32,1536]{1,0:T(8,128)(2,1)S(1)}, u32[]{:S(2)}, u32[]{:S(2)}) collective-permute-start(bf16[32,1536]{1,0:T(8,128)(2,1)S(1)} %add.25.rest_4_.own_ref), channel_id=1, source_target_pairs={{0,8},{1,9},{2,10},{3,11},{4,12},{5,13},{6,14},{7,15},{8,0},{9,1},... | collective-permute-start | bytes 294920 | tf_op jit(solution)/shard_map/ppermute | solution.py:765
  88.0 7.9 %collective-permute-start.22 = (bf16[2,48,1536]{2,1,0:T(8,128)(2,1)S(1)}, bf16[2,48,1536]{2,1,0:T(8,128)(2,1)S(1)}, u32[]{:S(2)}, u32[]{:S(2)}) collective-permute-start(bf16[2,48,1536]{2,1,0:T(8,128)(2,1)S(1)} %get-tuple-element.88), channel_id=1, source_target_pairs={{0,8},{1,9},{2,10},{3,11},{4,12},{5,13},{6,14},{7,15},{8,0},{9,1},... | collective-permute-start | bytes 884744 | tf_op jit(solution)/shard_map/ppermute | solution.py:765
  89.6 8.4 %collective-permute-start.17 = (bf16[32,1536]{1,0:T(8,128)(2,1)S(1)}, bf16[32,1536]{1,0:T(8,128)(2,1)S(1)}, u32[]{:S(2)}, u32[]{:S(2)}) collective-permute-start(bf16[32,1536]{1,0:T(8,128)(2,1)S(1)} %add.26.rest_4_.own_ref.refs_4_), channel_id=1, source_target_pairs={{0,2},{1,3},{2,0},{3,1},{4,6},{5,7},{6,4},{7,5},{8,10},{9,11},{10,... | collective-permute-start | bytes 294920 | tf_op jit(solution)/shard_map/ppermute | solution.py:765
  95.9 7.9 %collective-permute-start.23 = (bf16[1,48,1536]{2,1,0:T(8,128)(2,1)S(1)}, bf16[1,48,1536]{2,1,0:T(8,128)(2,1)S(1)}, u32[]{:S(2)}, u32[]{:S(2)}) collective-permute-start(bf16[1,48,1536]{2,1,0:T(8,128)(2,1)S(1)} %get-tuple-element.90), channel_id=1, source_target_pairs={{0,16},{1,17},{2,18},{3,19},{4,20},{5,21},{6,22},{7,23},{8,24},{9,... | collective-permute-start | bytes 442376 | tf_op jit(solution)/shard_map/ppermute | solution.py:765
  98.1 4.7 %collective-permute-start.24 = (bf16[32,1536]{1,0:T(8,128)(2,1)S(1)}, bf16[32,1536]{1,0:T(8,128)(2,1)S(1)}, u32[]{:S(2)}, u32[]{:S(2)}) collective-permute-start(bf16[32,1536]{1,0:T(8,128)(2,1)S(1)} %add.27.rest_0_.c_ref), channel_id=1, source_target_pairs={{0,4},{1,5},{2,6},{3,7},{4,0},{5,1},{6,2},{7,3},{8,12},{9,13},{10,... | collective-permute-start | bytes 294920 | tf_op jit(solution)/shard_map/ppermute | solution.py:765
